TPU v7x, 512 devices: a whole 4x4x16 slice. The times are simulated.
512 devices in a mesh: sy: 32 (over x_lo, z), sx: 16 (over y, x_hi, core).
Axes of the slice: x: 4 (x_hi: 2, x_lo: 2; x = x_hi * 2 + x_lo), y: 4, z: 16, core: 2. Of those that a mesh axis runs over, the one named last changes fastest.
Arguments:
- object_field: float32 [2, 2, 4096, 2048], P(None, None, 'sy', 'sx'), may hold values from -6 to 6
- probe_modes: float32 [2, 4, 128, 128], replicated, may hold values from -5 to 5
- prop_taps: float32 [2, 2, 31], replicated, may hold values from -2 to 2
- measured: float32 [32, 16, 2, 128, 128], P('sy', 'sx'), may hold values from 0 to 2
- offsets: int32 [32, 16, 2, 2], P('sy', 'sx'), may hold values from 0 to 127
- counts: int32 [32, 16], P('sy', 'sx'), may hold values from 1 to 2, as said below
Outputs:
- object_grad: float32 [2, 2, 4096, 2048], P(None, None, 'sy', 'sx')
- probe_grad: float32 [2, 4, 128, 128], replicated
Inputs may be any that keep to these rules, and one draw needn't show every extreme that they name: Slots j < counts of a tile are live, the others unused; in every draw some tile has all 2 slots live.
All inputs are finite; a program needn't handle non-finite values.
Results may differ from a plain program's by a relative error of at most 0.0003.
Values sent between devices are 32-bit elements; how exact they have to be, the bound alone decides.
No kernel may reach another device: no remote copies, remote signals or barrier semaphores. Data moves between devices by JAX's collectives and lax.ppermute only.
A program may use at most 64 MiB of HBM per device.

v0:
```python
import math

import jax
import jax.numpy as jnp
from jax import lax
from jax.sharding import PartitionSpec as P

HIGHEST_PRECISION = lax.Precision.HIGHEST


def padded_2(block, sides, width):
    for axis, dim in sides:
        count = lax.axis_size(axis)
        forward = [(i, i + 1) for i in range(count - 1)]
        backward = [(target, source) for source, target in forward]
        low = lax.ppermute(
            lax.slice_in_dim(block, block.shape[dim] - width, None, axis=dim), axis, forward
        )
        high = lax.ppermute(lax.slice_in_dim(block, 0, width, axis=dim), axis, backward)
        block = jnp.concatenate([low, block, high], axis=dim)
    return block


def band_matrix(taps_pair, extent):
    count_taps = taps_pair.shape[-1]
    tap_reach = count_taps // 2
    tap_index = lax.broadcasted_iota(jnp.int32, (count_taps, extent, extent), 0)
    row_index = lax.broadcasted_iota(jnp.int32, (count_taps, extent, extent), 1)
    col_index = lax.broadcasted_iota(jnp.int32, (count_taps, extent, extent), 2)
    select = col_index - row_index + tap_reach == tap_index
    real_part = jnp.sum(jnp.where(select, taps_pair[0][:, None, None], 0.0), axis=0)
    imag_part = jnp.sum(jnp.where(select, taps_pair[1][:, None, None], 0.0), axis=0)
    return (real_part, imag_part)


def operators(prop_taps, extent):
    row_real, row_imag = band_matrix(prop_taps[0], extent)
    col_real, col_imag = band_matrix(prop_taps[1], extent)
    left_op = jnp.stack([jnp.stack([row_real, -row_imag]), jnp.stack([row_imag, row_real])])
    right_op = jnp.stack([jnp.stack([col_real, col_imag]), jnp.stack([-col_imag, col_real])])
    return (left_op, right_op)


def propagate(wavefield, left_op, right_op):
    rows_done = jnp.einsum("abrk,bmkq->amrq", left_op, wavefield, precision=HIGHEST_PRECISION)
    return jnp.einsum("amrk,abqk->bmrq", rows_done, right_op, precision=HIGHEST_PRECISION)


def slot_loss(window, probe_modes, target, left_op, right_op):
    wavefield = probe_modes
    for layer_index in range(window.shape[1]):
        object_real = window[0, layer_index]
        object_imag = window[1, layer_index]
        modulated = jnp.stack(
            [
                wavefield[0] * object_real - wavefield[1] * object_imag,
                wavefield[0] * object_imag + wavefield[1] * object_real,
            ]
        )
        wavefield = propagate(modulated, left_op, right_op)
    intensity = jnp.sum(wavefield[0] * wavefield[0] + wavefield[1] * wavefield[1], axis=0)
    return 0.5 * jnp.sum((intensity - target) ** 2)


def slot_gradients(window, probe_modes, target, weight, left_op, right_op):
    loss_value, pullback = jax.vjp(
        lambda window_in, probe_in: slot_loss(window_in, probe_in, target, left_op, right_op),
        window,
        probe_modes,
    )
    return pullback(weight)


def body(object_field, probe_modes, prop_taps, measured, offsets, counts):
    window_size = probe_modes.shape[-1]
    half_width = window_size // 2
    layers = object_field.shape[1]
    left_op, right_op = operators(prop_taps, window_size)
    padded = padded_2(object_field, (("sy", 2), ("sx", 3)), half_width)
    live_count = counts[0, 0]
    anchor = jnp.zeros((), jnp.int32)
    targets = measured[0, 0]

    def accumulate(position, carry_state):
        grad_padded, probe_accum = carry_state
        row_start = offsets[0, 0, position, 0]
        col_start = offsets[0, 0, position, 1]
        corner = (anchor, anchor, row_start, col_start)
        window = lax.dynamic_slice(padded, corner, (2, layers, window_size, window_size))
        target = lax.dynamic_index_in_dim(targets, position, 0, keepdims=False)
        weight = (position < live_count).astype(padded.dtype)
        window_grad, probe_part = slot_gradients(
            window, probe_modes, target, weight, left_op, right_op
        )
        current = lax.dynamic_slice(grad_padded, corner, window.shape)
        grad_padded = lax.dynamic_update_slice(grad_padded, current + window_grad, corner)
        return (grad_padded, probe_accum + probe_part)

    start_state = (jnp.zeros_like(padded), jnp.zeros_like(probe_modes))
    final_state = lax.fori_loop(0, targets.shape[0], accumulate, start_state)
    grad_padded, probe_accum = final_state
    rim_rows = jnp.concatenate(
        [grad_padded[:, :, :half_width], grad_padded[:, :, -half_width:]], axis=2
    )
    extended = padded_2(rim_rows, (("sy", 2),), half_width)
    interior = grad_padded[:, :, half_width:-half_width]
    interior = interior.at[:, :, :half_width].add(extended[:, :, :half_width])
    interior = interior.at[:, :, -half_width:].add(extended[:, :, -half_width:])
    rim_cols = jnp.concatenate([interior[..., :half_width], interior[..., -half_width:]], axis=3)
    widened = padded_2(rim_cols, (("sx", 3),), half_width)
    result = interior[..., half_width:-half_width]
    result = result.at[..., :half_width].add(widened[..., :half_width])
    result = result.at[..., -half_width:].add(widened[..., -half_width:])
    tile_count = lax.axis_size("sy") * lax.axis_size("sx")
    normalizer = 1.0 / math.sqrt(tile_count)
    summed = lax.psum(probe_accum, ("sy", "sx"))
    return (result, summed * normalizer)


def solution(mesh):
    return jax.shard_map(
        body,
        mesh=mesh,
        in_specs=(
            P(None, None, "sy", "sx"),
            P(),
            P(),
            P("sy", "sx", None, None, None),
            P("sy", "sx", None, None),
            P("sy", "sx"),
        ),
        out_specs=(P(None, None, "sy", "sx"), P()),
        check_vma=False,
    )
```

profile of v0, /device:TPU:1, one launch (start us, length us, event | category | flops | bytes accessed | tf_op | source)
XLA Modules:
  0.0 581.4 jit_solution(9722622147237656480)
XLA Ops:
  7.2 1.1 copy.114
  8.4 4.4 collective-permute-start
  12.8 1.3 collective-permute-start.1
  16.1 4.0 collective-permute-done.1
  21.2 8.0 %collective-permute-start.2 = (f32[2,2,256,64]{2,3,1,0:T(8,128)}, f32[2,2,256,64]{2,3,1,0:T(8,128)S(1)}, u32[]{:S(2)}, u32[]{:S(2)}) collective-permute-start(f32[2,2,256,64]{2,3,1,0:T(8,128)} %get-tuple-element.353), channel_id=1, source_target_pairs={{0,1},{1,2},{2,3},{3,4},{4,5},{5,6},{6,7},{7,8},{8,9},{9,10},{10,1... | collective-permute-start | bytes 786440 | tf_op jit(solution)/shard_map/ppermute | solution.py:16
  29.3 1.9 collective-permute-start.3
  32.9 5.9 %collective-permute-done.3 = f32[2,2,256,64]{2,3,1,0:T(8,128)} collective-permute-done((f32[2,2,256,64]{2,3,1,0:T(8,128)}, f32[2,2,256,64]{2,3,1,0:T(8,128)}, u32[]{:S(2)}, u32[]{:S(2)}) %collective-permute-start.3) | collective-permute-done | bytes 262176 | tf_op jit(solution)/shard_map/ppermute | solution.py:19
  38.8 2.2 pad_maximum_fusion
  41.7 43.3 %while.20 = (s32[]{:T(128)}, f32[2,2,256,256]{3,2,1,0:T(8,128)S(1)}, f32[2,4,128,128]{2,3,0,1:T(8,128)S(1)}, s32[1,1,2,2]{3,2,1,0:T(2,128)S(1)}, f32[2,4,128,128...) while((s32[]{:T(128)}, ...), condition=%wide.region_14.15_spmd.clone, body=%wide.region_4.14_spmd.clone.sunk | while | flops 3226157056 | bytes 27459924 | solution.py:100
  46.8 1.3 dynamic-slice_bitcast_fusion.5
  58.8 1.0 add_add_fusion.3
  60.1 3.1 dynamic_update_slice.9
  68.4 1.3 dynamic-slice_bitcast_fusion.5
  81.7 3.2 dynamic_update_slice.9
  85.0 3.6 collective-permute-start.4
  88.6 3.2 collective-permute-done.4
  91.9 1.3 collective-permute-start.5
  94.3 6.6 %collective-permute-done.5 = f32[2,2,64,256]{3,2,1,0:T(8,128)S(1)} collective-permute-done((f32[2,2,64,256]{3,2,1,0:T(8,128)S(1)}, f32[2,2,64,256]{3,2,1,0:T(8,128)S(1)}, u32[]{:S(2)}, u32[]{:S(2)}) %collective-permute-start.5) | collective-permute-done | bytes 262176 | tf_op jit(solution)/shard_map/ppermute | solution.py:19
  101.0 6.1 %collective-permute-start.6 = (f32[2,2,128,64]{3,2,1,0:T(8,128)S(1)}, f32[2,2,128,64]{3,2,1,0:T(8,128)S(1)}, u32[]{:S(2)}, u32[]{:S(2)}) collective-permute-start(f32[2,2,128,64]{3,2,1,0:T(8,128)S(1)} %get-tuple-element.352), channel_id=1, source_target_pairs={{0,1},{1,2},{2,3},{3,4},{4,5},{5,6},{6,7},{7,8},{8,9},{9,10},{10,1... | collective-permute-start | bytes 393224 | tf_op jit(solution)/shard_map/ppermute | solution.py:16
  107.1 452.6 %all-reduce.16.cloned.1.call-done = f32[2,4,128,128]{3,2,1,0:T(8,128)} async-done(((f32[2,4,128,128]{3,2,1,0:T(8,128)}), f32[2,4,128,128]{3,2,1,0:T(8,128)}) %all-reduce.16.cloned.1.call-update) | async-done | bytes 524304 | tf_op jit(solution)/shard_map/psum | solution.py:116
  559.7 1.9 broadcast_multiply_fusion
  561.7 3.9 collective-permute-start.7
  566.2 6.2 %collective-permute-done.7 = f32[2,2,128,64]{3,2,1,0:T(8,128)S(1)} collective-permute-done((f32[2,2,128,64]{3,2,1,0:T(8,128)S(1)}, f32[2,2,128,64]{3,2,1,0:T(8,128)S(1)}, u32[]{:S(2)}, u32[]{:S(2)}) %collective-permute-start.7) | collective-permute-done | bytes 131104 | tf_op jit(solution)/shard_map/ppermute | solution.py:19
  572.6 1.2 scatter-add.19
  (96 shorter events, 32.3 us)
Async XLA Ops:
  7.2 7.0 %copy-start.3 = (f32[2,2,31]{2,1,0:T(2,128)S(1)}, f32[2,2,31]{2,1,0:T(2,128)}, u32[]{:S(2)}) copy-start(f32[2,2,31]{2,1,0:T(2,128)} %param.18) | copy-start | bytes 1492
  7.2 552.5 %all-reduce.16.cloned.1.call-start = ((), (), s32[]{:S(2)}) async-start(), calls=%async_computation | async-start | bytes 1048576 | tf_op jit(solution)/shard_map/psum | solution.py:116
  8.4 7.7 %collective-permute-start = (f32[2,2,64,128]{2,3,1,0:T(8,128)S(1)}, f32[2,2,64,128]{2,3,1,0:T(8,128)S(1)}, u32[]{:S(2)}, u32[]{:S(2)}) collective-permute-start(f32[2,2,64,128]{2,3,1,0:T(8,128)S(1)} %get-tuple-element.355), channel_id=1, source_target_pairs={{0,16},{16,32},{32,48},{48,64},{64,80},{80,96},{96,112},{112,128},... | collective-permute-start | bytes 393224 | tf_op jit(solution)/shard_map/ppermute | solution.py:16
  12.8 7.3 %collective-permute-start.1 = (f32[2,2,64,128]{2,3,1,0:T(8,128)S(1)}, f32[2,2,64,128]{2,3,1,0:T(8,128)S(1)}, u32[]{:S(2)}, u32[]{:S(2)}) collective-permute-start(f32[2,2,64,128]{2,3,1,0:T(8,128)S(1)} %get-tuple-element.356), channel_id=1, source_target_pairs={{16,0},{32,16},{48,32},{64,48},{80,64},{96,80},{112,96},{128,112},... | collective-permute-start | bytes 393224 | tf_op jit(solution)/shard_map/ppermute | solution.py:19
  20.4 10.9 %copy-start.1 = (f32[2,4,128,128]{3,2,1,0:T(8,128)S(1)}, f32[2,4,128,128]{3,2,1,0:T(8,128)}, u32[]{:S(2)}) copy-start(f32[2,4,128,128]{3,2,1,0:T(8,128)} %param.17) | copy-start | bytes 1572868
  21.2 11.6 %collective-permute-start.2 = (f32[2,2,256,64]{2,3,1,0:T(8,128)}, f32[2,2,256,64]{2,3,1,0:T(8,128)S(1)}, u32[]{:S(2)}, u32[]{:S(2)}) collective-permute-start(f32[2,2,256,64]{2,3,1,0:T(8,128)} %get-tuple-element.353), channel_id=1, source_target_pairs={{0,1},{1,2},{2,3},{3,4},{4,5},{5,6},{6,7},{7,8},{8,9},{9,10},{10,1... | collective-permute-start | bytes 786440 | tf_op jit(solution)/shard_map/ppermute | solution.py:16
  29.3 9.5 %collective-permute-start.3 = (f32[2,2,256,64]{2,3,1,0:T(8,128)}, f32[2,2,256,64]{2,3,1,0:T(8,128)}, u32[]{:S(2)}, u32[]{:S(2)}) collective-permute-start(f32[2,2,256,64]{2,3,1,0:T(8,128)} %get-tuple-element.354), channel_id=1, source_target_pairs={{1,0},{2,1},{3,2},{4,3},{5,4},{6,5},{7,6},{8,7},{9,8},{10,9},{11,1... | collective-permute-start | bytes 786440 | tf_op jit(solution)/shard_map/ppermute | solution.py:19
  41.0 0.7 copy-start.2
  85.0 6.9 %collective-permute-start.4 = (f32[2,2,64,256]{3,2,1,0:T(8,128)S(1)}, f32[2,2,64,256]{3,2,1,0:T(8,128)S(1)}, u32[]{:S(2)}, u32[]{:S(2)}) collective-permute-start(f32[2,2,64,256]{3,2,1,0:T(8,128)S(1)} %slice.256), channel_id=1, source_target_pairs={{0,16},{16,32},{32,48},{48,64},{64,80},{80,96},{96,112},{112,128},... | collective-permute-start | bytes 786440 | tf_op jit(solution)/shard_map/ppermute | solution.py:16
  91.9 8.9 %collective-permute-start.5 = (f32[2,2,64,256]{3,2,1,0:T(8,128)S(1)}, f32[2,2,64,256]{3,2,1,0:T(8,128)S(1)}, u32[]{:S(2)}, u32[]{:S(2)}) collective-permute-start(f32[2,2,64,256]{3,2,1,0:T(8,128)S(1)} %get-tuple-element.349), channel_id=1, source_target_pairs={{16,0},{32,16},{48,32},{64,48},{80,64},{96,80},{112,96},{128,112},... | collective-permute-start | bytes 786440 | tf_op jit(solution)/shard_map/ppermute | solution.py:19
  101.0 464.6 %collective-permute-start.6 = (f32[2,2,128,64]{3,2,1,0:T(8,128)S(1)}, f32[2,2,128,64]{3,2,1,0:T(8,128)S(1)}, u32[]{:S(2)}, u32[]{:S(2)}) collective-permute-start(f32[2,2,128,64]{3,2,1,0:T(8,128)S(1)} %get-tuple-element.352), channel_id=1, source_target_pairs={{0,1},{1,2},{2,3},{3,4},{4,5},{5,6},{6,7},{7,8},{8,9},{9,10},{10,1... | collective-permute-start | bytes 393224 | tf_op jit(solution)/shard_map/ppermute | solution.py:16
  561.7 10.8 %collective-permute-start.7 = (f32[2,2,128,64]{3,2,1,0:T(8,128)S(1)}, f32[2,2,128,64]{3,2,1,0:T(8,128)S(1)}, u32[]{:S(2)}, u32[]{:S(2)}) collective-permute-start(f32[2,2,128,64]{3,2,1,0:T(8,128)S(1)} %get-tuple-element.351), channel_id=1, source_target_pairs={{1,0},{2,1},{3,2},{4,3},{5,4},{6,5},{7,6},{8,7},{9,8},{10,9},{11,1... | collective-permute-start | bytes 393224 | tf_op jit(solution)/shard_map/ppermute | solution.py:19
  573.8 0.7 copy-start
Sparse Core Ops, SparseCore 0:
  94.4 465.2 all-reduce.15
where the time goes:
time: 582 us; the launch traced here: 581 us
  waiting for transfers between devices  479 us (82%)
  starting transfers between devices  30.6 us (5%)
  local copies, waits for them, and re-layouts  19.1 us (3%)
  other arithmetic  15.7 us (3%)
  between operations  14.3 us (2%)
  matrix products  13 us (2%)
  loops' own time  9.48 us (2%)
    psum x1, waiting for transfers between devices, body(): summed = lax.psum(probe_accum, ('sy', 'sx'))  453 us
    ppermute x4, waiting for transfers between devices, padded_2(): lax.ppermute(lax.slice_in_dim(block, 0, width, axis=dim), axis, backward)  22.7 us
    ppermute x4, starting transfers between devices, padded_2(): lax.ppermute(lax.slice_in_dim(block, block.shape[dim] - width, None, axis...  22.1 us
  transfers between devices with their start and end apart: 9, of which 8 were waited for; matrix products, arithmetic and copies ran while one was open for 1% of the time, Pallas kernels for 0%

commit v1 on v0

v1 whole, which is shorter than its diff:
```python
import functools
import math

import jax
import jax.numpy as jnp
from jax import lax
from jax.experimental import pallas as pl
from jax.experimental.pallas import tpu as pltpu
from jax.sharding import Mesh
from jax.sharding import PartitionSpec as P

F32 = jnp.float32
BF16 = jnp.bfloat16
ROW_AXES = ("xl", "za", "zb")
COL_AXES = ("y", "xh", "core")
NEAR_AXES = ("xl", "zb", "y", "xh", "core")
FAR_AXES = ("za",)
VMEM_LIMIT = 40 * 1024 * 1024
TILE = 128
HALF = 64
VM = pl.BlockSpec(memory_space=pltpu.VMEM)
SM = pl.BlockSpec(memory_space=pltpu.SMEM)
FAR = pl.BlockSpec(memory_space=pltpu.HBM)


def call(kernel, out_shape, in_specs, *args, scratch=(), out_specs=None, flops=0, moved=0):
    out_shape = tuple(out_shape)
    return pl.pallas_call(
        kernel,
        out_shape=out_shape,
        in_specs=in_specs,
        out_specs=tuple(out_specs or [VM] * len(out_shape)),
        scratch_shapes=list(scratch),
        compiler_params=pltpu.CompilerParams(vmem_limit_bytes=VMEM_LIMIT),
        cost_estimate=pl.CostEstimate(flops=flops, bytes_accessed=moved, transcendentals=0),
    )(*args)


def low_lanes(shape):
    return lax.broadcasted_iota(jnp.int32, shape, len(shape) - 1) < HALF


def split(value):
    high = value.astype(BF16)
    return high, (value - high.astype(F32)).astype(BF16)


def pack_columns(real, imag):
    low = low_lanes(real.shape)
    turned = pltpu.roll(imag, HALF, 1)
    return jnp.where(low, turned, real), jnp.where(low, real, turned)


def unpack_columns(from_left, from_right):
    low = low_lanes(from_left.shape)
    real = jnp.where(low, from_right, from_left)
    imag = pltpu.roll(jnp.where(low, from_left, from_right), HALF, 1)
    return real, imag


def pack_kernel(tile, to_right, to_left, to_down, to_up):
    for s in range(2):
        to_right[s], to_left[s] = pack_columns(tile[s], tile[2 + s])
    for p in range(4):
        to_up[p] = tile[p, :HALF]
        to_down[p] = tile[p, HALF:]


def corners_kernel(from_left, from_right, beside, to_down, to_up):
    for s in range(2):
        for p, plane in zip((s, 2 + s), unpack_columns(from_left[s], from_right[s])):
            beside[p] = plane
            to_up[p] = plane[:HALF]
            to_down[p] = plane[HALF:]


def operator_kernel(taps, probe, measured, high, low, probe_near, measured_near):
    probe_near[...] = probe[...]
    measured_near[...] = measured[...]
    rows = lax.broadcasted_iota(jnp.int32, (TILE, TILE), 0)
    cols = lax.broadcasted_iota(jnp.int32, (TILE, TILE), 1)
    forward = cols - rows + 15
    backward = rows - cols + 15

    def band(axis, part, place):
        total = jnp.zeros((TILE, TILE), F32)
        for t in range(31):
            total = jnp.where(place == t, taps[axis * 62 + part * 31 + t], total)
        return total

    def put(index, blocks):
        for i in range(2):
            for j in range(2):
                h, l = split(blocks[i][j])
                where = (index, pl.ds(i * TILE, TILE), pl.ds(j * TILE, TILE))
                high[where] = h
                low[where] = l

    yr, yi = band(0, 0, forward), band(0, 1, forward)
    put(0, ((yr, -yi), (yi, yr)))
    yr, yi = band(0, 0, backward), band(0, 1, backward)
    put(2, ((yr, yi), (-yi, yr)))
    xr, xi = band(1, 0, backward), band(1, 1, backward)
    put(1, ((xr, xi), (-xi, xr)))
    xr, xi = band(1, 0, forward), band(1, 1, forward)
    put(3, ((xr, -xi), (xi, xr)))


def dot(a, b):
    return jnp.dot(a, b, preferred_element_type=F32)


def main_kernel(
    offsets, counts, tile, beside, above, below, above_beside, below_beside,
    probe, measured, op_high, op_low,
    grad_tile, grad_beside, grad_above, grad_below, probe_grad,
    object_ext, grad_ext, field_high, field_low, mid_high, mid_low, wave_one, wave_two,
):
    for p in range(4):
        for b, parts in enumerate(((above, tile, below), (above_beside, beside, below_beside))):
            object_ext[b, p, :HALF] = parts[0][p]
            object_ext[b, p, HALF:HALF + TILE] = parts[1][p]
            object_ext[b, p, HALF + TILE:] = parts[2][p]
    grad_ext[...] = jnp.zeros_like(grad_ext)

    def block(m):
        return slice(m * TILE, (m + 1) * TILE)

    def put_field(slot, m, real, imag):
        for c, value in enumerate((real, imag)):
            h, l = split(value)
            field_high[slot, block(c), block(m)] = h
            field_low[slot, block(c), block(m)] = l

    def propagate(slot, which, take):
        for n in range(2):
            cols = slice(n * 256, (n + 1) * 256)
            fh, fl = field_high[slot, :, cols], field_low[slot, :, cols]
            mid = dot(op_high[which], fh) + (dot(op_high[which], fl) + dot(op_low[which], fh))
            for k in range(2):
                for c in range(2):
                    h, l = split(mid[block(c), block(k)])
                    mid_high[slot, block(2 * n + k), block(c)] = h
                    mid_low[slot, block(2 * n + k), block(c)] = l
        for m in range(4):
            gh, gl = mid_high[slot, block(m)], mid_low[slot, block(m)]
            done = dot(gh, op_high[which + 1]) + (dot(gl, op_high[which + 1]) + dot(gh, op_low[which + 1]))
            take(m, done[:, :TILE], done[:, TILE:])

    for slot in range(2):
        u = offsets[2 * slot]
        v = offsets[2 * slot + 1]
        weight = jnp.where(slot < counts[0], 1.0, 0.0).astype(F32)

        def window(p):
            rows = [object_ext[b, p, pl.ds(u, TILE), :] for b in range(2)]
            return pltpu.roll(jnp.concatenate(rows, axis=1), lax.rem(320 - v, 256), 1)[:, :TILE]

        def spread(p, value):
            wide = jnp.concatenate([value, jnp.zeros_like(value)], axis=1)
            wide = pltpu.roll(wide, lax.rem(v + 192, 256), 1)
            for b in range(2):
                grad_ext[b, p, pl.ds(u, TILE), :] += wide[:, block(b)]

        o0r, o0i, o1r, o1i = window(0), window(2), window(1), window(3)
        for m in range(4):
            pr, pi = probe[m], probe[4 + m]
            put_field(slot, m, pr * o0r - pi * o0i, pr * o0i + pi * o0r)

        def after_first(m, wr, wi):
            wave_one[slot, m, 0] = wr
            wave_one[slot, m, 1] = wi
            put_field(slot, m, wr * o1r - wi * o1i, wr * o1i + wi * o1r)

        propagate(slot, 0, after_first)
        intensity = [None]

        def after_second(m, wr, wi):
            wave_two[slot, m, 0] = wr
            wave_two[slot, m, 1] = wi
            term = wr * wr + wi * wi
            intensity[0] = term if m == 0 else intensity[0] + term

        propagate(slot, 0, after_second)
        residual = (intensity[0] - measured[slot]) * (2.0 * weight)
        for m in range(4):
            put_field(slot, m, residual * wave_two[slot, m, 0], residual * wave_two[slot, m, 1])
        sums = [None, None]

        def add(index, value, m):
            sums[index] = value if m == 0 else sums[index] + value

        def after_third(m, hr, hi):
            wr, wi = wave_one[slot, m, 0], wave_one[slot, m, 1]
            add(0, wr * hr + wi * hi, m)
            add(1, wr * hi - wi * hr, m)
            put_field(slot, m, hr * o1r + hi * o1i, hi * o1r - hr * o1i)

        propagate(slot, 2, after_third)
        spread(1, sums[0])
        spread(3, sums[1])

        def after_fourth(m, hr, hi):
            pr, pi = probe[m], probe[4 + m]
            add(0, pr * hr + pi * hi, m)
            add(1, pr * hi - pi * hr, m)
            dr = hr * o0r + hi * o0i
            di = hi * o0r - hr * o0i
            if slot == 0:
                probe_grad[m] = dr
                probe_grad[4 + m] = di
            else:
                probe_grad[m] += dr
                probe_grad[4 + m] += di

        propagate(slot, 2, after_fourth)
        spread(0, sums[0])
        spread(2, sums[1])

    for p in range(4):
        grad_tile[p] = grad_ext[0, p, HALF:HALF + TILE]
        grad_beside[p] = grad_ext[1, p, HALF:HALF + TILE]
        for b in range(2):
            grad_above[b, p] = grad_ext[b, p, :HALF]
            grad_below[b, p] = grad_ext[b, p, HALF + TILE:]


def fold_rows_kernel(
    shares, grad_tile, grad_beside, from_up, from_down, spread_share, result, to_right, to_left
):
    share = jnp.sum(shares[...], axis=0)
    for i in range(spread_share.shape[0]):
        spread_share[i] = share
    low = low_lanes((TILE, TILE))
    for s in range(2):
        planes = []
        for p in (s, 2 + s):
            result[p, :HALF] = grad_tile[p, :HALF] + from_up[0, p]
            result[p, HALF:] = grad_tile[p, HALF:] + from_down[0, p]
            planes.append(
                jnp.concatenate(
                    [grad_beside[p, :HALF] + from_up[1, p], grad_beside[p, HALF:] + from_down[1, p]], axis=0
                )
            )
        real, imag = planes
        turned = pltpu.roll(imag, HALF, 1)
        to_right[s] = jnp.where(low, real, turned)
        to_left[s] = jnp.where(low, turned, real)


def fold_cols_kernel(scale, shares, part, from_left, from_right, spread_share, result):
    share = jnp.sum(shares[...], axis=0) * scale
    for i in range(spread_share.shape[0]):
        spread_share[i] = share
    low = low_lanes((TILE, TILE))
    for s in range(2):
        result[s] = part[s] + jnp.where(low, from_left[s], from_right[s])
        turned = pltpu.roll(jnp.where(low, from_right[s], from_left[s]), HALF, 1)
        result[2 + s] = part[2 + s] + turned


def finish_kernel(result, gathered, result_far, probe_far, sems):
    moves = [pltpu.make_async_copy(result.at[p], result_far.at[p], sems.at[p]) for p in range(4)]
    for i in range(4):
        part = pl.ds(256 * i, 256)
        moves.append(pltpu.make_async_copy(gathered.at[part], probe_far.at[part], sems.at[4 + i]))
    for move in moves:
        move.start()
    for move in moves:
        move.wait()


def shift_pairs(count):
    forward = [(i, i + 1) for i in range(count - 1)]
    return forward, [(b, a) for a, b in forward]


def f32(*shape):
    return jax.ShapeDtypeStruct(shape, F32)


def body(object_field, probe_modes, prop_taps, measured, offsets, counts):
    down, up = shift_pairs(lax.axis_size(ROW_AXES))
    right, left = shift_pairs(lax.axis_size(COL_AXES))
    tile = object_field.reshape(4, TILE, TILE)
    strip = f32(2, TILE, TILE)
    rim = f32(2, 4, HALF, TILE)
    planes = f32(4, TILE, TILE)

    half = f32(4, HALF, TILE)
    to_right, to_left, to_down, to_up = call(pack_kernel, (strip, strip, half, half), [VM], tile)
    from_left = lax.ppermute(to_right, COL_AXES, right)
    from_right = lax.ppermute(to_left, COL_AXES, left)
    above = lax.ppermute(to_down, ROW_AXES, down)
    below = lax.ppermute(to_up, ROW_AXES, up)
    ops = jax.ShapeDtypeStruct((4, 2 * TILE, 2 * TILE), BF16)
    op_high, op_low, probe, targets = call(
        operator_kernel, (ops, ops, f32(8, TILE, TILE), strip), [SM, VM, VM],
        prop_taps.reshape(-1), probe_modes.reshape(8, TILE, TILE), measured.reshape(2, TILE, TILE),
    )
    beside, to_down, to_up = call(
        corners_kernel, (planes, half, half), [VM] * 2, from_left, from_right
    )
    above_beside = lax.ppermute(to_down, ROW_AXES, down)
    below_beside = lax.ppermute(to_up, ROW_AXES, up)

    grad_tile, grad_beside, grad_above, grad_below, probe_part = call(
        main_kernel,
        (planes, planes, rim, rim, f32(8, TILE, TILE)),
        [SM, SM] + [VM] * 10,
        offsets.reshape(-1), counts.reshape(-1), tile, beside, above, below, above_beside, below_beside,
        probe, targets, op_high, op_low,
        scratch=[
            pltpu.VMEM((2, 4, 256, TILE), F32),
            pltpu.VMEM((2, 4, 256, TILE), F32),
            pltpu.VMEM((2, 256, 512), BF16),
            pltpu.VMEM((2, 256, 512), BF16),
            pltpu.VMEM((2, 512, 256), BF16),
            pltpu.VMEM((2, 512, 256), BF16),
            pltpu.VMEM((2, 4, 2, TILE, TILE), F32),
            pltpu.VMEM((2, 4, 2, TILE, TILE), F32),
        ],
        flops=3_200_000_000, moved=4_000_000,
    )

    near = lax.axis_size(NEAR_AXES)
    far = lax.axis_size(FAR_AXES)
    rows = 8 * TILE // near
    shares = lax.all_to_all(probe_part.reshape(near, rows, TILE), NEAR_AXES, 0, 0, tiled=True)
    from_down = lax.ppermute(grad_above, ROW_AXES, up)
    from_up = lax.ppermute(grad_below, ROW_AXES, down)
    spread_share, part, to_right, to_left = call(
        fold_rows_kernel, (f32(far, rows, TILE), planes, strip, strip), [VM] * 5,
        shares, grad_tile, grad_beside, from_up, from_down,
    )
    from_left = lax.ppermute(to_right, COL_AXES, right)
    from_right = lax.ppermute(to_left, COL_AXES, left)
    shares = lax.all_to_all(spread_share, FAR_AXES, 0, 0, tiled=True)
    spread_share, result = call(
        functools.partial(fold_cols_kernel, 1.0 / math.sqrt(near * far)),
        (f32(near, rows, TILE), planes), [VM] * 4, shares, part, from_left, from_right,
    )
    gathered = lax.all_to_all(spread_share, NEAR_AXES, 0, 0, tiled=True)
    result, probe_grad = call(
        finish_kernel, (planes, f32(8 * TILE, TILE)), [VM] * 2,
        result, gathered.reshape(8 * TILE, TILE),
        scratch=[pltpu.SemaphoreType.DMA((8,))], out_specs=[FAR, FAR],
    )
    return result.reshape(object_field.shape), probe_grad.reshape(probe_modes.shape)


def solution(mesh):
    fine = Mesh(mesh.devices.reshape(2, 8, 2, 4, 2, 2), ROW_AXES + COL_AXES)
    return jax.shard_map(
        body,
        mesh=fine,
        in_specs=(
            P(None, None, ROW_AXES, COL_AXES),
            P(),
            P(),
            P(ROW_AXES, COL_AXES, None, None, None),
            P(ROW_AXES, COL_AXES, None, None),
            P(ROW_AXES, COL_AXES),
        ),
        out_specs=(P(None, None, ROW_AXES, COL_AXES), P()),
        check_vma=False,
    )
```

time: 582 us -> 108 us (0.19)
  waiting for transfers between devices: 479 us -> 16.4 us
  starting transfers between devices: 30.6 us -> 55.5 us
  blocking collectives: 0 us -> 20.1 us
  local copies, waits for them, and re-layouts: 19.1 us -> 2.68 us
  other arithmetic: 15.7 us -> 0 us
  matrix products: 13 us -> 0 us
  between operations: 14.3 us -> 1.48 us
  Pallas kernels: 0 us -> 11.2 us
  loops' own time: 9.48 us -> 0 us
    psum x1 -> x0, waiting for transfers between devices: 453 us -> none  [body(): summed = lax.psum(probe_accum, ('sy', 'sx'))]
    all_to_all x0 -> x2, starting transfers between devices: none -> 25.3 us  [the longest x1 17.6 us: body(): lax.all_to_all(probe_part.reshape(near, rows, TILE), NEAR_AXES, 0, 0, til...]
    all_to_all x0 -> x1, blocking collectives: none -> 20.1 us  [body(): gathered = lax.all_to_all(spread_share, NEAR_AXES, 0, 0, tiled=True)]
    dot_general x16 -> x0, matrix products: 13 us -> none  [the longest x8 6.61 us: propagate(): jnp.einsum('abrk,bmkq->amrq', left_op, wavefield, precision=HIGHEST_PRECI...]
    pallas_call x0 -> x7, Pallas kernels: none -> 11.2 us  [call(): pl.pallas_call(kernel, out_shape=out_shape, in_specs=in_specs, out_specs=...]
    ppermute x8 -> x10, waiting for transfers between devices: 26.6 us -> 16.4 us  [the longest x2 7.14 us: body(): from_right = lax.ppermute(to_left, COL_AXES, left)]
    another operation x1 -> x0, loops' own time: 9.48 us -> none  [body(): final_state = lax.fori_loop(0, targets.shape[0], accumulate, start_state)]
    dynamic_update_slice x2 -> x0, local copies, waits for them, and re-layouts: 6.34 us -> none  [accumulate(): lax.dynamic_update_slice(grad_padded, current + window_grad, corner)]
  transfers between devices with their start and end apart: 9 -> 12, of which waited for: 8 -> 5; matrix products, arithmetic and copies ran while one was open for 1% -> 0% of each run, Pallas kernels for 0% -> 2%
where the time goes in v1:
time: 108 us; the launch traced here: 107 us
  starting transfers between devices  55.5 us (51%)
  blocking collectives  20.1 us (19%)
  waiting for transfers between devices  16.4 us (15%)
  Pallas kernels  11.2 us (10%)
  local copies, waits for them, and re-layouts  2.68 us (2%)
  between operations  1.48 us (1%)
    all_to_all x1, blocking collectives, body(): gathered = lax.all_to_all(spread_share, NEAR_AXES, 0, 0, tiled=True)  20.1 us
    all_to_all x1, starting transfers between devices, body(): lax.all_to_all(probe_part.reshape(near, rows, TILE), NEAR_AXES, 0, 0, til...  17.6 us
    ppermute x2, starting transfers between devices, body(): from_left = lax.ppermute(to_right, COL_AXES, right)  12.1 us
    pallas_call x7, Pallas kernels, call(): pl.pallas_call(kernel, out_shape=out_shape, in_specs=in_specs, out_specs=...  11.2 us
    all_to_all x1, starting transfers between devices, body(): shares = lax.all_to_all(spread_share, FAR_AXES, 0, 0, tiled=True)  7.66 us
    ppermute x2, waiting for transfers between devices, body(): from_right = lax.ppermute(to_left, COL_AXES, left)  7.14 us
    ppermute x1, waiting for transfers between devices, body(): from_up = lax.ppermute(grad_below, ROW_AXES, down)  6.52 us
    ppermute x2, starting transfers between devices, body(): from_right = lax.ppermute(to_left, COL_AXES, left)  5.96 us
  transfers between devices with their start and end apart: 12, of which 5 were waited for; matrix products, arithmetic and copies ran while one was open for 0% of the time, Pallas kernels for 2%

profile of v1, /device:TPU:1, one launch (start us, length us, event | category | flops | bytes accessed | tf_op | source)
XLA Modules:
  0.0 107.4 jit_solution(10228231659024840815)
XLA Ops:
  0.7 1.0 copy-done.1
  1.8 6.0 %collective-permute-start = (f32[2,128,128]{2,1,0:T(8,128)S(1)}, f32[2,128,128]{2,1,0:T(8,128)S(1)}, u32[]{:S(2)}, u32[]{:S(2)}) collective-permute-start(f32[2,128,128]{2,1,0:T(8,128)S(1)} %get-tuple-element.26), channel_id=1, source_target_pairs={{0,1},{1,2},{2,3},{3,4},{4,5},{5,6},{6,7},{7,8},{8,9},{9,10},{10,1... | collective-permute-start | bytes 393224 | tf_op jit(solution)/shard_map/ppermute | solution.py:292
  7.8 4.0 %collective-permute-start.1 = (f32[2,128,128]{2,1,0:T(8,128)S(1)}, f32[2,128,128]{2,1,0:T(8,128)S(1)}, u32[]{:S(2)}, u32[]{:S(2)}) collective-permute-start(f32[2,128,128]{2,1,0:T(8,128)S(1)} %get-tuple-element.27), channel_id=1, source_target_pairs={{1,0},{2,1},{3,2},{4,3},{5,4},{6,5},{7,6},{8,7},{9,8},{10,9},{11,1... | collective-permute-start | bytes 393224 | tf_op jit(solution)/shard_map/ppermute | solution.py:293
  11.9 1.4 %collective-permute-start.2 = (f32[4,64,128]{2,1,0:T(8,128)S(1)}, f32[4,64,128]{2,1,0:T(8,128)S(1)}, u32[]{:S(2)}, u32[]{:S(2)}) collective-permute-start(f32[4,64,128]{2,1,0:T(8,128)S(1)} %get-tuple-element.29), channel_id=1, source_target_pairs={{0,16},{16,32},{32,48},{48,64},{64,80},{80,96},{96,112},{112,128},... | collective-permute-start | bytes 393224 | tf_op jit(solution)/shard_map/ppermute | solution.py:294
  13.3 1.3 %collective-permute-start.3 = (f32[4,64,128]{2,1,0:T(8,128)S(1)}, f32[4,64,128]{2,1,0:T(8,128)S(1)}, u32[]{:S(2)}, u32[]{:S(2)}) collective-permute-start(f32[4,64,128]{2,1,0:T(8,128)S(1)} %get-tuple-element.30), channel_id=1, source_target_pairs={{16,0},{32,16},{48,32},{64,48},{80,64},{96,80},{112,96},{128,112},... | collective-permute-start | bytes 393224 | tf_op jit(solution)/shard_map/ppermute | solution.py:295
  14.6 1.0 collective-permute-done.1.from_right
  15.7 3.5 %collective-permute-start.4 = (f32[4,64,128]{2,1,0:T(8,128)S(1)}, f32[4,64,128]{2,1,0:T(8,128)S(1)}, u32[]{:S(2)}, u32[]{:S(2)}) collective-permute-start(f32[4,64,128]{2,1,0:T(8,128)S(1)} %get-tuple-element.31), channel_id=1, source_target_pairs={{0,16},{16,32},{32,48},{48,64},{64,80},{80,96},{96,112},{112,128},... | collective-permute-start | bytes 393224 | tf_op jit(solution)/shard_map/ppermute | solution.py:304
  19.3 1.3 %collective-permute-start.5 = (f32[4,64,128]{2,1,0:T(8,128)S(1)}, f32[4,64,128]{2,1,0:T(8,128)S(1)}, u32[]{:S(2)}, u32[]{:S(2)}) collective-permute-start(f32[4,64,128]{2,1,0:T(8,128)S(1)} %get-tuple-element.32), channel_id=1, source_target_pairs={{16,0},{32,16},{48,32},{64,48},{80,64},{96,80},{112,96},{128,112},... | collective-permute-start | bytes 393224 | tf_op jit(solution)/shard_map/ppermute | solution.py:305
  22.0 0.9 copy-done.3
  22.9 2.1 %shard_map.79 = (bf16[4,256,256]{2,1,0:T(8,128)(2,1)S(1)}, bf16[4,256,256]{2,1,0:T(8,128)(2,1)S(1)}, f32[8,128,128]{2,1,0:T(8,128)S(1)}, f32[2,128,128]{2,1,0:T(8,128)S(1)}) custom-call(f32[124]{0:T(128)S(1)} %reshape.37.taps, f32[8,128,128]{2,1,0:T(8,128)S(1)} %bitcast.10, f32[2,128,128]{2,1,0:T(8,128)S(1)} %bitcast.13), custom_call_target="tpu_custom_call" | custom-call | tf_op jit(solution)/shard_map/pallas_call | solution.py:28
  25.0 1.1 %collective-permute-done.5.below_beside = f32[4,64,128]{2,1,0:T(8,128)S(1)} collective-permute-done((f32[4,64,128]{2,1,0:T(8,128)S(1)}, f32[4,64,128]{2,1,0:T(8,128)S(1)}, u32[]{:S(2)}, u32[]{:S(2)}) %collective-permute-start.5) | collective-permute-done | bytes 131104 | tf_op jit(solution)/shard_map/ppermute | solution.py:305
  26.1 7.2 %shard_map.80 = (f32[4,128,128]{2,1,0:T(8,128)S(1)}, f32[4,128,128]{2,1,0:T(8,128)S(1)}, f32[2,4,64,128]{3,2,1,0:T(8,128)S(1)}, f32[2,4,64,128]{3,2,1,0:T(8,128)S(1)}, f32[8,128,128]{2,1,0:T(8,128)}) custom-call(s32[4]{0:T(128)S(1)} %reshape.34.offsets, s32[1]{0:T(128)} %bitcast.8.counts, f32[4,128,128]{2,1,0:T(8,128)S(1)} %bitcast.12, ...), custom_call_target="tpu_custom_call" | custom-call | flops 3200000000 | bytes 4000000 | tf_op jit(solution)/shard_map/pallas_call | solution.py:28
  33.3 17.6 %all-to-all-start = ((f32[64,16,128]{2,1,0:T(8,128)}), f32[64,16,128]{2,1,0:T(8,128)S(1)}, u32[]{:S(2)}, u32[]{:S(2)}) async-start(f32[64,16,128]{2,1,0:T(8,128)} %bitcast.4), calls=%async_computation | async-start | bytes 1048576 | tf_op jit(solution)/shard_map/all_to_all | solution.py:329
  50.9 3.3 %collective-permute-start.6 = (f32[2,4,64,128]{3,2,1,0:T(8,128)S(1)}, f32[2,4,64,128]{3,2,1,0:T(8,128)S(1)}, u32[]{:S(2)}, u32[]{:S(2)}) collective-permute-start(f32[2,4,64,128]{3,2,1,0:T(8,128)S(1)} %get-tuple-element.40), channel_id=1, source_target_pairs={{0,16},{16,32},{32,48},{48,64},{64,80},{80,96},{96,112},{112,128},... | collective-permute-start | bytes 786440 | tf_op jit(solution)/shard_map/ppermute | solution.py:331
  54.3 1.3 %collective-permute-start.7 = (f32[2,4,64,128]{3,2,1,0:T(8,128)S(1)}, f32[2,4,64,128]{3,2,1,0:T(8,128)S(1)}, u32[]{:S(2)}, u32[]{:S(2)}) collective-permute-start(f32[2,4,64,128]{3,2,1,0:T(8,128)S(1)} %get-tuple-element.41), channel_id=1, source_target_pairs={{16,0},{32,16},{48,32},{64,48},{80,64},{96,80},{112,96},{128,112},... | collective-permute-start | bytes 786440 | tf_op jit(solution)/shard_map/ppermute | solution.py:330
  55.6 6.5 %collective-permute-done.6.from_up = f32[2,4,64,128]{3,2,1,0:T(8,128)S(1)} collective-permute-done((f32[2,4,64,128]{3,2,1,0:T(8,128)S(1)}, f32[2,4,64,128]{3,2,1,0:T(8,128)S(1)}, u32[]{:S(2)}, u32[]{:S(2)}) %collective-permute-start.6) | collective-permute-done | bytes 262176 | tf_op jit(solution)/shard_map/ppermute | solution.py:331
  62.1 1.6 %collective-permute-done.7.from_down = f32[2,4,64,128]{3,2,1,0:T(8,128)S(1)} collective-permute-done((f32[2,4,64,128]{3,2,1,0:T(8,128)S(1)}, f32[2,4,64,128]{3,2,1,0:T(8,128)S(1)}, u32[]{:S(2)}, u32[]{:S(2)}) %collective-permute-start.7) | collective-permute-done | bytes 262176 | tf_op jit(solution)/shard_map/ppermute | solution.py:330
  63.7 0.7 shard_map.81
  64.4 7.7 %all-to-all-start.1 = ((f32[8,16,128]{2,1,0:T(8,128)}), f32[8,16,128]{2,1,0:T(8,128)S(1)}, u32[]{:S(2)}, u32[]{:S(2)}) async-start(f32[8,16,128]{2,1,0:T(8,128)} %get-tuple-element.42), calls=%async_computation.1 | async-start | bytes 131072 | tf_op jit(solution)/shard_map/all_to_all | solution.py:338
  72.1 6.1 %collective-permute-start.8 = (f32[2,128,128]{2,1,0:T(8,128)S(1)}, f32[2,128,128]{2,1,0:T(8,128)S(1)}, u32[]{:S(2)}, u32[]{:S(2)}) collective-permute-start(f32[2,128,128]{2,1,0:T(8,128)S(1)} %get-tuple-element.44), channel_id=1, source_target_pairs={{0,1},{1,2},{2,3},{3,4},{4,5},{5,6},{6,7},{7,8},{8,9},{9,10},{10,1... | collective-permute-start | bytes 393224 | tf_op jit(solution)/shard_map/ppermute | solution.py:336
  78.2 1.9 %collective-permute-start.9 = (f32[2,128,128]{2,1,0:T(8,128)S(1)}, f32[2,128,128]{2,1,0:T(8,128)S(1)}, u32[]{:S(2)}, u32[]{:S(2)}) collective-permute-start(f32[2,128,128]{2,1,0:T(8,128)S(1)} %get-tuple-element.45), channel_id=1, source_target_pairs={{1,0},{2,1},{3,2},{4,3},{5,4},{6,5},{7,6},{8,7},{9,8},{10,9},{11,1... | collective-permute-start | bytes 393224 | tf_op jit(solution)/shard_map/ppermute | solution.py:337
  80.1 6.1 %collective-permute-done.9.from_right = f32[2,128,128]{2,1,0:T(8,128)S(1)} collective-permute-done((f32[2,128,128]{2,1,0:T(8,128)S(1)}, f32[2,128,128]{2,1,0:T(8,128)S(1)}, u32[]{:S(2)}, u32[]{:S(2)}) %collective-permute-start.9) | collective-permute-done | bytes 131104 | tf_op jit(solution)/shard_map/ppermute | solution.py:337
  86.4 20.1 %all_to_all.15 = f32[64,16,128]{2,1,0:T(8,128)S(1)} all-to-all(f32[64,16,128]{2,1,0:T(8,128)S(1)} %get-tuple-element.47), channel_id=1, replica_groups=mesh['xl'=2,'za'=8,'zb'=2,'y'=4,'xh'=2,'core'=2] {'xl','zb','y','xh','co..., dimensions={0} | all-to-all | bytes 1048576 | tf_op jit(solution)/shard_map/all_to_all | solution.py:343
  106.5 0.9 shard_map.83
  (22 shorter events, 1.1 us)
Async XLA Ops:
  0.6 21.4 %copy-start = (f32[2,4,128,128]{3,2,1,0:T(8,128)S(1)}, f32[2,4,128,128]{3,2,1,0:T(8,128)}, u32[]{:S(2)}) copy-start(f32[2,4,128,128]{3,2,1,0:T(8,128)} %param.7) | copy-start | bytes 1572868
  0.6 1.0 copy-start.1
  1.8 12.8 %collective-permute-start = (f32[2,128,128]{2,1,0:T(8,128)S(1)}, f32[2,128,128]{2,1,0:T(8,128)S(1)}, u32[]{:S(2)}, u32[]{:S(2)}) collective-permute-start(f32[2,128,128]{2,1,0:T(8,128)S(1)} %get-tuple-element.26), channel_id=1, source_target_pairs={{0,1},{1,2},{2,3},{3,4},{4,5},{5,6},{6,7},{7,8},{8,9},{9,10},{10,1... | collective-permute-start | bytes 393224 | tf_op jit(solution)/shard_map/ppermute | solution.py:292
  7.8 7.8 %collective-permute-start.1 = (f32[2,128,128]{2,1,0:T(8,128)S(1)}, f32[2,128,128]{2,1,0:T(8,128)S(1)}, u32[]{:S(2)}, u32[]{:S(2)}) collective-permute-start(f32[2,128,128]{2,1,0:T(8,128)S(1)} %get-tuple-element.27), channel_id=1, source_target_pairs={{1,0},{2,1},{3,2},{4,3},{5,4},{6,5},{7,6},{8,7},{9,8},{10,9},{11,1... | collective-permute-start | bytes 393224 | tf_op jit(solution)/shard_map/ppermute | solution.py:293
  11.9 13.1 %collective-permute-start.2 = (f32[4,64,128]{2,1,0:T(8,128)S(1)}, f32[4,64,128]{2,1,0:T(8,128)S(1)}, u32[]{:S(2)}, u32[]{:S(2)}) collective-permute-start(f32[4,64,128]{2,1,0:T(8,128)S(1)} %get-tuple-element.29), channel_id=1, source_target_pairs={{0,16},{16,32},{32,48},{48,64},{64,80},{80,96},{96,112},{112,128},... | collective-permute-start | bytes 393224 | tf_op jit(solution)/shard_map/ppermute | solution.py:294
  13.3 11.7 %collective-permute-start.3 = (f32[4,64,128]{2,1,0:T(8,128)S(1)}, f32[4,64,128]{2,1,0:T(8,128)S(1)}, u32[]{:S(2)}, u32[]{:S(2)}) collective-permute-start(f32[4,64,128]{2,1,0:T(8,128)S(1)} %get-tuple-element.30), channel_id=1, source_target_pairs={{16,0},{32,16},{48,32},{64,48},{80,64},{96,80},{112,96},{128,112},... | collective-permute-start | bytes 393224 | tf_op jit(solution)/shard_map/ppermute | solution.py:295
  15.7 5.5 %copy-start.4 = (f32[2,2,31]{2,1,0:T(2,128)S(1)}, f32[2,2,31]{2,1,0:T(2,128)}, u32[]{:S(2)}) copy-start(f32[2,2,31]{2,1,0:T(2,128)} %param.8) | copy-start | bytes 1492
  15.7 9.3 %collective-permute-start.4 = (f32[4,64,128]{2,1,0:T(8,128)S(1)}, f32[4,64,128]{2,1,0:T(8,128)S(1)}, u32[]{:S(2)}, u32[]{:S(2)}) collective-permute-start(f32[4,64,128]{2,1,0:T(8,128)S(1)} %get-tuple-element.31), channel_id=1, source_target_pairs={{0,16},{16,32},{32,48},{48,64},{64,80},{80,96},{96,112},{112,128},... | collective-permute-start | bytes 393224 | tf_op jit(solution)/shard_map/ppermute | solution.py:304
  19.3 6.9 %collective-permute-start.5 = (f32[4,64,128]{2,1,0:T(8,128)S(1)}, f32[4,64,128]{2,1,0:T(8,128)S(1)}, u32[]{:S(2)}, u32[]{:S(2)}) collective-permute-start(f32[4,64,128]{2,1,0:T(8,128)S(1)} %get-tuple-element.32), channel_id=1, source_target_pairs={{16,0},{32,16},{48,32},{64,48},{80,64},{96,80},{112,96},{128,112},... | collective-permute-start | bytes 393224 | tf_op jit(solution)/shard_map/ppermute | solution.py:305
  21.2 0.7 copy-start.5
  22.0 0.9 copy-start.3
  22.9 3.2 %copy-start.2 = (f32[2,2,128,128]{3,2,1,0:T(8,128)S(1)}, f32[2,2,128,128]{3,2,1,0:T(8,128)}, u32[]{:S(2)}) copy-start(f32[2,2,128,128]{3,2,1,0:T(8,128)} %param.6) | copy-start | bytes 786436
  33.3 30.4 %all-to-all-start = ((f32[64,16,128]{2,1,0:T(8,128)}), f32[64,16,128]{2,1,0:T(8,128)S(1)}, u32[]{:S(2)}, u32[]{:S(2)}) async-start(f32[64,16,128]{2,1,0:T(8,128)} %bitcast.4), calls=%async_computation | async-start | bytes 1048576 | tf_op jit(solution)/shard_map/all_to_all | solution.py:329
  50.9 11.1 %collective-permute-start.6 = (f32[2,4,64,128]{3,2,1,0:T(8,128)S(1)}, f32[2,4,64,128]{3,2,1,0:T(8,128)S(1)}, u32[]{:S(2)}, u32[]{:S(2)}) collective-permute-start(f32[2,4,64,128]{3,2,1,0:T(8,128)S(1)} %get-tuple-element.40), channel_id=1, source_target_pairs={{0,16},{16,32},{32,48},{48,64},{64,80},{80,96},{96,112},{112,128},... | collective-permute-start | bytes 786440 | tf_op jit(solution)/shard_map/ppermute | solution.py:331
  54.3 9.5 %collective-permute-start.7 = (f32[2,4,64,128]{3,2,1,0:T(8,128)S(1)}, f32[2,4,64,128]{3,2,1,0:T(8,128)S(1)}, u32[]{:S(2)}, u32[]{:S(2)}) collective-permute-start(f32[2,4,64,128]{3,2,1,0:T(8,128)S(1)} %get-tuple-element.41), channel_id=1, source_target_pairs={{16,0},{32,16},{48,32},{64,48},{80,64},{96,80},{112,96},{128,112},... | collective-permute-start | bytes 786440 | tf_op jit(solution)/shard_map/ppermute | solution.py:330
  64.4 21.8 %all-to-all-start.1 = ((f32[8,16,128]{2,1,0:T(8,128)}), f32[8,16,128]{2,1,0:T(8,128)S(1)}, u32[]{:S(2)}, u32[]{:S(2)}) async-start(f32[8,16,128]{2,1,0:T(8,128)} %get-tuple-element.42), calls=%async_computation.1 | async-start | bytes 131072 | tf_op jit(solution)/shard_map/all_to_all | solution.py:338
  72.1 8.0 %collective-permute-start.8 = (f32[2,128,128]{2,1,0:T(8,128)S(1)}, f32[2,128,128]{2,1,0:T(8,128)S(1)}, u32[]{:S(2)}, u32[]{:S(2)}) collective-permute-start(f32[2,128,128]{2,1,0:T(8,128)S(1)} %get-tuple-element.44), channel_id=1, source_target_pairs={{0,1},{1,2},{2,3},{3,4},{4,5},{5,6},{6,7},{7,8},{8,9},{9,10},{10,1... | collective-permute-start | bytes 393224 | tf_op jit(solution)/shard_map/ppermute | solution.py:336
  78.2 8.1 %collective-permute-start.9 = (f32[2,128,128]{2,1,0:T(8,128)S(1)}, f32[2,128,128]{2,1,0:T(8,128)S(1)}, u32[]{:S(2)}, u32[]{:S(2)}) collective-permute-start(f32[2,128,128]{2,1,0:T(8,128)S(1)} %get-tuple-element.45), channel_id=1, source_target_pairs={{1,0},{2,1},{3,2},{4,3},{5,4},{6,5},{7,6},{8,7},{9,8},{10,9},{11,1... | collective-permute-start | bytes 393224 | tf_op jit(solution)/shard_map/ppermute | solution.py:337

commit v2 on v1

v2 whole, which is shorter than its diff:
```python
import functools
import math

import jax
import jax.numpy as jnp
from jax import lax
from jax.experimental import pallas as pl
from jax.experimental.pallas import tpu as pltpu
from jax.sharding import Mesh
from jax.sharding import PartitionSpec as P

F32 = jnp.float32
BF16 = jnp.bfloat16
ROW_AXES = ("xl", "za", "zb")
COL_AXES = ("y", "xh", "core")
NEAR_AXES = ("xl", "zb", "y", "xh", "core")
FAR_AXES = ("za",)
VMEM_LIMIT = 40 * 1024 * 1024
TILE = 128
HALF = 64
VM = pl.BlockSpec(memory_space=pltpu.VMEM)
SM = pl.BlockSpec(memory_space=pltpu.SMEM)
FAR = pl.BlockSpec(memory_space=pltpu.HBM)


def call(kernel, out_shape, in_specs, *args, scratch=(), out_specs=None, flops=0, moved=0):
    out_shape = tuple(out_shape)
    return pl.pallas_call(
        kernel,
        out_shape=out_shape,
        in_specs=in_specs,
        out_specs=tuple(out_specs or [VM] * len(out_shape)),
        scratch_shapes=list(scratch),
        compiler_params=pltpu.CompilerParams(vmem_limit_bytes=VMEM_LIMIT),
        cost_estimate=pl.CostEstimate(flops=flops, bytes_accessed=moved, transcendentals=0),
    )(*args)


def low_lanes(shape):
    return lax.broadcasted_iota(jnp.int32, shape, len(shape) - 1) < HALF


def split(value):
    high = value.astype(BF16)
    return high, (value - high.astype(F32)).astype(BF16)


def pack_kernel(tile, to_right, to_left, to_down, to_up, down_right, down_left, up_right, up_left):
    low = low_lanes((TILE, TILE))
    for s in range(2):
        real, imag = tile[s], tile[2 + s]
        turned = pltpu.roll(imag, HALF, 1)
        right = jnp.where(low, turned, real)
        left = jnp.where(low, real, turned)
        to_right[s], to_left[s] = right, left
        down_right[s], down_left[s] = right[HALF:], left[HALF:]
        up_right[s], up_left[s] = right[:HALF], left[:HALF]
    for p in range(4):
        to_up[p] = tile[p, :HALF]
        to_down[p] = tile[p, HALF:]


def operator_kernel(taps, probe, measured, ops, probe_near, measured_near, padded):
    probe_near[...] = probe[...]
    measured_near[...] = measured[...]
    padded[...] = jnp.zeros_like(padded)
    for axis in range(2):
        padded[2 * axis:2 * axis + 2, :31] = taps[axis]

    def band(index):
        line = jnp.broadcast_to(padded[index:index + 1, :], (TILE, 2 * TILE))
        return pltpu.roll(line, 2 * TILE - 15, 1, stride=1, stride_axis=0)[:, :TILE]

    def put(index, blocks):
        for i in range(2):
            for j in range(2):
                high, low = split(blocks[i][j])
                cols = slice(j * TILE, (j + 1) * TILE)
                ops[index, i * TILE:(i + 1) * TILE, cols] = high
                ops[index, (2 + i) * TILE:(3 + i) * TILE, cols] = low

    yr, yi = band(0), band(1)
    put(0, ((yr, -yi), (yi, yr)))
    yr, yi = yr.T, yi.T
    put(2, ((yr, yi), (-yi, yr)))
    xr, xi = band(2), band(3)
    put(3, ((xr, -xi), (xi, xr)))
    xr, xi = xr.T, xi.T
    put(1, ((xr, xi), (-xi, xr)))


def dot(a, b):
    return jnp.dot(a, b, preferred_element_type=F32)


def block(m):
    return slice(m * TILE, (m + 1) * TILE)


def main_kernel(
    offsets, counts, tile, above, below, from_left, from_right,
    above_left, above_right, below_left, below_right, probe, measured, ops,
    probe_grad, grad_tile, to_up, to_down, to_right, to_left, up_right, up_left, down_right, down_left,
    object_ext, grad_ext, field_high, field_low, mid_high, mid_low, wave_one, wave_two,
):
    for p in range(4):
        object_ext[0, p, :HALF] = above[p]
        object_ext[0, p, HALF:HALF + TILE] = tile[p]
        object_ext[0, p, HALF + TILE:] = below[p]
    for start, end, left, right in (
        (0, HALF, above_left, above_right),
        (HALF, HALF + TILE, from_left, from_right),
        (HALF + TILE, 2 * TILE, below_left, below_right),
    ):
        low = low_lanes((end - start, TILE))
        for s in range(2):
            object_ext[1, s, start:end] = jnp.where(low, right[s], left[s])
            object_ext[1, 2 + s, start:end] = pltpu.roll(jnp.where(low, left[s], right[s]), HALF, 1)
    grad_ext[...] = jnp.zeros_like(grad_ext)

    def put_field(slot, m, real, imag):
        for c, value in enumerate((real, imag)):
            high, low = split(value)
            field_high[slot, block(c), block(m)] = high
            field_low[slot, block(c), block(m)] = low

    def rows_done(slot, which):
        for n in range(2):
            cols = slice(n * 256, (n + 1) * 256)
            both = dot(ops[which], field_high[slot, :, cols])
            mid = both[:256] + (both[256:] + dot(ops[which, :256], field_low[slot, :, cols]))
            for k in range(2):
                for c in range(2):
                    high, low = split(mid[block(c), block(k)])
                    mid_high[slot, block(2 * n + k), block(c)] = high
                    mid_low[slot, block(2 * n + k), block(c)] = low

    def cols_done(slot, which, take):
        high, low = ops[which, :256], ops[which, 256:]
        done = dot(mid_high[slot], high) + (dot(mid_low[slot], high) + dot(mid_high[slot], low))
        for m in range(4):
            take(slot, m, done[block(m), :TILE], done[block(m), TILE:])

    def propagate(which, take):
        for slot in range(2):
            rows_done(slot, which)
        for slot in range(2):
            cols_done(slot, which + 1, take)

    def window(slot, p):
        rows = [object_ext[b, p, pl.ds(offsets[2 * slot], TILE), :] for b in range(2)]
        shift = lax.rem(320 - offsets[2 * slot + 1], 256)
        return pltpu.roll(jnp.concatenate(rows, axis=1), shift, 1)[:, :TILE]

    def spread(slot, p, value):
        wide = jnp.concatenate([value, jnp.zeros_like(value)], axis=1)
        wide = pltpu.roll(wide, lax.rem(offsets[2 * slot + 1] + 192, 256), 1)
        for b in range(2):
            grad_ext[b, p, pl.ds(offsets[2 * slot], TILE), :] += wide[:, block(b)]

    views = [[window(slot, p) for p in range(4)] for slot in range(2)]
    for slot in range(2):
        o0r, o0i = views[slot][0], views[slot][2]
        for m in range(4):
            pr, pi = probe[m], probe[4 + m]
            put_field(slot, m, pr * o0r - pi * o0i, pr * o0i + pi * o0r)

    def after_first(slot, m, wr, wi):
        o1r, o1i = views[slot][1], views[slot][3]
        wave_one[slot, m, 0] = wr
        wave_one[slot, m, 1] = wi
        put_field(slot, m, wr * o1r - wi * o1i, wr * o1i + wi * o1r)

    propagate(0, after_first)
    intensity = [None, None]

    def after_second(slot, m, wr, wi):
        wave_two[slot, m, 0] = wr
        wave_two[slot, m, 1] = wi
        term = wr * wr + wi * wi
        intensity[slot] = term if m == 0 else intensity[slot] + term
        if m == 3:
            weight = jnp.where(slot < counts[0], 2.0, 0.0).astype(F32)
            residual = (intensity[slot] - measured[slot]) * weight
            for k in range(4):
                put_field(slot, k, residual * wave_two[slot, k, 0], residual * wave_two[slot, k, 1])

    propagate(0, after_second)
    sums = [[None, None], [None, None]]

    def add(slot, m, real, imag):
        pair = (real, imag) if m == 0 else (sums[slot][0] + real, sums[slot][1] + imag)
        sums[slot] = pair

    def after_third(slot, m, hr, hi):
        o1r, o1i = views[slot][1], views[slot][3]
        wr, wi = wave_one[slot, m, 0], wave_one[slot, m, 1]
        add(slot, m, wr * hr + wi * hi, wr * hi - wi * hr)
        put_field(slot, m, hr * o1r + hi * o1i, hi * o1r - hr * o1i)
        if m == 3:
            spread(slot, 1, sums[slot][0])
            spread(slot, 3, sums[slot][1])

    propagate(2, after_third)

    def after_fourth(slot, m, hr, hi):
        o0r, o0i = views[slot][0], views[slot][2]
        pr, pi = probe[m], probe[4 + m]
        add(slot, m, pr * hr + pi * hi, pr * hi - pi * hr)
        dr = hr * o0r + hi * o0i
        di = hi * o0r - hr * o0i
        if slot == 0:
            probe_grad[m] = dr
            probe_grad[4 + m] = di
        else:
            probe_grad[m] += dr
            probe_grad[4 + m] += di
        if m == 3:
            spread(slot, 0, sums[slot][0])
            spread(slot, 2, sums[slot][1])

    propagate(2, after_fourth)
    for p in range(4):
        to_up[p] = grad_ext[0, p, :HALF]
        grad_tile[p] = grad_ext[0, p, HALF:HALF + TILE]
        to_down[p] = grad_ext[0, p, HALF + TILE:]
    for start, end, left, right in (
        (0, HALF, up_left, up_right),
        (HALF, HALF + TILE, to_left, to_right),
        (HALF + TILE, 2 * TILE, down_left, down_right),
    ):
        low = low_lanes((end - start, TILE))
        for s in range(2):
            real = grad_ext[1, s, start:end]
            turned = pltpu.roll(grad_ext[1, 2 + s, start:end], HALF, 1)
            right[s] = jnp.where(low, real, turned)
            left[s] = jnp.where(low, turned, real)


def share_kernel(scale, shares, spread_share):
    share = jnp.sum(shares[...], axis=0) * scale
    for i in range(spread_share.shape[0]):
        spread_share[i] = share


def fold_sides(tile, from_up, from_down, from_left, from_right, result):
    low = low_lanes((TILE, TILE))
    for s in range(2):
        left, right = from_left[s], from_right[s]
        sides = (jnp.where(low, left, right), pltpu.roll(jnp.where(low, right, left), HALF, 1))
        for p, side in zip((s, 2 + s), sides):
            result[p, :HALF] = tile[p, :HALF] + from_up[p] + side[:HALF]
            result[p, HALF:] = tile[p, HALF:] + from_down[p] + side[HALF:]


def fold_corners(tile, up_left, up_right, down_left, down_right, result):
    low = low_lanes((HALF, TILE))
    for s in range(2):
        for rows, left, right in (
            (slice(0, HALF), up_left[s], up_right[s]),
            (slice(HALF, TILE), down_left[s], down_right[s]),
        ):
            result[s, rows] = tile[s, rows] + jnp.where(low, left, right)
            turned = pltpu.roll(jnp.where(low, right, left), HALF, 1)
            result[2 + s, rows] = tile[2 + s, rows] + turned


def near_kernel(shares, tile, from_up, from_down, from_left, from_right, spread_share, result):
    share_kernel(1.0, shares, spread_share)
    fold_sides(tile, from_up, from_down, from_left, from_right, result)


def far_kernel(scale, shares, tile, up_left, up_right, down_left, down_right, spread_share, result):
    share_kernel(scale, shares, spread_share)
    fold_corners(tile, up_left, up_right, down_left, down_right, result)


def finish_kernel(result, gathered, result_far, probe_far, sems):
    moves = [pltpu.make_async_copy(result.at[p], result_far.at[p], sems.at[p]) for p in range(4)]
    for i in range(4):
        part = pl.ds(256 * i, 256)
        moves.append(pltpu.make_async_copy(gathered.at[part], probe_far.at[part], sems.at[4 + i]))
    for move in moves:
        move.start()
    for move in moves:
        move.wait()


def shift(value, down, right):
    height, width = lax.axis_size(ROW_AXES), lax.axis_size(COL_AXES)
    if right == 0:
        return lax.ppermute(value, ROW_AXES, [(i, i + down) for i in range(height) if 0 <= i + down < height])
    if down == 0:
        return lax.ppermute(value, COL_AXES, [(j, j + right) for j in range(width) if 0 <= j + right < width])
    pairs = [
        (i * width + j, (i + down) * width + j + right)
        for i in range(height)
        for j in range(width)
        if 0 <= i + down < height and 0 <= j + right < width
    ]
    return lax.ppermute(value, ROW_AXES + COL_AXES, pairs)


def f32(*shape):
    return jax.ShapeDtypeStruct(shape, F32)


def body(object_field, probe_modes, prop_taps, measured, offsets, counts):
    tile = object_field.reshape(4, TILE, TILE)
    planes, half = f32(4, TILE, TILE), f32(4, HALF, TILE)
    strip, corner = f32(2, TILE, TILE), f32(2, HALF, TILE)

    to_right, to_left, to_down, to_up, down_right, down_left, up_right, up_left = call(
        pack_kernel, (strip, strip, half, half) + (corner,) * 4, [VM], tile
    )
    from_left = shift(to_right, 0, 1)
    from_right = shift(to_left, 0, -1)
    above = shift(to_down, 1, 0)
    below = shift(to_up, -1, 0)
    above_left = shift(down_right, 1, 1)
    above_right = shift(down_left, 1, -1)
    below_left = shift(up_right, -1, 1)
    below_right = shift(up_left, -1, -1)
    ops, probe, targets = call(
        operator_kernel,
        (jax.ShapeDtypeStruct((4, 512, 256), BF16), f32(8, TILE, TILE), strip), [VM, VM, VM],
        prop_taps, probe_modes.reshape(8, TILE, TILE), measured.reshape(2, TILE, TILE),
        scratch=[pltpu.VMEM((8, 2 * TILE), F32)],
    )
    (
        probe_part, grad_tile, to_up, to_down, to_right, to_left,
        up_right, up_left, down_right, down_left,
    ) = call(
        main_kernel,
        (f32(8, TILE, TILE), planes, half, half, strip, strip) + (corner,) * 4,
        [SM, SM] + [VM] * 12,
        offsets.reshape(-1), counts.reshape(-1), tile, above, below, from_left, from_right,
        above_left, above_right, below_left, below_right, probe, targets, ops,
        scratch=[
            pltpu.VMEM((2, 4, 256, TILE), F32),
            pltpu.VMEM((2, 4, 256, TILE), F32),
            pltpu.VMEM((2, 256, 512), BF16),
            pltpu.VMEM((2, 256, 512), BF16),
            pltpu.VMEM((2, 512, 256), BF16),
            pltpu.VMEM((2, 512, 256), BF16),
            pltpu.VMEM((2, 4, 2, TILE, TILE), F32),
            pltpu.VMEM((2, 4, 2, TILE, TILE), F32),
        ],
        flops=3_200_000_000, moved=4_000_000,
    )

    near = lax.axis_size(NEAR_AXES)
    far = lax.axis_size(FAR_AXES)
    rows = 8 * TILE // near
    sides = (shift(to_down, 1, 0), shift(to_up, -1, 0), shift(to_right, 0, 1), shift(to_left, 0, -1))
    shares = lax.all_to_all(probe_part.reshape(near, rows, TILE), NEAR_AXES, 0, 0, tiled=True)
    spread_share, part = call(
        near_kernel, (f32(far, rows, TILE), planes), [VM] * 6, shares, grad_tile, *sides
    )
    shares = lax.all_to_all(spread_share, FAR_AXES, 0, 0, tiled=True)
    corners = (
        shift(down_right, 1, 1), shift(down_left, 1, -1), shift(up_right, -1, 1), shift(up_left, -1, -1)
    )
    spread_share, result = call(
        functools.partial(far_kernel, 1.0 / math.sqrt(near * far)),
        (f32(near, rows, TILE), planes), [VM] * 6, shares, part, *corners,
    )
    gathered = lax.all_to_all(spread_share, NEAR_AXES, 0, 0, tiled=True)
    result, probe_grad = call(
        finish_kernel, (planes, f32(8 * TILE, TILE)), [VM] * 2,
        result, gathered.reshape(8 * TILE, TILE),
        scratch=[pltpu.SemaphoreType.DMA((8,))], out_specs=[FAR, FAR],
    )
    return result.reshape(object_field.shape), probe_grad.reshape(probe_modes.shape)


def solution(mesh):
    fine = Mesh(mesh.devices.reshape(2, 8, 2, 4, 2, 2), ROW_AXES + COL_AXES)
    return jax.shard_map(
        body,
        mesh=fine,
        in_specs=(
            P(None, None, ROW_AXES, COL_AXES),
            P(),
            P(),
            P(ROW_AXES, COL_AXES, None, None, None),
            P(ROW_AXES, COL_AXES, None, None),
            P(ROW_AXES, COL_AXES),
        ),
        out_specs=(P(None, None, ROW_AXES, COL_AXES), P()),
        check_vma=False,
    )
```

time: 108 us -> 131 us (1.21); the launches traced: 107 us -> 129 us
  starting transfers between devices: 55.5 us -> 72.1 us
  blocking collectives: 20.1 us -> 24.9 us
  Pallas kernels: 11.2 us -> 8.67 us
  waiting for transfers between devices: 16.4 us -> 18.7 us
    ppermute x10 -> x16, starting transfers between devices: 30.2 us -> 47 us  [the longest x8 20.6 us: shift(): return lax.ppermute(value, ROW_AXES + COL_AXES, pairs)]
    all_to_all x1, starting transfers between devices: 17.6 us -> 12.1 us  [body(): lax.all_to_all(probe_part.reshape(near, rows, TILE), NEAR_AXES, 0, 0, til...]
    all_to_all x1, starting transfers between devices: 7.66 us -> 12.9 us  [body(): shares = lax.all_to_all(spread_share, FAR_AXES, 0, 0, tiled=True)]
    all_to_all x1, blocking collectives: 20.1 us -> 24.9 us  [body(): gathered = lax.all_to_all(spread_share, NEAR_AXES, 0, 0, tiled=True)]
    pallas_call x7 -> x6, Pallas kernels: 11.2 us -> 8.67 us  [call(): pl.pallas_call(kernel, out_shape=out_shape, in_specs=in_specs, out_specs=...]
    ppermute x10 -> x16, waiting for transfers between devices: 16.4 us -> 18.7 us  [the longest x8 12.9 us: shift(): return lax.ppermute(value, ROW_AXES + COL_AXES, pairs)]
  transfers between devices with their start and end apart: 12 -> 18, of which waited for: 5 -> 4; matrix products, arithmetic and copies ran while one was open for 0% -> 0% of each run, Pallas kernels for 2% -> 0%
where the time goes in v2:
time: 131 us; the launch traced here: 129 us
  starting transfers between devices  72.1 us (55%)
  blocking collectives  24.9 us (19%)
  waiting for transfers between devices  18.7 us (14%)
  Pallas kernels  8.67 us (7%)
  local copies, waits for them, and re-layouts  2.76 us (2%)
  between operations  1.55 us (1%)
    all_to_all x1, blocking collectives, body(): gathered = lax.all_to_all(spread_share, NEAR_AXES, 0, 0, tiled=True)  24.9 us
    ppermute x8, starting transfers between devices, shift(): return lax.ppermute(value, ROW_AXES + COL_AXES, pairs)  20.6 us
    ppermute x4, starting transfers between devices, shift(): lax.ppermute(value, ROW_AXES, [(i, i + down) for i in range(height) if 0...  14.8 us
    all_to_all x1, starting transfers between devices, body(): shares = lax.all_to_all(spread_share, FAR_AXES, 0, 0, tiled=True)  12.9 us
    ppermute x8, waiting for transfers between devices, shift(): return lax.ppermute(value, ROW_AXES + COL_AXES, pairs)  12.9 us
    all_to_all x1, starting transfers between devices, body(): lax.all_to_all(probe_part.reshape(near, rows, TILE), NEAR_AXES, 0, 0, til...  12.1 us
    ppermute x4, starting transfers between devices, shift(): lax.ppermute(value, COL_AXES, [(j, j + right) for j in range(width) if 0...  11.6 us
    pallas_call x6, Pallas kernels, call(): pl.pallas_call(kernel, out_shape=out_shape, in_specs=in_specs, out_specs=...  8.67 us
  transfers between devices with their start and end apart: 18, of which 4 were waited for; matrix products, arithmetic and copies ran while one was open for 0% of the time, Pallas kernels for 0%

profile of v2, /device:TPU:1, one launch (start us, length us, event | category | flops | bytes accessed | tf_op | source)
XLA Modules:
  0.0 128.7 jit_solution(5182111031839014780)
XLA Ops:
  1.7 7.4 %collective-permute-start.4 = (f32[2,64,128]{2,1,0:T(8,128)S(1)}, f32[2,64,128]{2,1,0:T(8,128)S(1)}, u32[]{:S(2)}, u32[]{:S(2)}) collective-permute-start(f32[2,64,128]{2,1,0:T(8,128)S(1)} %get-tuple-element.33), channel_id=1, source_target_pairs={{0,17},{1,18},{2,19},{3,20},{4,21},{5,22},{6,23},{7,24},{8,25},{9,... | collective-permute-start | bytes 196616 | tf_op jit(solution)/shard_map/ppermute | solution.py:301
  9.1 1.3 %collective-permute-start.5 = (f32[2,64,128]{2,1,0:T(8,128)S(1)}, f32[2,64,128]{2,1,0:T(8,128)S(1)}, u32[]{:S(2)}, u32[]{:S(2)}) collective-permute-start(f32[2,64,128]{2,1,0:T(8,128)S(1)} %get-tuple-element.34), channel_id=1, source_target_pairs={{1,16},{2,17},{3,18},{4,19},{5,20},{6,21},{7,22},{8,23},{9,24},{10... | collective-permute-start | bytes 196616 | tf_op jit(solution)/shard_map/ppermute | solution.py:301
  10.4 1.3 %collective-permute-start.6 = (f32[2,64,128]{2,1,0:T(8,128)S(1)}, f32[2,64,128]{2,1,0:T(8,128)S(1)}, u32[]{:S(2)}, u32[]{:S(2)}) collective-permute-start(f32[2,64,128]{2,1,0:T(8,128)S(1)} %get-tuple-element.35), channel_id=1, source_target_pairs={{16,1},{17,2},{18,3},{19,4},{20,5},{21,6},{22,7},{23,8},{24,9},{25... | collective-permute-start | bytes 196616 | tf_op jit(solution)/shard_map/ppermute | solution.py:301
  11.7 8.9 %collective-permute-start = (f32[4,64,128]{2,1,0:T(8,128)S(1)}, f32[4,64,128]{2,1,0:T(8,128)S(1)}, u32[]{:S(2)}, u32[]{:S(2)}) collective-permute-start(f32[4,64,128]{2,1,0:T(8,128)S(1)} %get-tuple-element.29), channel_id=1, source_target_pairs={{0,16},{16,32},{32,48},{48,64},{64,80},{80,96},{96,112},{112,128},... | collective-permute-start | bytes 393224 | tf_op jit(solution)/shard_map/ppermute | solution.py:292
  20.6 1.3 %collective-permute-start.1 = (f32[4,64,128]{2,1,0:T(8,128)S(1)}, f32[4,64,128]{2,1,0:T(8,128)S(1)}, u32[]{:S(2)}, u32[]{:S(2)}) collective-permute-start(f32[4,64,128]{2,1,0:T(8,128)S(1)} %get-tuple-element.30), channel_id=1, source_target_pairs={{16,0},{32,16},{48,32},{64,48},{80,64},{96,80},{112,96},{128,112},... | collective-permute-start | bytes 393224 | tf_op jit(solution)/shard_map/ppermute | solution.py:292
  21.9 2.7 %collective-permute-start.2 = (f32[2,128,128]{2,1,0:T(8,128)S(1)}, f32[2,128,128]{2,1,0:T(8,128)S(1)}, u32[]{:S(2)}, u32[]{:S(2)}) collective-permute-start(f32[2,128,128]{2,1,0:T(8,128)S(1)} %get-tuple-element.31), channel_id=1, source_target_pairs={{0,1},{1,2},{2,3},{3,4},{4,5},{5,6},{6,7},{7,8},{8,9},{9,10},{10,1... | collective-permute-start | bytes 393224 | tf_op jit(solution)/shard_map/ppermute | solution.py:294
  24.6 1.9 %collective-permute-start.3 = (f32[2,128,128]{2,1,0:T(8,128)S(1)}, f32[2,128,128]{2,1,0:T(8,128)S(1)}, u32[]{:S(2)}, u32[]{:S(2)}) collective-permute-start(f32[2,128,128]{2,1,0:T(8,128)S(1)} %get-tuple-element.32), channel_id=1, source_target_pairs={{1,0},{2,1},{3,2},{4,3},{5,4},{6,5},{7,6},{8,7},{9,8},{10,9},{11,1... | collective-permute-start | bytes 393224 | tf_op jit(solution)/shard_map/ppermute | solution.py:294
  26.6 1.3 %collective-permute-start.7 = (f32[2,64,128]{2,1,0:T(8,128)S(1)}, f32[2,64,128]{2,1,0:T(8,128)S(1)}, u32[]{:S(2)}, u32[]{:S(2)}) collective-permute-start(f32[2,64,128]{2,1,0:T(8,128)S(1)} %get-tuple-element.36), channel_id=1, source_target_pairs={{17,0},{18,1},{19,2},{20,3},{21,4},{22,5},{23,6},{24,7},{25,8},{26... | collective-permute-start | bytes 196616 | tf_op jit(solution)/shard_map/ppermute | solution.py:301
  30.7 6.2 %collective-permute-done.7.below_right = f32[2,64,128]{2,1,0:T(8,128)S(1)} collective-permute-done((f32[2,64,128]{2,1,0:T(8,128)S(1)}, f32[2,64,128]{2,1,0:T(8,128)S(1)}, u32[]{:S(2)}, u32[]{:S(2)}) %collective-permute-start.7) | collective-permute-done | bytes 65568 | tf_op jit(solution)/shard_map/ppermute | solution.py:301
  36.9 6.5 %shard_map.79 = (f32[8,128,128]{2,1,0:T(8,128)}, f32[4,128,128]{2,1,0:T(8,128)S(1)}, f32[4,64,128]{2,1,0:T(8,128)S(1)}, f32[4,64,128]{2,1,0:T(8,128)S(1)}, f32[2...) custom-call(s32[4]{0:T(128)S(1)} %reshape.31.offsets, ...), custom_call_target="tpu_custom_call" | custom-call | flops 3200000000 | bytes 4000000 | tf_op jit(solution)/shard_map/pallas_call | solution.py:28
  43.3 12.1 %all-to-all-start = ((f32[64,16,128]{2,1,0:T(8,128)}), f32[64,16,128]{2,1,0:T(8,128)S(1)}, u32[]{:S(2)}, u32[]{:S(2)}) async-start(f32[64,16,128]{2,1,0:T(8,128)} %bitcast.4), calls=%async_computation | async-start | bytes 1048576 | tf_op jit(solution)/shard_map/all_to_all | solution.py:356
  55.5 3.3 %collective-permute-start.8 = (f32[4,64,128]{2,1,0:T(8,128)S(1)}, f32[4,64,128]{2,1,0:T(8,128)S(1)}, u32[]{:S(2)}, u32[]{:S(2)}) collective-permute-start(f32[4,64,128]{2,1,0:T(8,128)S(1)} %get-tuple-element.42), channel_id=1, source_target_pairs={{0,16},{16,32},{32,48},{48,64},{64,80},{80,96},{96,112},{112,128},... | collective-permute-start | bytes 393224 | tf_op jit(solution)/shard_map/ppermute | solution.py:292
  58.8 1.3 %collective-permute-start.9 = (f32[4,64,128]{2,1,0:T(8,128)S(1)}, f32[4,64,128]{2,1,0:T(8,128)S(1)}, u32[]{:S(2)}, u32[]{:S(2)}) collective-permute-start(f32[4,64,128]{2,1,0:T(8,128)S(1)} %get-tuple-element.43), channel_id=1, source_target_pairs={{16,0},{32,16},{48,32},{64,48},{80,64},{96,80},{112,96},{128,112},... | collective-permute-start | bytes 393224 | tf_op jit(solution)/shard_map/ppermute | solution.py:292
  60.1 5.1 %collective-permute-start.10 = (f32[2,128,128]{2,1,0:T(8,128)S(1)}, f32[2,128,128]{2,1,0:T(8,128)S(1)}, u32[]{:S(2)}, u32[]{:S(2)}) collective-permute-start(f32[2,128,128]{2,1,0:T(8,128)S(1)} %get-tuple-element.44), channel_id=1, source_target_pairs={{0,1},{1,2},{2,3},{3,4},{4,5},{5,6},{6,7},{7,8},{8,9},{9,10},{10,1... | collective-permute-start | bytes 393224 | tf_op jit(solution)/shard_map/ppermute | solution.py:294
  65.2 1.9 %collective-permute-start.11 = (f32[2,128,128]{2,1,0:T(8,128)S(1)}, f32[2,128,128]{2,1,0:T(8,128)S(1)}, u32[]{:S(2)}, u32[]{:S(2)}) collective-permute-start(f32[2,128,128]{2,1,0:T(8,128)S(1)} %get-tuple-element.45), channel_id=1, source_target_pairs={{1,0},{2,1},{3,2},{4,3},{5,4},{6,5},{7,6},{8,7},{9,8},{10,9},{11,1... | collective-permute-start | bytes 393224 | tf_op jit(solution)/shard_map/ppermute | solution.py:294
  67.2 5.8 %collective-permute-done.11.from_right = f32[2,128,128]{2,1,0:T(8,128)S(1)} collective-permute-done((f32[2,128,128]{2,1,0:T(8,128)S(1)}, f32[2,128,128]{2,1,0:T(8,128)S(1)}, u32[]{:S(2)}, u32[]{:S(2)}) %collective-permute-start.11) | collective-permute-done | bytes 131104 | tf_op jit(solution)/shard_map/ppermute | solution.py:294
  73.8 12.9 %all-to-all-start.1 = ((f32[8,16,128]{2,1,0:T(8,128)}), f32[8,16,128]{2,1,0:T(8,128)S(1)}, u32[]{:S(2)}, u32[]{:S(2)}) async-start(f32[8,16,128]{2,1,0:T(8,128)} %get-tuple-element.46), calls=%async_computation.1 | async-start | bytes 131072 | tf_op jit(solution)/shard_map/all_to_all | solution.py:360
  86.7 1.7 %collective-permute-start.12 = (f32[2,64,128]{2,1,0:T(8,128)S(1)}, f32[2,64,128]{2,1,0:T(8,128)S(1)}, u32[]{:S(2)}, u32[]{:S(2)}) collective-permute-start(f32[2,64,128]{2,1,0:T(8,128)S(1)} %get-tuple-element.48), channel_id=1, source_target_pairs={{0,17},{1,18},{2,19},{3,20},{4,21},{5,22},{6,23},{7,24},{8,25},{9,... | collective-permute-start | bytes 196616 | tf_op jit(solution)/shard_map/ppermute | solution.py:301
  88.4 5.0 %collective-permute-start.13 = (f32[2,64,128]{2,1,0:T(8,128)S(1)}, f32[2,64,128]{2,1,0:T(8,128)S(1)}, u32[]{:S(2)}, u32[]{:S(2)}) collective-permute-start(f32[2,64,128]{2,1,0:T(8,128)S(1)} %get-tuple-element.49), channel_id=1, source_target_pairs={{1,16},{2,17},{3,18},{4,19},{5,20},{6,21},{7,22},{8,23},{9,24},{10... | collective-permute-start | bytes 196616 | tf_op jit(solution)/shard_map/ppermute | solution.py:301
  93.4 1.3 %collective-permute-start.14 = (f32[2,64,128]{2,1,0:T(8,128)S(1)}, f32[2,64,128]{2,1,0:T(8,128)S(1)}, u32[]{:S(2)}, u32[]{:S(2)}) collective-permute-start(f32[2,64,128]{2,1,0:T(8,128)S(1)} %get-tuple-element.50), channel_id=1, source_target_pairs={{16,1},{17,2},{18,3},{19,4},{20,5},{21,6},{22,7},{23,8},{24,9},{25... | collective-permute-start | bytes 196616 | tf_op jit(solution)/shard_map/ppermute | solution.py:301
  94.7 1.3 %collective-permute-start.15 = (f32[2,64,128]{2,1,0:T(8,128)S(1)}, f32[2,64,128]{2,1,0:T(8,128)S(1)}, u32[]{:S(2)}, u32[]{:S(2)}) collective-permute-start(f32[2,64,128]{2,1,0:T(8,128)S(1)} %get-tuple-element.51), channel_id=1, source_target_pairs={{17,0},{18,1},{19,2},{20,3},{21,4},{22,5},{23,6},{24,7},{25,8},{26... | collective-permute-start | bytes 196616 | tf_op jit(solution)/shard_map/ppermute | solution.py:301
  96.0 3.0 %collective-permute-done.14.down_left = f32[2,64,128]{2,1,0:T(8,128)S(1)} collective-permute-done((f32[2,64,128]{2,1,0:T(8,128)S(1)}, f32[2,64,128]{2,1,0:T(8,128)S(1)}, u32[]{:S(2)}, u32[]{:S(2)}) %collective-permute-start.14) | collective-permute-done | bytes 65568 | tf_op jit(solution)/shard_map/ppermute | solution.py:301
  99.0 3.7 %collective-permute-done.15.down_right = f32[2,64,128]{2,1,0:T(8,128)S(1)} collective-permute-done((f32[2,64,128]{2,1,0:T(8,128)S(1)}, f32[2,64,128]{2,1,0:T(8,128)S(1)}, u32[]{:S(2)}, u32[]{:S(2)}) %collective-permute-start.15) | collective-permute-done | bytes 65568 | tf_op jit(solution)/shard_map/ppermute | solution.py:301
  102.8 24.9 %all_to_all.15 = f32[64,16,128]{2,1,0:T(8,128)S(1)} all-to-all(f32[64,16,128]{2,1,0:T(8,128)S(1)} %get-tuple-element.53), channel_id=1, replica_groups=mesh['xl'=2,'za'=8,'zb'=2,'y'=4,'xh'=2,'core'=2] {'xl','zb','y','xh','co..., dimensions={0} | all-to-all | bytes 1048576 | tf_op jit(solution)/shard_map/all_to_all | solution.py:368
  (32 shorter events, 5.0 us)
Async XLA Ops:
  0.6 1.0 copy-start.1
  1.6 27.0 %copy-start.3 = (f32[1,1,2,128,128]{4,3,2,1,0:T(8,128)S(1)}, f32[1,1,2,128,128]{4,3,2,1,0:T(8,128)}, u32[]{:S(2)}) copy-start(f32[1,1,2,128,128]{4,3,2,1,0:T(8,128)} %param.9) | copy-start | bytes 393220
  1.7 20.2 %collective-permute-start.4 = (f32[2,64,128]{2,1,0:T(8,128)S(1)}, f32[2,64,128]{2,1,0:T(8,128)S(1)}, u32[]{:S(2)}, u32[]{:S(2)}) collective-permute-start(f32[2,64,128]{2,1,0:T(8,128)S(1)} %get-tuple-element.33), channel_id=1, source_target_pairs={{0,17},{1,18},{2,19},{3,20},{4,21},{5,22},{6,23},{7,24},{8,25},{9,... | collective-permute-start | bytes 196616 | tf_op jit(solution)/shard_map/ppermute | solution.py:301
  9.1 15.5 %collective-permute-start.5 = (f32[2,64,128]{2,1,0:T(8,128)S(1)}, f32[2,64,128]{2,1,0:T(8,128)S(1)}, u32[]{:S(2)}, u32[]{:S(2)}) collective-permute-start(f32[2,64,128]{2,1,0:T(8,128)S(1)} %get-tuple-element.34), channel_id=1, source_target_pairs={{1,16},{2,17},{3,18},{4,19},{5,20},{6,21},{7,22},{8,23},{9,24},{10... | collective-permute-start | bytes 196616 | tf_op jit(solution)/shard_map/ppermute | solution.py:301
  10.4 16.2 %collective-permute-start.6 = (f32[2,64,128]{2,1,0:T(8,128)S(1)}, f32[2,64,128]{2,1,0:T(8,128)S(1)}, u32[]{:S(2)}, u32[]{:S(2)}) collective-permute-start(f32[2,64,128]{2,1,0:T(8,128)S(1)} %get-tuple-element.35), channel_id=1, source_target_pairs={{16,1},{17,2},{18,3},{19,4},{20,5},{21,6},{22,7},{23,8},{24,9},{25... | collective-permute-start | bytes 196616 | tf_op jit(solution)/shard_map/ppermute | solution.py:301
  11.7 25.2 %collective-permute-start = (f32[4,64,128]{2,1,0:T(8,128)S(1)}, f32[4,64,128]{2,1,0:T(8,128)S(1)}, u32[]{:S(2)}, u32[]{:S(2)}) collective-permute-start(f32[4,64,128]{2,1,0:T(8,128)S(1)} %get-tuple-element.29), channel_id=1, source_target_pairs={{0,16},{16,32},{32,48},{48,64},{64,80},{80,96},{96,112},{112,128},... | collective-permute-start | bytes 393224 | tf_op jit(solution)/shard_map/ppermute | solution.py:292
  20.6 16.2 %collective-permute-start.1 = (f32[4,64,128]{2,1,0:T(8,128)S(1)}, f32[4,64,128]{2,1,0:T(8,128)S(1)}, u32[]{:S(2)}, u32[]{:S(2)}) collective-permute-start(f32[4,64,128]{2,1,0:T(8,128)S(1)} %get-tuple-element.30), channel_id=1, source_target_pairs={{16,0},{32,16},{48,32},{64,48},{80,64},{96,80},{112,96},{128,112},... | collective-permute-start | bytes 393224 | tf_op jit(solution)/shard_map/ppermute | solution.py:292
  21.9 14.9 %collective-permute-start.2 = (f32[2,128,128]{2,1,0:T(8,128)S(1)}, f32[2,128,128]{2,1,0:T(8,128)S(1)}, u32[]{:S(2)}, u32[]{:S(2)}) collective-permute-start(f32[2,128,128]{2,1,0:T(8,128)S(1)} %get-tuple-element.31), channel_id=1, source_target_pairs={{0,1},{1,2},{2,3},{3,4},{4,5},{5,6},{6,7},{7,8},{8,9},{9,10},{10,1... | collective-permute-start | bytes 393224 | tf_op jit(solution)/shard_map/ppermute | solution.py:294
  24.6 12.2 %collective-permute-start.3 = (f32[2,128,128]{2,1,0:T(8,128)S(1)}, f32[2,128,128]{2,1,0:T(8,128)S(1)}, u32[]{:S(2)}, u32[]{:S(2)}) collective-permute-start(f32[2,128,128]{2,1,0:T(8,128)S(1)} %get-tuple-element.32), channel_id=1, source_target_pairs={{1,0},{2,1},{3,2},{4,3},{5,4},{6,5},{7,6},{8,7},{9,8},{10,9},{11,1... | collective-permute-start | bytes 393224 | tf_op jit(solution)/shard_map/ppermute | solution.py:294
  26.6 2.0 %copy-start.5 = (s32[1,1,2,2]{3,2,1,0:T(2,128)S(1)}, s32[1,1,2,2]{3,2,1,0:T(2,128)}, u32[]{:S(2)}) copy-start(s32[1,1,2,2]{3,2,1,0:T(2,128)} %param.10) | copy-start | bytes 52
  26.6 10.3 %collective-permute-start.7 = (f32[2,64,128]{2,1,0:T(8,128)S(1)}, f32[2,64,128]{2,1,0:T(8,128)S(1)}, u32[]{:S(2)}, u32[]{:S(2)}) collective-permute-start(f32[2,64,128]{2,1,0:T(8,128)S(1)} %get-tuple-element.36), channel_id=1, source_target_pairs={{17,0},{18,1},{19,2},{20,3},{21,4},{22,5},{23,6},{24,7},{25,8},{26... | collective-permute-start | bytes 196616 | tf_op jit(solution)/shard_map/ppermute | solution.py:301
  28.6 0.7 copy-start.4
  29.3 1.0 copy-start
  30.3 6.5 %copy-start.2 = (f32[2,2,128,128]{3,2,1,0:T(8,128)S(1)}, f32[2,2,128,128]{3,2,1,0:T(8,128)}, u32[]{:S(2)}) copy-start(f32[2,2,128,128]{3,2,1,0:T(8,128)} %param.6) | copy-start | bytes 786436
  43.3 29.7 %all-to-all-start = ((f32[64,16,128]{2,1,0:T(8,128)}), f32[64,16,128]{2,1,0:T(8,128)S(1)}, u32[]{:S(2)}, u32[]{:S(2)}) async-start(f32[64,16,128]{2,1,0:T(8,128)} %bitcast.4), calls=%async_computation | async-start | bytes 1048576 | tf_op jit(solution)/shard_map/all_to_all | solution.py:356
  55.5 11.7 %collective-permute-start.8 = (f32[4,64,128]{2,1,0:T(8,128)S(1)}, f32[4,64,128]{2,1,0:T(8,128)S(1)}, u32[]{:S(2)}, u32[]{:S(2)}) collective-permute-start(f32[4,64,128]{2,1,0:T(8,128)S(1)} %get-tuple-element.42), channel_id=1, source_target_pairs={{0,16},{16,32},{32,48},{48,64},{64,80},{80,96},{96,112},{112,128},... | collective-permute-start | bytes 393224 | tf_op jit(solution)/shard_map/ppermute | solution.py:292
  58.8 8.4 %collective-permute-start.9 = (f32[4,64,128]{2,1,0:T(8,128)S(1)}, f32[4,64,128]{2,1,0:T(8,128)S(1)}, u32[]{:S(2)}, u32[]{:S(2)}) collective-permute-start(f32[4,64,128]{2,1,0:T(8,128)S(1)} %get-tuple-element.43), channel_id=1, source_target_pairs={{16,0},{32,16},{48,32},{64,48},{80,64},{96,80},{112,96},{128,112},... | collective-permute-start | bytes 393224 | tf_op jit(solution)/shard_map/ppermute | solution.py:292
  60.1 7.1 %collective-permute-start.10 = (f32[2,128,128]{2,1,0:T(8,128)S(1)}, f32[2,128,128]{2,1,0:T(8,128)S(1)}, u32[]{:S(2)}, u32[]{:S(2)}) collective-permute-start(f32[2,128,128]{2,1,0:T(8,128)S(1)} %get-tuple-element.44), channel_id=1, source_target_pairs={{0,1},{1,2},{2,3},{3,4},{4,5},{5,6},{6,7},{7,8},{8,9},{9,10},{10,1... | collective-permute-start | bytes 393224 | tf_op jit(solution)/shard_map/ppermute | solution.py:294
  65.2 7.8 %collective-permute-start.11 = (f32[2,128,128]{2,1,0:T(8,128)S(1)}, f32[2,128,128]{2,1,0:T(8,128)S(1)}, u32[]{:S(2)}, u32[]{:S(2)}) collective-permute-start(f32[2,128,128]{2,1,0:T(8,128)S(1)} %get-tuple-element.45), channel_id=1, source_target_pairs={{1,0},{2,1},{3,2},{4,3},{5,4},{6,5},{7,6},{8,7},{9,8},{10,9},{11,1... | collective-permute-start | bytes 393224 | tf_op jit(solution)/shard_map/ppermute | solution.py:294
  73.8 29.0 %all-to-all-start.1 = ((f32[8,16,128]{2,1,0:T(8,128)}), f32[8,16,128]{2,1,0:T(8,128)S(1)}, u32[]{:S(2)}, u32[]{:S(2)}) async-start(f32[8,16,128]{2,1,0:T(8,128)} %get-tuple-element.46), calls=%async_computation.1 | async-start | bytes 131072 | tf_op jit(solution)/shard_map/all_to_all | solution.py:360
  86.7 9.3 %collective-permute-start.12 = (f32[2,64,128]{2,1,0:T(8,128)S(1)}, f32[2,64,128]{2,1,0:T(8,128)S(1)}, u32[]{:S(2)}, u32[]{:S(2)}) collective-permute-start(f32[2,64,128]{2,1,0:T(8,128)S(1)} %get-tuple-element.48), channel_id=1, source_target_pairs={{0,17},{1,18},{2,19},{3,20},{4,21},{5,22},{6,23},{7,24},{8,25},{9,... | collective-permute-start | bytes 196616 | tf_op jit(solution)/shard_map/ppermute | solution.py:301
  88.4 7.6 %collective-permute-start.13 = (f32[2,64,128]{2,1,0:T(8,128)S(1)}, f32[2,64,128]{2,1,0:T(8,128)S(1)}, u32[]{:S(2)}, u32[]{:S(2)}) collective-permute-start(f32[2,64,128]{2,1,0:T(8,128)S(1)} %get-tuple-element.49), channel_id=1, source_target_pairs={{1,16},{2,17},{3,18},{4,19},{5,20},{6,21},{7,22},{8,23},{9,24},{10... | collective-permute-start | bytes 196616 | tf_op jit(solution)/shard_map/ppermute | solution.py:301
  93.4 5.6 %collective-permute-start.14 = (f32[2,64,128]{2,1,0:T(8,128)S(1)}, f32[2,64,128]{2,1,0:T(8,128)S(1)}, u32[]{:S(2)}, u32[]{:S(2)}) collective-permute-start(f32[2,64,128]{2,1,0:T(8,128)S(1)} %get-tuple-element.50), channel_id=1, source_target_pairs={{16,1},{17,2},{18,3},{19,4},{20,5},{21,6},{22,7},{23,8},{24,9},{25... | collective-permute-start | bytes 196616 | tf_op jit(solution)/shard_map/ppermute | solution.py:301
  94.7 8.0 %collective-permute-start.15 = (f32[2,64,128]{2,1,0:T(8,128)S(1)}, f32[2,64,128]{2,1,0:T(8,128)S(1)}, u32[]{:S(2)}, u32[]{:S(2)}) collective-permute-start(f32[2,64,128]{2,1,0:T(8,128)S(1)} %get-tuple-element.51), channel_id=1, source_target_pairs={{17,0},{18,1},{19,2},{20,3},{21,4},{22,5},{23,6},{24,7},{25,8},{26... | collective-permute-start | bytes 196616 | tf_op jit(solution)/shard_map/ppermute | solution.py:301

commit v3 on v2

--- a/solution.py
+++ b/solution.py
@@ -45,19 +45,39 @@
     return high, (value - high.astype(F32)).astype(BF16)
 
 
-def pack_kernel(tile, to_right, to_left, to_down, to_up, down_right, down_left, up_right, up_left):
+def even_column():
+    return lax.axis_index("core") == 0
+
+
+def even_row():
+    return lax.axis_index("zb") == 0
+
+
+def by_parity(even, first, second):
+    return jnp.where(even, first, second), jnp.where(even, second, first)
+
+
+def pack_kernel(tile, cross, mate):
     low = low_lanes((TILE, TILE))
+    even = even_column()
     for s in range(2):
-        real, imag = tile[s], tile[2 + s]
-        turned = pltpu.roll(imag, HALF, 1)
-        right = jnp.where(low, turned, real)
-        left = jnp.where(low, real, turned)
-        to_right[s], to_left[s] = right, left
-        down_right[s], down_left[s] = right[HALF:], left[HALF:]
-        up_right[s], up_left[s] = right[:HALF], left[:HALF]
-    for p in range(4):
-        to_up[p] = tile[p, :HALF]
-        to_down[p] = tile[p, HALF:]
+        turned = pltpu.roll(tile[2 + s], HALF, 1)
+        to_right = jnp.where(low, turned, tile[s])
+        to_left = jnp.where(low, tile[s], turned)
+        mate[s], cross[s] = by_parity(even, to_right, to_left)
+
+
+def rows_kernel(tile, from_cross, from_mate, beside, cross, mate):
+    low = low_lanes((TILE, TILE))
+    even = even_column()
+    for s in range(2):
+        from_right, from_left = by_parity(even, from_mate[s], from_cross[s])
+        beside[s] = jnp.where(low, from_right, from_left)
+        beside[2 + s] = pltpu.roll(jnp.where(low, from_left, from_right), HALF, 1)
+    even = even_row()
+    for b, plane in enumerate((tile, beside)):
+        for p in range(4):
+            mate[b, p], cross[b, p] = by_parity(even, plane[p, HALF:], plane[p, :HALF])
 
 
 def operator_kernel(taps, probe, measured, ops, probe_near, measured_near, padded):
@@ -98,24 +118,18 @@
 
 
 def main_kernel(
-    offsets, counts, tile, above, below, from_left, from_right,
-    above_left, above_right, below_left, below_right, probe, measured, ops,
-    probe_grad, grad_tile, to_up, to_down, to_right, to_left, up_right, up_left, down_right, down_left,
+    offsets, counts, tile, beside, from_cross, from_mate, probe, measured, ops,
+    probe_grad, grad_tile, grad_beside, cross, mate,
     object_ext, grad_ext, field_high, field_low, mid_high, mid_low, wave_one, wave_two,
 ):
-    for p in range(4):
-        object_ext[0, p, :HALF] = above[p]
-        object_ext[0, p, HALF:HALF + TILE] = tile[p]
-        object_ext[0, p, HALF + TILE:] = below[p]
-    for start, end, left, right in (
-        (0, HALF, above_left, above_right),
-        (HALF, HALF + TILE, from_left, from_right),
-        (HALF + TILE, 2 * TILE, below_left, below_right),
-    ):
-        low = low_lanes((end - start, TILE))
-        for s in range(2):
-            object_ext[1, s, start:end] = jnp.where(low, right[s], left[s])
-            object_ext[1, 2 + s, start:end] = pltpu.roll(jnp.where(low, left[s], right[s]), HALF, 1)
+    even = even_row()
+    mate_rows = pl.ds(pl.multiple_of(jnp.where(even, HALF + TILE, 0), HALF), HALF)
+    cross_rows = pl.ds(pl.multiple_of(jnp.where(even, 0, HALF + TILE), HALF), HALF)
+    for b, plane in enumerate((tile, beside)):
+        for p in range(4):
+            object_ext[b, p, HALF:HALF + TILE] = plane[p]
+            object_ext[b, p, mate_rows] = from_mate[b, p]
+            object_ext[b, p, cross_rows] = from_cross[b, p]
     grad_ext[...] = jnp.zeros_like(grad_ext)
 
     def put_field(slot, m, real, imag):
@@ -180,7 +194,7 @@
         term = wr * wr + wi * wi
         intensity[slot] = term if m == 0 else intensity[slot] + term
         if m == 3:
-            weight = jnp.where(slot < counts[0], 2.0, 0.0).astype(F32)
+            weight = jnp.where(slot < counts[0, 0], 2.0, 0.0).astype(F32)
             residual = (intensity[slot] - measured[slot]) * weight
             for k in range(4):
                 put_field(slot, k, residual * wave_two[slot, k, 0], residual * wave_two[slot, k, 1])
@@ -220,59 +234,47 @@
             spread(slot, 2, sums[slot][1])
 
     propagate(2, after_fourth)
-    for p in range(4):
-        to_up[p] = grad_ext[0, p, :HALF]
-        grad_tile[p] = grad_ext[0, p, HALF:HALF + TILE]
-        to_down[p] = grad_ext[0, p, HALF + TILE:]
-    for start, end, left, right in (
-        (0, HALF, up_left, up_right),
-        (HALF, HALF + TILE, to_left, to_right),
-        (HALF + TILE, 2 * TILE, down_left, down_right),
-    ):
-        low = low_lanes((end - start, TILE))
-        for s in range(2):
-            real = grad_ext[1, s, start:end]
-            turned = pltpu.roll(grad_ext[1, 2 + s, start:end], HALF, 1)
-            right[s] = jnp.where(low, real, turned)
-            left[s] = jnp.where(low, turned, real)
-
-
-def share_kernel(scale, shares, spread_share):
+    for b, plane in enumerate((grad_tile, grad_beside)):
+        for p in range(4):
+            plane[p] = grad_ext[b, p, HALF:HALF + TILE]
+            mate[b, p] = grad_ext[b, p, mate_rows]
+            cross[b, p] = grad_ext[b, p, cross_rows]
+
+
+def spread_sum(scale, shares, spread_share):
     share = jnp.sum(shares[...], axis=0) * scale
     for i in range(spread_share.shape[0]):
         spread_share[i] = share
 
 
-def fold_sides(tile, from_up, from_down, from_left, from_right, result):
+def near_kernel(
+    shares, grad_tile, grad_beside, from_cross, from_mate, spread_share, part, cross, mate, beside
+):
+    spread_sum(1.0, shares, spread_share)
+    even = even_row()
+    mate_rows = pl.ds(pl.multiple_of(jnp.where(even, HALF, 0), HALF), HALF)
+    cross_rows = pl.ds(pl.multiple_of(jnp.where(even, 0, HALF), HALF), HALF)
+    for b, (plane, total) in enumerate(((grad_tile, part), (grad_beside, beside))):
+        for p in range(4):
+            total[p, mate_rows] = plane[p, mate_rows] + from_mate[b, p]
+            total[p, cross_rows] = plane[p, cross_rows] + from_cross[b, p]
     low = low_lanes((TILE, TILE))
+    even = even_column()
     for s in range(2):
-        left, right = from_left[s], from_right[s]
-        sides = (jnp.where(low, left, right), pltpu.roll(jnp.where(low, right, left), HALF, 1))
-        for p, side in zip((s, 2 + s), sides):
-            result[p, :HALF] = tile[p, :HALF] + from_up[p] + side[:HALF]
-            result[p, HALF:] = tile[p, HALF:] + from_down[p] + side[HALF:]
-
-
-def fold_corners(tile, up_left, up_right, down_left, down_right, result):
-    low = low_lanes((HALF, TILE))
+        turned = pltpu.roll(beside[2 + s], HALF, 1)
+        to_right = jnp.where(low, beside[s], turned)
+        to_left = jnp.where(low, turned, beside[s])
+        mate[s], cross[s] = by_parity(even, to_right, to_left)
+
+
+def far_kernel(scale, shares, part, from_cross, from_mate, spread_share, result):
+    spread_sum(scale, shares, spread_share)
+    low = low_lanes((TILE, TILE))
+    even = even_column()
     for s in range(2):
-        for rows, left, right in (
-            (slice(0, HALF), up_left[s], up_right[s]),
-            (slice(HALF, TILE), down_left[s], down_right[s]),
-        ):
-            result[s, rows] = tile[s, rows] + jnp.where(low, left, right)
-            turned = pltpu.roll(jnp.where(low, right, left), HALF, 1)
-            result[2 + s, rows] = tile[2 + s, rows] + turned
-
-
-def near_kernel(shares, tile, from_up, from_down, from_left, from_right, spread_share, result):
-    share_kernel(1.0, shares, spread_share)
-    fold_sides(tile, from_up, from_down, from_left, from_right, result)
-
-
-def far_kernel(scale, shares, tile, up_left, up_right, down_left, down_right, spread_share, result):
-    share_kernel(scale, shares, spread_share)
-    fold_corners(tile, up_left, up_right, down_left, down_right, result)
+        from_right, from_left = by_parity(even, from_mate[s], from_cross[s])
+        result[s] = part[s] + jnp.where(low, from_left, from_right)
+        result[2 + s] = part[2 + s] + pltpu.roll(jnp.where(low, from_right, from_left), HALF, 1)
 
 
 def finish_kernel(result, gathered, result_far, probe_far, sems):
@@ -286,19 +288,13 @@
         move.wait()
 
 
-def shift(value, down, right):
-    height, width = lax.axis_size(ROW_AXES), lax.axis_size(COL_AXES)
-    if right == 0:
-        return lax.ppermute(value, ROW_AXES, [(i, i + down) for i in range(height) if 0 <= i + down < height])
-    if down == 0:
-        return lax.ppermute(value, COL_AXES, [(j, j + right) for j in range(width) if 0 <= j + right < width])
-    pairs = [
-        (i * width + j, (i + down) * width + j + right)
-        for i in range(height)
-        for j in range(width)
-        if 0 <= i + down < height and 0 <= j + right < width
-    ]
-    return lax.ppermute(value, ROW_AXES + COL_AXES, pairs)
+def exchange(cross, mate, axes):
+    count = lax.axis_size(axes)
+    pairs = [(i, i + 1) for i in range(1, count - 1, 2)]
+    from_cross = lax.ppermute(cross, axes, pairs + [(b, a) for a, b in pairs])
+    pairs = [(i, i + 1) for i in range(0, count, 2)]
+    from_mate = lax.ppermute(mate, axes, pairs + [(b, a) for a, b in pairs])
+    return from_cross, from_mate
 
 
 def f32(*shape):
@@ -307,35 +303,21 @@
 
 def body(object_field, probe_modes, prop_taps, measured, offsets, counts):
     tile = object_field.reshape(4, TILE, TILE)
-    planes, half = f32(4, TILE, TILE), f32(4, HALF, TILE)
-    strip, corner = f32(2, TILE, TILE), f32(2, HALF, TILE)
-
-    to_right, to_left, to_down, to_up, down_right, down_left, up_right, up_left = call(
-        pack_kernel, (strip, strip, half, half) + (corner,) * 4, [VM], tile
-    )
-    from_left = shift(to_right, 0, 1)
-    from_right = shift(to_left, 0, -1)
-    above = shift(to_down, 1, 0)
-    below = shift(to_up, -1, 0)
-    above_left = shift(down_right, 1, 1)
-    above_right = shift(down_left, 1, -1)
-    below_left = shift(up_right, -1, 1)
-    below_right = shift(up_left, -1, -1)
+    planes, strip, rim = f32(4, TILE, TILE), f32(2, TILE, TILE), f32(2, 4, HALF, TILE)
+
+    strips = exchange(*call(pack_kernel, (strip, strip), [VM], tile), COL_AXES)
+    beside, cross, mate = call(rows_kernel, (planes, rim, rim), [VM] * 3, tile, *strips)
+    rims = exchange(cross, mate, ROW_AXES)
     ops, probe, targets = call(
         operator_kernel,
         (jax.ShapeDtypeStruct((4, 512, 256), BF16), f32(8, TILE, TILE), strip), [VM, VM, VM],
         prop_taps, probe_modes.reshape(8, TILE, TILE), measured.reshape(2, TILE, TILE),
         scratch=[pltpu.VMEM((8, 2 * TILE), F32)],
     )
-    (
-        probe_part, grad_tile, to_up, to_down, to_right, to_left,
-        up_right, up_left, down_right, down_left,
-    ) = call(
+    probe_part, grad_tile, grad_beside, cross, mate = call(
         main_kernel,
-        (f32(8, TILE, TILE), planes, half, half, strip, strip) + (corner,) * 4,
-        [SM, SM] + [VM] * 12,
-        offsets.reshape(-1), counts.reshape(-1), tile, above, below, from_left, from_right,
-        above_left, above_right, below_left, below_right, probe, targets, ops,
+        (f32(8, TILE, TILE), planes, planes, rim, rim), [SM, SM] + [VM] * 7,
+        offsets.reshape(-1), counts.reshape(1, 1), tile, beside, *rims, probe, targets, ops,
         scratch=[
             pltpu.VMEM((2, 4, 256, TILE), F32),
             pltpu.VMEM((2, 4, 256, TILE), F32),
@@ -352,18 +334,17 @@
     near = lax.axis_size(NEAR_AXES)
     far = lax.axis_size(FAR_AXES)
     rows = 8 * TILE // near
-    sides = (shift(to_down, 1, 0), shift(to_up, -1, 0), shift(to_right, 0, 1), shift(to_left, 0, -1))
     shares = lax.all_to_all(probe_part.reshape(near, rows, TILE), NEAR_AXES, 0, 0, tiled=True)
-    spread_share, part = call(
-        near_kernel, (f32(far, rows, TILE), planes), [VM] * 6, shares, grad_tile, *sides
-    )
+    rims = exchange(cross, mate, ROW_AXES)
+    spread_share, part, cross, mate = call(
+        near_kernel, (f32(far, rows, TILE), planes, strip, strip), [VM] * 5,
+        shares, grad_tile, grad_beside, *rims, scratch=[pltpu.VMEM((4, TILE, TILE), F32)],
+    )
+    strips = exchange(cross, mate, COL_AXES)
     shares = lax.all_to_all(spread_share, FAR_AXES, 0, 0, tiled=True)
-    corners = (
-        shift(down_right, 1, 1), shift(down_left, 1, -1), shift(up_right, -1, 1), shift(up_left, -1, -1)
-    )
     spread_share, result = call(
         functools.partial(far_kernel, 1.0 / math.sqrt(near * far)),
-        (f32(near, rows, TILE), planes), [VM] * 6, shares, part, *corners,
+        (f32(near, rows, TILE), planes), [VM] * 4, shares, part, *strips,
     )
     gathered = lax.all_to_all(spread_share, NEAR_AXES, 0, 0, tiled=True)
     result, probe_grad = call(

time: 131 us -> 105 us (0.80); the launches traced: 129 us -> 105 us
  starting transfers between devices: 72.1 us -> 53.4 us
  blocking collectives: 24.9 us -> 22.2 us
  waiting for transfers between devices: 18.7 us -> 17.3 us
    ppermute x16 -> x8, starting transfers between devices: 47 us -> 29.1 us  [the longest x4 15.3 us: exchange(): from_mate = lax.ppermute(mate, axes, pairs + [(b, a) for a, b in pairs])]
    all_to_all x1, starting transfers between devices: 12.9 us -> 7.17 us  [body(): shares = lax.all_to_all(spread_share, FAR_AXES, 0, 0, tiled=True)]
    all_to_all x1, starting transfers between devices: 12.1 us -> 17.1 us  [body(): lax.all_to_all(probe_part.reshape(near, rows, TILE), NEAR_AXES, 0, 0, til...]
    ppermute x16 -> x8, waiting for transfers between devices: 18.7 us -> 15 us  [the longest x4 13.5 us: exchange(): from_mate = lax.ppermute(mate, axes, pairs + [(b, a) for a, b in pairs])]
    all_to_all x1, blocking collectives: 24.9 us -> 22.2 us  [body(): gathered = lax.all_to_all(spread_share, NEAR_AXES, 0, 0, tiled=True)]
    all_to_all x1, waiting for transfers between devices: 0.01 us -> 2.32 us  [body(): shares = lax.all_to_all(spread_share, FAR_AXES, 0, 0, tiled=True)]
    pallas_call x6 -> x7, Pallas kernels: 8.67 us -> 8.55 us  [call(): pl.pallas_call(kernel, out_shape=out_shape, in_specs=in_specs, out_specs=...]
  transfers between devices with their start and end apart: 18 -> 10, of which waited for: 4 -> 5; matrix products, arithmetic and copies ran while one was open for 0% -> 0% of each run, Pallas kernels for 0% -> 0%
where the time goes in v3:
time: 105 us
  starting transfers between devices  53.4 us (51%)
  blocking collectives  22.2 us (21%)
  waiting for transfers between devices  17.3 us (16%)
  Pallas kernels  8.55 us (8%)
  local copies, waits for them, and re-layouts  1.72 us (2%)
  between operations  1.43 us (1%)
    all_to_all x1, blocking collectives, body(): gathered = lax.all_to_all(spread_share, NEAR_AXES, 0, 0, tiled=True)  22.2 us
    all_to_all x1, starting transfers between devices, body(): lax.all_to_all(probe_part.reshape(near, rows, TILE), NEAR_AXES, 0, 0, til...  17.1 us
    ppermute x4, starting transfers between devices, exchange(): from_mate = lax.ppermute(mate, axes, pairs + [(b, a) for a, b in pairs])  15.3 us
    ppermute x4, starting transfers between devices, exchange(): from_cross = lax.ppermute(cross, axes, pairs + [(b, a) for a, b in pairs])  13.8 us
    ppermute x4, waiting for transfers between devices, exchange(): from_mate = lax.ppermute(mate, axes, pairs + [(b, a) for a, b in pairs])  13.5 us
    pallas_call x7, Pallas kernels, call(): pl.pallas_call(kernel, out_shape=out_shape, in_specs=in_specs, out_specs=...  8.55 us
    all_to_all x1, starting transfers between devices, body(): shares = lax.all_to_all(spread_share, FAR_AXES, 0, 0, tiled=True)  7.17 us
    all_to_all x1, waiting for transfers between devices, body(): shares = lax.all_to_all(spread_share, FAR_AXES, 0, 0, tiled=True)  2.32 us
  transfers between devices with their start and end apart: 10, of which 5 were waited for; matrix products, arithmetic and copies ran while one was open for 0% of the time, Pallas kernels for 0%

profile of v3, /device:TPU:1, one launch (start us, length us, event | category | flops | bytes accessed | tf_op | source)
XLA Modules:
  0.0 104.6 jit_solution(15332727180689334055)
XLA Ops:
  0.6 0.9 copy-done
  1.7 6.2 %collective-permute-start = (f32[2,128,128]{2,1,0:T(8,128)S(1)}, f32[2,128,128]{2,1,0:T(8,128)S(1)}, u32[]{:S(2)}, u32[]{:S(2)}) collective-permute-start(f32[2,128,128]{2,1,0:T(8,128)S(1)} %get-tuple-element.23), channel_id=1, source_target_pairs={{1,2},{3,4},{5,6},{7,8},{9,10},{11,12},{13,14},{2,1},{4,3},{6,5},{... | collective-permute-start | bytes 393224 | tf_op jit(solution)/shard_map/ppermute | solution.py:294
  7.9 3.5 %collective-permute-start.1 = (f32[2,128,128]{2,1,0:T(8,128)S(1)}, f32[2,128,128]{2,1,0:T(8,128)S(1)}, u32[]{:S(2)}, u32[]{:S(2)}) collective-permute-start(f32[2,128,128]{2,1,0:T(8,128)S(1)} %get-tuple-element.24), channel_id=1, source_target_pairs={{0,1},{2,3},{4,5},{6,7},{8,9},{10,11},{12,13},{14,15},{1,0},{3,2},... | collective-permute-start | bytes 393224 | tf_op jit(solution)/shard_map/ppermute | solution.py:296
  11.4 1.0 collective-permute-done.1.from_mate
  12.4 0.1 shard_map.78
  12.5 0.7 collective-permute-start.2
  13.2 5.3 %collective-permute-start.3 = (f32[2,4,64,128]{3,2,1,0:T(8,128)S(1)}, f32[2,4,64,128]{3,2,1,0:T(8,128)S(1)}, u32[]{:S(2)}, u32[]{:S(2)}) collective-permute-start(f32[2,4,64,128]{3,2,1,0:T(8,128)S(1)} %get-tuple-element.27), channel_id=1, source_target_pairs={{0,16},{32,48},{64,80},{96,112},{128,144},{160,176},{192,208},{224... | collective-permute-start | bytes 786440 | tf_op jit(solution)/shard_map/ppermute | solution.py:296
  19.2 0.7 copy-done.4
  19.9 0.3 shard_map.79
  20.3 4.5 %collective-permute-done.3.from_mate = f32[2,4,64,128]{3,2,1,0:T(8,128)S(1)} collective-permute-done((f32[2,4,64,128]{3,2,1,0:T(8,128)S(1)}, f32[2,4,64,128]{3,2,1,0:T(8,128)S(1)}, u32[]{:S(2)}, u32[]{:S(2)}) %collective-permute-start.3) | collective-permute-done | bytes 262176 | tf_op jit(solution)/shard_map/ppermute | solution.py:296
  24.8 6.2 %shard_map.80 = (f32[8,128,128]{2,1,0:T(8,128)}, f32[4,128,128]{2,1,0:T(8,128)S(1)}, f32[4,128,128]{2,1,0:T(8,128)S(1)}, f32[2,4,64,128]{3,2,1,0:T(8,128)S(1)}, f32[2,4,64,128]{3,2,1,0:T(8,128)S(1)}) custom-call(s32[4]{0:T(128)S(1)} %reshape.28.offsets, s32[1,1]{1,0:T(1,128)S(6)} %copy.8.counts, f32[4,128,128]{2,1,0:T(8,128)S(1)} %bitcast.10, ...), custom_call_target="tpu_custom_call" | custom-call | flops 3200000000 | bytes 4000000 | tf_op jit(solution)/shard_map/pallas_call | solution.py:28
  30.9 17.1 %all-to-all-start = ((f32[64,16,128]{2,1,0:T(8,128)}), f32[64,16,128]{2,1,0:T(8,128)S(1)}, u32[]{:S(2)}, u32[]{:S(2)}) async-start(f32[64,16,128]{2,1,0:T(8,128)} %bitcast.3), calls=%async_computation | async-start | bytes 1048576 | tf_op jit(solution)/shard_map/all_to_all | solution.py:337
  48.1 0.7 collective-permute-start.4
  48.8 4.5 %collective-permute-start.5 = (f32[2,4,64,128]{3,2,1,0:T(8,128)S(1)}, f32[2,4,64,128]{3,2,1,0:T(8,128)S(1)}, u32[]{:S(2)}, u32[]{:S(2)}) collective-permute-start(f32[2,4,64,128]{3,2,1,0:T(8,128)S(1)} %get-tuple-element.35), channel_id=1, source_target_pairs={{0,16},{32,48},{64,80},{96,112},{128,144},{160,176},{192,208},{224... | collective-permute-start | bytes 786440 | tf_op jit(solution)/shard_map/ppermute | solution.py:296
  53.4 8.0 %collective-permute-done.5.from_mate = f32[2,4,64,128]{3,2,1,0:T(8,128)S(1)} collective-permute-done((f32[2,4,64,128]{3,2,1,0:T(8,128)S(1)}, f32[2,4,64,128]{3,2,1,0:T(8,128)S(1)}, u32[]{:S(2)}, u32[]{:S(2)}) %collective-permute-start.5) | collective-permute-done | bytes 262176 | tf_op jit(solution)/shard_map/ppermute | solution.py:296
  61.3 0.8 shard_map.81
  62.1 7.2 %all-to-all-start.1 = ((f32[8,16,128]{2,1,0:T(8,128)}), f32[8,16,128]{2,1,0:T(8,128)S(1)}, u32[]{:S(2)}, u32[]{:S(2)}) async-start(f32[8,16,128]{2,1,0:T(8,128)} %get-tuple-element.36), calls=%async_computation.1 | async-start | bytes 131072 | tf_op jit(solution)/shard_map/all_to_all | solution.py:344
  69.3 6.3 %collective-permute-start.6 = (f32[2,128,128]{2,1,0:T(8,128)S(1)}, f32[2,128,128]{2,1,0:T(8,128)S(1)}, u32[]{:S(2)}, u32[]{:S(2)}) collective-permute-start(f32[2,128,128]{2,1,0:T(8,128)S(1)} %get-tuple-element.38), channel_id=1, source_target_pairs={{1,2},{3,4},{5,6},{7,8},{9,10},{11,12},{13,14},{2,1},{4,3},{6,5},{... | collective-permute-start | bytes 393224 | tf_op jit(solution)/shard_map/ppermute | solution.py:294
  75.6 1.9 %collective-permute-start.7 = (f32[2,128,128]{2,1,0:T(8,128)S(1)}, f32[2,128,128]{2,1,0:T(8,128)S(1)}, u32[]{:S(2)}, u32[]{:S(2)}) collective-permute-start(f32[2,128,128]{2,1,0:T(8,128)S(1)} %get-tuple-element.39), channel_id=1, source_target_pairs={{0,1},{2,3},{4,5},{6,7},{8,9},{10,11},{12,13},{14,15},{1,0},{3,2},... | collective-permute-start | bytes 393224 | tf_op jit(solution)/shard_map/ppermute | solution.py:296
  77.5 1.5 %collective-permute-done.6.from_cross = f32[2,128,128]{2,1,0:T(8,128)S(1)} collective-permute-done((f32[2,128,128]{2,1,0:T(8,128)S(1)}, f32[2,128,128]{2,1,0:T(8,128)S(1)}, u32[]{:S(2)}, u32[]{:S(2)}) %collective-permute-start.6) | collective-permute-done | bytes 131104 | tf_op jit(solution)/shard_map/ppermute | solution.py:294
  79.0 2.3 %all-to-all-done.1.shares = f32[8,16,128]{2,1,0:T(8,128)S(1)} async-done(((f32[8,16,128]{2,1,0:T(8,128)}), f32[8,16,128]{2,1,0:T(8,128)S(1)}, u32[]{:S(2)}, u32[]{:S(2)}) %all-to-all-start.1) | async-done | bytes 65568 | tf_op jit(solution)/shard_map/all_to_all | solution.py:344
  81.4 0.1 shard_map.82
  81.5 22.2 %all_to_all.15 = f32[64,16,128]{2,1,0:T(8,128)S(1)} all-to-all(f32[64,16,128]{2,1,0:T(8,128)S(1)} %get-tuple-element.41), channel_id=1, replica_groups=mesh['xl'=2,'za'=8,'zb'=2,'y'=4,'xh'=2,'core'=2] {'xl','zb','y','xh','co..., dimensions={0} | all-to-all | bytes 1048576 | tf_op jit(solution)/shard_map/all_to_all | solution.py:349
  103.6 0.9 shard_map.83
  (17 shorter events, 0.2 us)
Async XLA Ops:
  0.6 1.0 copy-start
  1.6 17.7 %copy-start.2 = (f32[2,4,128,128]{3,2,1,0:T(8,128)S(1)}, f32[2,4,128,128]{3,2,1,0:T(8,128)}, u32[]{:S(2)}) copy-start(f32[2,4,128,128]{3,2,1,0:T(8,128)} %param.7) | copy-start | bytes 1572868
  1.7 9.7 %collective-permute-start = (f32[2,128,128]{2,1,0:T(8,128)S(1)}, f32[2,128,128]{2,1,0:T(8,128)S(1)}, u32[]{:S(2)}, u32[]{:S(2)}) collective-permute-start(f32[2,128,128]{2,1,0:T(8,128)S(1)} %get-tuple-element.23), channel_id=1, source_target_pairs={{1,2},{3,4},{5,6},{7,8},{9,10},{11,12},{13,14},{2,1},{4,3},{6,5},{... | collective-permute-start | bytes 393224 | tf_op jit(solution)/shard_map/ppermute | solution.py:294
  7.9 11.4 %copy-start.3 = (f32[1,1,2,128,128]{4,3,2,1,0:T(8,128)S(1)}, f32[1,1,2,128,128]{4,3,2,1,0:T(8,128)}, u32[]{:S(2)}) copy-start(f32[1,1,2,128,128]{4,3,2,1,0:T(8,128)} %param.9) | copy-start | bytes 393220
  7.9 4.5 %collective-permute-start.1 = (f32[2,128,128]{2,1,0:T(8,128)S(1)}, f32[2,128,128]{2,1,0:T(8,128)S(1)}, u32[]{:S(2)}, u32[]{:S(2)}) collective-permute-start(f32[2,128,128]{2,1,0:T(8,128)S(1)} %get-tuple-element.24), channel_id=1, source_target_pairs={{0,1},{2,3},{4,5},{6,7},{8,9},{10,11},{12,13},{14,15},{1,0},{3,2},... | collective-permute-start | bytes 393224 | tf_op jit(solution)/shard_map/ppermute | solution.py:296
  12.5 7.7 %collective-permute-start.2 = (f32[2,4,64,128]{3,2,1,0:T(8,128)S(1)}, f32[2,4,64,128]{3,2,1,0:T(8,128)S(1)}, u32[]{:S(2)}, u32[]{:S(2)}) collective-permute-start(f32[2,4,64,128]{3,2,1,0:T(8,128)S(1)} %get-tuple-element.26), channel_id=1, source_target_pairs={{16,32},{48,64},{80,96},{112,128},{144,160},{176,192},{208,224},{2... | collective-permute-start | bytes 786440 | tf_op jit(solution)/shard_map/ppermute | solution.py:294
  13.2 5.9 %copy-start.5 = (s32[1,1,2,2]{3,2,1,0:T(2,128)S(1)}, s32[1,1,2,2]{3,2,1,0:T(2,128)}, u32[]{:S(2)}) copy-start(s32[1,1,2,2]{3,2,1,0:T(2,128)} %param.10) | copy-start | bytes 52
  13.2 11.6 %collective-permute-start.3 = (f32[2,4,64,128]{3,2,1,0:T(8,128)S(1)}, f32[2,4,64,128]{3,2,1,0:T(8,128)S(1)}, u32[]{:S(2)}, u32[]{:S(2)}) collective-permute-start(f32[2,4,64,128]{3,2,1,0:T(8,128)S(1)} %get-tuple-element.27), channel_id=1, source_target_pairs={{0,16},{32,48},{64,80},{96,112},{128,144},{160,176},{192,208},{224... | collective-permute-start | bytes 786440 | tf_op jit(solution)/shard_map/ppermute | solution.py:296
  19.2 0.7 copy-start.4
  19.9 4.9 %copy-start.1 = (f32[2,2,128,128]{3,2,1,0:T(8,128)S(1)}, f32[2,2,128,128]{3,2,1,0:T(8,128)}, u32[]{:S(2)}) copy-start(f32[2,2,128,128]{3,2,1,0:T(8,128)} %param.6) | copy-start | bytes 786436
  30.9 30.4 %all-to-all-start = ((f32[64,16,128]{2,1,0:T(8,128)}), f32[64,16,128]{2,1,0:T(8,128)S(1)}, u32[]{:S(2)}, u32[]{:S(2)}) async-start(f32[64,16,128]{2,1,0:T(8,128)} %bitcast.3), calls=%async_computation | async-start | bytes 1048576 | tf_op jit(solution)/shard_map/all_to_all | solution.py:337
  48.1 5.2 %collective-permute-start.4 = (f32[2,4,64,128]{3,2,1,0:T(8,128)S(1)}, f32[2,4,64,128]{3,2,1,0:T(8,128)S(1)}, u32[]{:S(2)}, u32[]{:S(2)}) collective-permute-start(f32[2,4,64,128]{3,2,1,0:T(8,128)S(1)} %get-tuple-element.34), channel_id=1, source_target_pairs={{16,32},{48,64},{80,96},{112,128},{144,160},{176,192},{208,224},{2... | collective-permute-start | bytes 786440 | tf_op jit(solution)/shard_map/ppermute | solution.py:294
  48.8 12.6 %collective-permute-start.5 = (f32[2,4,64,128]{3,2,1,0:T(8,128)S(1)}, f32[2,4,64,128]{3,2,1,0:T(8,128)S(1)}, u32[]{:S(2)}, u32[]{:S(2)}) collective-permute-start(f32[2,4,64,128]{3,2,1,0:T(8,128)S(1)} %get-tuple-element.35), channel_id=1, source_target_pairs={{0,16},{32,48},{64,80},{96,112},{128,144},{160,176},{192,208},{224... | collective-permute-start | bytes 786440 | tf_op jit(solution)/shard_map/ppermute | solution.py:296
  62.1 19.2 %all-to-all-start.1 = ((f32[8,16,128]{2,1,0:T(8,128)}), f32[8,16,128]{2,1,0:T(8,128)S(1)}, u32[]{:S(2)}, u32[]{:S(2)}) async-start(f32[8,16,128]{2,1,0:T(8,128)} %get-tuple-element.36), calls=%async_computation.1 | async-start | bytes 131072 | tf_op jit(solution)/shard_map/all_to_all | solution.py:344
  69.3 9.7 %collective-permute-start.6 = (f32[2,128,128]{2,1,0:T(8,128)S(1)}, f32[2,128,128]{2,1,0:T(8,128)S(1)}, u32[]{:S(2)}, u32[]{:S(2)}) collective-permute-start(f32[2,128,128]{2,1,0:T(8,128)S(1)} %get-tuple-element.38), channel_id=1, source_target_pairs={{1,2},{3,4},{5,6},{7,8},{9,10},{11,12},{13,14},{2,1},{4,3},{6,5},{... | collective-permute-start | bytes 393224 | tf_op jit(solution)/shard_map/ppermute | solution.py:294
  75.6 3.5 %collective-permute-start.7 = (f32[2,128,128]{2,1,0:T(8,128)S(1)}, f32[2,128,128]{2,1,0:T(8,128)S(1)}, u32[]{:S(2)}, u32[]{:S(2)}) collective-permute-start(f32[2,128,128]{2,1,0:T(8,128)S(1)} %get-tuple-element.39), channel_id=1, source_target_pairs={{0,1},{2,3},{4,5},{6,7},{8,9},{10,11},{12,13},{14,15},{1,0},{3,2},... | collective-permute-start | bytes 393224 | tf_op jit(solution)/shard_map/ppermute | solution.py:296

commit v4 on v3

--- a/solution.py
+++ b/solution.py
@@ -57,27 +57,35 @@
     return jnp.where(even, first, second), jnp.where(even, second, first)
 
 
-def pack_kernel(tile, cross, mate):
-    low = low_lanes((TILE, TILE))
+def pack_columns(real, imag):
+    low = low_lanes(real.shape)
+    turned = pltpu.roll(imag, HALF, 1)
+    return jnp.where(low, turned, real), jnp.where(low, real, turned)
+
+
+def unpack_columns(from_left, from_right):
+    low = low_lanes(from_left.shape)
+    real = jnp.where(low, from_right, from_left)
+    return real, pltpu.roll(jnp.where(low, from_left, from_right), HALF, 1)
+
+
+def rows_kernel(tile, cross, mate):
+    even = even_row()
+    for p in range(4):
+        mate[p], cross[p] = by_parity(even, tile[p, HALF:], tile[p, :HALF])
+
+
+def columns_kernel(tile, from_cross, from_mate, tall, cross, mate):
+    even = even_row()
+    for p in range(4):
+        below, above = by_parity(even, from_mate[p], from_cross[p])
+        tall[p, :HALF] = above
+        tall[p, HALF:HALF + TILE] = tile[p]
+        tall[p, HALF + TILE:] = below
     even = even_column()
     for s in range(2):
-        turned = pltpu.roll(tile[2 + s], HALF, 1)
-        to_right = jnp.where(low, turned, tile[s])
-        to_left = jnp.where(low, tile[s], turned)
+        to_right, to_left = pack_columns(tall[s], tall[2 + s])
         mate[s], cross[s] = by_parity(even, to_right, to_left)
-
-
-def rows_kernel(tile, from_cross, from_mate, beside, cross, mate):
-    low = low_lanes((TILE, TILE))
-    even = even_column()
-    for s in range(2):
-        from_right, from_left = by_parity(even, from_mate[s], from_cross[s])
-        beside[s] = jnp.where(low, from_right, from_left)
-        beside[2 + s] = pltpu.roll(jnp.where(low, from_left, from_right), HALF, 1)
-    even = even_row()
-    for b, plane in enumerate((tile, beside)):
-        for p in range(4):
-            mate[b, p], cross[b, p] = by_parity(even, plane[p, HALF:], plane[p, :HALF])
 
 
 def operator_kernel(taps, probe, measured, ops, probe_near, measured_near, padded):
@@ -118,19 +126,17 @@
 
 
 def main_kernel(
-    offsets, counts, tile, beside, from_cross, from_mate, probe, measured, ops,
-    probe_grad, grad_tile, grad_beside, cross, mate,
-    object_ext, grad_ext, field_high, field_low, mid_high, mid_low, wave_one, wave_two,
+    offsets, counts, tall, from_cross, from_mate, probe, measured, ops,
+    probe_grad, grad_tall, cross, mate,
+    beside, grad_beside, field_high, field_low, mid_high, mid_low, wave_one, wave_two,
 ):
-    even = even_row()
-    mate_rows = pl.ds(pl.multiple_of(jnp.where(even, HALF + TILE, 0), HALF), HALF)
-    cross_rows = pl.ds(pl.multiple_of(jnp.where(even, 0, HALF + TILE), HALF), HALF)
-    for b, plane in enumerate((tile, beside)):
-        for p in range(4):
-            object_ext[b, p, HALF:HALF + TILE] = plane[p]
-            object_ext[b, p, mate_rows] = from_mate[b, p]
-            object_ext[b, p, cross_rows] = from_cross[b, p]
-    grad_ext[...] = jnp.zeros_like(grad_ext)
+    even = even_column()
+    for s in range(2):
+        from_right, from_left = by_parity(even, from_mate[s], from_cross[s])
+        beside[s], beside[2 + s] = unpack_columns(from_left, from_right)
+    object_ext, grad_ext = (tall, beside), (grad_tall, grad_beside)
+    for total in grad_ext:
+        total[...] = jnp.zeros_like(total)
 
     def put_field(slot, m, real, imag):
         for c, value in enumerate((real, imag)):
@@ -162,7 +168,7 @@
             cols_done(slot, which + 1, take)
 
     def window(slot, p):
-        rows = [object_ext[b, p, pl.ds(offsets[2 * slot], TILE), :] for b in range(2)]
+        rows = [object_ext[b][p, pl.ds(offsets[2 * slot], TILE), :] for b in range(2)]
         shift = lax.rem(320 - offsets[2 * slot + 1], 256)
         return pltpu.roll(jnp.concatenate(rows, axis=1), shift, 1)[:, :TILE]
 
@@ -170,7 +176,7 @@
         wide = jnp.concatenate([value, jnp.zeros_like(value)], axis=1)
         wide = pltpu.roll(wide, lax.rem(offsets[2 * slot + 1] + 192, 256), 1)
         for b in range(2):
-            grad_ext[b, p, pl.ds(offsets[2 * slot], TILE), :] += wide[:, block(b)]
+            grad_ext[b][p, pl.ds(offsets[2 * slot], TILE), :] += wide[:, block(b)]
 
     views = [[window(slot, p) for p in range(4)] for slot in range(2)]
     for slot in range(2):
@@ -234,11 +240,9 @@
             spread(slot, 2, sums[slot][1])
 
     propagate(2, after_fourth)
-    for b, plane in enumerate((grad_tile, grad_beside)):
-        for p in range(4):
-            plane[p] = grad_ext[b, p, HALF:HALF + TILE]
-            mate[b, p] = grad_ext[b, p, mate_rows]
-            cross[b, p] = grad_ext[b, p, cross_rows]
+    for s in range(2):
+        to_left, to_right = pack_columns(grad_beside[s], grad_beside[2 + s])
+        mate[s], cross[s] = by_parity(even, to_right, to_left)
 
 
 def spread_sum(scale, shares, spread_share):
@@ -247,34 +251,24 @@
         spread_share[i] = share
 
 
-def near_kernel(
-    shares, grad_tile, grad_beside, from_cross, from_mate, spread_share, part, cross, mate, beside
-):
+def near_kernel(shares, grad_tall, from_cross, from_mate, spread_share, part, cross, mate):
     spread_sum(1.0, shares, spread_share)
-    even = even_row()
-    mate_rows = pl.ds(pl.multiple_of(jnp.where(even, HALF, 0), HALF), HALF)
-    cross_rows = pl.ds(pl.multiple_of(jnp.where(even, 0, HALF), HALF), HALF)
-    for b, (plane, total) in enumerate(((grad_tile, part), (grad_beside, beside))):
-        for p in range(4):
-            total[p, mate_rows] = plane[p, mate_rows] + from_mate[b, p]
-            total[p, cross_rows] = plane[p, cross_rows] + from_cross[b, p]
-    low = low_lanes((TILE, TILE))
-    even = even_column()
+    even, even_down = even_column(), even_row()
     for s in range(2):
-        turned = pltpu.roll(beside[2 + s], HALF, 1)
-        to_right = jnp.where(low, beside[s], turned)
-        to_left = jnp.where(low, turned, beside[s])
-        mate[s], cross[s] = by_parity(even, to_right, to_left)
+        from_right, from_left = by_parity(even, from_mate[s], from_cross[s])
+        for p, sides in zip((s, 2 + s), unpack_columns(from_right, from_left)):
+            total = grad_tall[p] + sides
+            part[p] = total[HALF:HALF + TILE]
+            mate[p], cross[p] = by_parity(even_down, total[HALF + TILE:], total[:HALF])
 
 
 def far_kernel(scale, shares, part, from_cross, from_mate, spread_share, result):
     spread_sum(scale, shares, spread_share)
-    low = low_lanes((TILE, TILE))
-    even = even_column()
-    for s in range(2):
-        from_right, from_left = by_parity(even, from_mate[s], from_cross[s])
-        result[s] = part[s] + jnp.where(low, from_left, from_right)
-        result[2 + s] = part[2 + s] + pltpu.roll(jnp.where(low, from_right, from_left), HALF, 1)
+    even = even_row()
+    for p in range(4):
+        below, above = by_parity(even, from_mate[p], from_cross[p])
+        result[p, :HALF] = part[p, :HALF] + above
+        result[p, HALF:] = part[p, HALF:] + below
 
 
 def finish_kernel(result, gathered, result_far, probe_far, sems):
@@ -303,24 +297,27 @@
 
 def body(object_field, probe_modes, prop_taps, measured, offsets, counts):
     tile = object_field.reshape(4, TILE, TILE)
-    planes, strip, rim = f32(4, TILE, TILE), f32(2, TILE, TILE), f32(2, 4, HALF, TILE)
-
-    strips = exchange(*call(pack_kernel, (strip, strip), [VM], tile), COL_AXES)
-    beside, cross, mate = call(rows_kernel, (planes, rim, rim), [VM] * 3, tile, *strips)
-    rims = exchange(cross, mate, ROW_AXES)
+    planes, strip, half = f32(4, TILE, TILE), f32(2, TILE, TILE), f32(4, HALF, TILE)
+    tall, tall_strip = f32(4, 2 * TILE, TILE), f32(2, 2 * TILE, TILE)
+
+    rims = exchange(*call(rows_kernel, (half, half), [VM], tile), ROW_AXES)
+    object_tall, cross, mate = call(
+        columns_kernel, (tall, tall_strip, tall_strip), [VM] * 3, tile, *rims
+    )
+    strips = exchange(cross, mate, COL_AXES)
     ops, probe, targets = call(
         operator_kernel,
         (jax.ShapeDtypeStruct((4, 512, 256), BF16), f32(8, TILE, TILE), strip), [VM, VM, VM],
         prop_taps, probe_modes.reshape(8, TILE, TILE), measured.reshape(2, TILE, TILE),
         scratch=[pltpu.VMEM((8, 2 * TILE), F32)],
     )
-    probe_part, grad_tile, grad_beside, cross, mate = call(
+    probe_part, grad_tall, cross, mate = call(
         main_kernel,
-        (f32(8, TILE, TILE), planes, planes, rim, rim), [SM, SM] + [VM] * 7,
-        offsets.reshape(-1), counts.reshape(1, 1), tile, beside, *rims, probe, targets, ops,
+        (f32(8, TILE, TILE), tall, tall_strip, tall_strip), [SM, SM] + [VM] * 6,
+        offsets.reshape(-1), counts.reshape(1, 1), object_tall, *strips, probe, targets, ops,
         scratch=[
-            pltpu.VMEM((2, 4, 256, TILE), F32),
-            pltpu.VMEM((2, 4, 256, TILE), F32),
+            pltpu.VMEM((4, 256, TILE), F32),
+            pltpu.VMEM((4, 256, TILE), F32),
             pltpu.VMEM((2, 256, 512), BF16),
             pltpu.VMEM((2, 256, 512), BF16),
             pltpu.VMEM((2, 512, 256), BF16),
@@ -335,16 +332,15 @@
     far = lax.axis_size(FAR_AXES)
     rows = 8 * TILE // near
     shares = lax.all_to_all(probe_part.reshape(near, rows, TILE), NEAR_AXES, 0, 0, tiled=True)
+    strips = exchange(cross, mate, COL_AXES)
+    spread_share, part, cross, mate = call(
+        near_kernel, (f32(far, rows, TILE), planes, half, half), [VM] * 4, shares, grad_tall, *strips
+    )
     rims = exchange(cross, mate, ROW_AXES)
-    spread_share, part, cross, mate = call(
-        near_kernel, (f32(far, rows, TILE), planes, strip, strip), [VM] * 5,
-        shares, grad_tile, grad_beside, *rims, scratch=[pltpu.VMEM((4, TILE, TILE), F32)],
-    )
-    strips = exchange(cross, mate, COL_AXES)
     shares = lax.all_to_all(spread_share, FAR_AXES, 0, 0, tiled=True)
     spread_share, result = call(
         functools.partial(far_kernel, 1.0 / math.sqrt(near * far)),
-        (f32(near, rows, TILE), planes), [VM] * 4, shares, part, *strips,
+        (f32(near, rows, TILE), planes), [VM] * 4, shares, part, *rims,
     )
     gathered = lax.all_to_all(spread_share, NEAR_AXES, 0, 0, tiled=True)
     result, probe_grad = call(

time: 105 us -> 103 us (0.981)
  blocking collectives: 22.2 us -> 19.9 us
  starting transfers between devices: 53.4 us -> 52 us
  waiting for transfers between devices: 17.3 us -> 18.7 us
    ppermute x4, waiting for transfers between devices: 1.54 us -> 10.3 us  [exchange(): from_cross = lax.ppermute(cross, axes, pairs + [(b, a) for a, b in pairs])]
    ppermute x4, waiting for transfers between devices: 13.5 us -> 6.26 us  [exchange(): from_mate = lax.ppermute(mate, axes, pairs + [(b, a) for a, b in pairs])]
    all_to_all x1, blocking collectives: 22.2 us -> 19.9 us  [body(): gathered = lax.all_to_all(spread_share, NEAR_AXES, 0, 0, tiled=True)]
    all_to_all x1, starting transfers between devices: 17.1 us -> 15.3 us  [body(): lax.all_to_all(probe_part.reshape(near, rows, TILE), NEAR_AXES, 0, 0, til...]
    ppermute x4, starting transfers between devices: 15.3 us -> 17 us  [exchange(): from_mate = lax.ppermute(mate, axes, pairs + [(b, a) for a, b in pairs])]
where the time goes in v4:
time: 103 us; the launch traced here: 102 us
  starting transfers between devices  52 us (50%)
  blocking collectives  19.9 us (19%)
  waiting for transfers between devices  18.7 us (18%)
  Pallas kernels  8.61 us (8%)
  local copies, waits for them, and re-layouts  1.72 us (2%)
  between operations  1.43 us (1%)
    all_to_all x1, blocking collectives, body(): gathered = lax.all_to_all(spread_share, NEAR_AXES, 0, 0, tiled=True)  19.9 us
    ppermute x4, starting transfers between devices, exchange(): from_mate = lax.ppermute(mate, axes, pairs + [(b, a) for a, b in pairs])  17 us
    all_to_all x1, starting transfers between devices, body(): lax.all_to_all(probe_part.reshape(near, rows, TILE), NEAR_AXES, 0, 0, til...  15.3 us
    ppermute x4, starting transfers between devices, exchange(): from_cross = lax.ppermute(cross, axes, pairs + [(b, a) for a, b in pairs])  13.1 us
    ppermute x4, waiting for transfers between devices, exchange(): from_cross = lax.ppermute(cross, axes, pairs + [(b, a) for a, b in pairs])  10.3 us
    pallas_call x7, Pallas kernels, call(): pl.pallas_call(kernel, out_shape=out_shape, in_specs=in_specs, out_specs=...  8.61 us
    all_to_all x1, starting transfers between devices, body(): shares = lax.all_to_all(spread_share, FAR_AXES, 0, 0, tiled=True)  6.54 us
    ppermute x4, waiting for transfers between devices, exchange(): from_mate = lax.ppermute(mate, axes, pairs + [(b, a) for a, b in pairs])  6.26 us
  transfers between devices with their start and end apart: 10, of which 5 were waited for; matrix products, arithmetic and copies ran while one was open for 0% of the time, Pallas kernels for 0%

profile of v4, /device:TPU:1, one launch (start us, length us, event | category | flops | bytes accessed | tf_op | source)
XLA Modules:
  0.0 102.3 jit_solution(15689272481399919489)
XLA Ops:
  0.6 0.9 copy-done
  1.6 0.8 collective-permute-start
  2.4 7.4 %collective-permute-start.1 = (f32[4,64,128]{2,1,0:T(8,128)S(1)}, f32[4,64,128]{2,1,0:T(8,128)S(1)}, u32[]{:S(2)}, u32[]{:S(2)}) collective-permute-start(f32[4,64,128]{2,1,0:T(8,128)S(1)} %get-tuple-element.23), channel_id=1, source_target_pairs={{0,16},{32,48},{64,80},{96,112},{128,144},{160,176},{192,208},{224... | collective-permute-start | bytes 393224 | tf_op jit(solution)/shard_map/ppermute | solution.py:290
  9.8 2.3 %collective-permute-done.1.from_mate = f32[4,64,128]{2,1,0:T(8,128)S(1)} collective-permute-done((f32[4,64,128]{2,1,0:T(8,128)S(1)}, f32[4,64,128]{2,1,0:T(8,128)S(1)}, u32[]{:S(2)}, u32[]{:S(2)}) %collective-permute-start.1) | collective-permute-done | bytes 131104 | tf_op jit(solution)/shard_map/ppermute | solution.py:290
  12.2 0.1 shard_map.78
  12.3 6.6 %collective-permute-start.2 = (f32[2,256,128]{2,1,0:T(8,128)S(1)}, f32[2,256,128]{2,1,0:T(8,128)S(1)}, u32[]{:S(2)}, u32[]{:S(2)}) collective-permute-start(f32[2,256,128]{2,1,0:T(8,128)S(1)} %get-tuple-element.25), channel_id=1, source_target_pairs={{1,2},{3,4},{5,6},{7,8},{9,10},{11,12},{13,14},{2,1},{4,3},{6,5},{... | collective-permute-start | bytes 786440 | tf_op jit(solution)/shard_map/ppermute | solution.py:288
  19.0 1.9 %collective-permute-start.3 = (f32[2,256,128]{2,1,0:T(8,128)S(1)}, f32[2,256,128]{2,1,0:T(8,128)S(1)}, u32[]{:S(2)}, u32[]{:S(2)}) collective-permute-start(f32[2,256,128]{2,1,0:T(8,128)S(1)} %get-tuple-element.26), channel_id=1, source_target_pairs={{0,1},{2,3},{4,5},{6,7},{8,9},{10,11},{12,13},{14,15},{1,0},{3,2},... | collective-permute-start | bytes 786440 | tf_op jit(solution)/shard_map/ppermute | solution.py:290
  21.6 0.1 reshape.28.offsets
  21.6 0.7 copy-done.3
  22.3 0.3 shard_map.79
  22.6 2.2 %collective-permute-done.2.from_cross = f32[2,256,128]{2,1,0:T(8,128)S(1)} collective-permute-done((f32[2,256,128]{2,1,0:T(8,128)S(1)}, f32[2,256,128]{2,1,0:T(8,128)S(1)}, u32[]{:S(2)}, u32[]{:S(2)}) %collective-permute-start.2) | collective-permute-done | bytes 262176 | tf_op jit(solution)/shard_map/ppermute | solution.py:288
  24.9 6.4 %shard_map.80 = (f32[8,128,128]{2,1,0:T(8,128)}, f32[4,256,128]{2,1,0:T(8,128)S(1)}, f32[2,256,128]{2,1,0:T(8,128)S(1)}, f32[2,256,128]{2,1,0:T(8,128)S(1)}) custom-call(s32[4]{0:T(128)S(1)} %reshape.28.offsets, s32[1,1]{1,0:T(1,128)S(6)} %copy.8.counts, f32[4,256,128]{2,1,0:T(8,128)S(1)} %get-tuple-element.24.tall, ...), custom_call_target="tpu_custom_call" | custom-call | flops 3200000000 | bytes 4000000 | tf_op jit(solution)/shard_map/pallas_call | solution.py:28
  31.2 15.3 %all-to-all-start = ((f32[64,16,128]{2,1,0:T(8,128)}), f32[64,16,128]{2,1,0:T(8,128)S(1)}, u32[]{:S(2)}, u32[]{:S(2)}) async-start(f32[64,16,128]{2,1,0:T(8,128)} %bitcast.3), calls=%async_computation | async-start | bytes 1048576 | tf_op jit(solution)/shard_map/all_to_all | solution.py:334
  46.5 5.0 %collective-permute-start.4 = (f32[2,256,128]{2,1,0:T(8,128)S(1)}, f32[2,256,128]{2,1,0:T(8,128)S(1)}, u32[]{:S(2)}, u32[]{:S(2)}) collective-permute-start(f32[2,256,128]{2,1,0:T(8,128)S(1)} %get-tuple-element.32), channel_id=1, source_target_pairs={{1,2},{3,4},{5,6},{7,8},{9,10},{11,12},{13,14},{2,1},{4,3},{6,5},{... | collective-permute-start | bytes 786440 | tf_op jit(solution)/shard_map/ppermute | solution.py:288
  51.6 1.9 %collective-permute-start.5 = (f32[2,256,128]{2,1,0:T(8,128)S(1)}, f32[2,256,128]{2,1,0:T(8,128)S(1)}, u32[]{:S(2)}, u32[]{:S(2)}) collective-permute-start(f32[2,256,128]{2,1,0:T(8,128)S(1)} %get-tuple-element.33), channel_id=1, source_target_pairs={{0,1},{2,3},{4,5},{6,7},{8,9},{10,11},{12,13},{14,15},{1,0},{3,2},... | collective-permute-start | bytes 786440 | tf_op jit(solution)/shard_map/ppermute | solution.py:290
  53.5 8.1 %collective-permute-done.4.from_cross = f32[2,256,128]{2,1,0:T(8,128)S(1)} collective-permute-done((f32[2,256,128]{2,1,0:T(8,128)S(1)}, f32[2,256,128]{2,1,0:T(8,128)S(1)}, u32[]{:S(2)}, u32[]{:S(2)}) %collective-permute-start.4) | collective-permute-done | bytes 262176 | tf_op jit(solution)/shard_map/ppermute | solution.py:288
  61.6 0.8 shard_map.81
  62.4 6.5 %all-to-all-start.1 = ((f32[8,16,128]{2,1,0:T(8,128)}), f32[8,16,128]{2,1,0:T(8,128)S(1)}, u32[]{:S(2)}, u32[]{:S(2)}) async-start(f32[8,16,128]{2,1,0:T(8,128)} %get-tuple-element.34), calls=%async_computation.1 | async-start | bytes 131072 | tf_op jit(solution)/shard_map/all_to_all | solution.py:340
  68.9 0.7 collective-permute-start.6
  69.6 5.8 %collective-permute-start.7 = (f32[4,64,128]{2,1,0:T(8,128)S(1)}, f32[4,64,128]{2,1,0:T(8,128)S(1)}, u32[]{:S(2)}, u32[]{:S(2)}) collective-permute-start(f32[4,64,128]{2,1,0:T(8,128)S(1)} %get-tuple-element.37), channel_id=1, source_target_pairs={{0,16},{32,48},{64,80},{96,112},{128,144},{160,176},{192,208},{224... | collective-permute-start | bytes 393224 | tf_op jit(solution)/shard_map/ppermute | solution.py:290
  75.4 3.9 %collective-permute-done.7.from_mate = f32[4,64,128]{2,1,0:T(8,128)S(1)} collective-permute-done((f32[4,64,128]{2,1,0:T(8,128)S(1)}, f32[4,64,128]{2,1,0:T(8,128)S(1)}, u32[]{:S(2)}, u32[]{:S(2)}) %collective-permute-start.7) | collective-permute-done | bytes 131104 | tf_op jit(solution)/shard_map/ppermute | solution.py:290
  79.3 2.1 %all-to-all-done.1.shares = f32[8,16,128]{2,1,0:T(8,128)S(1)} async-done(((f32[8,16,128]{2,1,0:T(8,128)}), f32[8,16,128]{2,1,0:T(8,128)S(1)}, u32[]{:S(2)}, u32[]{:S(2)}) %all-to-all-start.1) | async-done | bytes 65568 | tf_op jit(solution)/shard_map/all_to_all | solution.py:340
  81.5 19.9 %all_to_all.15 = f32[64,16,128]{2,1,0:T(8,128)S(1)} all-to-all(f32[64,16,128]{2,1,0:T(8,128)S(1)} %get-tuple-element.39), channel_id=1, replica_groups=mesh['xl'=2,'za'=8,'zb'=2,'y'=4,'xh'=2,'core'=2] {'xl','zb','y','xh','co..., dimensions={0} | all-to-all | bytes 1048576 | tf_op jit(solution)/shard_map/all_to_all | solution.py:345
  101.4 0.9 shard_map.83
  (15 shorter events, 0.1 us)
Async XLA Ops:
  0.6 1.0 copy-start
  1.6 20.1 %copy-start.1 = (f32[2,4,128,128]{3,2,1,0:T(8,128)S(1)}, f32[2,4,128,128]{3,2,1,0:T(8,128)}, u32[]{:S(2)}) copy-start(f32[2,4,128,128]{3,2,1,0:T(8,128)} %param.7) | copy-start | bytes 1572868
  1.6 8.2 %collective-permute-start = (f32[4,64,128]{2,1,0:T(8,128)S(1)}, f32[4,64,128]{2,1,0:T(8,128)S(1)}, u32[]{:S(2)}, u32[]{:S(2)}) collective-permute-start(f32[4,64,128]{2,1,0:T(8,128)S(1)} %get-tuple-element.22), channel_id=1, source_target_pairs={{16,32},{48,64},{80,96},{112,128},{144,160},{176,192},{208,224},{2... | collective-permute-start | bytes 393224 | tf_op jit(solution)/shard_map/ppermute | solution.py:288
  2.4 19.2 %copy-start.2 = (f32[1,1,2,128,128]{4,3,2,1,0:T(8,128)S(1)}, f32[1,1,2,128,128]{4,3,2,1,0:T(8,128)}, u32[]{:S(2)}) copy-start(f32[1,1,2,128,128]{4,3,2,1,0:T(8,128)} %param.9) | copy-start | bytes 393220
  2.4 9.7 %collective-permute-start.1 = (f32[4,64,128]{2,1,0:T(8,128)S(1)}, f32[4,64,128]{2,1,0:T(8,128)S(1)}, u32[]{:S(2)}, u32[]{:S(2)}) collective-permute-start(f32[4,64,128]{2,1,0:T(8,128)S(1)} %get-tuple-element.23), channel_id=1, source_target_pairs={{0,16},{32,48},{64,80},{96,112},{128,144},{160,176},{192,208},{224... | collective-permute-start | bytes 393224 | tf_op jit(solution)/shard_map/ppermute | solution.py:290
  12.3 12.6 %collective-permute-start.2 = (f32[2,256,128]{2,1,0:T(8,128)S(1)}, f32[2,256,128]{2,1,0:T(8,128)S(1)}, u32[]{:S(2)}, u32[]{:S(2)}) collective-permute-start(f32[2,256,128]{2,1,0:T(8,128)S(1)} %get-tuple-element.25), channel_id=1, source_target_pairs={{1,2},{3,4},{5,6},{7,8},{9,10},{11,12},{13,14},{2,1},{4,3},{6,5},{... | collective-permute-start | bytes 786440 | tf_op jit(solution)/shard_map/ppermute | solution.py:288
  19.0 2.6 %copy-start.4 = (s32[1,1,2,2]{3,2,1,0:T(2,128)S(1)}, s32[1,1,2,2]{3,2,1,0:T(2,128)}, u32[]{:S(2)}) copy-start(s32[1,1,2,2]{3,2,1,0:T(2,128)} %param.10) | copy-start | bytes 52
  19.0 5.9 %collective-permute-start.3 = (f32[2,256,128]{2,1,0:T(8,128)S(1)}, f32[2,256,128]{2,1,0:T(8,128)S(1)}, u32[]{:S(2)}, u32[]{:S(2)}) collective-permute-start(f32[2,256,128]{2,1,0:T(8,128)S(1)} %get-tuple-element.26), channel_id=1, source_target_pairs={{0,1},{2,3},{4,5},{6,7},{8,9},{10,11},{12,13},{14,15},{1,0},{3,2},... | collective-permute-start | bytes 786440 | tf_op jit(solution)/shard_map/ppermute | solution.py:290
  21.6 0.7 copy-start.3
  31.2 30.4 %all-to-all-start = ((f32[64,16,128]{2,1,0:T(8,128)}), f32[64,16,128]{2,1,0:T(8,128)S(1)}, u32[]{:S(2)}, u32[]{:S(2)}) async-start(f32[64,16,128]{2,1,0:T(8,128)} %bitcast.3), calls=%async_computation | async-start | bytes 1048576 | tf_op jit(solution)/shard_map/all_to_all | solution.py:334
  46.5 15.1 %collective-permute-start.4 = (f32[2,256,128]{2,1,0:T(8,128)S(1)}, f32[2,256,128]{2,1,0:T(8,128)S(1)}, u32[]{:S(2)}, u32[]{:S(2)}) collective-permute-start(f32[2,256,128]{2,1,0:T(8,128)S(1)} %get-tuple-element.32), channel_id=1, source_target_pairs={{1,2},{3,4},{5,6},{7,8},{9,10},{11,12},{13,14},{2,1},{4,3},{6,5},{... | collective-permute-start | bytes 786440 | tf_op jit(solution)/shard_map/ppermute | solution.py:288
  51.6 10.0 %collective-permute-start.5 = (f32[2,256,128]{2,1,0:T(8,128)S(1)}, f32[2,256,128]{2,1,0:T(8,128)S(1)}, u32[]{:S(2)}, u32[]{:S(2)}) collective-permute-start(f32[2,256,128]{2,1,0:T(8,128)S(1)} %get-tuple-element.33), channel_id=1, source_target_pairs={{0,1},{2,3},{4,5},{6,7},{8,9},{10,11},{12,13},{14,15},{1,0},{3,2},... | collective-permute-start | bytes 786440 | tf_op jit(solution)/shard_map/ppermute | solution.py:290
  62.4 19.0 %all-to-all-start.1 = ((f32[8,16,128]{2,1,0:T(8,128)}), f32[8,16,128]{2,1,0:T(8,128)S(1)}, u32[]{:S(2)}, u32[]{:S(2)}) async-start(f32[8,16,128]{2,1,0:T(8,128)} %get-tuple-element.34), calls=%async_computation.1 | async-start | bytes 131072 | tf_op jit(solution)/shard_map/all_to_all | solution.py:340
  68.9 6.5 %collective-permute-start.6 = (f32[4,64,128]{2,1,0:T(8,128)S(1)}, f32[4,64,128]{2,1,0:T(8,128)S(1)}, u32[]{:S(2)}, u32[]{:S(2)}) collective-permute-start(f32[4,64,128]{2,1,0:T(8,128)S(1)} %get-tuple-element.36), channel_id=1, source_target_pairs={{16,32},{48,64},{80,96},{112,128},{144,160},{176,192},{208,224},{2... | collective-permute-start | bytes 393224 | tf_op jit(solution)/shard_map/ppermute | solution.py:288
  69.6 9.7 %collective-permute-start.7 = (f32[4,64,128]{2,1,0:T(8,128)S(1)}, f32[4,64,128]{2,1,0:T(8,128)S(1)}, u32[]{:S(2)}, u32[]{:S(2)}) collective-permute-start(f32[4,64,128]{2,1,0:T(8,128)S(1)} %get-tuple-element.37), channel_id=1, source_target_pairs={{0,16},{32,48},{64,80},{96,112},{128,144},{160,176},{192,208},{224... | collective-permute-start | bytes 393224 | tf_op jit(solution)/shard_map/ppermute | solution.py:290

commit v5 on v4

--- a/solution.py
+++ b/solution.py
@@ -251,8 +251,12 @@
         spread_share[i] = share
 
 
-def near_kernel(shares, grad_tall, from_cross, from_mate, spread_share, part, cross, mate):
+def near_kernel(shares, spread_share):
     spread_sum(1.0, shares, spread_share)
+
+
+def far_kernel(scale, shares, grad_tall, from_cross, from_mate, spread_share, part, cross, mate):
+    spread_sum(scale, shares, spread_share)
     even, even_down = even_column(), even_row()
     for s in range(2):
         from_right, from_left = by_parity(even, from_mate[s], from_cross[s])
@@ -262,22 +266,19 @@
             mate[p], cross[p] = by_parity(even_down, total[HALF + TILE:], total[:HALF])
 
 
-def far_kernel(scale, shares, part, from_cross, from_mate, spread_share, result):
-    spread_sum(scale, shares, spread_share)
+def finish_kernel(part, from_cross, from_mate, gathered, result_far, probe_far, result, sems):
+    moves = []
+    for i in range(4):
+        rows = pl.ds(256 * i, 256)
+        moves.append(pltpu.make_async_copy(gathered.at[rows], probe_far.at[rows], sems.at[i]))
+        moves[i].start()
     even = even_row()
     for p in range(4):
         below, above = by_parity(even, from_mate[p], from_cross[p])
         result[p, :HALF] = part[p, :HALF] + above
         result[p, HALF:] = part[p, HALF:] + below
-
-
-def finish_kernel(result, gathered, result_far, probe_far, sems):
-    moves = [pltpu.make_async_copy(result.at[p], result_far.at[p], sems.at[p]) for p in range(4)]
-    for i in range(4):
-        part = pl.ds(256 * i, 256)
-        moves.append(pltpu.make_async_copy(gathered.at[part], probe_far.at[part], sems.at[4 + i]))
-    for move in moves:
-        move.start()
+        moves.append(pltpu.make_async_copy(result.at[p], result_far.at[p], sems.at[4 + p]))
+        moves[-1].start()
     for move in moves:
         move.wait()
 
@@ -332,21 +333,20 @@
     far = lax.axis_size(FAR_AXES)
     rows = 8 * TILE // near
     shares = lax.all_to_all(probe_part.reshape(near, rows, TILE), NEAR_AXES, 0, 0, tiled=True)
+    (spread_share,) = call(near_kernel, (f32(far, rows, TILE),), [VM], shares)
     strips = exchange(cross, mate, COL_AXES)
+    shares = lax.all_to_all(spread_share, FAR_AXES, 0, 0, tiled=True)
     spread_share, part, cross, mate = call(
-        near_kernel, (f32(far, rows, TILE), planes, half, half), [VM] * 4, shares, grad_tall, *strips
+        functools.partial(far_kernel, 1.0 / math.sqrt(near * far)),
+        (f32(near, rows, TILE), planes, half, half), [VM] * 4, shares, grad_tall, *strips,
     )
     rims = exchange(cross, mate, ROW_AXES)
-    shares = lax.all_to_all(spread_share, FAR_AXES, 0, 0, tiled=True)
-    spread_share, result = call(
-        functools.partial(far_kernel, 1.0 / math.sqrt(near * far)),
-        (f32(near, rows, TILE), planes), [VM] * 4, shares, part, *rims,
-    )
     gathered = lax.all_to_all(spread_share, NEAR_AXES, 0, 0, tiled=True)
     result, probe_grad = call(
-        finish_kernel, (planes, f32(8 * TILE, TILE)), [VM] * 2,
-        result, gathered.reshape(8 * TILE, TILE),
-        scratch=[pltpu.SemaphoreType.DMA((8,))], out_specs=[FAR, FAR],
+        finish_kernel, (planes, f32(8 * TILE, TILE)), [VM] * 4,
+        part, *rims, gathered.reshape(8 * TILE, TILE),
+        scratch=[pltpu.VMEM((4, TILE, TILE), F32), pltpu.SemaphoreType.DMA((8,))],
+        out_specs=[FAR, FAR],
     )
     return result.reshape(object_field.shape), probe_grad.reshape(probe_modes.shape)
 

time: 103 us -> 104 us (level)
  blocking collectives: 19.9 us -> 0 us
  waiting for transfers between devices: 18.7 us -> 29 us
  starting transfers between devices: 52 us -> 61.5 us
    all_to_all x1 -> x0, blocking collectives: 19.9 us -> none  [body(): gathered = lax.all_to_all(spread_share, NEAR_AXES, 0, 0, tiled=True)]
    all_to_all x1, waiting for transfers between devices: 2.09 us -> 12.9 us  [body(): shares = lax.all_to_all(spread_share, FAR_AXES, 0, 0, tiled=True)]
    all_to_all x0 -> x1, starting transfers between devices: none -> 10.8 us  [body(): gathered = lax.all_to_all(spread_share, NEAR_AXES, 0, 0, tiled=True)]
    ppermute x4, waiting for transfers between devices: 10.3 us -> 2.24 us  [exchange(): from_cross = lax.ppermute(cross, axes, pairs + [(b, a) for a, b in pairs])]
    all_to_all x1, waiting for transfers between devices: 0.01 us -> 5.02 us  [body(): lax.all_to_all(probe_part.reshape(near, rows, TILE), NEAR_AXES, 0, 0, til...]
    all_to_all x0 -> x1, waiting for transfers between devices: none -> 1.33 us  [body(): gathered = lax.all_to_all(spread_share, NEAR_AXES, 0, 0, tiled=True)]
    ppermute x4, waiting for transfers between devices: 6.26 us -> 7.52 us  [exchange(): from_mate = lax.ppermute(mate, axes, pairs + [(b, a) for a, b in pairs])]
    ppermute x4, starting transfers between devices: 17 us -> 15.8 us  [exchange(): from_mate = lax.ppermute(mate, axes, pairs + [(b, a) for a, b in pairs])]
  transfers between devices with their start and end apart: 10 -> 11, of which waited for: 5 -> 6; matrix products, arithmetic and copies ran while one was open for 0% -> 0% of each run, Pallas kernels for 0% -> 1%
where the time goes in v5:
time: 104 us; the launch traced here: 103 us
  starting transfers between devices  61.5 us (59%)
  waiting for transfers between devices  29 us (28%)
  Pallas kernels  9.37 us (9%)
  local copies, waits for them, and re-layouts  1.72 us (2%)
  between operations  1.45 us (1%)
    ppermute x4, starting transfers between devices, exchange(): from_mate = lax.ppermute(mate, axes, pairs + [(b, a) for a, b in pairs])  15.8 us
    all_to_all x1, starting transfers between devices, body(): lax.all_to_all(probe_part.reshape(near, rows, TILE), NEAR_AXES, 0, 0, til...  15.3 us
    ppermute x4, starting transfers between devices, exchange(): from_cross = lax.ppermute(cross, axes, pairs + [(b, a) for a, b in pairs])  13.1 us
    all_to_all x1, waiting for transfers between devices, body(): shares = lax.all_to_all(spread_share, FAR_AXES, 0, 0, tiled=True)  12.9 us
    all_to_all x1, starting transfers between devices, body(): gathered = lax.all_to_all(spread_share, NEAR_AXES, 0, 0, tiled=True)  10.8 us
    pallas_call x7, Pallas kernels, call(): pl.pallas_call(kernel, out_shape=out_shape, in_specs=in_specs, out_specs=...  9.37 us
    ppermute x4, waiting for transfers between devices, exchange(): from_mate = lax.ppermute(mate, axes, pairs + [(b, a) for a, b in pairs])  7.52 us
    all_to_all x1, starting transfers between devices, body(): shares = lax.all_to_all(spread_share, FAR_AXES, 0, 0, tiled=True)  6.52 us
  transfers between devices with their start and end apart: 11, of which 6 were waited for; matrix products, arithmetic and copies ran while one was open for 0% of the time, Pallas kernels for 1%

profile of v5, /device:TPU:1, one launch (start us, length us, event | category | flops | bytes accessed | tf_op | source)
XLA Modules:
  0.0 103.0 jit_solution(127034928990209419)
XLA Ops:
  0.6 0.9 copy-done
  1.6 0.8 collective-permute-start
  2.4 7.4 %collective-permute-start.1 = (f32[4,64,128]{2,1,0:T(8,128)S(1)}, f32[4,64,128]{2,1,0:T(8,128)S(1)}, u32[]{:S(2)}, u32[]{:S(2)}) collective-permute-start(f32[4,64,128]{2,1,0:T(8,128)S(1)} %get-tuple-element.21), channel_id=1, source_target_pairs={{0,16},{32,48},{64,80},{96,112},{128,144},{160,176},{192,208},{224... | collective-permute-start | bytes 393224 | tf_op jit(solution)/shard_map/ppermute | solution.py:291
  9.8 2.3 %collective-permute-done.1.from_mate = f32[4,64,128]{2,1,0:T(8,128)S(1)} collective-permute-done((f32[4,64,128]{2,1,0:T(8,128)S(1)}, f32[4,64,128]{2,1,0:T(8,128)S(1)}, u32[]{:S(2)}, u32[]{:S(2)}) %collective-permute-start.1) | collective-permute-done | bytes 131104 | tf_op jit(solution)/shard_map/ppermute | solution.py:291
  12.3 6.6 %collective-permute-start.2 = (f32[2,256,128]{2,1,0:T(8,128)S(1)}, f32[2,256,128]{2,1,0:T(8,128)S(1)}, u32[]{:S(2)}, u32[]{:S(2)}) collective-permute-start(f32[2,256,128]{2,1,0:T(8,128)S(1)} %get-tuple-element.23), channel_id=1, source_target_pairs={{1,2},{3,4},{5,6},{7,8},{9,10},{11,12},{13,14},{2,1},{4,3},{6,5},{... | collective-permute-start | bytes 786440 | tf_op jit(solution)/shard_map/ppermute | solution.py:289
  19.0 1.9 %collective-permute-start.3 = (f32[2,256,128]{2,1,0:T(8,128)S(1)}, f32[2,256,128]{2,1,0:T(8,128)S(1)}, u32[]{:S(2)}, u32[]{:S(2)}) collective-permute-start(f32[2,256,128]{2,1,0:T(8,128)S(1)} %get-tuple-element.24), channel_id=1, source_target_pairs={{0,1},{2,3},{4,5},{6,7},{8,9},{10,11},{12,13},{14,15},{1,0},{3,2},... | collective-permute-start | bytes 786440 | tf_op jit(solution)/shard_map/ppermute | solution.py:291
  21.6 0.7 copy-done.3
  22.3 0.3 shard_map.79
  22.6 2.2 %collective-permute-done.2.from_cross = f32[2,256,128]{2,1,0:T(8,128)S(1)} collective-permute-done((f32[2,256,128]{2,1,0:T(8,128)S(1)}, f32[2,256,128]{2,1,0:T(8,128)S(1)}, u32[]{:S(2)}, u32[]{:S(2)}) %collective-permute-start.2) | collective-permute-done | bytes 262176 | tf_op jit(solution)/shard_map/ppermute | solution.py:289
  24.9 6.3 %shard_map.80 = (f32[8,128,128]{2,1,0:T(8,128)}, f32[4,256,128]{2,1,0:T(8,128)S(1)}, f32[2,256,128]{2,1,0:T(8,128)S(1)}, f32[2,256,128]{2,1,0:T(8,128)S(1)}) custom-call(s32[4]{0:T(128)S(1)} %reshape.28.offsets, s32[1,1]{1,0:T(1,128)S(6)} %copy.8.counts, f32[4,256,128]{2,1,0:T(8,128)S(1)} %get-tuple-element.22.tall, ...), custom_call_target="tpu_custom_call" | custom-call | flops 3200000000 | bytes 4000000 | tf_op jit(solution)/shard_map/pallas_call | solution.py:28
  31.2 15.3 %all-to-all-start = ((f32[64,16,128]{2,1,0:T(8,128)}), f32[64,16,128]{2,1,0:T(8,128)S(1)}, u32[]{:S(2)}, u32[]{:S(2)}) async-start(f32[64,16,128]{2,1,0:T(8,128)} %bitcast.3), calls=%async_computation | async-start | bytes 1048576 | tf_op jit(solution)/shard_map/all_to_all | solution.py:335
  46.5 5.0 %collective-permute-start.4 = (f32[2,256,128]{2,1,0:T(8,128)S(1)}, f32[2,256,128]{2,1,0:T(8,128)S(1)}, u32[]{:S(2)}, u32[]{:S(2)}) collective-permute-start(f32[2,256,128]{2,1,0:T(8,128)S(1)} %get-tuple-element.30), channel_id=1, source_target_pairs={{1,2},{3,4},{5,6},{7,8},{9,10},{11,12},{13,14},{2,1},{4,3},{6,5},{... | collective-permute-start | bytes 786440 | tf_op jit(solution)/shard_map/ppermute | solution.py:289
  51.6 1.9 %collective-permute-start.5 = (f32[2,256,128]{2,1,0:T(8,128)S(1)}, f32[2,256,128]{2,1,0:T(8,128)S(1)}, u32[]{:S(2)}, u32[]{:S(2)}) collective-permute-start(f32[2,256,128]{2,1,0:T(8,128)S(1)} %get-tuple-element.31), channel_id=1, source_target_pairs={{0,1},{2,3},{4,5},{6,7},{8,9},{10,11},{12,13},{14,15},{1,0},{3,2},... | collective-permute-start | bytes 786440 | tf_op jit(solution)/shard_map/ppermute | solution.py:291
  53.5 5.0 %all-to-all-done.shares = f32[64,16,128]{2,1,0:T(8,128)S(1)} async-done(((f32[64,16,128]{2,1,0:T(8,128)}), f32[64,16,128]{2,1,0:T(8,128)S(1)}, u32[]{:S(2)}, u32[]{:S(2)}) %all-to-all-start) | async-done | bytes 524320 | tf_op jit(solution)/shard_map/all_to_all | solution.py:335
  58.5 0.7 shard_map.81
  59.2 6.5 %all-to-all-start.1 = ((f32[8,16,128]{2,1,0:T(8,128)}), f32[8,16,128]{2,1,0:T(8,128)S(1)}, u32[]{:S(2)}, u32[]{:S(2)}) async-start(f32[8,16,128]{2,1,0:T(8,128)} %shard_map.81), calls=%async_computation.1 | async-start | bytes 131072 | tf_op jit(solution)/shard_map/all_to_all | solution.py:338
  65.8 12.9 %all-to-all-done.1.shares = f32[8,16,128]{2,1,0:T(8,128)S(1)} async-done(((f32[8,16,128]{2,1,0:T(8,128)}), f32[8,16,128]{2,1,0:T(8,128)S(1)}, u32[]{:S(2)}, u32[]{:S(2)}) %all-to-all-start.1) | async-done | bytes 65568 | tf_op jit(solution)/shard_map/all_to_all | solution.py:338
  78.6 0.9 shard_map.82
  79.5 10.8 %all-to-all-start.2 = ((f32[64,16,128]{2,1,0:T(8,128)}), f32[64,16,128]{2,1,0:T(8,128)S(1)}, u32[]{:S(2)}, u32[]{:S(2)}) async-start(f32[64,16,128]{2,1,0:T(8,128)} %get-tuple-element.35), calls=%async_computation.2 | async-start | bytes 1048576 | tf_op jit(solution)/shard_map/all_to_all | solution.py:344
  90.3 0.7 collective-permute-start.6
  91.0 4.6 %collective-permute-start.7 = (f32[4,64,128]{2,1,0:T(8,128)S(1)}, f32[4,64,128]{2,1,0:T(8,128)S(1)}, u32[]{:S(2)}, u32[]{:S(2)}) collective-permute-start(f32[4,64,128]{2,1,0:T(8,128)S(1)} %get-tuple-element.34), channel_id=1, source_target_pairs={{0,16},{32,48},{64,80},{96,112},{128,144},{160,176},{192,208},{224... | collective-permute-start | bytes 393224 | tf_op jit(solution)/shard_map/ppermute | solution.py:291
  95.6 5.2 %collective-permute-done.7.from_mate = f32[4,64,128]{2,1,0:T(8,128)S(1)} collective-permute-done((f32[4,64,128]{2,1,0:T(8,128)S(1)}, f32[4,64,128]{2,1,0:T(8,128)S(1)}, u32[]{:S(2)}, u32[]{:S(2)}) %collective-permute-start.7) | collective-permute-done | bytes 131104 | tf_op jit(solution)/shard_map/ppermute | solution.py:291
  100.7 1.3 %all-to-all-done.2 = f32[64,16,128]{2,1,0:T(8,128)S(1)} async-done(((f32[64,16,128]{2,1,0:T(8,128)}), f32[64,16,128]{2,1,0:T(8,128)S(1)}, u32[]{:S(2)}, u32[]{:S(2)}) %all-to-all-start.2) | async-done | bytes 524320 | tf_op jit(solution)/shard_map/all_to_all | solution.py:344
  102.1 0.9 shard_map.83
  (16 shorter events, 0.3 us)
Async XLA Ops:
  0.6 1.0 copy-start
  1.6 20.1 %copy-start.1 = (f32[2,4,128,128]{3,2,1,0:T(8,128)S(1)}, f32[2,4,128,128]{3,2,1,0:T(8,128)}, u32[]{:S(2)}) copy-start(f32[2,4,128,128]{3,2,1,0:T(8,128)} %param.7) | copy-start | bytes 1572868
  1.6 8.2 %collective-permute-start = (f32[4,64,128]{2,1,0:T(8,128)S(1)}, f32[4,64,128]{2,1,0:T(8,128)S(1)}, u32[]{:S(2)}, u32[]{:S(2)}) collective-permute-start(f32[4,64,128]{2,1,0:T(8,128)S(1)} %get-tuple-element.20), channel_id=1, source_target_pairs={{16,32},{48,64},{80,96},{112,128},{144,160},{176,192},{208,224},{2... | collective-permute-start | bytes 393224 | tf_op jit(solution)/shard_map/ppermute | solution.py:289
  2.4 19.2 %copy-start.2 = (f32[1,1,2,128,128]{4,3,2,1,0:T(8,128)S(1)}, f32[1,1,2,128,128]{4,3,2,1,0:T(8,128)}, u32[]{:S(2)}) copy-start(f32[1,1,2,128,128]{4,3,2,1,0:T(8,128)} %param.9) | copy-start | bytes 393220
  2.4 9.7 %collective-permute-start.1 = (f32[4,64,128]{2,1,0:T(8,128)S(1)}, f32[4,64,128]{2,1,0:T(8,128)S(1)}, u32[]{:S(2)}, u32[]{:S(2)}) collective-permute-start(f32[4,64,128]{2,1,0:T(8,128)S(1)} %get-tuple-element.21), channel_id=1, source_target_pairs={{0,16},{32,48},{64,80},{96,112},{128,144},{160,176},{192,208},{224... | collective-permute-start | bytes 393224 | tf_op jit(solution)/shard_map/ppermute | solution.py:291
  12.3 12.6 %collective-permute-start.2 = (f32[2,256,128]{2,1,0:T(8,128)S(1)}, f32[2,256,128]{2,1,0:T(8,128)S(1)}, u32[]{:S(2)}, u32[]{:S(2)}) collective-permute-start(f32[2,256,128]{2,1,0:T(8,128)S(1)} %get-tuple-element.23), channel_id=1, source_target_pairs={{1,2},{3,4},{5,6},{7,8},{9,10},{11,12},{13,14},{2,1},{4,3},{6,5},{... | collective-permute-start | bytes 786440 | tf_op jit(solution)/shard_map/ppermute | solution.py:289
  19.0 2.6 %copy-start.4 = (s32[1,1,2,2]{3,2,1,0:T(2,128)S(1)}, s32[1,1,2,2]{3,2,1,0:T(2,128)}, u32[]{:S(2)}) copy-start(s32[1,1,2,2]{3,2,1,0:T(2,128)} %param.10) | copy-start | bytes 52
  19.0 5.9 %collective-permute-start.3 = (f32[2,256,128]{2,1,0:T(8,128)S(1)}, f32[2,256,128]{2,1,0:T(8,128)S(1)}, u32[]{:S(2)}, u32[]{:S(2)}) collective-permute-start(f32[2,256,128]{2,1,0:T(8,128)S(1)} %get-tuple-element.24), channel_id=1, source_target_pairs={{0,1},{2,3},{4,5},{6,7},{8,9},{10,11},{12,13},{14,15},{1,0},{3,2},... | collective-permute-start | bytes 786440 | tf_op jit(solution)/shard_map/ppermute | solution.py:291
  21.6 0.7 copy-start.3
  31.2 27.3 %all-to-all-start = ((f32[64,16,128]{2,1,0:T(8,128)}), f32[64,16,128]{2,1,0:T(8,128)S(1)}, u32[]{:S(2)}, u32[]{:S(2)}) async-start(f32[64,16,128]{2,1,0:T(8,128)} %bitcast.3), calls=%async_computation | async-start | bytes 1048576 | tf_op jit(solution)/shard_map/all_to_all | solution.py:335
  46.5 19.2 %collective-permute-start.4 = (f32[2,256,128]{2,1,0:T(8,128)S(1)}, f32[2,256,128]{2,1,0:T(8,128)S(1)}, u32[]{:S(2)}, u32[]{:S(2)}) collective-permute-start(f32[2,256,128]{2,1,0:T(8,128)S(1)} %get-tuple-element.30), channel_id=1, source_target_pairs={{1,2},{3,4},{5,6},{7,8},{9,10},{11,12},{13,14},{2,1},{4,3},{6,5},{... | collective-permute-start | bytes 786440 | tf_op jit(solution)/shard_map/ppermute | solution.py:289
  51.6 14.2 %collective-permute-start.5 = (f32[2,256,128]{2,1,0:T(8,128)S(1)}, f32[2,256,128]{2,1,0:T(8,128)S(1)}, u32[]{:S(2)}, u32[]{:S(2)}) collective-permute-start(f32[2,256,128]{2,1,0:T(8,128)S(1)} %get-tuple-element.31), channel_id=1, source_target_pairs={{0,1},{2,3},{4,5},{6,7},{8,9},{10,11},{12,13},{14,15},{1,0},{3,2},... | collective-permute-start | bytes 786440 | tf_op jit(solution)/shard_map/ppermute | solution.py:291
  59.2 19.4 %all-to-all-start.1 = ((f32[8,16,128]{2,1,0:T(8,128)}), f32[8,16,128]{2,1,0:T(8,128)S(1)}, u32[]{:S(2)}, u32[]{:S(2)}) async-start(f32[8,16,128]{2,1,0:T(8,128)} %shard_map.81), calls=%async_computation.1 | async-start | bytes 131072 | tf_op jit(solution)/shard_map/all_to_all | solution.py:338
  79.5 22.5 %all-to-all-start.2 = ((f32[64,16,128]{2,1,0:T(8,128)}), f32[64,16,128]{2,1,0:T(8,128)S(1)}, u32[]{:S(2)}, u32[]{:S(2)}) async-start(f32[64,16,128]{2,1,0:T(8,128)} %get-tuple-element.35), calls=%async_computation.2 | async-start | bytes 1048576 | tf_op jit(solution)/shard_map/all_to_all | solution.py:344
  90.3 5.2 %collective-permute-start.6 = (f32[4,64,128]{2,1,0:T(8,128)S(1)}, f32[4,64,128]{2,1,0:T(8,128)S(1)}, u32[]{:S(2)}, u32[]{:S(2)}) collective-permute-start(f32[4,64,128]{2,1,0:T(8,128)S(1)} %get-tuple-element.33), channel_id=1, source_target_pairs={{16,32},{48,64},{80,96},{112,128},{144,160},{176,192},{208,224},{2... | collective-permute-start | bytes 393224 | tf_op jit(solution)/shard_map/ppermute | solution.py:289
  91.0 9.8 %collective-permute-start.7 = (f32[4,64,128]{2,1,0:T(8,128)S(1)}, f32[4,64,128]{2,1,0:T(8,128)S(1)}, u32[]{:S(2)}, u32[]{:S(2)}) collective-permute-start(f32[4,64,128]{2,1,0:T(8,128)S(1)} %get-tuple-element.34), channel_id=1, source_target_pairs={{0,16},{32,48},{64,80},{96,112},{128,144},{160,176},{192,208},{224... | collective-permute-start | bytes 393224 | tf_op jit(solution)/shard_map/ppermute | solution.py:291

commit v6 on v4

--- a/solution.py
+++ b/solution.py
@@ -245,14 +245,13 @@
         mate[s], cross[s] = by_parity(even, to_right, to_left)
 
 
-def spread_sum(scale, shares, spread_share):
+def share_kernel(scale, shares, spread_share):
     share = jnp.sum(shares[...], axis=0) * scale
     for i in range(spread_share.shape[0]):
         spread_share[i] = share
 
 
-def near_kernel(shares, grad_tall, from_cross, from_mate, spread_share, part, cross, mate):
-    spread_sum(1.0, shares, spread_share)
+def fold_columns_kernel(grad_tall, from_cross, from_mate, part, cross, mate):
     even, even_down = even_column(), even_row()
     for s in range(2):
         from_right, from_left = by_parity(even, from_mate[s], from_cross[s])
@@ -262,8 +261,8 @@
             mate[p], cross[p] = by_parity(even_down, total[HALF + TILE:], total[:HALF])
 
 
-def far_kernel(scale, shares, part, from_cross, from_mate, spread_share, result):
-    spread_sum(scale, shares, spread_share)
+def fold_rows_kernel(scale, shares, part, from_cross, from_mate, spread_share, result):
+    share_kernel(scale, shares, spread_share)
     even = even_row()
     for p in range(4):
         below, above = by_parity(even, from_mate[p], from_cross[p])
@@ -332,14 +331,17 @@
     far = lax.axis_size(FAR_AXES)
     rows = 8 * TILE // near
     shares = lax.all_to_all(probe_part.reshape(near, rows, TILE), NEAR_AXES, 0, 0, tiled=True)
+    (spread_share,) = call(
+        functools.partial(share_kernel, 1.0), (f32(far, rows, TILE),), [VM], shares
+    )
     strips = exchange(cross, mate, COL_AXES)
-    spread_share, part, cross, mate = call(
-        near_kernel, (f32(far, rows, TILE), planes, half, half), [VM] * 4, shares, grad_tall, *strips
+    shares = lax.all_to_all(spread_share, FAR_AXES, 0, 0, tiled=True)
+    part, cross, mate = call(
+        fold_columns_kernel, (planes, half, half), [VM] * 3, grad_tall, *strips
     )
     rims = exchange(cross, mate, ROW_AXES)
-    shares = lax.all_to_all(spread_share, FAR_AXES, 0, 0, tiled=True)
     spread_share, result = call(
-        functools.partial(far_kernel, 1.0 / math.sqrt(near * far)),
+        functools.partial(fold_rows_kernel, 1.0 / math.sqrt(near * far)),
         (f32(near, rows, TILE), planes), [VM] * 4, shares, part, *rims,
     )
     gathered = lax.all_to_all(spread_share, NEAR_AXES, 0, 0, tiled=True)

time: 103 us -> 103 us (level)
  waiting for transfers between devices: 18.7 us -> 15.8 us
  blocking collectives: 19.9 us -> 22.4 us
    ppermute x4, waiting for transfers between devices: 10.3 us -> 2.24 us  [exchange(): from_cross = lax.ppermute(cross, axes, pairs + [(b, a) for a, b in pairs])]
    all_to_all x1, waiting for transfers between devices: 0.01 us -> 5.02 us  [body(): lax.all_to_all(probe_part.reshape(near, rows, TILE), NEAR_AXES, 0, 0, til...]
    all_to_all x1, blocking collectives: 19.9 us -> 22.4 us  [body(): gathered = lax.all_to_all(spread_share, NEAR_AXES, 0, 0, tiled=True)]
    pallas_call x7 -> x8, Pallas kernels: 8.61 us -> 8.69 us  [call(): pl.pallas_call(kernel, out_shape=out_shape, in_specs=in_specs, out_specs=...]
  transfers between devices with their start and end apart: 10 -> 10, of which waited for: 5 -> 5; matrix products, arithmetic and copies ran while one was open for 0% -> 0% of each run, Pallas kernels for 0% -> 1%
where the time goes in v6:
time: 103 us; the launch traced here: 102 us
  starting transfers between devices  52 us (50%)
  blocking collectives  22.4 us (22%)
  waiting for transfers between devices  15.8 us (15%)
  Pallas kernels  8.69 us (8%)
  local copies, waits for them, and re-layouts  1.72 us (2%)
  between operations  1.45 us (1%)
    all_to_all x1, blocking collectives, body(): gathered = lax.all_to_all(spread_share, NEAR_AXES, 0, 0, tiled=True)  22.4 us
    ppermute x4, starting transfers between devices, exchange(): from_mate = lax.ppermute(mate, axes, pairs + [(b, a) for a, b in pairs])  17 us
    all_to_all x1, starting transfers between devices, body(): lax.all_to_all(probe_part.reshape(near, rows, TILE), NEAR_AXES, 0, 0, til...  15.3 us
    ppermute x4, starting transfers between devices, exchange(): from_cross = lax.ppermute(cross, axes, pairs + [(b, a) for a, b in pairs])  13.1 us
    pallas_call x8, Pallas kernels, call(): pl.pallas_call(kernel, out_shape=out_shape, in_specs=in_specs, out_specs=...  8.69 us
    all_to_all x1, starting transfers between devices, body(): shares = lax.all_to_all(spread_share, FAR_AXES, 0, 0, tiled=True)  6.52 us
    ppermute x4, waiting for transfers between devices, exchange(): from_mate = lax.ppermute(mate, axes, pairs + [(b, a) for a, b in pairs])  5.62 us
    all_to_all x1, waiting for transfers between devices, body(): lax.all_to_all(probe_part.reshape(near, rows, TILE), NEAR_AXES, 0, 0, til...  5.02 us
  transfers between devices with their start and end apart: 10, of which 5 were waited for; matrix products, arithmetic and copies ran while one was open for 0% of the time, Pallas kernels for 1%

profile of v6, /device:TPU:1, one launch (start us, length us, event | category | flops | bytes accessed | tf_op | source)
XLA Modules:
  0.0 102.0 jit_solution(10866113969455550380)
XLA Ops:
  0.6 0.9 copy-done
  1.6 0.8 collective-permute-start
  2.4 7.4 %collective-permute-start.1 = (f32[4,64,128]{2,1,0:T(8,128)S(1)}, f32[4,64,128]{2,1,0:T(8,128)S(1)}, u32[]{:S(2)}, u32[]{:S(2)}) collective-permute-start(f32[4,64,128]{2,1,0:T(8,128)S(1)} %get-tuple-element.22), channel_id=1, source_target_pairs={{0,16},{32,48},{64,80},{96,112},{128,144},{160,176},{192,208},{224... | collective-permute-start | bytes 393224 | tf_op jit(solution)/shard_map/ppermute | solution.py:289
  9.8 2.3 %collective-permute-done.1.from_mate = f32[4,64,128]{2,1,0:T(8,128)S(1)} collective-permute-done((f32[4,64,128]{2,1,0:T(8,128)S(1)}, f32[4,64,128]{2,1,0:T(8,128)S(1)}, u32[]{:S(2)}, u32[]{:S(2)}) %collective-permute-start.1) | collective-permute-done | bytes 131104 | tf_op jit(solution)/shard_map/ppermute | solution.py:289
  12.2 0.1 shard_map.78
  12.3 6.6 %collective-permute-start.2 = (f32[2,256,128]{2,1,0:T(8,128)S(1)}, f32[2,256,128]{2,1,0:T(8,128)S(1)}, u32[]{:S(2)}, u32[]{:S(2)}) collective-permute-start(f32[2,256,128]{2,1,0:T(8,128)S(1)} %get-tuple-element.24), channel_id=1, source_target_pairs={{1,2},{3,4},{5,6},{7,8},{9,10},{11,12},{13,14},{2,1},{4,3},{6,5},{... | collective-permute-start | bytes 786440 | tf_op jit(solution)/shard_map/ppermute | solution.py:287
  19.0 1.9 %collective-permute-start.3 = (f32[2,256,128]{2,1,0:T(8,128)S(1)}, f32[2,256,128]{2,1,0:T(8,128)S(1)}, u32[]{:S(2)}, u32[]{:S(2)}) collective-permute-start(f32[2,256,128]{2,1,0:T(8,128)S(1)} %get-tuple-element.25), channel_id=1, source_target_pairs={{0,1},{2,3},{4,5},{6,7},{8,9},{10,11},{12,13},{14,15},{1,0},{3,2},... | collective-permute-start | bytes 786440 | tf_op jit(solution)/shard_map/ppermute | solution.py:289
  21.6 0.7 copy-done.3
  22.3 0.3 shard_map.79
  22.6 2.2 %collective-permute-done.2.from_cross = f32[2,256,128]{2,1,0:T(8,128)S(1)} collective-permute-done((f32[2,256,128]{2,1,0:T(8,128)S(1)}, f32[2,256,128]{2,1,0:T(8,128)S(1)}, u32[]{:S(2)}, u32[]{:S(2)}) %collective-permute-start.2) | collective-permute-done | bytes 262176 | tf_op jit(solution)/shard_map/ppermute | solution.py:287
  24.9 6.3 %shard_map.80 = (f32[8,128,128]{2,1,0:T(8,128)}, f32[4,256,128]{2,1,0:T(8,128)S(1)}, f32[2,256,128]{2,1,0:T(8,128)S(1)}, f32[2,256,128]{2,1,0:T(8,128)S(1)}) custom-call(s32[4]{0:T(128)S(1)} %reshape.28.offsets, s32[1,1]{1,0:T(1,128)S(6)} %copy.8.counts, f32[4,256,128]{2,1,0:T(8,128)S(1)} %get-tuple-element.23.tall, ...), custom_call_target="tpu_custom_call" | custom-call | flops 3200000000 | bytes 4000000 | tf_op jit(solution)/shard_map/pallas_call | solution.py:28
  31.2 15.3 %all-to-all-start = ((f32[64,16,128]{2,1,0:T(8,128)}), f32[64,16,128]{2,1,0:T(8,128)S(1)}, u32[]{:S(2)}, u32[]{:S(2)}) async-start(f32[64,16,128]{2,1,0:T(8,128)} %bitcast.3), calls=%async_computation | async-start | bytes 1048576 | tf_op jit(solution)/shard_map/all_to_all | solution.py:333
  46.5 5.0 %collective-permute-start.4 = (f32[2,256,128]{2,1,0:T(8,128)S(1)}, f32[2,256,128]{2,1,0:T(8,128)S(1)}, u32[]{:S(2)}, u32[]{:S(2)}) collective-permute-start(f32[2,256,128]{2,1,0:T(8,128)S(1)} %get-tuple-element.31), channel_id=1, source_target_pairs={{1,2},{3,4},{5,6},{7,8},{9,10},{11,12},{13,14},{2,1},{4,3},{6,5},{... | collective-permute-start | bytes 786440 | tf_op jit(solution)/shard_map/ppermute | solution.py:287
  51.6 1.9 %collective-permute-start.5 = (f32[2,256,128]{2,1,0:T(8,128)S(1)}, f32[2,256,128]{2,1,0:T(8,128)S(1)}, u32[]{:S(2)}, u32[]{:S(2)}) collective-permute-start(f32[2,256,128]{2,1,0:T(8,128)S(1)} %get-tuple-element.32), channel_id=1, source_target_pairs={{0,1},{2,3},{4,5},{6,7},{8,9},{10,11},{12,13},{14,15},{1,0},{3,2},... | collective-permute-start | bytes 786440 | tf_op jit(solution)/shard_map/ppermute | solution.py:289
  53.5 5.0 %all-to-all-done.shares = f32[64,16,128]{2,1,0:T(8,128)S(1)} async-done(((f32[64,16,128]{2,1,0:T(8,128)}), f32[64,16,128]{2,1,0:T(8,128)S(1)}, u32[]{:S(2)}, u32[]{:S(2)}) %all-to-all-start) | async-done | bytes 524320 | tf_op jit(solution)/shard_map/all_to_all | solution.py:333
  58.5 0.7 shard_map.81
  59.2 6.5 %all-to-all-start.1 = ((f32[8,16,128]{2,1,0:T(8,128)}), f32[8,16,128]{2,1,0:T(8,128)S(1)}, u32[]{:S(2)}, u32[]{:S(2)}) async-start(f32[8,16,128]{2,1,0:T(8,128)} %shard_map.81), calls=%async_computation.1 | async-start | bytes 131072 | tf_op jit(solution)/shard_map/all_to_all | solution.py:338
  65.8 0.1 shard_map.82
  65.9 0.7 collective-permute-start.6
  66.6 5.8 %collective-permute-start.7 = (f32[4,64,128]{2,1,0:T(8,128)S(1)}, f32[4,64,128]{2,1,0:T(8,128)S(1)}, u32[]{:S(2)}, u32[]{:S(2)}) collective-permute-start(f32[4,64,128]{2,1,0:T(8,128)S(1)} %get-tuple-element.35), channel_id=1, source_target_pairs={{0,16},{32,48},{64,80},{96,112},{128,144},{160,176},{192,208},{224... | collective-permute-start | bytes 393224 | tf_op jit(solution)/shard_map/ppermute | solution.py:289
  72.4 3.3 %collective-permute-done.7.from_mate = f32[4,64,128]{2,1,0:T(8,128)S(1)} collective-permute-done((f32[4,64,128]{2,1,0:T(8,128)S(1)}, f32[4,64,128]{2,1,0:T(8,128)S(1)}, u32[]{:S(2)}, u32[]{:S(2)}) %collective-permute-start.7) | collective-permute-done | bytes 131104 | tf_op jit(solution)/shard_map/ppermute | solution.py:289
  75.7 3.0 %all-to-all-done.1.shares = f32[8,16,128]{2,1,0:T(8,128)S(1)} async-done(((f32[8,16,128]{2,1,0:T(8,128)}), f32[8,16,128]{2,1,0:T(8,128)S(1)}, u32[]{:S(2)}, u32[]{:S(2)}) %all-to-all-start.1) | async-done | bytes 65568 | tf_op jit(solution)/shard_map/all_to_all | solution.py:338
  78.7 22.4 %all_to_all.15 = f32[64,16,128]{2,1,0:T(8,128)S(1)} all-to-all(f32[64,16,128]{2,1,0:T(8,128)S(1)} %get-tuple-element.37), channel_id=1, replica_groups=mesh['xl'=2,'za'=8,'zb'=2,'y'=4,'xh'=2,'core'=2] {'xl','zb','y','xh','co..., dimensions={0} | all-to-all | bytes 1048576 | tf_op jit(solution)/shard_map/all_to_all | solution.py:347
  101.1 0.9 shard_map.84
  (16 shorter events, 0.2 us)
Async XLA Ops:
  0.6 1.0 copy-start
  1.6 20.1 %copy-start.1 = (f32[2,4,128,128]{3,2,1,0:T(8,128)S(1)}, f32[2,4,128,128]{3,2,1,0:T(8,128)}, u32[]{:S(2)}) copy-start(f32[2,4,128,128]{3,2,1,0:T(8,128)} %param.7) | copy-start | bytes 1572868
  1.6 8.2 %collective-permute-start = (f32[4,64,128]{2,1,0:T(8,128)S(1)}, f32[4,64,128]{2,1,0:T(8,128)S(1)}, u32[]{:S(2)}, u32[]{:S(2)}) collective-permute-start(f32[4,64,128]{2,1,0:T(8,128)S(1)} %get-tuple-element.21), channel_id=1, source_target_pairs={{16,32},{48,64},{80,96},{112,128},{144,160},{176,192},{208,224},{2... | collective-permute-start | bytes 393224 | tf_op jit(solution)/shard_map/ppermute | solution.py:287
  2.4 19.2 %copy-start.2 = (f32[1,1,2,128,128]{4,3,2,1,0:T(8,128)S(1)}, f32[1,1,2,128,128]{4,3,2,1,0:T(8,128)}, u32[]{:S(2)}) copy-start(f32[1,1,2,128,128]{4,3,2,1,0:T(8,128)} %param.9) | copy-start | bytes 393220
  2.4 9.7 %collective-permute-start.1 = (f32[4,64,128]{2,1,0:T(8,128)S(1)}, f32[4,64,128]{2,1,0:T(8,128)S(1)}, u32[]{:S(2)}, u32[]{:S(2)}) collective-permute-start(f32[4,64,128]{2,1,0:T(8,128)S(1)} %get-tuple-element.22), channel_id=1, source_target_pairs={{0,16},{32,48},{64,80},{96,112},{128,144},{160,176},{192,208},{224... | collective-permute-start | bytes 393224 | tf_op jit(solution)/shard_map/ppermute | solution.py:289
  12.3 12.6 %collective-permute-start.2 = (f32[2,256,128]{2,1,0:T(8,128)S(1)}, f32[2,256,128]{2,1,0:T(8,128)S(1)}, u32[]{:S(2)}, u32[]{:S(2)}) collective-permute-start(f32[2,256,128]{2,1,0:T(8,128)S(1)} %get-tuple-element.24), channel_id=1, source_target_pairs={{1,2},{3,4},{5,6},{7,8},{9,10},{11,12},{13,14},{2,1},{4,3},{6,5},{... | collective-permute-start | bytes 786440 | tf_op jit(solution)/shard_map/ppermute | solution.py:287
  19.0 2.6 %copy-start.4 = (s32[1,1,2,2]{3,2,1,0:T(2,128)S(1)}, s32[1,1,2,2]{3,2,1,0:T(2,128)}, u32[]{:S(2)}) copy-start(s32[1,1,2,2]{3,2,1,0:T(2,128)} %param.10) | copy-start | bytes 52
  19.0 5.9 %collective-permute-start.3 = (f32[2,256,128]{2,1,0:T(8,128)S(1)}, f32[2,256,128]{2,1,0:T(8,128)S(1)}, u32[]{:S(2)}, u32[]{:S(2)}) collective-permute-start(f32[2,256,128]{2,1,0:T(8,128)S(1)} %get-tuple-element.25), channel_id=1, source_target_pairs={{0,1},{2,3},{4,5},{6,7},{8,9},{10,11},{12,13},{14,15},{1,0},{3,2},... | collective-permute-start | bytes 786440 | tf_op jit(solution)/shard_map/ppermute | solution.py:289
  21.6 0.7 copy-start.3
  31.2 27.3 %all-to-all-start = ((f32[64,16,128]{2,1,0:T(8,128)}), f32[64,16,128]{2,1,0:T(8,128)S(1)}, u32[]{:S(2)}, u32[]{:S(2)}) async-start(f32[64,16,128]{2,1,0:T(8,128)} %bitcast.3), calls=%async_computation | async-start | bytes 1048576 | tf_op jit(solution)/shard_map/all_to_all | solution.py:333
  46.5 19.2 %collective-permute-start.4 = (f32[2,256,128]{2,1,0:T(8,128)S(1)}, f32[2,256,128]{2,1,0:T(8,128)S(1)}, u32[]{:S(2)}, u32[]{:S(2)}) collective-permute-start(f32[2,256,128]{2,1,0:T(8,128)S(1)} %get-tuple-element.31), channel_id=1, source_target_pairs={{1,2},{3,4},{5,6},{7,8},{9,10},{11,12},{13,14},{2,1},{4,3},{6,5},{... | collective-permute-start | bytes 786440 | tf_op jit(solution)/shard_map/ppermute | solution.py:287
  51.6 14.2 %collective-permute-start.5 = (f32[2,256,128]{2,1,0:T(8,128)S(1)}, f32[2,256,128]{2,1,0:T(8,128)S(1)}, u32[]{:S(2)}, u32[]{:S(2)}) collective-permute-start(f32[2,256,128]{2,1,0:T(8,128)S(1)} %get-tuple-element.32), channel_id=1, source_target_pairs={{0,1},{2,3},{4,5},{6,7},{8,9},{10,11},{12,13},{14,15},{1,0},{3,2},... | collective-permute-start | bytes 786440 | tf_op jit(solution)/shard_map/ppermute | solution.py:289
  59.2 19.4 %all-to-all-start.1 = ((f32[8,16,128]{2,1,0:T(8,128)}), f32[8,16,128]{2,1,0:T(8,128)S(1)}, u32[]{:S(2)}, u32[]{:S(2)}) async-start(f32[8,16,128]{2,1,0:T(8,128)} %shard_map.81), calls=%async_computation.1 | async-start | bytes 131072 | tf_op jit(solution)/shard_map/all_to_all | solution.py:338
  65.9 6.5 %collective-permute-start.6 = (f32[4,64,128]{2,1,0:T(8,128)S(1)}, f32[4,64,128]{2,1,0:T(8,128)S(1)}, u32[]{:S(2)}, u32[]{:S(2)}) collective-permute-start(f32[4,64,128]{2,1,0:T(8,128)S(1)} %get-tuple-element.34), channel_id=1, source_target_pairs={{16,32},{48,64},{80,96},{112,128},{144,160},{176,192},{208,224},{2... | collective-permute-start | bytes 393224 | tf_op jit(solution)/shard_map/ppermute | solution.py:287
  66.6 9.1 %collective-permute-start.7 = (f32[4,64,128]{2,1,0:T(8,128)S(1)}, f32[4,64,128]{2,1,0:T(8,128)S(1)}, u32[]{:S(2)}, u32[]{:S(2)}) collective-permute-start(f32[4,64,128]{2,1,0:T(8,128)S(1)} %get-tuple-element.35), channel_id=1, source_target_pairs={{0,16},{32,48},{64,80},{96,112},{128,144},{160,176},{192,208},{224... | collective-permute-start | bytes 393224 | tf_op jit(solution)/shard_map/ppermute | solution.py:289

commit v7 on v6

--- a/solution.py
+++ b/solution.py
@@ -13,8 +13,8 @@
 BF16 = jnp.bfloat16
 ROW_AXES = ("xl", "za", "zb")
 COL_AXES = ("y", "xh", "core")
-NEAR_AXES = ("xl", "zb", "y", "xh", "core")
-FAR_AXES = ("za",)
+NEAR_AXES = ("xl", "y", "xh", "core")
+FAR_AXES = ("za", "zb")
 VMEM_LIMIT = 40 * 1024 * 1024
 TILE = 128
 HALF = 64

time: 103 us -> 105 us (1.019)
  blocking collectives: 22.4 us -> 44.4 us
  starting transfers between devices: 52 us -> 35.1 us
  waiting for transfers between devices: 15.8 us -> 13.4 us
    all_to_all x0 -> x1, blocking collectives: none -> 25.8 us  [body(): lax.all_to_all(probe_part.reshape(near, rows, TILE), NEAR_AXES, 0, 0, til...]
    all_to_all x1 -> x0, starting transfers between devices: 15.3 us -> none  [body(): lax.all_to_all(probe_part.reshape(near, rows, TILE), NEAR_AXES, 0, 0, til...]
    ppermute x4, waiting for transfers between devices: 2.24 us -> 8.68 us  [exchange(): from_cross = lax.ppermute(cross, axes, pairs + [(b, a) for a, b in pairs])]
    all_to_all x1 -> x0, waiting for transfers between devices: 5.02 us -> none  [body(): lax.all_to_all(probe_part.reshape(near, rows, TILE), NEAR_AXES, 0, 0, til...]
    all_to_all x1, blocking collectives: 22.4 us -> 18.6 us  [body(): gathered = lax.all_to_all(spread_share, NEAR_AXES, 0, 0, tiled=True)]
    all_to_all x1, waiting for transfers between devices: 2.97 us -> 0.01 us  [body(): shares = lax.all_to_all(spread_share, FAR_AXES, 0, 0, tiled=True)]
    ppermute x4, starting transfers between devices: 13.1 us -> 11.7 us  [exchange(): from_cross = lax.ppermute(cross, axes, pairs + [(b, a) for a, b in pairs])]
  transfers between devices with their start and end apart: 10 -> 9, of which waited for: 5 -> 4; matrix products, arithmetic and copies ran while one was open for 0% -> 0% of each run, Pallas kernels for 1% -> 0%
where the time goes in v7:
time: 105 us; the launch traced here: 104 us
  blocking collectives  44.4 us (42%)
  starting transfers between devices  35.1 us (33%)
  waiting for transfers between devices  13.4 us (13%)
  Pallas kernels  8.08 us (8%)
  local copies, waits for them, and re-layouts  1.72 us (2%)
  between operations  1.45 us (1%)
    all_to_all x1, blocking collectives, body(): lax.all_to_all(probe_part.reshape(near, rows, TILE), NEAR_AXES, 0, 0, til...  25.8 us
    all_to_all x1, blocking collectives, body(): gathered = lax.all_to_all(spread_share, NEAR_AXES, 0, 0, tiled=True)  18.6 us
    ppermute x4, starting transfers between devices, exchange(): from_mate = lax.ppermute(mate, axes, pairs + [(b, a) for a, b in pairs])  17.2 us
    ppermute x4, starting transfers between devices, exchange(): from_cross = lax.ppermute(cross, axes, pairs + [(b, a) for a, b in pairs])  11.7 us
    ppermute x4, waiting for transfers between devices, exchange(): from_cross = lax.ppermute(cross, axes, pairs + [(b, a) for a, b in pairs])  8.68 us
    pallas_call x8, Pallas kernels, call(): pl.pallas_call(kernel, out_shape=out_shape, in_specs=in_specs, out_specs=...  8.08 us
    all_to_all x1, starting transfers between devices, body(): shares = lax.all_to_all(spread_share, FAR_AXES, 0, 0, tiled=True)  6.19 us
    ppermute x4, waiting for transfers between devices, exchange(): from_mate = lax.ppermute(mate, axes, pairs + [(b, a) for a, b in pairs])  4.67 us
  transfers between devices with their start and end apart: 9, of which 4 were waited for; matrix products, arithmetic and copies ran while one was open for 0% of the time, Pallas kernels for 0%

profile of v7, /device:TPU:1, one launch (start us, length us, event | category | flops | bytes accessed | tf_op | source)
XLA Modules:
  0.0 104.1 jit_solution(9991785900923953517)
XLA Ops:
  0.6 0.9 copy-done
  1.6 0.8 collective-permute-start
  2.4 7.4 %collective-permute-start.1 = (f32[4,64,128]{2,1,0:T(8,128)S(1)}, f32[4,64,128]{2,1,0:T(8,128)S(1)}, u32[]{:S(2)}, u32[]{:S(2)}) collective-permute-start(f32[4,64,128]{2,1,0:T(8,128)S(1)} %get-tuple-element.22), channel_id=1, source_target_pairs={{0,16},{32,48},{64,80},{96,112},{128,144},{160,176},{192,208},{224... | collective-permute-start | bytes 393224 | tf_op jit(solution)/shard_map/ppermute | solution.py:289
  9.8 2.3 %collective-permute-done.1.from_mate = f32[4,64,128]{2,1,0:T(8,128)S(1)} collective-permute-done((f32[4,64,128]{2,1,0:T(8,128)S(1)}, f32[4,64,128]{2,1,0:T(8,128)S(1)}, u32[]{:S(2)}, u32[]{:S(2)}) %collective-permute-start.1) | collective-permute-done | bytes 131104 | tf_op jit(solution)/shard_map/ppermute | solution.py:289
  12.2 0.1 shard_map.78
  12.3 6.6 %collective-permute-start.2 = (f32[2,256,128]{2,1,0:T(8,128)S(1)}, f32[2,256,128]{2,1,0:T(8,128)S(1)}, u32[]{:S(2)}, u32[]{:S(2)}) collective-permute-start(f32[2,256,128]{2,1,0:T(8,128)S(1)} %get-tuple-element.24), channel_id=1, source_target_pairs={{1,2},{3,4},{5,6},{7,8},{9,10},{11,12},{13,14},{2,1},{4,3},{6,5},{... | collective-permute-start | bytes 786440 | tf_op jit(solution)/shard_map/ppermute | solution.py:287
  19.0 1.9 %collective-permute-start.3 = (f32[2,256,128]{2,1,0:T(8,128)S(1)}, f32[2,256,128]{2,1,0:T(8,128)S(1)}, u32[]{:S(2)}, u32[]{:S(2)}) collective-permute-start(f32[2,256,128]{2,1,0:T(8,128)S(1)} %get-tuple-element.25), channel_id=1, source_target_pairs={{0,1},{2,3},{4,5},{6,7},{8,9},{10,11},{12,13},{14,15},{1,0},{3,2},... | collective-permute-start | bytes 786440 | tf_op jit(solution)/shard_map/ppermute | solution.py:289
  21.6 0.7 copy-done.3
  22.3 0.3 shard_map.79
  22.6 2.2 %collective-permute-done.2.from_cross = f32[2,256,128]{2,1,0:T(8,128)S(1)} collective-permute-done((f32[2,256,128]{2,1,0:T(8,128)S(1)}, f32[2,256,128]{2,1,0:T(8,128)S(1)}, u32[]{:S(2)}, u32[]{:S(2)}) %collective-permute-start.2) | collective-permute-done | bytes 262176 | tf_op jit(solution)/shard_map/ppermute | solution.py:287
  24.9 5.7 %shard_map.80 = (f32[8,128,128]{2,1,0:T(8,128)S(1)}, f32[4,256,128]{2,1,0:T(8,128)S(1)}, f32[2,256,128]{2,1,0:T(8,128)S(1)}, f32[2,256,128]{2,1,0:T(8,128)S(1)}) custom-call(s32[4]{0:T(128)S(1)} %reshape.28.offsets, s32[1,1]{1,0:T(1,128)S(6)} %copy.8.counts, f32[4,256,128]{2,1,0:T(8,128)S(1)} %get-tuple-element.23.tall, ...), custom_call_target="tpu_custom_call" | custom-call | flops 3200000000 | bytes 4000000 | tf_op jit(solution)/shard_map/pallas_call | solution.py:28
  30.5 25.8 %all_to_all.15.shares = f32[32,32,128]{2,1,0:T(8,128)S(1)} all-to-all(f32[32,32,128]{2,1,0:T(8,128)S(1)} %bitcast.11), channel_id=1, replica_groups=mesh['xl'=2,'za'=8,'zb'=2,'y'=4,'xh'=2,'core'=2] {'xl','y','xh','core'}, dimensions={0} | all-to-all | bytes 1048576 | tf_op jit(solution)/shard_map/all_to_all | solution.py:333
  56.4 0.8 shard_map.81
  57.1 6.2 %all-to-all-start.1 = ((f32[16,32,128]{2,1,0:T(8,128)}), f32[16,32,128]{2,1,0:T(8,128)S(1)}, u32[]{:S(2)}, u32[]{:S(2)}) async-start(f32[16,32,128]{2,1,0:T(8,128)} %shard_map.81), calls=%async_computation.1 | async-start | bytes 524288 | tf_op jit(solution)/shard_map/all_to_all | solution.py:338
  63.3 3.6 %collective-permute-start.4 = (f32[2,256,128]{2,1,0:T(8,128)S(1)}, f32[2,256,128]{2,1,0:T(8,128)S(1)}, u32[]{:S(2)}, u32[]{:S(2)}) collective-permute-start(f32[2,256,128]{2,1,0:T(8,128)S(1)} %get-tuple-element.31), channel_id=1, source_target_pairs={{1,2},{3,4},{5,6},{7,8},{9,10},{11,12},{13,14},{2,1},{4,3},{6,5},{... | collective-permute-start | bytes 786440 | tf_op jit(solution)/shard_map/ppermute | solution.py:287
  67.0 1.9 %collective-permute-start.5 = (f32[2,256,128]{2,1,0:T(8,128)S(1)}, f32[2,256,128]{2,1,0:T(8,128)S(1)}, u32[]{:S(2)}, u32[]{:S(2)}) collective-permute-start(f32[2,256,128]{2,1,0:T(8,128)S(1)} %get-tuple-element.32), channel_id=1, source_target_pairs={{0,1},{2,3},{4,5},{6,7},{8,9},{10,11},{12,13},{14,15},{1,0},{3,2},... | collective-permute-start | bytes 786440 | tf_op jit(solution)/shard_map/ppermute | solution.py:289
  68.9 6.5 %collective-permute-done.4.from_cross = f32[2,256,128]{2,1,0:T(8,128)S(1)} collective-permute-done((f32[2,256,128]{2,1,0:T(8,128)S(1)}, f32[2,256,128]{2,1,0:T(8,128)S(1)}, u32[]{:S(2)}, u32[]{:S(2)}) %collective-permute-start.4) | collective-permute-done | bytes 262176 | tf_op jit(solution)/shard_map/ppermute | solution.py:287
  75.4 0.1 shard_map.82
  75.5 0.7 collective-permute-start.6
  76.2 6.0 %collective-permute-start.7 = (f32[4,64,128]{2,1,0:T(8,128)S(1)}, f32[4,64,128]{2,1,0:T(8,128)S(1)}, u32[]{:S(2)}, u32[]{:S(2)}) collective-permute-start(f32[4,64,128]{2,1,0:T(8,128)S(1)} %get-tuple-element.35), channel_id=1, source_target_pairs={{0,16},{32,48},{64,80},{96,112},{128,144},{160,176},{192,208},{224... | collective-permute-start | bytes 393224 | tf_op jit(solution)/shard_map/ppermute | solution.py:289
  82.2 2.3 %collective-permute-done.7.from_mate = f32[4,64,128]{2,1,0:T(8,128)S(1)} collective-permute-done((f32[4,64,128]{2,1,0:T(8,128)S(1)}, f32[4,64,128]{2,1,0:T(8,128)S(1)}, u32[]{:S(2)}, u32[]{:S(2)}) %collective-permute-start.7) | collective-permute-done | bytes 131104 | tf_op jit(solution)/shard_map/ppermute | solution.py:289
  84.5 0.1 shard_map.83
  84.6 18.6 %all_to_all.16 = f32[32,32,128]{2,1,0:T(8,128)S(1)} all-to-all(f32[32,32,128]{2,1,0:T(8,128)S(1)} %get-tuple-element.37), channel_id=1, replica_groups=mesh['xl'=2,'za'=8,'zb'=2,'y'=4,'xh'=2,'core'=2] {'xl','y','xh','core'}, dimensions={0} | all-to-all | bytes 1048576 | tf_op jit(solution)/shard_map/all_to_all | solution.py:347
  103.2 0.9 shard_map.84
  (15 shorter events, 0.1 us)
Async XLA Ops:
  0.6 1.0 copy-start
  1.6 20.1 %copy-start.1 = (f32[2,4,128,128]{3,2,1,0:T(8,128)S(1)}, f32[2,4,128,128]{3,2,1,0:T(8,128)}, u32[]{:S(2)}) copy-start(f32[2,4,128,128]{3,2,1,0:T(8,128)} %param.7) | copy-start | bytes 1572868
  1.6 8.2 %collective-permute-start = (f32[4,64,128]{2,1,0:T(8,128)S(1)}, f32[4,64,128]{2,1,0:T(8,128)S(1)}, u32[]{:S(2)}, u32[]{:S(2)}) collective-permute-start(f32[4,64,128]{2,1,0:T(8,128)S(1)} %get-tuple-element.21), channel_id=1, source_target_pairs={{16,32},{48,64},{80,96},{112,128},{144,160},{176,192},{208,224},{2... | collective-permute-start | bytes 393224 | tf_op jit(solution)/shard_map/ppermute | solution.py:287
  2.4 19.2 %copy-start.2 = (f32[1,1,2,128,128]{4,3,2,1,0:T(8,128)S(1)}, f32[1,1,2,128,128]{4,3,2,1,0:T(8,128)}, u32[]{:S(2)}) copy-start(f32[1,1,2,128,128]{4,3,2,1,0:T(8,128)} %param.9) | copy-start | bytes 393220
  2.4 9.7 %collective-permute-start.1 = (f32[4,64,128]{2,1,0:T(8,128)S(1)}, f32[4,64,128]{2,1,0:T(8,128)S(1)}, u32[]{:S(2)}, u32[]{:S(2)}) collective-permute-start(f32[4,64,128]{2,1,0:T(8,128)S(1)} %get-tuple-element.22), channel_id=1, source_target_pairs={{0,16},{32,48},{64,80},{96,112},{128,144},{160,176},{192,208},{224... | collective-permute-start | bytes 393224 | tf_op jit(solution)/shard_map/ppermute | solution.py:289
  12.3 12.6 %collective-permute-start.2 = (f32[2,256,128]{2,1,0:T(8,128)S(1)}, f32[2,256,128]{2,1,0:T(8,128)S(1)}, u32[]{:S(2)}, u32[]{:S(2)}) collective-permute-start(f32[2,256,128]{2,1,0:T(8,128)S(1)} %get-tuple-element.24), channel_id=1, source_target_pairs={{1,2},{3,4},{5,6},{7,8},{9,10},{11,12},{13,14},{2,1},{4,3},{6,5},{... | collective-permute-start | bytes 786440 | tf_op jit(solution)/shard_map/ppermute | solution.py:287
  19.0 2.6 %copy-start.4 = (s32[1,1,2,2]{3,2,1,0:T(2,128)S(1)}, s32[1,1,2,2]{3,2,1,0:T(2,128)}, u32[]{:S(2)}) copy-start(s32[1,1,2,2]{3,2,1,0:T(2,128)} %param.10) | copy-start | bytes 52
  19.0 5.9 %collective-permute-start.3 = (f32[2,256,128]{2,1,0:T(8,128)S(1)}, f32[2,256,128]{2,1,0:T(8,128)S(1)}, u32[]{:S(2)}, u32[]{:S(2)}) collective-permute-start(f32[2,256,128]{2,1,0:T(8,128)S(1)} %get-tuple-element.25), channel_id=1, source_target_pairs={{0,1},{2,3},{4,5},{6,7},{8,9},{10,11},{12,13},{14,15},{1,0},{3,2},... | collective-permute-start | bytes 786440 | tf_op jit(solution)/shard_map/ppermute | solution.py:289
  21.6 0.7 copy-start.3
  57.1 27.4 %all-to-all-start.1 = ((f32[16,32,128]{2,1,0:T(8,128)}), f32[16,32,128]{2,1,0:T(8,128)S(1)}, u32[]{:S(2)}, u32[]{:S(2)}) async-start(f32[16,32,128]{2,1,0:T(8,128)} %shard_map.81), calls=%async_computation.1 | async-start | bytes 524288 | tf_op jit(solution)/shard_map/all_to_all | solution.py:338
  63.3 12.0 %collective-permute-start.4 = (f32[2,256,128]{2,1,0:T(8,128)S(1)}, f32[2,256,128]{2,1,0:T(8,128)S(1)}, u32[]{:S(2)}, u32[]{:S(2)}) collective-permute-start(f32[2,256,128]{2,1,0:T(8,128)S(1)} %get-tuple-element.31), channel_id=1, source_target_pairs={{1,2},{3,4},{5,6},{7,8},{9,10},{11,12},{13,14},{2,1},{4,3},{6,5},{... | collective-permute-start | bytes 786440 | tf_op jit(solution)/shard_map/ppermute | solution.py:287
  67.0 8.4 %collective-permute-start.5 = (f32[2,256,128]{2,1,0:T(8,128)S(1)}, f32[2,256,128]{2,1,0:T(8,128)S(1)}, u32[]{:S(2)}, u32[]{:S(2)}) collective-permute-start(f32[2,256,128]{2,1,0:T(8,128)S(1)} %get-tuple-element.32), channel_id=1, source_target_pairs={{0,1},{2,3},{4,5},{6,7},{8,9},{10,11},{12,13},{14,15},{1,0},{3,2},... | collective-permute-start | bytes 786440 | tf_op jit(solution)/shard_map/ppermute | solution.py:289
  75.5 6.6 %collective-permute-start.6 = (f32[4,64,128]{2,1,0:T(8,128)S(1)}, f32[4,64,128]{2,1,0:T(8,128)S(1)}, u32[]{:S(2)}, u32[]{:S(2)}) collective-permute-start(f32[4,64,128]{2,1,0:T(8,128)S(1)} %get-tuple-element.34), channel_id=1, source_target_pairs={{16,32},{48,64},{80,96},{112,128},{144,160},{176,192},{208,224},{2... | collective-permute-start | bytes 393224 | tf_op jit(solution)/shard_map/ppermute | solution.py:287
  76.2 8.3 %collective-permute-start.7 = (f32[4,64,128]{2,1,0:T(8,128)S(1)}, f32[4,64,128]{2,1,0:T(8,128)S(1)}, u32[]{:S(2)}, u32[]{:S(2)}) collective-permute-start(f32[4,64,128]{2,1,0:T(8,128)S(1)} %get-tuple-element.35), channel_id=1, source_target_pairs={{0,16},{32,48},{64,80},{96,112},{128,144},{160,176},{192,208},{224... | collective-permute-start | bytes 393224 | tf_op jit(solution)/shard_map/ppermute | solution.py:289

commit v8 on v5

--- a/solution.py
+++ b/solution.py
@@ -13,9 +13,9 @@
 BF16 = jnp.bfloat16
 ROW_AXES = ("xl", "za", "zb")
 COL_AXES = ("y", "xh", "core")
-NEAR_AXES = ("xl", "zb", "y", "xh", "core")
-FAR_AXES = ("za",)
-VMEM_LIMIT = 40 * 1024 * 1024
+NEAR_AXES = ("xl", "y", "xh", "core")
+FAR_AXES = ("za", "zb")
+VMEM_LIMIT = 12 * 1024 * 1024
 TILE = 128
 HALF = 64
 VM = pl.BlockSpec(memory_space=pltpu.VMEM)
@@ -127,16 +127,14 @@
 
 def main_kernel(
     offsets, counts, tall, from_cross, from_mate, probe, measured, ops,
-    probe_grad, grad_tall, cross, mate,
-    beside, grad_beside, field_high, field_low, mid_high, mid_low, wave_one, wave_two,
+    probe_grad, object_grad,
+    beside, field_high, field_low, mid_high, mid_low, wave_one, wave_two,
 ):
     even = even_column()
     for s in range(2):
         from_right, from_left = by_parity(even, from_mate[s], from_cross[s])
         beside[s], beside[2 + s] = unpack_columns(from_left, from_right)
-    object_ext, grad_ext = (tall, beside), (grad_tall, grad_beside)
-    for total in grad_ext:
-        total[...] = jnp.zeros_like(total)
+    object_ext = (tall, beside)
 
     def put_field(slot, m, real, imag):
         for c, value in enumerate((real, imag)):
@@ -157,9 +155,12 @@
 
     def cols_done(slot, which, take):
         high, low = ops[which, :256], ops[which, 256:]
-        done = dot(mid_high[slot], high) + (dot(mid_low[slot], high) + dot(mid_high[slot], low))
-        for m in range(4):
-            take(slot, m, done[block(m), :TILE], done[block(m), TILE:])
+        for n in range(2):
+            rows = slice(n * 256, (n + 1) * 256)
+            gh, gl = mid_high[slot, rows], mid_low[slot, rows]
+            done = dot(gh, high) + (dot(gl, high) + dot(gh, low))
+            for k in range(2):
+                take(slot, 2 * n + k, done[block(k), :TILE], done[block(k), TILE:])
 
     def propagate(which, take):
         for slot in range(2):
@@ -171,12 +172,6 @@
         rows = [object_ext[b][p, pl.ds(offsets[2 * slot], TILE), :] for b in range(2)]
         shift = lax.rem(320 - offsets[2 * slot + 1], 256)
         return pltpu.roll(jnp.concatenate(rows, axis=1), shift, 1)[:, :TILE]
-
-    def spread(slot, p, value):
-        wide = jnp.concatenate([value, jnp.zeros_like(value)], axis=1)
-        wide = pltpu.roll(wide, lax.rem(offsets[2 * slot + 1] + 192, 256), 1)
-        for b in range(2):
-            grad_ext[b][p, pl.ds(offsets[2 * slot], TILE), :] += wide[:, block(b)]
 
     views = [[window(slot, p) for p in range(4)] for slot in range(2)]
     for slot in range(2):
@@ -206,27 +201,26 @@
                 put_field(slot, k, residual * wave_two[slot, k, 0], residual * wave_two[slot, k, 1])
 
     propagate(0, after_second)
-    sums = [[None, None], [None, None]]
-
-    def add(slot, m, real, imag):
-        pair = (real, imag) if m == 0 else (sums[slot][0] + real, sums[slot][1] + imag)
-        sums[slot] = pair
+
+    def add(slot, s, m, real, imag):
+        for p, value in zip((s, 2 + s), (real, imag)):
+            if m == 0:
+                object_grad[slot, p] = value
+            else:
+                object_grad[slot, p] += value
 
     def after_third(slot, m, hr, hi):
         o1r, o1i = views[slot][1], views[slot][3]
         wr, wi = wave_one[slot, m, 0], wave_one[slot, m, 1]
-        add(slot, m, wr * hr + wi * hi, wr * hi - wi * hr)
+        add(slot, 1, m, wr * hr + wi * hi, wr * hi - wi * hr)
         put_field(slot, m, hr * o1r + hi * o1i, hi * o1r - hr * o1i)
-        if m == 3:
-            spread(slot, 1, sums[slot][0])
-            spread(slot, 3, sums[slot][1])
 
     propagate(2, after_third)
 
     def after_fourth(slot, m, hr, hi):
         o0r, o0i = views[slot][0], views[slot][2]
         pr, pi = probe[m], probe[4 + m]
-        add(slot, m, pr * hr + pi * hi, pr * hi - pi * hr)
+        add(slot, 0, m, pr * hr + pi * hi, pr * hi - pi * hr)
         dr = hr * o0r + hi * o0i
         di = hi * o0r - hr * o0i
         if slot == 0:
@@ -235,11 +229,22 @@
         else:
             probe_grad[m] += dr
             probe_grad[4 + m] += di
-        if m == 3:
-            spread(slot, 0, sums[slot][0])
-            spread(slot, 2, sums[slot][1])
 
     propagate(2, after_fourth)
+
+
+def object_kernel(offsets, object_grad, grad_tall, cross, mate, grad_beside):
+    grad_ext = (grad_tall, grad_beside)
+    for total in grad_ext:
+        total[...] = jnp.zeros_like(total)
+    for slot in range(2):
+        for p in range(4):
+            value = object_grad[slot, p]
+            wide = jnp.concatenate([value, jnp.zeros_like(value)], axis=1)
+            wide = pltpu.roll(wide, lax.rem(offsets[2 * slot + 1] + 192, 256), 1)
+            for b in range(2):
+                grad_ext[b][p, pl.ds(offsets[2 * slot], TILE), :] += wide[:, block(b)]
+    even = even_column()
     for s in range(2):
         to_left, to_right = pack_columns(grad_beside[s], grad_beside[2 + s])
         mate[s], cross[s] = by_parity(even, to_right, to_left)
@@ -312,12 +317,11 @@
         prop_taps, probe_modes.reshape(8, TILE, TILE), measured.reshape(2, TILE, TILE),
         scratch=[pltpu.VMEM((8, 2 * TILE), F32)],
     )
-    probe_part, grad_tall, cross, mate = call(
+    probe_part, object_grad = call(
         main_kernel,
-        (f32(8, TILE, TILE), tall, tall_strip, tall_strip), [SM, SM] + [VM] * 6,
+        (f32(8, TILE, TILE), f32(2, 4, TILE, TILE)), [SM, SM] + [VM] * 6,
         offsets.reshape(-1), counts.reshape(1, 1), object_tall, *strips, probe, targets, ops,
         scratch=[
-            pltpu.VMEM((4, 256, TILE), F32),
             pltpu.VMEM((4, 256, TILE), F32),
             pltpu.VMEM((2, 256, 512), BF16),
             pltpu.VMEM((2, 256, 512), BF16),
@@ -327,6 +331,11 @@
             pltpu.VMEM((2, 4, 2, TILE, TILE), F32),
         ],
         flops=3_200_000_000, moved=4_000_000,
+    )
+    grad_tall, cross, mate = call(
+        object_kernel, (tall, tall_strip, tall_strip), [SM, VM],
+        offsets.reshape(-1), object_grad,
+        scratch=[pltpu.VMEM((4, 256, TILE), F32)],
     )
 
     near = lax.axis_size(NEAR_AXES)

time: 104 us -> 100 us (0.962)
  blocking collectives: 0 us -> 25.9 us
  starting transfers between devices: 61.5 us -> 43.4 us
  waiting for transfers between devices: 29 us -> 17.4 us
    all_to_all x0 -> x1, blocking collectives: none -> 25.9 us  [body(): lax.all_to_all(probe_part.reshape(near, rows, TILE), NEAR_AXES, 0, 0, til...]
    all_to_all x1 -> x0, starting transfers between devices: 15.3 us -> none  [body(): lax.all_to_all(probe_part.reshape(near, rows, TILE), NEAR_AXES, 0, 0, til...]
    all_to_all x1, waiting for transfers between devices: 12.9 us -> 1.06 us  [body(): shares = lax.all_to_all(spread_share, FAR_AXES, 0, 0, tiled=True)]
    ppermute x4, waiting for transfers between devices: 2.24 us -> 8.69 us  [exchange(): from_cross = lax.ppermute(cross, axes, pairs + [(b, a) for a, b in pairs])]
    all_to_all x1 -> x0, waiting for transfers between devices: 5.02 us -> none  [body(): lax.all_to_all(probe_part.reshape(near, rows, TILE), NEAR_AXES, 0, 0, til...]
    all_to_all x1, starting transfers between devices: 10.8 us -> 8.7 us  [body(): gathered = lax.all_to_all(spread_share, NEAR_AXES, 0, 0, tiled=True)]
    ppermute x4, waiting for transfers between devices: 7.52 us -> 5.71 us  [exchange(): from_mate = lax.ppermute(mate, axes, pairs + [(b, a) for a, b in pairs])]
    ppermute x4, starting transfers between devices: 13.1 us -> 11.7 us  [exchange(): from_cross = lax.ppermute(cross, axes, pairs + [(b, a) for a, b in pairs])]
  transfers between devices with their start and end apart: 11 -> 10, of which waited for: 6 -> 6; matrix products, arithmetic and copies ran while one was open for 0% -> 0% of each run, Pallas kernels for 1% -> 1%
where the time goes in v8:
time: 100 us; the launch traced here: 98.7 us
  starting transfers between devices  43.4 us (43%)
  blocking collectives  25.9 us (26%)
  waiting for transfers between devices  17.4 us (17%)
  Pallas kernels  8.86 us (9%)
  local copies, waits for them, and re-layouts  1.72 us (2%)
  between operations  1.45 us (1%)
    all_to_all x1, blocking collectives, body(): lax.all_to_all(probe_part.reshape(near, rows, TILE), NEAR_AXES, 0, 0, til...  25.9 us
    ppermute x4, starting transfers between devices, exchange(): from_mate = lax.ppermute(mate, axes, pairs + [(b, a) for a, b in pairs])  16.8 us
    ppermute x4, starting transfers between devices, exchange(): from_cross = lax.ppermute(cross, axes, pairs + [(b, a) for a, b in pairs])  11.7 us
    pallas_call x8, Pallas kernels, call(): pl.pallas_call(kernel, out_shape=out_shape, in_specs=in_specs, out_specs=...  8.86 us
    all_to_all x1, starting transfers between devices, body(): gathered = lax.all_to_all(spread_share, NEAR_AXES, 0, 0, tiled=True)  8.7 us
    ppermute x4, waiting for transfers between devices, exchange(): from_cross = lax.ppermute(cross, axes, pairs + [(b, a) for a, b in pairs])  8.69 us
    all_to_all x1, starting transfers between devices, body(): shares = lax.all_to_all(spread_share, FAR_AXES, 0, 0, tiled=True)  6.18 us
    ppermute x4, waiting for transfers between devices, exchange(): from_mate = lax.ppermute(mate, axes, pairs + [(b, a) for a, b in pairs])  5.71 us
  transfers between devices with their start and end apart: 10, of which 6 were waited for; matrix products, arithmetic and copies ran while one was open for 0% of the time, Pallas kernels for 1%

profile of v8, /device:TPU:1, one launch (start us, length us, event | category | flops | bytes accessed | tf_op | source)
XLA Modules:
  0.0 98.7 jit_solution(12037800936918729726)
XLA Ops:
  0.6 0.9 copy-done
  1.6 0.8 collective-permute-start
  2.4 7.4 %collective-permute-start.1 = (f32[4,64,128]{2,1,0:T(8,128)S(1)}, f32[4,64,128]{2,1,0:T(8,128)S(1)}, u32[]{:S(2)}, u32[]{:S(2)}) collective-permute-start(f32[4,64,128]{2,1,0:T(8,128)S(1)} %get-tuple-element.22), channel_id=1, source_target_pairs={{0,16},{32,48},{64,80},{96,112},{128,144},{160,176},{192,208},{224... | collective-permute-start | bytes 393224 | tf_op jit(solution)/shard_map/ppermute | solution.py:296
  9.8 2.3 %collective-permute-done.1.from_mate = f32[4,64,128]{2,1,0:T(8,128)S(1)} collective-permute-done((f32[4,64,128]{2,1,0:T(8,128)S(1)}, f32[4,64,128]{2,1,0:T(8,128)S(1)}, u32[]{:S(2)}, u32[]{:S(2)}) %collective-permute-start.1) | collective-permute-done | bytes 131104 | tf_op jit(solution)/shard_map/ppermute | solution.py:296
  12.3 6.6 %collective-permute-start.2 = (f32[2,256,128]{2,1,0:T(8,128)S(1)}, f32[2,256,128]{2,1,0:T(8,128)S(1)}, u32[]{:S(2)}, u32[]{:S(2)}) collective-permute-start(f32[2,256,128]{2,1,0:T(8,128)S(1)} %get-tuple-element.24), channel_id=1, source_target_pairs={{1,2},{3,4},{5,6},{7,8},{9,10},{11,12},{13,14},{2,1},{4,3},{6,5},{... | collective-permute-start | bytes 786440 | tf_op jit(solution)/shard_map/ppermute | solution.py:294
  19.0 1.9 %collective-permute-start.3 = (f32[2,256,128]{2,1,0:T(8,128)S(1)}, f32[2,256,128]{2,1,0:T(8,128)S(1)}, u32[]{:S(2)}, u32[]{:S(2)}) collective-permute-start(f32[2,256,128]{2,1,0:T(8,128)S(1)} %get-tuple-element.25), channel_id=1, source_target_pairs={{0,1},{2,3},{4,5},{6,7},{8,9},{10,11},{12,13},{14,15},{1,0},{3,2},... | collective-permute-start | bytes 786440 | tf_op jit(solution)/shard_map/ppermute | solution.py:296
  21.6 0.7 copy-done.3
  22.6 2.2 %collective-permute-done.2.from_cross = f32[2,256,128]{2,1,0:T(8,128)S(1)} collective-permute-done((f32[2,256,128]{2,1,0:T(8,128)S(1)}, f32[2,256,128]{2,1,0:T(8,128)S(1)}, u32[]{:S(2)}, u32[]{:S(2)}) %collective-permute-start.2) | collective-permute-done | bytes 262176 | tf_op jit(solution)/shard_map/ppermute | solution.py:294
  24.9 4.8 %shard_map.80 = (f32[8,128,128]{2,1,0:T(8,128)S(1)}, f32[2,4,128,128]{3,2,1,0:T(8,128)S(1)}) custom-call(s32[4]{0:T(128)S(1)} %reshape.29.offsets, s32[1,1]{1,0:T(1,128)S(6)} %copy.8.counts, f32[4,256,128]{2,1,0:T(8,128)S(1)} %get-tuple-element.23.tall, f32[2,256,128]{2,1,0:T(8,128)S(1)} %collective-permute-done.2.from_cross, ...), custom_call_target="tpu_custom_call" | custom-call | flops 3200000000 | bytes 4000000 | tf_op jit(solution)/shard_map/pallas_call | solution.py:28
  29.7 25.9 %all_to_all.15.shares = f32[32,32,128]{2,1,0:T(8,128)S(1)} all-to-all(f32[32,32,128]{2,1,0:T(8,128)S(1)} %bitcast.11), channel_id=1, replica_groups=mesh['xl'=2,'za'=8,'zb'=2,'y'=4,'xh'=2,'core'=2] {'xl','y','xh','core'}, dimensions={0} | all-to-all | bytes 1048576 | tf_op jit(solution)/shard_map/all_to_all | solution.py:344
  55.6 0.8 shard_map.81
  56.3 6.2 %all-to-all-start.1 = ((f32[16,32,128]{2,1,0:T(8,128)}), f32[16,32,128]{2,1,0:T(8,128)S(1)}, u32[]{:S(2)}, u32[]{:S(2)}) async-start(f32[16,32,128]{2,1,0:T(8,128)} %shard_map.81), calls=%async_computation.1 | async-start | bytes 524288 | tf_op jit(solution)/shard_map/all_to_all | solution.py:347
  62.5 0.9 shard_map.82
  63.5 3.6 %collective-permute-start.4 = (f32[2,256,128]{2,1,0:T(8,128)S(1)}, f32[2,256,128]{2,1,0:T(8,128)S(1)}, u32[]{:S(2)}, u32[]{:S(2)}) collective-permute-start(f32[2,256,128]{2,1,0:T(8,128)S(1)} %get-tuple-element.32), channel_id=1, source_target_pairs={{1,2},{3,4},{5,6},{7,8},{9,10},{11,12},{13,14},{2,1},{4,3},{6,5},{... | collective-permute-start | bytes 786440 | tf_op jit(solution)/shard_map/ppermute | solution.py:294
  67.1 1.9 %collective-permute-start.5 = (f32[2,256,128]{2,1,0:T(8,128)S(1)}, f32[2,256,128]{2,1,0:T(8,128)S(1)}, u32[]{:S(2)}, u32[]{:S(2)}) collective-permute-start(f32[2,256,128]{2,1,0:T(8,128)S(1)} %get-tuple-element.33), channel_id=1, source_target_pairs={{0,1},{2,3},{4,5},{6,7},{8,9},{10,11},{12,13},{14,15},{1,0},{3,2},... | collective-permute-start | bytes 786440 | tf_op jit(solution)/shard_map/ppermute | solution.py:296
  69.0 6.5 %collective-permute-done.4.from_cross = f32[2,256,128]{2,1,0:T(8,128)S(1)} collective-permute-done((f32[2,256,128]{2,1,0:T(8,128)S(1)}, f32[2,256,128]{2,1,0:T(8,128)S(1)}, u32[]{:S(2)}, u32[]{:S(2)}) %collective-permute-start.4) | collective-permute-done | bytes 262176 | tf_op jit(solution)/shard_map/ppermute | solution.py:294
  75.5 1.1 %all-to-all-done.1.shares = f32[16,32,128]{2,1,0:T(8,128)S(1)} async-done(((f32[16,32,128]{2,1,0:T(8,128)}), f32[16,32,128]{2,1,0:T(8,128)S(1)}, u32[]{:S(2)}, u32[]{:S(2)}) %all-to-all-start.1) | async-done | bytes 262176 | tf_op jit(solution)/shard_map/all_to_all | solution.py:347
  76.5 0.9 shard_map.83
  77.5 8.7 %all-to-all-start.2 = ((f32[32,32,128]{2,1,0:T(8,128)}), f32[32,32,128]{2,1,0:T(8,128)S(1)}, u32[]{:S(2)}, u32[]{:S(2)}) async-start(f32[32,32,128]{2,1,0:T(8,128)} %get-tuple-element.37), calls=%async_computation.2 | async-start | bytes 1048576 | tf_op jit(solution)/shard_map/all_to_all | solution.py:353
  86.2 0.7 collective-permute-start.6
  86.8 5.6 %collective-permute-start.7 = (f32[4,64,128]{2,1,0:T(8,128)S(1)}, f32[4,64,128]{2,1,0:T(8,128)S(1)}, u32[]{:S(2)}, u32[]{:S(2)}) collective-permute-start(f32[4,64,128]{2,1,0:T(8,128)S(1)} %get-tuple-element.36), channel_id=1, source_target_pairs={{0,16},{32,48},{64,80},{96,112},{128,144},{160,176},{192,208},{224... | collective-permute-start | bytes 393224 | tf_op jit(solution)/shard_map/ppermute | solution.py:296
  92.4 3.4 %collective-permute-done.7.from_mate = f32[4,64,128]{2,1,0:T(8,128)S(1)} collective-permute-done((f32[4,64,128]{2,1,0:T(8,128)S(1)}, f32[4,64,128]{2,1,0:T(8,128)S(1)}, u32[]{:S(2)}, u32[]{:S(2)}) %collective-permute-start.7) | collective-permute-done | bytes 131104 | tf_op jit(solution)/shard_map/ppermute | solution.py:296
  95.8 1.9 %all-to-all-done.2 = f32[32,32,128]{2,1,0:T(8,128)S(1)} async-done(((f32[32,32,128]{2,1,0:T(8,128)}), f32[32,32,128]{2,1,0:T(8,128)S(1)}, u32[]{:S(2)}, u32[]{:S(2)}) %all-to-all-start.2) | async-done | bytes 524320 | tf_op jit(solution)/shard_map/all_to_all | solution.py:353
  97.7 0.9 shard_map.84
  (16 shorter events, 0.6 us)
Async XLA Ops:
  0.6 1.0 copy-start
  1.6 20.1 %copy-start.1 = (f32[2,4,128,128]{3,2,1,0:T(8,128)S(1)}, f32[2,4,128,128]{3,2,1,0:T(8,128)}, u32[]{:S(2)}) copy-start(f32[2,4,128,128]{3,2,1,0:T(8,128)} %param.7) | copy-start | bytes 1572868
  1.6 8.2 %collective-permute-start = (f32[4,64,128]{2,1,0:T(8,128)S(1)}, f32[4,64,128]{2,1,0:T(8,128)S(1)}, u32[]{:S(2)}, u32[]{:S(2)}) collective-permute-start(f32[4,64,128]{2,1,0:T(8,128)S(1)} %get-tuple-element.21), channel_id=1, source_target_pairs={{16,32},{48,64},{80,96},{112,128},{144,160},{176,192},{208,224},{2... | collective-permute-start | bytes 393224 | tf_op jit(solution)/shard_map/ppermute | solution.py:294
  2.4 19.2 %copy-start.2 = (f32[1,1,2,128,128]{4,3,2,1,0:T(8,128)S(1)}, f32[1,1,2,128,128]{4,3,2,1,0:T(8,128)}, u32[]{:S(2)}) copy-start(f32[1,1,2,128,128]{4,3,2,1,0:T(8,128)} %param.9) | copy-start | bytes 393220
  2.4 9.7 %collective-permute-start.1 = (f32[4,64,128]{2,1,0:T(8,128)S(1)}, f32[4,64,128]{2,1,0:T(8,128)S(1)}, u32[]{:S(2)}, u32[]{:S(2)}) collective-permute-start(f32[4,64,128]{2,1,0:T(8,128)S(1)} %get-tuple-element.22), channel_id=1, source_target_pairs={{0,16},{32,48},{64,80},{96,112},{128,144},{160,176},{192,208},{224... | collective-permute-start | bytes 393224 | tf_op jit(solution)/shard_map/ppermute | solution.py:296
  12.3 12.6 %collective-permute-start.2 = (f32[2,256,128]{2,1,0:T(8,128)S(1)}, f32[2,256,128]{2,1,0:T(8,128)S(1)}, u32[]{:S(2)}, u32[]{:S(2)}) collective-permute-start(f32[2,256,128]{2,1,0:T(8,128)S(1)} %get-tuple-element.24), channel_id=1, source_target_pairs={{1,2},{3,4},{5,6},{7,8},{9,10},{11,12},{13,14},{2,1},{4,3},{6,5},{... | collective-permute-start | bytes 786440 | tf_op jit(solution)/shard_map/ppermute | solution.py:294
  19.0 2.6 %copy-start.4 = (s32[1,1,2,2]{3,2,1,0:T(2,128)S(1)}, s32[1,1,2,2]{3,2,1,0:T(2,128)}, u32[]{:S(2)}) copy-start(s32[1,1,2,2]{3,2,1,0:T(2,128)} %param.10) | copy-start | bytes 52
  19.0 5.9 %collective-permute-start.3 = (f32[2,256,128]{2,1,0:T(8,128)S(1)}, f32[2,256,128]{2,1,0:T(8,128)S(1)}, u32[]{:S(2)}, u32[]{:S(2)}) collective-permute-start(f32[2,256,128]{2,1,0:T(8,128)S(1)} %get-tuple-element.25), channel_id=1, source_target_pairs={{0,1},{2,3},{4,5},{6,7},{8,9},{10,11},{12,13},{14,15},{1,0},{3,2},... | collective-permute-start | bytes 786440 | tf_op jit(solution)/shard_map/ppermute | solution.py:296
  21.6 0.7 copy-start.3
  56.3 20.2 %all-to-all-start.1 = ((f32[16,32,128]{2,1,0:T(8,128)}), f32[16,32,128]{2,1,0:T(8,128)S(1)}, u32[]{:S(2)}, u32[]{:S(2)}) async-start(f32[16,32,128]{2,1,0:T(8,128)} %shard_map.81), calls=%async_computation.1 | async-start | bytes 524288 | tf_op jit(solution)/shard_map/all_to_all | solution.py:347
  63.5 12.0 %collective-permute-start.4 = (f32[2,256,128]{2,1,0:T(8,128)S(1)}, f32[2,256,128]{2,1,0:T(8,128)S(1)}, u32[]{:S(2)}, u32[]{:S(2)}) collective-permute-start(f32[2,256,128]{2,1,0:T(8,128)S(1)} %get-tuple-element.32), channel_id=1, source_target_pairs={{1,2},{3,4},{5,6},{7,8},{9,10},{11,12},{13,14},{2,1},{4,3},{6,5},{... | collective-permute-start | bytes 786440 | tf_op jit(solution)/shard_map/ppermute | solution.py:294
  67.1 8.4 %collective-permute-start.5 = (f32[2,256,128]{2,1,0:T(8,128)S(1)}, f32[2,256,128]{2,1,0:T(8,128)S(1)}, u32[]{:S(2)}, u32[]{:S(2)}) collective-permute-start(f32[2,256,128]{2,1,0:T(8,128)S(1)} %get-tuple-element.33), channel_id=1, source_target_pairs={{0,1},{2,3},{4,5},{6,7},{8,9},{10,11},{12,13},{14,15},{1,0},{3,2},... | collective-permute-start | bytes 786440 | tf_op jit(solution)/shard_map/ppermute | solution.py:296
  77.5 20.3 %all-to-all-start.2 = ((f32[32,32,128]{2,1,0:T(8,128)}), f32[32,32,128]{2,1,0:T(8,128)S(1)}, u32[]{:S(2)}, u32[]{:S(2)}) async-start(f32[32,32,128]{2,1,0:T(8,128)} %get-tuple-element.37), calls=%async_computation.2 | async-start | bytes 1048576 | tf_op jit(solution)/shard_map/all_to_all | solution.py:353
  86.2 6.3 %collective-permute-start.6 = (f32[4,64,128]{2,1,0:T(8,128)S(1)}, f32[4,64,128]{2,1,0:T(8,128)S(1)}, u32[]{:S(2)}, u32[]{:S(2)}) collective-permute-start(f32[4,64,128]{2,1,0:T(8,128)S(1)} %get-tuple-element.35), channel_id=1, source_target_pairs={{16,32},{48,64},{80,96},{112,128},{144,160},{176,192},{208,224},{2... | collective-permute-start | bytes 393224 | tf_op jit(solution)/shard_map/ppermute | solution.py:294
  86.8 9.0 %collective-permute-start.7 = (f32[4,64,128]{2,1,0:T(8,128)S(1)}, f32[4,64,128]{2,1,0:T(8,128)S(1)}, u32[]{:S(2)}, u32[]{:S(2)}) collective-permute-start(f32[4,64,128]{2,1,0:T(8,128)S(1)} %get-tuple-element.36), channel_id=1, source_target_pairs={{0,16},{32,48},{64,80},{96,112},{128,144},{160,176},{192,208},{224... | collective-permute-start | bytes 393224 | tf_op jit(solution)/shard_map/ppermute | solution.py:296

commit v9 on v8

--- a/solution.py
+++ b/solution.py
@@ -13,11 +13,12 @@
 BF16 = jnp.bfloat16
 ROW_AXES = ("xl", "za", "zb")
 COL_AXES = ("y", "xh", "core")
-NEAR_AXES = ("xl", "y", "xh", "core")
-FAR_AXES = ("za", "zb")
+NEAR_AXES = ("xl", "zb", "y", "xh", "core")
+FAR_AXES = ("za",)
 VMEM_LIMIT = 12 * 1024 * 1024
 TILE = 128
 HALF = 64
+BESIDE = 100_000_000_000
 VM = pl.BlockSpec(memory_space=pltpu.VMEM)
 SM = pl.BlockSpec(memory_space=pltpu.SMEM)
 FAR = pl.BlockSpec(memory_space=pltpu.HBM)
@@ -256,12 +257,7 @@
         spread_share[i] = share
 
 
-def near_kernel(shares, spread_share):
-    spread_sum(1.0, shares, spread_share)
-
-
-def far_kernel(scale, shares, grad_tall, from_cross, from_mate, spread_share, part, cross, mate):
-    spread_sum(scale, shares, spread_share)
+def fold_columns_kernel(grad_tall, from_cross, from_mate, part, cross, mate):
     even, even_down = even_column(), even_row()
     for s in range(2):
         from_right, from_left = by_parity(even, from_mate[s], from_cross[s])
@@ -271,19 +267,21 @@
             mate[p], cross[p] = by_parity(even_down, total[HALF + TILE:], total[:HALF])
 
 
-def finish_kernel(part, from_cross, from_mate, gathered, result_far, probe_far, result, sems):
-    moves = []
-    for i in range(4):
-        rows = pl.ds(256 * i, 256)
-        moves.append(pltpu.make_async_copy(gathered.at[rows], probe_far.at[rows], sems.at[i]))
-        moves[i].start()
+def fold_rows_kernel(part, from_cross, from_mate, result):
     even = even_row()
     for p in range(4):
         below, above = by_parity(even, from_mate[p], from_cross[p])
         result[p, :HALF] = part[p, :HALF] + above
         result[p, HALF:] = part[p, HALF:] + below
-        moves.append(pltpu.make_async_copy(result.at[p], result_far.at[p], sems.at[4 + p]))
-        moves[-1].start()
+
+
+def finish_kernel(result, gathered, result_far, probe_far, sems):
+    moves = [pltpu.make_async_copy(result.at[p], result_far.at[p], sems.at[p]) for p in range(4)]
+    for i in range(4):
+        part = pl.ds(256 * i, 256)
+        moves.append(pltpu.make_async_copy(gathered.at[part], probe_far.at[part], sems.at[4 + i]))
+    for move in moves:
+        move.start()
     for move in moves:
         move.wait()
 
@@ -342,20 +340,26 @@
     far = lax.axis_size(FAR_AXES)
     rows = 8 * TILE // near
     shares = lax.all_to_all(probe_part.reshape(near, rows, TILE), NEAR_AXES, 0, 0, tiled=True)
-    (spread_share,) = call(near_kernel, (f32(far, rows, TILE),), [VM], shares)
+    (spread_share,) = call(
+        functools.partial(spread_sum, 1.0), (f32(far, rows, TILE),), [VM], shares
+    )
     strips = exchange(cross, mate, COL_AXES)
     shares = lax.all_to_all(spread_share, FAR_AXES, 0, 0, tiled=True)
-    spread_share, part, cross, mate = call(
-        functools.partial(far_kernel, 1.0 / math.sqrt(near * far)),
-        (f32(near, rows, TILE), planes, half, half), [VM] * 4, shares, grad_tall, *strips,
+    part, cross, mate = call(
+        fold_columns_kernel, (planes, half, half), [VM] * 3, grad_tall, *strips
     )
     rims = exchange(cross, mate, ROW_AXES)
+    (spread_share,) = call(
+        functools.partial(spread_sum, 1.0 / math.sqrt(near * far)), (f32(near, rows, TILE),), [VM], shares
+    )
     gathered = lax.all_to_all(spread_share, NEAR_AXES, 0, 0, tiled=True)
+    (result,) = call(
+        fold_rows_kernel, (planes,), [VM] * 3, part, *rims, flops=BESIDE, moved=1
+    )
     result, probe_grad = call(
-        finish_kernel, (planes, f32(8 * TILE, TILE)), [VM] * 4,
-        part, *rims, gathered.reshape(8 * TILE, TILE),
-        scratch=[pltpu.VMEM((4, TILE, TILE), F32), pltpu.SemaphoreType.DMA((8,))],
-        out_specs=[FAR, FAR],
+        finish_kernel, (planes, f32(8 * TILE, TILE)), [VM] * 2,
+        result, gathered.reshape(8 * TILE, TILE),
+        scratch=[pltpu.SemaphoreType.DMA((8,))], out_specs=[FAR, FAR],
     )
     return result.reshape(object_field.shape), probe_grad.reshape(probe_modes.shape)
 

time: 100 us -> 98.4 us (0.984)
  blocking collectives: 25.9 us -> 0 us
  starting transfers between devices: 43.4 us -> 58.2 us
  waiting for transfers between devices: 17.4 us -> 26.7 us
    all_to_all x1 -> x0, blocking collectives: 25.9 us -> none  [body(): lax.all_to_all(probe_part.reshape(near, rows, TILE), NEAR_AXES, 0, 0, til...]
    all_to_all x0 -> x1, starting transfers between devices: none -> 15.3 us  [body(): lax.all_to_all(probe_part.reshape(near, rows, TILE), NEAR_AXES, 0, 0, til...]
    all_to_all x1, waiting for transfers between devices: 1.91 us -> 11.8 us  [body(): gathered = lax.all_to_all(spread_share, NEAR_AXES, 0, 0, tiled=True)]
    ppermute x4, waiting for transfers between devices: 8.69 us -> 2.24 us  [exchange(): from_cross = lax.ppermute(cross, axes, pairs + [(b, a) for a, b in pairs])]
    all_to_all x1, waiting for transfers between devices: 1.06 us -> 6.26 us  [body(): shares = lax.all_to_all(spread_share, FAR_AXES, 0, 0, tiled=True)]
    all_to_all x0 -> x1, waiting for transfers between devices: none -> 4.1 us  [body(): lax.all_to_all(probe_part.reshape(near, rows, TILE), NEAR_AXES, 0, 0, til...]
    ppermute x4, waiting for transfers between devices: 5.71 us -> 2.34 us  [exchange(): from_mate = lax.ppermute(mate, axes, pairs + [(b, a) for a, b in pairs])]
    all_to_all x1, starting transfers between devices: 8.7 us -> 6.24 us  [body(): gathered = lax.all_to_all(spread_share, NEAR_AXES, 0, 0, tiled=True)]
  transfers between devices with their start and end apart: 10 -> 11, of which waited for: 6 -> 5; matrix products, arithmetic and copies ran while one was open for 0% -> 0% of each run, Pallas kernels for 1% -> 3%
where the time goes in v9:
time: 98.4 us; the launch traced here: 97.8 us
  starting transfers between devices  58.2 us (59%)
  waiting for transfers between devices  26.7 us (27%)
  Pallas kernels  9.66 us (10%)
  local copies, waits for them, and re-layouts  1.72 us (2%)
  between operations  1.48 us (2%)
    ppermute x4, starting transfers between devices, exchange(): from_mate = lax.ppermute(mate, axes, pairs + [(b, a) for a, b in pairs])  17 us
    all_to_all x1, starting transfers between devices, body(): lax.all_to_all(probe_part.reshape(near, rows, TILE), NEAR_AXES, 0, 0, til...  15.3 us
    ppermute x4, starting transfers between devices, exchange(): from_cross = lax.ppermute(cross, axes, pairs + [(b, a) for a, b in pairs])  13.1 us
    all_to_all x1, waiting for transfers between devices, body(): gathered = lax.all_to_all(spread_share, NEAR_AXES, 0, 0, tiled=True)  11.8 us
    pallas_call x10, Pallas kernels, call(): pl.pallas_call(kernel, out_shape=out_shape, in_specs=in_specs, out_specs=...  9.66 us
    all_to_all x1, starting transfers between devices, body(): shares = lax.all_to_all(spread_share, FAR_AXES, 0, 0, tiled=True)  6.53 us
    all_to_all x1, waiting for transfers between devices, body(): shares = lax.all_to_all(spread_share, FAR_AXES, 0, 0, tiled=True)  6.26 us
    all_to_all x1, starting transfers between devices, body(): gathered = lax.all_to_all(spread_share, NEAR_AXES, 0, 0, tiled=True)  6.24 us
  transfers between devices with their start and end apart: 11, of which 5 were waited for; matrix products, arithmetic and copies ran while one was open for 0% of the time, Pallas kernels for 3%

profile of v9, /device:TPU:1, one launch (start us, length us, event | category | flops | bytes accessed | tf_op | source)
XLA Modules:
  0.0 97.8 jit_solution(10475177451102409587)
XLA Ops:
  0.6 0.9 copy-done
  1.6 0.8 collective-permute-start
  2.4 7.4 %collective-permute-start.1 = (f32[4,64,128]{2,1,0:T(8,128)S(1)}, f32[4,64,128]{2,1,0:T(8,128)S(1)}, u32[]{:S(2)}, u32[]{:S(2)}) collective-permute-start(f32[4,64,128]{2,1,0:T(8,128)S(1)} %get-tuple-element.21), channel_id=1, source_target_pairs={{0,16},{32,48},{64,80},{96,112},{128,144},{160,176},{192,208},{224... | collective-permute-start | bytes 393224 | tf_op jit(solution)/shard_map/ppermute | solution.py:294
  9.8 2.3 %collective-permute-done.1.from_mate = f32[4,64,128]{2,1,0:T(8,128)S(1)} collective-permute-done((f32[4,64,128]{2,1,0:T(8,128)S(1)}, f32[4,64,128]{2,1,0:T(8,128)S(1)}, u32[]{:S(2)}, u32[]{:S(2)}) %collective-permute-start.1) | collective-permute-done | bytes 131104 | tf_op jit(solution)/shard_map/ppermute | solution.py:294
  12.3 6.6 %collective-permute-start.2 = (f32[2,256,128]{2,1,0:T(8,128)S(1)}, f32[2,256,128]{2,1,0:T(8,128)S(1)}, u32[]{:S(2)}, u32[]{:S(2)}) collective-permute-start(f32[2,256,128]{2,1,0:T(8,128)S(1)} %get-tuple-element.23), channel_id=1, source_target_pairs={{1,2},{3,4},{5,6},{7,8},{9,10},{11,12},{13,14},{2,1},{4,3},{6,5},{... | collective-permute-start | bytes 786440 | tf_op jit(solution)/shard_map/ppermute | solution.py:292
  19.0 1.9 %collective-permute-start.3 = (f32[2,256,128]{2,1,0:T(8,128)S(1)}, f32[2,256,128]{2,1,0:T(8,128)S(1)}, u32[]{:S(2)}, u32[]{:S(2)}) collective-permute-start(f32[2,256,128]{2,1,0:T(8,128)S(1)} %get-tuple-element.24), channel_id=1, source_target_pairs={{0,1},{2,3},{4,5},{6,7},{8,9},{10,11},{12,13},{14,15},{1,0},{3,2},... | collective-permute-start | bytes 786440 | tf_op jit(solution)/shard_map/ppermute | solution.py:294
  21.6 0.7 copy-done.3
  22.3 0.3 shard_map.79
  22.6 2.2 %collective-permute-done.2.from_cross = f32[2,256,128]{2,1,0:T(8,128)S(1)} collective-permute-done((f32[2,256,128]{2,1,0:T(8,128)S(1)}, f32[2,256,128]{2,1,0:T(8,128)S(1)}, u32[]{:S(2)}, u32[]{:S(2)}) %collective-permute-start.2) | collective-permute-done | bytes 262176 | tf_op jit(solution)/shard_map/ppermute | solution.py:292
  24.9 5.6 %shard_map.80 = (f32[8,128,128]{2,1,0:T(8,128)}, f32[2,4,128,128]{3,2,1,0:T(8,128)S(1)}) custom-call(s32[4]{0:T(128)S(1)} %reshape.29.offsets, s32[1,1]{1,0:T(1,128)S(6)} %copy.8.counts, f32[4,256,128]{2,1,0:T(8,128)S(1)} %get-tuple-element.22.tall, f32[2,256,128]{2,1,0:T(8,128)S(1)} %collective-permute-done.2.from_cross, ...), custom_call_target="tpu_custom_call" | custom-call | flops 3200000000 | bytes 4000000 | tf_op jit(solution)/shard_map/pallas_call | solution.py:29
  30.5 15.3 %all-to-all-start = ((f32[64,16,128]{2,1,0:T(8,128)}), f32[64,16,128]{2,1,0:T(8,128)S(1)}, u32[]{:S(2)}, u32[]{:S(2)}) async-start(f32[64,16,128]{2,1,0:T(8,128)} %bitcast.3), calls=%async_computation | async-start | bytes 1048576 | tf_op jit(solution)/shard_map/all_to_all | solution.py:342
  45.8 0.9 shard_map.81
  46.7 5.0 %collective-permute-start.4 = (f32[2,256,128]{2,1,0:T(8,128)S(1)}, f32[2,256,128]{2,1,0:T(8,128)S(1)}, u32[]{:S(2)}, u32[]{:S(2)}) collective-permute-start(f32[2,256,128]{2,1,0:T(8,128)S(1)} %get-tuple-element.30), channel_id=1, source_target_pairs={{1,2},{3,4},{5,6},{7,8},{9,10},{11,12},{13,14},{2,1},{4,3},{6,5},{... | collective-permute-start | bytes 786440 | tf_op jit(solution)/shard_map/ppermute | solution.py:292
  51.7 1.9 %collective-permute-start.5 = (f32[2,256,128]{2,1,0:T(8,128)S(1)}, f32[2,256,128]{2,1,0:T(8,128)S(1)}, u32[]{:S(2)}, u32[]{:S(2)}) collective-permute-start(f32[2,256,128]{2,1,0:T(8,128)S(1)} %get-tuple-element.31), channel_id=1, source_target_pairs={{0,1},{2,3},{4,5},{6,7},{8,9},{10,11},{12,13},{14,15},{1,0},{3,2},... | collective-permute-start | bytes 786440 | tf_op jit(solution)/shard_map/ppermute | solution.py:294
  53.7 4.1 %all-to-all-done.shares = f32[64,16,128]{2,1,0:T(8,128)S(1)} async-done(((f32[64,16,128]{2,1,0:T(8,128)}), f32[64,16,128]{2,1,0:T(8,128)S(1)}, u32[]{:S(2)}, u32[]{:S(2)}) %all-to-all-start) | async-done | bytes 524320 | tf_op jit(solution)/shard_map/all_to_all | solution.py:342
  57.8 0.7 shard_map.84
  58.5 6.5 %all-to-all-start.1 = ((f32[8,16,128]{2,1,0:T(8,128)}), f32[8,16,128]{2,1,0:T(8,128)S(1)}, u32[]{:S(2)}, u32[]{:S(2)}) async-start(f32[8,16,128]{2,1,0:T(8,128)} %shard_map.84), calls=%async_computation.1 | async-start | bytes 131072 | tf_op jit(solution)/shard_map/all_to_all | solution.py:347
  65.2 0.7 collective-permute-start.6
  65.9 5.8 %collective-permute-start.7 = (f32[4,64,128]{2,1,0:T(8,128)S(1)}, f32[4,64,128]{2,1,0:T(8,128)S(1)}, u32[]{:S(2)}, u32[]{:S(2)}) collective-permute-start(f32[4,64,128]{2,1,0:T(8,128)S(1)} %get-tuple-element.34), channel_id=1, source_target_pairs={{0,16},{32,48},{64,80},{96,112},{128,144},{160,176},{192,208},{224... | collective-permute-start | bytes 393224 | tf_op jit(solution)/shard_map/ppermute | solution.py:294
  71.6 6.3 %all-to-all-done.1.shares = f32[8,16,128]{2,1,0:T(8,128)S(1)} async-done(((f32[8,16,128]{2,1,0:T(8,128)}), f32[8,16,128]{2,1,0:T(8,128)S(1)}, u32[]{:S(2)}, u32[]{:S(2)}) %all-to-all-start.1) | async-done | bytes 65568 | tf_op jit(solution)/shard_map/all_to_all | solution.py:347
  77.9 0.8 shard_map.85
  78.7 6.2 %all-to-all-start.2 = ((f32[64,16,128]{2,1,0:T(8,128)}), f32[64,16,128]{2,1,0:T(8,128)S(1)}, u32[]{:S(2)}, u32[]{:S(2)}) async-start(f32[64,16,128]{2,1,0:T(8,128)} %shard_map.85), calls=%async_computation.2 | async-start | bytes 1048576 | tf_op jit(solution)/shard_map/all_to_all | solution.py:355
  85.1 11.8 %all-to-all-done.2 = f32[64,16,128]{2,1,0:T(8,128)S(1)} async-done(((f32[64,16,128]{2,1,0:T(8,128)}), f32[64,16,128]{2,1,0:T(8,128)S(1)}, u32[]{:S(2)}, u32[]{:S(2)}) %all-to-all-start.2) | async-done | bytes 524320 | tf_op jit(solution)/shard_map/all_to_all | solution.py:355
  96.9 0.9 shard_map.86
  (19 shorter events, 0.5 us)
Async XLA Ops:
  0.6 1.0 copy-start
  1.6 20.1 %copy-start.1 = (f32[2,4,128,128]{3,2,1,0:T(8,128)S(1)}, f32[2,4,128,128]{3,2,1,0:T(8,128)}, u32[]{:S(2)}) copy-start(f32[2,4,128,128]{3,2,1,0:T(8,128)} %param.7) | copy-start | bytes 1572868
  1.6 8.2 %collective-permute-start = (f32[4,64,128]{2,1,0:T(8,128)S(1)}, f32[4,64,128]{2,1,0:T(8,128)S(1)}, u32[]{:S(2)}, u32[]{:S(2)}) collective-permute-start(f32[4,64,128]{2,1,0:T(8,128)S(1)} %get-tuple-element.20), channel_id=1, source_target_pairs={{16,32},{48,64},{80,96},{112,128},{144,160},{176,192},{208,224},{2... | collective-permute-start | bytes 393224 | tf_op jit(solution)/shard_map/ppermute | solution.py:292
  2.4 19.2 %copy-start.2 = (f32[1,1,2,128,128]{4,3,2,1,0:T(8,128)S(1)}, f32[1,1,2,128,128]{4,3,2,1,0:T(8,128)}, u32[]{:S(2)}) copy-start(f32[1,1,2,128,128]{4,3,2,1,0:T(8,128)} %param.9) | copy-start | bytes 393220
  2.4 9.7 %collective-permute-start.1 = (f32[4,64,128]{2,1,0:T(8,128)S(1)}, f32[4,64,128]{2,1,0:T(8,128)S(1)}, u32[]{:S(2)}, u32[]{:S(2)}) collective-permute-start(f32[4,64,128]{2,1,0:T(8,128)S(1)} %get-tuple-element.21), channel_id=1, source_target_pairs={{0,16},{32,48},{64,80},{96,112},{128,144},{160,176},{192,208},{224... | collective-permute-start | bytes 393224 | tf_op jit(solution)/shard_map/ppermute | solution.py:294
  12.3 12.6 %collective-permute-start.2 = (f32[2,256,128]{2,1,0:T(8,128)S(1)}, f32[2,256,128]{2,1,0:T(8,128)S(1)}, u32[]{:S(2)}, u32[]{:S(2)}) collective-permute-start(f32[2,256,128]{2,1,0:T(8,128)S(1)} %get-tuple-element.23), channel_id=1, source_target_pairs={{1,2},{3,4},{5,6},{7,8},{9,10},{11,12},{13,14},{2,1},{4,3},{6,5},{... | collective-permute-start | bytes 786440 | tf_op jit(solution)/shard_map/ppermute | solution.py:292
  19.0 2.6 %copy-start.4 = (s32[1,1,2,2]{3,2,1,0:T(2,128)S(1)}, s32[1,1,2,2]{3,2,1,0:T(2,128)}, u32[]{:S(2)}) copy-start(s32[1,1,2,2]{3,2,1,0:T(2,128)} %param.10) | copy-start | bytes 52
  19.0 5.9 %collective-permute-start.3 = (f32[2,256,128]{2,1,0:T(8,128)S(1)}, f32[2,256,128]{2,1,0:T(8,128)S(1)}, u32[]{:S(2)}, u32[]{:S(2)}) collective-permute-start(f32[2,256,128]{2,1,0:T(8,128)S(1)} %get-tuple-element.24), channel_id=1, source_target_pairs={{0,1},{2,3},{4,5},{6,7},{8,9},{10,11},{12,13},{14,15},{1,0},{3,2},... | collective-permute-start | bytes 786440 | tf_op jit(solution)/shard_map/ppermute | solution.py:294
  21.6 0.7 copy-start.3
  30.5 27.3 %all-to-all-start = ((f32[64,16,128]{2,1,0:T(8,128)}), f32[64,16,128]{2,1,0:T(8,128)S(1)}, u32[]{:S(2)}, u32[]{:S(2)}) async-start(f32[64,16,128]{2,1,0:T(8,128)} %bitcast.3), calls=%async_computation | async-start | bytes 1048576 | tf_op jit(solution)/shard_map/all_to_all | solution.py:342
  46.7 18.3 %collective-permute-start.4 = (f32[2,256,128]{2,1,0:T(8,128)S(1)}, f32[2,256,128]{2,1,0:T(8,128)S(1)}, u32[]{:S(2)}, u32[]{:S(2)}) collective-permute-start(f32[2,256,128]{2,1,0:T(8,128)S(1)} %get-tuple-element.30), channel_id=1, source_target_pairs={{1,2},{3,4},{5,6},{7,8},{9,10},{11,12},{13,14},{2,1},{4,3},{6,5},{... | collective-permute-start | bytes 786440 | tf_op jit(solution)/shard_map/ppermute | solution.py:292
  51.7 13.3 %collective-permute-start.5 = (f32[2,256,128]{2,1,0:T(8,128)S(1)}, f32[2,256,128]{2,1,0:T(8,128)S(1)}, u32[]{:S(2)}, u32[]{:S(2)}) collective-permute-start(f32[2,256,128]{2,1,0:T(8,128)S(1)} %get-tuple-element.31), channel_id=1, source_target_pairs={{0,1},{2,3},{4,5},{6,7},{8,9},{10,11},{12,13},{14,15},{1,0},{3,2},... | collective-permute-start | bytes 786440 | tf_op jit(solution)/shard_map/ppermute | solution.py:294
  58.5 19.4 %all-to-all-start.1 = ((f32[8,16,128]{2,1,0:T(8,128)}), f32[8,16,128]{2,1,0:T(8,128)S(1)}, u32[]{:S(2)}, u32[]{:S(2)}) async-start(f32[8,16,128]{2,1,0:T(8,128)} %shard_map.84), calls=%async_computation.1 | async-start | bytes 131072 | tf_op jit(solution)/shard_map/all_to_all | solution.py:347
  65.2 19.8 %collective-permute-start.6 = (f32[4,64,128]{2,1,0:T(8,128)S(1)}, f32[4,64,128]{2,1,0:T(8,128)S(1)}, u32[]{:S(2)}, u32[]{:S(2)}) collective-permute-start(f32[4,64,128]{2,1,0:T(8,128)S(1)} %get-tuple-element.33), channel_id=1, source_target_pairs={{16,32},{48,64},{80,96},{112,128},{144,160},{176,192},{208,224},{2... | collective-permute-start | bytes 393224 | tf_op jit(solution)/shard_map/ppermute | solution.py:292
  65.9 19.2 %collective-permute-start.7 = (f32[4,64,128]{2,1,0:T(8,128)S(1)}, f32[4,64,128]{2,1,0:T(8,128)S(1)}, u32[]{:S(2)}, u32[]{:S(2)}) collective-permute-start(f32[4,64,128]{2,1,0:T(8,128)S(1)} %get-tuple-element.34), channel_id=1, source_target_pairs={{0,16},{32,48},{64,80},{96,112},{128,144},{160,176},{192,208},{224... | collective-permute-start | bytes 393224 | tf_op jit(solution)/shard_map/ppermute | solution.py:294
  78.7 18.1 %all-to-all-start.2 = ((f32[64,16,128]{2,1,0:T(8,128)}), f32[64,16,128]{2,1,0:T(8,128)S(1)}, u32[]{:S(2)}, u32[]{:S(2)}) async-start(f32[64,16,128]{2,1,0:T(8,128)} %shard_map.85), calls=%async_computation.2 | async-start | bytes 1048576 | tf_op jit(solution)/shard_map/all_to_all | solution.py:355

commit v10 on v9

--- a/solution.py
+++ b/solution.py
@@ -68,12 +68,6 @@
     low = low_lanes(from_left.shape)
     real = jnp.where(low, from_right, from_left)
     return real, pltpu.roll(jnp.where(low, from_left, from_right), HALF, 1)
-
-
-def rows_kernel(tile, cross, mate):
-    even = even_row()
-    for p in range(4):
-        mate[p], cross[p] = by_parity(even, tile[p, HALF:], tile[p, :HALF])
 
 
 def columns_kernel(tile, from_cross, from_mate, tall, cross, mate):
@@ -275,13 +269,12 @@
         result[p, HALF:] = part[p, HALF:] + below
 
 
-def finish_kernel(result, gathered, result_far, probe_far, sems):
-    moves = [pltpu.make_async_copy(result.at[p], result_far.at[p], sems.at[p]) for p in range(4)]
+def finish_kernel(gathered, probe_far, sems):
+    moves = []
     for i in range(4):
         part = pl.ds(256 * i, 256)
-        moves.append(pltpu.make_async_copy(gathered.at[part], probe_far.at[part], sems.at[4 + i]))
-    for move in moves:
-        move.start()
+        moves.append(pltpu.make_async_copy(gathered.at[part], probe_far.at[part], sems.at[i]))
+        moves[i].start()
     for move in moves:
         move.wait()
 
@@ -304,7 +297,10 @@
     planes, strip, half = f32(4, TILE, TILE), f32(2, TILE, TILE), f32(4, HALF, TILE)
     tall, tall_strip = f32(4, 2 * TILE, TILE), f32(2, 2 * TILE, TILE)
 
-    rims = exchange(*call(rows_kernel, (half, half), [VM], tile), ROW_AXES)
+    upper = jnp.where(even_row(), 0, HALF)
+    cross = lax.dynamic_slice_in_dim(tile, upper, HALF, axis=1)
+    mate = lax.dynamic_slice_in_dim(tile, HALF - upper, HALF, axis=1)
+    rims = exchange(cross, mate, ROW_AXES)
     object_tall, cross, mate = call(
         columns_kernel, (tall, tall_strip, tall_strip), [VM] * 3, tile, *rims
     )
@@ -340,9 +336,7 @@
     far = lax.axis_size(FAR_AXES)
     rows = 8 * TILE // near
     shares = lax.all_to_all(probe_part.reshape(near, rows, TILE), NEAR_AXES, 0, 0, tiled=True)
-    (spread_share,) = call(
-        functools.partial(spread_sum, 1.0), (f32(far, rows, TILE),), [VM], shares
-    )
+    spread_share = jnp.broadcast_to(jnp.sum(shares, axis=0)[None], (far, rows, TILE))
     strips = exchange(cross, mate, COL_AXES)
     shares = lax.all_to_all(spread_share, FAR_AXES, 0, 0, tiled=True)
     part, cross, mate = call(
@@ -356,10 +350,9 @@
     (result,) = call(
         fold_rows_kernel, (planes,), [VM] * 3, part, *rims, flops=BESIDE, moved=1
     )
-    result, probe_grad = call(
-        finish_kernel, (planes, f32(8 * TILE, TILE)), [VM] * 2,
-        result, gathered.reshape(8 * TILE, TILE),
-        scratch=[pltpu.SemaphoreType.DMA((8,))], out_specs=[FAR, FAR],
+    (probe_grad,) = call(
+        finish_kernel, (f32(8 * TILE, TILE),), [VM], gathered.reshape(8 * TILE, TILE),
+        scratch=[pltpu.SemaphoreType.DMA((4,))], out_specs=[FAR],
     )
     return result.reshape(object_field.shape), probe_grad.reshape(probe_modes.shape)
 

time: 98.4 us -> 99 us (level)
    ppermute x4, starting transfers between devices: 17 us -> 15 us  [exchange(): from_mate = lax.ppermute(mate, axes, pairs + [(b, a) for a, b in pairs])]
    ppermute x4, waiting for transfers between devices: 2.24 us -> 3.99 us  [exchange(): from_cross = lax.ppermute(cross, axes, pairs + [(b, a) for a, b in pairs])]
    all_to_all x1, starting transfers between devices: 6.53 us -> 7.73 us  [body(): shares = lax.all_to_all(spread_share, FAR_AXES, 0, 0, tiled=True)]
    dynamic_slice x0 -> x1, local copies, waits for them, and re-layouts: none -> 1.06 us  [body(): mate = lax.dynamic_slice_in_dim(tile, HALF - upper, HALF, axis=1)]
    pallas_call x10 -> x8, Pallas kernels: 9.66 us -> 9.53 us  [call(): pl.pallas_call(kernel, out_shape=out_shape, in_specs=in_specs, out_specs=...]
  transfers between devices with their start and end apart: 11 -> 11, of which waited for: 5 -> 5; matrix products, arithmetic and copies ran while one was open for 0% -> 1% of each run, Pallas kernels for 3% -> 3%
where the time goes in v10:
time: 99 us; the launch traced here: 98.4 us
  starting transfers between devices  57.9 us (58%)
  waiting for transfers between devices  27 us (27%)
  Pallas kernels  9.53 us (10%)
  local copies, waits for them, and re-layouts  2.48 us (3%)
  between operations  1.48 us (1%)
    all_to_all x1, starting transfers between devices, body(): lax.all_to_all(probe_part.reshape(near, rows, TILE), NEAR_AXES, 0, 0, til...  15.7 us
    ppermute x4, starting transfers between devices, exchange(): from_mate = lax.ppermute(mate, axes, pairs + [(b, a) for a, b in pairs])  15 us
    ppermute x4, starting transfers between devices, exchange(): from_cross = lax.ppermute(cross, axes, pairs + [(b, a) for a, b in pairs])  13.1 us
    all_to_all x1, waiting for transfers between devices, body(): gathered = lax.all_to_all(spread_share, NEAR_AXES, 0, 0, tiled=True)  11.1 us
    pallas_call x8, Pallas kernels, call(): pl.pallas_call(kernel, out_shape=out_shape, in_specs=in_specs, out_specs=...  9.53 us
    all_to_all x1, starting transfers between devices, body(): shares = lax.all_to_all(spread_share, FAR_AXES, 0, 0, tiled=True)  7.73 us
    all_to_all x1, waiting for transfers between devices, body(): shares = lax.all_to_all(spread_share, FAR_AXES, 0, 0, tiled=True)  6.26 us
    all_to_all x1, starting transfers between devices, body(): gathered = lax.all_to_all(spread_share, NEAR_AXES, 0, 0, tiled=True)  6.24 us
  transfers between devices with their start and end apart: 11, of which 5 were waited for; matrix products, arithmetic and copies ran while one was open for 1% of the time, Pallas kernels for 3%

profile of v10, /device:TPU:1, one launch (start us, length us, event | category | flops | bytes accessed | tf_op | source)
XLA Modules:
  0.0 98.4 jit_solution(10976649321870502281)
XLA Ops:
  0.7 1.1 %constant_dynamic-slice_fusion = (f32[4,64,128]{2,1,0:T(8,128)S(1)}, f32[4,64,128]{2,1,0:T(8,128)S(1)}) fusion(f32[4,128,128]{2,1,0:T(8,128)} %bitcast.8, s32[]{:T(128)S(6)} %select_n.9, s32[]{:T(128)S(6)} %select_n.8), kind=kLoop, calls=%fused_computation | loop fusion | bytes 524296 | tf_op jit(solution)/shard_map/dynamic_slice | solution.py:302
  1.7 4.4 %collective-permute-start.1 = (f32[4,64,128]{2,1,0:T(8,128)S(1)}, f32[4,64,128]{2,1,0:T(8,128)S(1)}, u32[]{:S(2)}, u32[]{:S(2)}) collective-permute-start(f32[4,64,128]{2,1,0:T(8,128)S(1)} %get-tuple-element.30), channel_id=1, source_target_pairs={{0,16},{32,48},{64,80},{96,112},{128,144},{160,176},{192,208},{224... | collective-permute-start | bytes 393224 | tf_op jit(solution)/shard_map/ppermute | solution.py:287
  6.1 0.8 collective-permute-start
  6.9 1.5 %collective-permute-done.1.from_mate = f32[4,64,128]{2,1,0:T(8,128)S(1)} collective-permute-done((f32[4,64,128]{2,1,0:T(8,128)S(1)}, f32[4,64,128]{2,1,0:T(8,128)S(1)}, u32[]{:S(2)}, u32[]{:S(2)}) %collective-permute-start.1) | collective-permute-done | bytes 131104 | tf_op jit(solution)/shard_map/ppermute | solution.py:287
  8.6 6.6 %collective-permute-start.2 = (f32[2,256,128]{2,1,0:T(8,128)S(1)}, f32[2,256,128]{2,1,0:T(8,128)S(1)}, u32[]{:S(2)}, u32[]{:S(2)}) collective-permute-start(f32[2,256,128]{2,1,0:T(8,128)S(1)} %get-tuple-element.17), channel_id=1, source_target_pairs={{1,2},{3,4},{5,6},{7,8},{9,10},{11,12},{13,14},{2,1},{4,3},{6,5},{... | collective-permute-start | bytes 786440 | tf_op jit(solution)/shard_map/ppermute | solution.py:285
  15.3 3.0 %collective-permute-start.3 = (f32[2,256,128]{2,1,0:T(8,128)S(1)}, f32[2,256,128]{2,1,0:T(8,128)S(1)}, u32[]{:S(2)}, u32[]{:S(2)}) collective-permute-start(f32[2,256,128]{2,1,0:T(8,128)S(1)} %get-tuple-element.18), channel_id=1, source_target_pairs={{0,1},{2,3},{4,5},{6,7},{8,9},{10,11},{12,13},{14,15},{1,0},{3,2},... | collective-permute-start | bytes 786440 | tf_op jit(solution)/shard_map/ppermute | solution.py:287
  19.0 0.7 copy-done.3
  20.0 4.0 %collective-permute-done.2.from_cross = f32[2,256,128]{2,1,0:T(8,128)S(1)} collective-permute-done((f32[2,256,128]{2,1,0:T(8,128)S(1)}, f32[2,256,128]{2,1,0:T(8,128)S(1)}, u32[]{:S(2)}, u32[]{:S(2)}) %collective-permute-start.2) | collective-permute-done | bytes 262176 | tf_op jit(solution)/shard_map/ppermute | solution.py:285
  24.0 5.6 %shard_map.79 = (f32[8,128,128]{2,1,0:T(8,128)}, f32[2,4,128,128]{3,2,1,0:T(8,128)S(1)}) custom-call(s32[4]{0:T(128)S(1)} %reshape.30.offsets, s32[1,1]{1,0:T(1,128)S(6)} %copy.8.counts, f32[4,256,128]{2,1,0:T(8,128)S(1)} %get-tuple-element.16.tall, f32[2,256,128]{2,1,0:T(8,128)S(1)} %collective-permute-done.2.from_cross, ...), custom_call_target="tpu_custom_call" | custom-call | flops 3200000000 | bytes 4000000 | tf_op jit(solution)/shard_map/pallas_call | solution.py:29
  29.6 15.7 %all-to-all-start = ((f32[64,16,128]{2,1,0:T(8,128)}), f32[64,16,128]{2,1,0:T(8,128)S(1)}, u32[]{:S(2)}, u32[]{:S(2)}) async-start(f32[64,16,128]{2,1,0:T(8,128)} %bitcast.4), calls=%async_computation | async-start | bytes 1048576 | tf_op jit(solution)/shard_map/all_to_all | solution.py:338
  45.3 0.9 shard_map.80
  46.2 5.0 %collective-permute-start.4 = (f32[2,256,128]{2,1,0:T(8,128)S(1)}, f32[2,256,128]{2,1,0:T(8,128)S(1)}, u32[]{:S(2)}, u32[]{:S(2)}) collective-permute-start(f32[2,256,128]{2,1,0:T(8,128)S(1)} %get-tuple-element.24), channel_id=1, source_target_pairs={{1,2},{3,4},{5,6},{7,8},{9,10},{11,12},{13,14},{2,1},{4,3},{6,5},{... | collective-permute-start | bytes 786440 | tf_op jit(solution)/shard_map/ppermute | solution.py:285
  51.3 1.9 %collective-permute-start.5 = (f32[2,256,128]{2,1,0:T(8,128)S(1)}, f32[2,256,128]{2,1,0:T(8,128)S(1)}, u32[]{:S(2)}, u32[]{:S(2)}) collective-permute-start(f32[2,256,128]{2,1,0:T(8,128)S(1)} %get-tuple-element.25), channel_id=1, source_target_pairs={{0,1},{2,3},{4,5},{6,7},{8,9},{10,11},{12,13},{14,15},{1,0},{3,2},... | collective-permute-start | bytes 786440 | tf_op jit(solution)/shard_map/ppermute | solution.py:287
  53.2 4.1 %all-to-all-done = f32[64,16,128]{2,1,0:T(8,128)S(1)} async-done(((f32[64,16,128]{2,1,0:T(8,128)}), f32[64,16,128]{2,1,0:T(8,128)S(1)}, u32[]{:S(2)}, u32[]{:S(2)}) %all-to-all-start) | async-done | bytes 524320 | tf_op jit(solution)/shard_map/all_to_all | solution.py:338
  57.4 0.6 broadcast_in_dim.2
  58.0 7.7 %all-to-all-start.1 = ((f32[8,16,128]{2,1,0:T(8,128)}), f32[8,16,128]{2,1,0:T(8,128)S(1)}, u32[]{:S(2)}, u32[]{:S(2)}) async-start(f32[8,16,128]{2,1,0:T(8,128)} %broadcast_in_dim.2), calls=%async_computation.1 | async-start | bytes 131072 | tf_op jit(solution)/shard_map/all_to_all | solution.py:341
  65.9 0.7 collective-permute-start.6
  66.6 5.8 %collective-permute-start.7 = (f32[4,64,128]{2,1,0:T(8,128)S(1)}, f32[4,64,128]{2,1,0:T(8,128)S(1)}, u32[]{:S(2)}, u32[]{:S(2)}) collective-permute-start(f32[4,64,128]{2,1,0:T(8,128)S(1)} %get-tuple-element.28), channel_id=1, source_target_pairs={{0,16},{32,48},{64,80},{96,112},{128,144},{160,176},{192,208},{224... | collective-permute-start | bytes 393224 | tf_op jit(solution)/shard_map/ppermute | solution.py:287
  72.4 6.3 %all-to-all-done.1.shares = f32[8,16,128]{2,1,0:T(8,128)S(1)} async-done(((f32[8,16,128]{2,1,0:T(8,128)}), f32[8,16,128]{2,1,0:T(8,128)S(1)}, u32[]{:S(2)}, u32[]{:S(2)}) %all-to-all-start.1) | async-done | bytes 65568 | tf_op jit(solution)/shard_map/all_to_all | solution.py:341
  78.6 0.8 shard_map.83
  79.5 6.2 %all-to-all-start.2 = ((f32[64,16,128]{2,1,0:T(8,128)}), f32[64,16,128]{2,1,0:T(8,128)S(1)}, u32[]{:S(2)}, u32[]{:S(2)}) async-start(f32[64,16,128]{2,1,0:T(8,128)} %shard_map.83), calls=%async_computation.2 | async-start | bytes 1048576 | tf_op jit(solution)/shard_map/all_to_all | solution.py:349
  85.7 0.7 shard_map.82
  86.5 11.1 %all-to-all-done.2 = f32[64,16,128]{2,1,0:T(8,128)S(1)} async-done(((f32[64,16,128]{2,1,0:T(8,128)}), f32[64,16,128]{2,1,0:T(8,128)S(1)}, u32[]{:S(2)}, u32[]{:S(2)}) %all-to-all-start.2) | async-done | bytes 524320 | tf_op jit(solution)/shard_map/all_to_all | solution.py:349
  97.6 0.8 shard_map.84
  (20 shorter events, 0.8 us)
Async XLA Ops:
  0.6 7.8 %copy-start = (f32[2,2,128,128]{3,2,1,0:T(8,128)S(1)}, f32[2,2,128,128]{3,2,1,0:T(8,128)}, u32[]{:S(2)}) copy-start(f32[2,2,128,128]{3,2,1,0:T(8,128)} %param.6) | copy-start | bytes 786436
  0.6 18.3 %copy-start.1 = (f32[2,4,128,128]{3,2,1,0:T(8,128)S(1)}, f32[2,4,128,128]{3,2,1,0:T(8,128)}, u32[]{:S(2)}) copy-start(f32[2,4,128,128]{3,2,1,0:T(8,128)} %param.7) | copy-start | bytes 1572868
  1.7 6.7 %collective-permute-start.1 = (f32[4,64,128]{2,1,0:T(8,128)S(1)}, f32[4,64,128]{2,1,0:T(8,128)S(1)}, u32[]{:S(2)}, u32[]{:S(2)}) collective-permute-start(f32[4,64,128]{2,1,0:T(8,128)S(1)} %get-tuple-element.30), channel_id=1, source_target_pairs={{0,16},{32,48},{64,80},{96,112},{128,144},{160,176},{192,208},{224... | collective-permute-start | bytes 393224 | tf_op jit(solution)/shard_map/ppermute | solution.py:287
  6.1 12.9 %copy-start.2 = (f32[1,1,2,128,128]{4,3,2,1,0:T(8,128)S(1)}, f32[1,1,2,128,128]{4,3,2,1,0:T(8,128)}, u32[]{:S(2)}) copy-start(f32[1,1,2,128,128]{4,3,2,1,0:T(8,128)} %param.9) | copy-start | bytes 393220
  6.1 2.3 %collective-permute-start = (f32[4,64,128]{2,1,0:T(8,128)S(1)}, f32[4,64,128]{2,1,0:T(8,128)S(1)}, u32[]{:S(2)}, u32[]{:S(2)}) collective-permute-start(f32[4,64,128]{2,1,0:T(8,128)S(1)} %get-tuple-element.31), channel_id=1, source_target_pairs={{16,32},{48,64},{80,96},{112,128},{144,160},{176,192},{208,224},{2... | collective-permute-start | bytes 393224 | tf_op jit(solution)/shard_map/ppermute | solution.py:285
  8.6 15.4 %collective-permute-start.2 = (f32[2,256,128]{2,1,0:T(8,128)S(1)}, f32[2,256,128]{2,1,0:T(8,128)S(1)}, u32[]{:S(2)}, u32[]{:S(2)}) collective-permute-start(f32[2,256,128]{2,1,0:T(8,128)S(1)} %get-tuple-element.17), channel_id=1, source_target_pairs={{1,2},{3,4},{5,6},{7,8},{9,10},{11,12},{13,14},{2,1},{4,3},{6,5},{... | collective-permute-start | bytes 786440 | tf_op jit(solution)/shard_map/ppermute | solution.py:285
  15.2 3.6 %copy-start.4 = (s32[1,1,2,2]{3,2,1,0:T(2,128)S(1)}, s32[1,1,2,2]{3,2,1,0:T(2,128)}, u32[]{:S(2)}) copy-start(s32[1,1,2,2]{3,2,1,0:T(2,128)} %param.10) | copy-start | bytes 52
  15.3 8.7 %collective-permute-start.3 = (f32[2,256,128]{2,1,0:T(8,128)S(1)}, f32[2,256,128]{2,1,0:T(8,128)S(1)}, u32[]{:S(2)}, u32[]{:S(2)}) collective-permute-start(f32[2,256,128]{2,1,0:T(8,128)S(1)} %get-tuple-element.18), channel_id=1, source_target_pairs={{0,1},{2,3},{4,5},{6,7},{8,9},{10,11},{12,13},{14,15},{1,0},{3,2},... | collective-permute-start | bytes 786440 | tf_op jit(solution)/shard_map/ppermute | solution.py:287
  19.0 0.7 copy-start.3
  29.6 27.7 %all-to-all-start = ((f32[64,16,128]{2,1,0:T(8,128)}), f32[64,16,128]{2,1,0:T(8,128)S(1)}, u32[]{:S(2)}, u32[]{:S(2)}) async-start(f32[64,16,128]{2,1,0:T(8,128)} %bitcast.4), calls=%async_computation | async-start | bytes 1048576 | tf_op jit(solution)/shard_map/all_to_all | solution.py:338
  46.2 19.5 %collective-permute-start.4 = (f32[2,256,128]{2,1,0:T(8,128)S(1)}, f32[2,256,128]{2,1,0:T(8,128)S(1)}, u32[]{:S(2)}, u32[]{:S(2)}) collective-permute-start(f32[2,256,128]{2,1,0:T(8,128)S(1)} %get-tuple-element.24), channel_id=1, source_target_pairs={{1,2},{3,4},{5,6},{7,8},{9,10},{11,12},{13,14},{2,1},{4,3},{6,5},{... | collective-permute-start | bytes 786440 | tf_op jit(solution)/shard_map/ppermute | solution.py:285
  51.3 14.5 %collective-permute-start.5 = (f32[2,256,128]{2,1,0:T(8,128)S(1)}, f32[2,256,128]{2,1,0:T(8,128)S(1)}, u32[]{:S(2)}, u32[]{:S(2)}) collective-permute-start(f32[2,256,128]{2,1,0:T(8,128)S(1)} %get-tuple-element.25), channel_id=1, source_target_pairs={{0,1},{2,3},{4,5},{6,7},{8,9},{10,11},{12,13},{14,15},{1,0},{3,2},... | collective-permute-start | bytes 786440 | tf_op jit(solution)/shard_map/ppermute | solution.py:287
  58.0 20.6 %all-to-all-start.1 = ((f32[8,16,128]{2,1,0:T(8,128)}), f32[8,16,128]{2,1,0:T(8,128)S(1)}, u32[]{:S(2)}, u32[]{:S(2)}) async-start(f32[8,16,128]{2,1,0:T(8,128)} %broadcast_in_dim.2), calls=%async_computation.1 | async-start | bytes 131072 | tf_op jit(solution)/shard_map/all_to_all | solution.py:341
  65.9 19.8 %collective-permute-start.6 = (f32[4,64,128]{2,1,0:T(8,128)S(1)}, f32[4,64,128]{2,1,0:T(8,128)S(1)}, u32[]{:S(2)}, u32[]{:S(2)}) collective-permute-start(f32[4,64,128]{2,1,0:T(8,128)S(1)} %get-tuple-element.27), channel_id=1, source_target_pairs={{16,32},{48,64},{80,96},{112,128},{144,160},{176,192},{208,224},{2... | collective-permute-start | bytes 393224 | tf_op jit(solution)/shard_map/ppermute | solution.py:285
  66.6 19.2 %collective-permute-start.7 = (f32[4,64,128]{2,1,0:T(8,128)S(1)}, f32[4,64,128]{2,1,0:T(8,128)S(1)}, u32[]{:S(2)}, u32[]{:S(2)}) collective-permute-start(f32[4,64,128]{2,1,0:T(8,128)S(1)} %get-tuple-element.28), channel_id=1, source_target_pairs={{0,16},{32,48},{64,80},{96,112},{128,144},{160,176},{192,208},{224... | collective-permute-start | bytes 393224 | tf_op jit(solution)/shard_map/ppermute | solution.py:287
  79.5 18.1 %all-to-all-start.2 = ((f32[64,16,128]{2,1,0:T(8,128)}), f32[64,16,128]{2,1,0:T(8,128)S(1)}, u32[]{:S(2)}, u32[]{:S(2)}) async-start(f32[64,16,128]{2,1,0:T(8,128)} %shard_map.83), calls=%async_computation.2 | async-start | bytes 1048576 | tf_op jit(solution)/shard_map/all_to_all | solution.py:349

commit v11 on v10

--- a/solution.py
+++ b/solution.py
@@ -13,7 +13,8 @@
 BF16 = jnp.bfloat16
 ROW_AXES = ("xl", "za", "zb")
 COL_AXES = ("y", "xh", "core")
-NEAR_AXES = ("xl", "zb", "y", "xh", "core")
+NEAR_AXES = ("xl", "zb", "y", "xh")
+ALL_NEAR_AXES = ("core",) + NEAR_AXES
 FAR_AXES = ("za",)
 VMEM_LIMIT = 12 * 1024 * 1024
 TILE = 128
@@ -122,7 +123,7 @@
 
 def main_kernel(
     offsets, counts, tall, from_cross, from_mate, probe, measured, ops,
-    probe_grad, object_grad,
+    probe_keep, probe_send, object_grad,
     beside, field_high, field_low, mid_high, mid_low, wave_one, wave_two,
 ):
     even = even_column()
@@ -218,12 +219,13 @@
         add(slot, 0, m, pr * hr + pi * hi, pr * hi - pi * hr)
         dr = hr * o0r + hi * o0i
         di = hi * o0r - hr * o0i
+        keep, send = by_parity(even, dr, di)
         if slot == 0:
-            probe_grad[m] = dr
-            probe_grad[4 + m] = di
+            probe_keep[m] = keep
+            probe_send[m] = send
         else:
-            probe_grad[m] += dr
-            probe_grad[4 + m] += di
+            probe_keep[m] += keep
+            probe_send[m] += send
 
     propagate(2, after_fourth)
 
@@ -288,6 +290,10 @@
     return from_cross, from_mate
 
 
+def swap_cores(value):
+    return lax.ppermute(value, "core", [(0, 1), (1, 0)])
+
+
 def f32(*shape):
     return jax.ShapeDtypeStruct(shape, F32)
 
@@ -311,9 +317,9 @@
         prop_taps, probe_modes.reshape(8, TILE, TILE), measured.reshape(2, TILE, TILE),
         scratch=[pltpu.VMEM((8, 2 * TILE), F32)],
     )
-    probe_part, object_grad = call(
+    probe_keep, probe_send, object_grad = call(
         main_kernel,
-        (f32(8, TILE, TILE), f32(2, 4, TILE, TILE)), [SM, SM] + [VM] * 6,
+        (planes, planes, f32(2, 4, TILE, TILE)), [SM, SM] + [VM] * 6,
         offsets.reshape(-1), counts.reshape(1, 1), object_tall, *strips, probe, targets, ops,
         scratch=[
             pltpu.VMEM((4, 256, TILE), F32),
@@ -334,8 +340,9 @@
 
     near = lax.axis_size(NEAR_AXES)
     far = lax.axis_size(FAR_AXES)
-    rows = 8 * TILE // near
-    shares = lax.all_to_all(probe_part.reshape(near, rows, TILE), NEAR_AXES, 0, 0, tiled=True)
+    rows = 4 * TILE // near
+    half_sum = probe_keep + swap_cores(probe_send)
+    shares = lax.all_to_all(half_sum.reshape(near, rows, TILE), NEAR_AXES, 0, 0, tiled=True)
     spread_share = jnp.broadcast_to(jnp.sum(shares, axis=0)[None], (far, rows, TILE))
     strips = exchange(cross, mate, COL_AXES)
     shares = lax.all_to_all(spread_share, FAR_AXES, 0, 0, tiled=True)
@@ -344,9 +351,9 @@
     )
     rims = exchange(cross, mate, ROW_AXES)
     (spread_share,) = call(
-        functools.partial(spread_sum, 1.0 / math.sqrt(near * far)), (f32(near, rows, TILE),), [VM], shares
-    )
-    gathered = lax.all_to_all(spread_share, NEAR_AXES, 0, 0, tiled=True)
+        functools.partial(spread_sum, 1.0 / math.sqrt(2 * near * far)), (f32(2 * near, rows, TILE),), [VM], shares
+    )
+    gathered = lax.all_to_all(spread_share, ALL_NEAR_AXES, 0, 0, tiled=True)
     (result,) = call(
         fold_rows_kernel, (planes,), [VM] * 3, part, *rims, flops=BESIDE, moved=1
     )

time: 99 us -> 101 us (1.020)
  starting transfers between devices: 57.9 us -> 61.8 us
  waiting for transfers between devices: 27 us -> 25.1 us
    all_to_all x2, waiting for transfers between devices: 15.2 us -> 12.3 us  [the longest x1 11.8 us: body(): gathered = lax.all_to_all(spread_share, ALL_NEAR_AXES, 0, 0, tiled=True)]
    ppermute x0 -> x1, starting transfers between devices: none -> 1.92 us  [swap_cores(): return lax.ppermute(value, 'core', [(0, 1), (1, 0)])]
    all_to_all x2, starting transfers between devices: 21.9 us -> 23.5 us  [the longest x1 14.9 us: body(): lax.all_to_all(half_sum.reshape(near, rows, TILE), NEAR_AXES, 0, 0, tiled...]
    ppermute x0 -> x1, waiting for transfers between devices: none -> 1.5 us  [swap_cores(): return lax.ppermute(value, 'core', [(0, 1), (1, 0)])]
  transfers between devices with their start and end apart: 11 -> 12, of which waited for: 5 -> 6; matrix products, arithmetic and copies ran while one was open for 1% -> 1% of each run, Pallas kernels for 3% -> 3%
where the time goes in v11:
time: 101 us; the launch traced here: 100 us
  starting transfers between devices  61.8 us (61%)
  waiting for transfers between devices  25.1 us (25%)
  Pallas kernels  8.78 us (9%)
  local copies, waits for them, and re-layouts  2.48 us (2%)
  between operations  1.49 us (1%)
    ppermute x4, starting transfers between devices, exchange(): from_mate = lax.ppermute(mate, axes, pairs + [(b, a) for a, b in pairs])  15 us
    all_to_all x1, starting transfers between devices, body(): lax.all_to_all(half_sum.reshape(near, rows, TILE), NEAR_AXES, 0, 0, tiled...  14.9 us
    ppermute x4, starting transfers between devices, exchange(): from_cross = lax.ppermute(cross, axes, pairs + [(b, a) for a, b in pairs])  13.6 us
    all_to_all x1, waiting for transfers between devices, body(): gathered = lax.all_to_all(spread_share, ALL_NEAR_AXES, 0, 0, tiled=True)  11.8 us
    pallas_call x8, Pallas kernels, call(): pl.pallas_call(kernel, out_shape=out_shape, in_specs=in_specs, out_specs=...  8.78 us
    all_to_all x1, starting transfers between devices, body(): gathered = lax.all_to_all(spread_share, ALL_NEAR_AXES, 0, 0, tiled=True)  8.64 us
    all_to_all x1, starting transfers between devices, body(): shares = lax.all_to_all(spread_share, FAR_AXES, 0, 0, tiled=True)  7.72 us
    all_to_all x1, waiting for transfers between devices, body(): shares = lax.all_to_all(spread_share, FAR_AXES, 0, 0, tiled=True)  5.72 us
  transfers between devices with their start and end apart: 12, of which 6 were waited for; matrix products, arithmetic and copies ran while one was open for 1% of the time, Pallas kernels for 3%

profile of v11, /device:TPU:1, one launch (start us, length us, event | category | flops | bytes accessed | tf_op | source)
XLA Modules:
  0.0 100.4 jit_solution(11064047734669809031)
XLA Ops:
  0.7 1.1 %constant_dynamic-slice_fusion = (f32[4,64,128]{2,1,0:T(8,128)S(1)}, f32[4,64,128]{2,1,0:T(8,128)S(1)}) fusion(f32[4,128,128]{2,1,0:T(8,128)} %bitcast.8, s32[]{:T(128)S(6)} %select_n.9, s32[]{:T(128)S(6)} %select_n.8), kind=kLoop, calls=%fused_computation | loop fusion | bytes 524296 | tf_op jit(solution)/shard_map/dynamic_slice | solution.py:308
  1.7 4.4 %collective-permute-start.1 = (f32[4,64,128]{2,1,0:T(8,128)S(1)}, f32[4,64,128]{2,1,0:T(8,128)S(1)}, u32[]{:S(2)}, u32[]{:S(2)}) collective-permute-start(f32[4,64,128]{2,1,0:T(8,128)S(1)} %get-tuple-element.32), channel_id=1, source_target_pairs={{0,16},{32,48},{64,80},{96,112},{128,144},{160,176},{192,208},{224... | collective-permute-start | bytes 393224 | tf_op jit(solution)/shard_map/ppermute | solution.py:289
  6.1 0.8 collective-permute-start
  6.9 1.5 %collective-permute-done.1.from_mate = f32[4,64,128]{2,1,0:T(8,128)S(1)} collective-permute-done((f32[4,64,128]{2,1,0:T(8,128)S(1)}, f32[4,64,128]{2,1,0:T(8,128)S(1)}, u32[]{:S(2)}, u32[]{:S(2)}) %collective-permute-start.1) | collective-permute-done | bytes 131104 | tf_op jit(solution)/shard_map/ppermute | solution.py:289
  8.6 6.6 %collective-permute-start.2 = (f32[2,256,128]{2,1,0:T(8,128)S(1)}, f32[2,256,128]{2,1,0:T(8,128)S(1)}, u32[]{:S(2)}, u32[]{:S(2)}) collective-permute-start(f32[2,256,128]{2,1,0:T(8,128)S(1)} %get-tuple-element.18), channel_id=1, source_target_pairs={{1,2},{3,4},{5,6},{7,8},{9,10},{11,12},{13,14},{2,1},{4,3},{6,5},{... | collective-permute-start | bytes 786440 | tf_op jit(solution)/shard_map/ppermute | solution.py:287
  15.3 3.0 %collective-permute-start.3 = (f32[2,256,128]{2,1,0:T(8,128)S(1)}, f32[2,256,128]{2,1,0:T(8,128)S(1)}, u32[]{:S(2)}, u32[]{:S(2)}) collective-permute-start(f32[2,256,128]{2,1,0:T(8,128)S(1)} %get-tuple-element.19), channel_id=1, source_target_pairs={{0,1},{2,3},{4,5},{6,7},{8,9},{10,11},{12,13},{14,15},{1,0},{3,2},... | collective-permute-start | bytes 786440 | tf_op jit(solution)/shard_map/ppermute | solution.py:289
  19.0 0.7 copy-done.3
  20.0 4.0 %collective-permute-done.2.from_cross = f32[2,256,128]{2,1,0:T(8,128)S(1)} collective-permute-done((f32[2,256,128]{2,1,0:T(8,128)S(1)}, f32[2,256,128]{2,1,0:T(8,128)S(1)}, u32[]{:S(2)}, u32[]{:S(2)}) %collective-permute-start.2) | collective-permute-done | bytes 262176 | tf_op jit(solution)/shard_map/ppermute | solution.py:287
  24.0 4.9 %shard_map.79 = (f32[4,128,128]{2,1,0:T(8,128)S(1)}, f32[4,128,128]{2,1,0:T(8,128)S(1)}, f32[2,4,128,128]{3,2,1,0:T(8,128)S(1)}) custom-call(s32[4]{0:T(128)S(1)} %reshape.30.offsets, s32[1,1]{1,0:T(1,128)S(6)} %copy.8.counts, f32[4,256,128]{2,1,0:T(8,128)S(1)} %get-tuple-element.17.tall, f32[2,256,128]{2,1,0:T(8,128)S(1)} %collective-permute-done.2.from_cross, ...), custom_call_target="tpu_custom_call" | custom-call | flops 3200000000 | bytes 4000000 | tf_op jit(solution)/shard_map/pallas_call | solution.py:30
  28.8 1.9 %collective-permute-start.8 = (f32[4,128,128]{2,1,0:T(8,128)S(1)}, f32[4,128,128]{2,1,0:T(8,128)S(1)}, u32[]{:S(2)}, u32[]{:S(2)}) collective-permute-start(f32[4,128,128]{2,1,0:T(8,128)S(1)} %get-tuple-element.31), channel_id=1, source_target_pairs={{0,1},{1,0},{2,3},{3,2},{4,5},{5,4},{6,7},{7,6},{8,9},{9,8},{10,11... | collective-permute-start | bytes 786440 | tf_op jit(solution)/shard_map/ppermute | solution.py:294
  30.8 1.5 %collective-permute-done.8 = f32[4,128,128]{2,1,0:T(8,128)S(1)} collective-permute-done((f32[4,128,128]{2,1,0:T(8,128)S(1)}, f32[4,128,128]{2,1,0:T(8,128)S(1)}, u32[]{:S(2)}, u32[]{:S(2)}) %collective-permute-start.8) | collective-permute-done | bytes 262176 | tf_op jit(solution)/shard_map/ppermute | solution.py:294
  32.3 0.7 add.9
  33.0 14.9 %all-to-all-start = ((f32[32,16,128]{2,1,0:T(8,128)}), f32[32,16,128]{2,1,0:T(8,128)S(1)}, u32[]{:S(2)}, u32[]{:S(2)}) async-start(f32[32,16,128]{2,1,0:T(8,128)} %bitcast.4), calls=%async_computation | async-start | bytes 524288 | tf_op jit(solution)/shard_map/all_to_all | solution.py:345
  47.9 0.9 shard_map.80
  48.9 5.5 %collective-permute-start.4 = (f32[2,256,128]{2,1,0:T(8,128)S(1)}, f32[2,256,128]{2,1,0:T(8,128)S(1)}, u32[]{:S(2)}, u32[]{:S(2)}) collective-permute-start(f32[2,256,128]{2,1,0:T(8,128)S(1)} %get-tuple-element.25), channel_id=1, source_target_pairs={{1,2},{3,4},{5,6},{7,8},{9,10},{11,12},{13,14},{2,1},{4,3},{6,5},{... | collective-permute-start | bytes 786440 | tf_op jit(solution)/shard_map/ppermute | solution.py:287
  54.3 1.9 %collective-permute-start.5 = (f32[2,256,128]{2,1,0:T(8,128)S(1)}, f32[2,256,128]{2,1,0:T(8,128)S(1)}, u32[]{:S(2)}, u32[]{:S(2)}) collective-permute-start(f32[2,256,128]{2,1,0:T(8,128)S(1)} %get-tuple-element.26), channel_id=1, source_target_pairs={{0,1},{2,3},{4,5},{6,7},{8,9},{10,11},{12,13},{14,15},{1,0},{3,2},... | collective-permute-start | bytes 786440 | tf_op jit(solution)/shard_map/ppermute | solution.py:289
  57.4 7.7 %all-to-all-start.1 = ((f32[8,16,128]{2,1,0:T(8,128)}), f32[8,16,128]{2,1,0:T(8,128)S(1)}, u32[]{:S(2)}, u32[]{:S(2)}) async-start(f32[8,16,128]{2,1,0:T(8,128)} %broadcast_in_dim.2), calls=%async_computation.1 | async-start | bytes 131072 | tf_op jit(solution)/shard_map/all_to_all | solution.py:348
  66.0 5.8 %collective-permute-start.7 = (f32[4,64,128]{2,1,0:T(8,128)S(1)}, f32[4,64,128]{2,1,0:T(8,128)S(1)}, u32[]{:S(2)}, u32[]{:S(2)}) collective-permute-start(f32[4,64,128]{2,1,0:T(8,128)S(1)} %get-tuple-element.29), channel_id=1, source_target_pairs={{0,16},{32,48},{64,80},{96,112},{128,144},{160,176},{192,208},{224... | collective-permute-start | bytes 393224 | tf_op jit(solution)/shard_map/ppermute | solution.py:289
  71.8 5.7 %all-to-all-done.1.shares = f32[8,16,128]{2,1,0:T(8,128)S(1)} async-done(((f32[8,16,128]{2,1,0:T(8,128)}), f32[8,16,128]{2,1,0:T(8,128)S(1)}, u32[]{:S(2)}, u32[]{:S(2)}) %all-to-all-start.1) | async-done | bytes 65568 | tf_op jit(solution)/shard_map/all_to_all | solution.py:348
  77.5 0.8 shard_map.83
  78.4 8.6 %all-to-all-start.2 = ((f32[64,16,128]{2,1,0:T(8,128)}), f32[64,16,128]{2,1,0:T(8,128)S(1)}, u32[]{:S(2)}, u32[]{:S(2)}) async-start(f32[64,16,128]{2,1,0:T(8,128)} %shard_map.83), calls=%async_computation.2 | async-start | bytes 1048576 | tf_op jit(solution)/shard_map/all_to_all | solution.py:356
  87.0 0.7 shard_map.82
  87.8 11.8 %all-to-all-done.2 = f32[64,16,128]{2,1,0:T(8,128)S(1)} async-done(((f32[64,16,128]{2,1,0:T(8,128)}), f32[64,16,128]{2,1,0:T(8,128)S(1)}, u32[]{:S(2)}, u32[]{:S(2)}) %all-to-all-start.2) | async-done | bytes 524320 | tf_op jit(solution)/shard_map/all_to_all | solution.py:356
  99.6 0.8 shard_map.84
  (23 shorter events, 2.6 us)
Async XLA Ops:
  0.6 7.8 %copy-start = (f32[2,2,128,128]{3,2,1,0:T(8,128)S(1)}, f32[2,2,128,128]{3,2,1,0:T(8,128)}, u32[]{:S(2)}) copy-start(f32[2,2,128,128]{3,2,1,0:T(8,128)} %param.6) | copy-start | bytes 786436
  0.6 18.3 %copy-start.1 = (f32[2,4,128,128]{3,2,1,0:T(8,128)S(1)}, f32[2,4,128,128]{3,2,1,0:T(8,128)}, u32[]{:S(2)}) copy-start(f32[2,4,128,128]{3,2,1,0:T(8,128)} %param.7) | copy-start | bytes 1572868
  1.7 6.7 %collective-permute-start.1 = (f32[4,64,128]{2,1,0:T(8,128)S(1)}, f32[4,64,128]{2,1,0:T(8,128)S(1)}, u32[]{:S(2)}, u32[]{:S(2)}) collective-permute-start(f32[4,64,128]{2,1,0:T(8,128)S(1)} %get-tuple-element.32), channel_id=1, source_target_pairs={{0,16},{32,48},{64,80},{96,112},{128,144},{160,176},{192,208},{224... | collective-permute-start | bytes 393224 | tf_op jit(solution)/shard_map/ppermute | solution.py:289
  6.1 12.9 %copy-start.2 = (f32[1,1,2,128,128]{4,3,2,1,0:T(8,128)S(1)}, f32[1,1,2,128,128]{4,3,2,1,0:T(8,128)}, u32[]{:S(2)}) copy-start(f32[1,1,2,128,128]{4,3,2,1,0:T(8,128)} %param.9) | copy-start | bytes 393220
  6.1 2.3 %collective-permute-start = (f32[4,64,128]{2,1,0:T(8,128)S(1)}, f32[4,64,128]{2,1,0:T(8,128)S(1)}, u32[]{:S(2)}, u32[]{:S(2)}) collective-permute-start(f32[4,64,128]{2,1,0:T(8,128)S(1)} %get-tuple-element.33), channel_id=1, source_target_pairs={{16,32},{48,64},{80,96},{112,128},{144,160},{176,192},{208,224},{2... | collective-permute-start | bytes 393224 | tf_op jit(solution)/shard_map/ppermute | solution.py:287
  8.6 15.4 %collective-permute-start.2 = (f32[2,256,128]{2,1,0:T(8,128)S(1)}, f32[2,256,128]{2,1,0:T(8,128)S(1)}, u32[]{:S(2)}, u32[]{:S(2)}) collective-permute-start(f32[2,256,128]{2,1,0:T(8,128)S(1)} %get-tuple-element.18), channel_id=1, source_target_pairs={{1,2},{3,4},{5,6},{7,8},{9,10},{11,12},{13,14},{2,1},{4,3},{6,5},{... | collective-permute-start | bytes 786440 | tf_op jit(solution)/shard_map/ppermute | solution.py:287
  15.2 3.6 %copy-start.4 = (s32[1,1,2,2]{3,2,1,0:T(2,128)S(1)}, s32[1,1,2,2]{3,2,1,0:T(2,128)}, u32[]{:S(2)}) copy-start(s32[1,1,2,2]{3,2,1,0:T(2,128)} %param.10) | copy-start | bytes 52
  15.3 8.7 %collective-permute-start.3 = (f32[2,256,128]{2,1,0:T(8,128)S(1)}, f32[2,256,128]{2,1,0:T(8,128)S(1)}, u32[]{:S(2)}, u32[]{:S(2)}) collective-permute-start(f32[2,256,128]{2,1,0:T(8,128)S(1)} %get-tuple-element.19), channel_id=1, source_target_pairs={{0,1},{2,3},{4,5},{6,7},{8,9},{10,11},{12,13},{14,15},{1,0},{3,2},... | collective-permute-start | bytes 786440 | tf_op jit(solution)/shard_map/ppermute | solution.py:289
  19.0 0.7 copy-start.3
  28.8 3.4 %collective-permute-start.8 = (f32[4,128,128]{2,1,0:T(8,128)S(1)}, f32[4,128,128]{2,1,0:T(8,128)S(1)}, u32[]{:S(2)}, u32[]{:S(2)}) collective-permute-start(f32[4,128,128]{2,1,0:T(8,128)S(1)} %get-tuple-element.31), channel_id=1, source_target_pairs={{0,1},{1,0},{2,3},{3,2},{4,5},{5,4},{6,7},{7,6},{8,9},{9,8},{10,11... | collective-permute-start | bytes 786440 | tf_op jit(solution)/shard_map/ppermute | solution.py:294
  33.0 23.8 %all-to-all-start = ((f32[32,16,128]{2,1,0:T(8,128)}), f32[32,16,128]{2,1,0:T(8,128)S(1)}, u32[]{:S(2)}, u32[]{:S(2)}) async-start(f32[32,16,128]{2,1,0:T(8,128)} %bitcast.4), calls=%async_computation | async-start | bytes 524288 | tf_op jit(solution)/shard_map/all_to_all | solution.py:345
  48.9 16.3 %collective-permute-start.4 = (f32[2,256,128]{2,1,0:T(8,128)S(1)}, f32[2,256,128]{2,1,0:T(8,128)S(1)}, u32[]{:S(2)}, u32[]{:S(2)}) collective-permute-start(f32[2,256,128]{2,1,0:T(8,128)S(1)} %get-tuple-element.25), channel_id=1, source_target_pairs={{1,2},{3,4},{5,6},{7,8},{9,10},{11,12},{13,14},{2,1},{4,3},{6,5},{... | collective-permute-start | bytes 786440 | tf_op jit(solution)/shard_map/ppermute | solution.py:287
  54.3 10.8 %collective-permute-start.5 = (f32[2,256,128]{2,1,0:T(8,128)S(1)}, f32[2,256,128]{2,1,0:T(8,128)S(1)}, u32[]{:S(2)}, u32[]{:S(2)}) collective-permute-start(f32[2,256,128]{2,1,0:T(8,128)S(1)} %get-tuple-element.26), channel_id=1, source_target_pairs={{0,1},{2,3},{4,5},{6,7},{8,9},{10,11},{12,13},{14,15},{1,0},{3,2},... | collective-permute-start | bytes 786440 | tf_op jit(solution)/shard_map/ppermute | solution.py:289
  57.4 20.1 %all-to-all-start.1 = ((f32[8,16,128]{2,1,0:T(8,128)}), f32[8,16,128]{2,1,0:T(8,128)S(1)}, u32[]{:S(2)}, u32[]{:S(2)}) async-start(f32[8,16,128]{2,1,0:T(8,128)} %broadcast_in_dim.2), calls=%async_computation.1 | async-start | bytes 131072 | tf_op jit(solution)/shard_map/all_to_all | solution.py:348
  65.3 21.7 %collective-permute-start.6 = (f32[4,64,128]{2,1,0:T(8,128)S(1)}, f32[4,64,128]{2,1,0:T(8,128)S(1)}, u32[]{:S(2)}, u32[]{:S(2)}) collective-permute-start(f32[4,64,128]{2,1,0:T(8,128)S(1)} %get-tuple-element.28), channel_id=1, source_target_pairs={{16,32},{48,64},{80,96},{112,128},{144,160},{176,192},{208,224},{2... | collective-permute-start | bytes 393224 | tf_op jit(solution)/shard_map/ppermute | solution.py:287
  66.0 21.0 %collective-permute-start.7 = (f32[4,64,128]{2,1,0:T(8,128)S(1)}, f32[4,64,128]{2,1,0:T(8,128)S(1)}, u32[]{:S(2)}, u32[]{:S(2)}) collective-permute-start(f32[4,64,128]{2,1,0:T(8,128)S(1)} %get-tuple-element.29), channel_id=1, source_target_pairs={{0,16},{32,48},{64,80},{96,112},{128,144},{160,176},{192,208},{224... | collective-permute-start | bytes 393224 | tf_op jit(solution)/shard_map/ppermute | solution.py:289
  78.4 21.2 %all-to-all-start.2 = ((f32[64,16,128]{2,1,0:T(8,128)}), f32[64,16,128]{2,1,0:T(8,128)S(1)}, u32[]{:S(2)}, u32[]{:S(2)}) async-start(f32[64,16,128]{2,1,0:T(8,128)} %shard_map.83), calls=%async_computation.2 | async-start | bytes 1048576 | tf_op jit(solution)/shard_map/all_to_all | solution.py:356

commit v12 on v10

--- a/solution.py
+++ b/solution.py
@@ -70,7 +70,18 @@
     return real, pltpu.roll(jnp.where(low, from_left, from_right), HALF, 1)
 
 
-def columns_kernel(tile, from_cross, from_mate, tall, cross, mate):
+def rows_kernel(tile, cross, mate, columns):
+    even = even_row()
+    for p in range(4):
+        mate[p], cross[p] = by_parity(even, tile[p, HALF:], tile[p, :HALF])
+    even = even_column()
+    for s in range(2):
+        to_right, to_left = pack_columns(tile[s], tile[2 + s])
+        columns[s] = jnp.where(even, to_left, to_right)
+
+
+def columns_kernel(tile, from_cross, from_mate, columns, tall, cross, mate, columns_near):
+    columns_near[...] = columns[...]
     even = even_row()
     for p in range(4):
         below, above = by_parity(even, from_mate[p], from_cross[p])
@@ -80,7 +91,10 @@
     even = even_column()
     for s in range(2):
         to_right, to_left = pack_columns(tall[s], tall[2 + s])
-        mate[s], cross[s] = by_parity(even, to_right, to_left)
+        to_mate, to_cross = by_parity(even, to_right, to_left)
+        mate[s] = to_mate
+        cross[s, :HALF] = to_cross[:HALF]
+        cross[s, HALF:] = to_cross[HALF + TILE:]
 
 
 def operator_kernel(taps, probe, measured, ops, probe_near, measured_near, padded):
@@ -121,13 +135,14 @@
 
 
 def main_kernel(
-    offsets, counts, tall, from_cross, from_mate, probe, measured, ops,
-    probe_grad, object_grad,
-    beside, field_high, field_low, mid_high, mid_low, wave_one, wave_two,
+    offsets, counts, tall, columns, corners, from_mate, probe, measured, ops,
+    probe_far, object_grad,
+    probe_grad, sems, beside, field_high, field_low, mid_high, mid_low, wave_one, wave_two,
 ):
     even = even_column()
     for s in range(2):
-        from_right, from_left = by_parity(even, from_mate[s], from_cross[s])
+        from_cross = jnp.concatenate([corners[s, :HALF], columns[s], corners[s, HALF:]], axis=0)
+        from_right, from_left = by_parity(even, from_mate[s], from_cross)
         beside[s], beside[2 + s] = unpack_columns(from_left, from_right)
     object_ext = (tall, beside)
 
@@ -224,8 +239,14 @@
         else:
             probe_grad[m] += dr
             probe_grad[4 + m] += di
-
+            for part in (m, 4 + m):
+                moves.append(pltpu.make_async_copy(probe_grad.at[part], probe_far.at[part], sems.at[part]))
+                moves[-1].start()
+
+    moves = []
     propagate(2, after_fourth)
+    for move in moves:
+        move.wait()
 
 
 def object_kernel(offsets, object_grad, grad_tall, cross, mate, grad_beside):
@@ -279,13 +300,18 @@
         move.wait()
 
 
+def to_cross(value, axes):
+    pairs = [(i, i + 1) for i in range(1, lax.axis_size(axes) - 1, 2)]
+    return lax.ppermute(value, axes, pairs + [(b, a) for a, b in pairs])
+
+
+def to_mate(value, axes):
+    pairs = [(i, i + 1) for i in range(0, lax.axis_size(axes), 2)]
+    return lax.ppermute(value, axes, pairs + [(b, a) for a, b in pairs])
+
+
 def exchange(cross, mate, axes):
-    count = lax.axis_size(axes)
-    pairs = [(i, i + 1) for i in range(1, count - 1, 2)]
-    from_cross = lax.ppermute(cross, axes, pairs + [(b, a) for a, b in pairs])
-    pairs = [(i, i + 1) for i in range(0, count, 2)]
-    from_mate = lax.ppermute(mate, axes, pairs + [(b, a) for a, b in pairs])
-    return from_cross, from_mate
+    return to_cross(cross, axes), to_mate(mate, axes)
 
 
 def f32(*shape):
@@ -297,12 +323,11 @@
     planes, strip, half = f32(4, TILE, TILE), f32(2, TILE, TILE), f32(4, HALF, TILE)
     tall, tall_strip = f32(4, 2 * TILE, TILE), f32(2, 2 * TILE, TILE)
 
-    upper = jnp.where(even_row(), 0, HALF)
-    cross = lax.dynamic_slice_in_dim(tile, upper, HALF, axis=1)
-    mate = lax.dynamic_slice_in_dim(tile, HALF - upper, HALF, axis=1)
+    cross, mate, columns = call(rows_kernel, (half, half, strip), [VM], tile)
     rims = exchange(cross, mate, ROW_AXES)
-    object_tall, cross, mate = call(
-        columns_kernel, (tall, tall_strip, tall_strip), [VM] * 3, tile, *rims
+    columns = to_cross(columns, COL_AXES)
+    object_tall, cross, mate, columns = call(
+        columns_kernel, (tall, strip, tall_strip, strip), [VM] * 4, tile, *rims, columns
     )
     strips = exchange(cross, mate, COL_AXES)
     ops, probe, targets = call(
@@ -313,9 +338,12 @@
     )
     probe_part, object_grad = call(
         main_kernel,
-        (f32(8, TILE, TILE), f32(2, 4, TILE, TILE)), [SM, SM] + [VM] * 6,
-        offsets.reshape(-1), counts.reshape(1, 1), object_tall, *strips, probe, targets, ops,
+        (f32(8, TILE, TILE), f32(2, 4, TILE, TILE)), [SM, SM] + [VM] * 7,
+        offsets.reshape(-1), counts.reshape(1, 1), object_tall, columns, *strips, probe, targets, ops,
+        out_specs=[FAR, VM],
         scratch=[
+            pltpu.VMEM((8, TILE, TILE), F32),
+            pltpu.SemaphoreType.DMA((8,)),
             pltpu.VMEM((4, 256, TILE), F32),
             pltpu.VMEM((2, 256, 512), BF16),
             pltpu.VMEM((2, 256, 512), BF16),

time: 99 us -> 104 us (1.051)
  waiting for transfers between devices: 27 us -> 30 us
  starting transfers between devices: 57.9 us -> 59.4 us
    ppermute x8 -> x9, starting transfers between devices: 28.2 us -> 33.4 us  [the longest x4 16.9 us: to_mate(): return lax.ppermute(value, axes, pairs + [(b, a) for a, b in pairs])]
    ppermute x8 -> x9, waiting for transfers between devices: 5.52 us -> 8.55 us  [the longest x5 8.54 us: to_cross(): return lax.ppermute(value, axes, pairs + [(b, a) for a, b in pairs])]
    all_to_all x1, starting transfers between devices: 7.73 us -> 5.89 us  [body(): shares = lax.all_to_all(spread_share, FAR_AXES, 0, 0, tiled=True)]
    all_to_all x1, starting transfers between devices: 15.7 us -> 13.9 us  [body(): lax.all_to_all(probe_part.reshape(near, rows, TILE), NEAR_AXES, 0, 0, til...]
    dynamic_slice x1 -> x0, local copies, waits for them, and re-layouts: 1.06 us -> none  [body(): mate = lax.dynamic_slice_in_dim(tile, HALF - upper, HALF, axis=1)]
    pallas_call x8 -> x9, Pallas kernels: 9.53 us -> 9.64 us  [call(): pl.pallas_call(kernel, out_shape=out_shape, in_specs=in_specs, out_specs=...]
  transfers between devices with their start and end apart: 11 -> 12, of which waited for: 5 -> 5; matrix products, arithmetic and copies ran while one was open for 1% -> 1% of each run, Pallas kernels for 3% -> 3%
where the time goes in v12:
time: 104 us; the launch traced here: 103 us
  starting transfers between devices  59.4 us (57%)
  waiting for transfers between devices  30 us (29%)
  Pallas kernels  9.64 us (9%)
  local copies, waits for them, and re-layouts  2.35 us (2%)
  between operations  1.5 us (1%)
    ppermute x4, starting transfers between devices, to_mate(): return lax.ppermute(value, axes, pairs + [(b, a) for a, b in pairs])  16.9 us
    ppermute x5, starting transfers between devices, to_cross(): return lax.ppermute(value, axes, pairs + [(b, a) for a, b in pairs])  16.5 us
    all_to_all x1, starting transfers between devices, body(): lax.all_to_all(probe_part.reshape(near, rows, TILE), NEAR_AXES, 0, 0, til...  13.9 us
    all_to_all x1, waiting for transfers between devices, body(): gathered = lax.all_to_all(spread_share, NEAR_AXES, 0, 0, tiled=True)  11.1 us
    pallas_call x9, Pallas kernels, call(): pl.pallas_call(kernel, out_shape=out_shape, in_specs=in_specs, out_specs=...  9.64 us
    ppermute x5, waiting for transfers between devices, to_cross(): return lax.ppermute(value, axes, pairs + [(b, a) for a, b in pairs])  8.54 us
    all_to_all x1, waiting for transfers between devices, body(): shares = lax.all_to_all(spread_share, FAR_AXES, 0, 0, tiled=True)  6.26 us
    all_to_all x1, starting transfers between devices, body(): gathered = lax.all_to_all(spread_share, NEAR_AXES, 0, 0, tiled=True)  6.24 us
  transfers between devices with their start and end apart: 12, of which 5 were waited for; matrix products, arithmetic and copies ran while one was open for 1% of the time, Pallas kernels for 3%

profile of v12, /device:TPU:1, one launch (start us, length us, event | category | flops | bytes accessed | tf_op | source)
XLA Modules:
  0.0 103.0 jit_solution(3173393009775376685)
XLA Ops:
  0.6 0.9 copy-done
  1.7 0.8 collective-permute-start
  2.5 7.3 %collective-permute-start.1 = (f32[4,64,128]{2,1,0:T(8,128)S(1)}, f32[4,64,128]{2,1,0:T(8,128)S(1)}, u32[]{:S(2)}, u32[]{:S(2)}) collective-permute-start(f32[4,64,128]{2,1,0:T(8,128)S(1)} %get-tuple-element.21), channel_id=1, source_target_pairs={{0,16},{32,48},{64,80},{96,112},{128,144},{160,176},{192,208},{224... | collective-permute-start | bytes 393224 | tf_op jit(solution)/shard_map/ppermute | solution.py:310
  9.8 5.9 %collective-permute-start.2 = (f32[2,128,128]{2,1,0:T(8,128)S(1)}, f32[2,128,128]{2,1,0:T(8,128)S(1)}, u32[]{:S(2)}, u32[]{:S(2)}) collective-permute-start(f32[2,128,128]{2,1,0:T(8,128)S(1)} %get-tuple-element.22), channel_id=1, source_target_pairs={{1,2},{3,4},{5,6},{7,8},{9,10},{11,12},{13,14},{2,1},{4,3},{6,5},{... | collective-permute-start | bytes 393224 | tf_op jit(solution)/shard_map/ppermute | solution.py:305
  15.7 6.5 %collective-permute-done.2.columns = f32[2,128,128]{2,1,0:T(8,128)S(1)} collective-permute-done((f32[2,128,128]{2,1,0:T(8,128)S(1)}, f32[2,128,128]{2,1,0:T(8,128)S(1)}, u32[]{:S(2)}, u32[]{:S(2)}) %collective-permute-start.2) | collective-permute-done | bytes 131104 | tf_op jit(solution)/shard_map/ppermute | solution.py:305
  22.3 1.9 %collective-permute-start.4 = (f32[2,256,128]{2,1,0:T(8,128)S(1)}, f32[2,256,128]{2,1,0:T(8,128)S(1)}, u32[]{:S(2)}, u32[]{:S(2)}) collective-permute-start(f32[2,256,128]{2,1,0:T(8,128)S(1)} %get-tuple-element.26), channel_id=1, source_target_pairs={{0,1},{2,3},{4,5},{6,7},{8,9},{10,11},{12,13},{14,15},{1,0},{3,2},... | collective-permute-start | bytes 786440 | tf_op jit(solution)/shard_map/ppermute | solution.py:310
  24.3 4.1 %collective-permute-start.3 = (f32[2,128,128]{2,1,0:T(8,128)S(1)}, f32[2,128,128]{2,1,0:T(8,128)S(1)}, u32[]{:S(2)}, u32[]{:S(2)}) collective-permute-start(f32[2,128,128]{2,1,0:T(8,128)S(1)} %get-tuple-element.25), channel_id=1, source_target_pairs={{1,2},{3,4},{5,6},{7,8},{9,10},{11,12},{13,14},{2,1},{4,3},{6,5},{... | collective-permute-start | bytes 393224 | tf_op jit(solution)/shard_map/ppermute | solution.py:305
  29.1 0.7 copy-done.3
  30.1 2.1 %collective-permute-done.3.corners = f32[2,128,128]{2,1,0:T(8,128)S(1)} collective-permute-done((f32[2,128,128]{2,1,0:T(8,128)S(1)}, f32[2,128,128]{2,1,0:T(8,128)S(1)}, u32[]{:S(2)}, u32[]{:S(2)}) %collective-permute-start.3) | collective-permute-done | bytes 131104 | tf_op jit(solution)/shard_map/ppermute | solution.py:305
  32.2 5.6 %shard_map.80 = (f32[8,128,128]{2,1,0:T(8,128)}, f32[2,4,128,128]{3,2,1,0:T(8,128)S(1)}) custom-call(s32[4]{0:T(128)S(1)} %reshape.30.offsets, s32[1,1]{1,0:T(1,128)S(6)} %copy.8.counts, f32[4,256,128]{2,1,0:T(8,128)S(1)} %get-tuple-element.23.tall, f32[2,128,128]{2,1,0:T(8,128)S(1)} %get-tuple-element.24.columns, ...), custom_call_target="tpu_custom_call" | custom-call | flops 3200000000 | bytes 4000000 | tf_op jit(solution)/shard_map/pallas_call | solution.py:29
  37.8 13.9 %all-to-all-start = ((f32[64,16,128]{2,1,0:T(8,128)}), f32[64,16,128]{2,1,0:T(8,128)S(1)}, u32[]{:S(2)}, u32[]{:S(2)}) async-start(f32[64,16,128]{2,1,0:T(8,128)} %bitcast.4), calls=%async_computation | async-start | bytes 1048576 | tf_op jit(solution)/shard_map/all_to_all | solution.py:366
  51.7 0.9 shard_map.81
  52.7 5.0 %collective-permute-start.5 = (f32[2,256,128]{2,1,0:T(8,128)S(1)}, f32[2,256,128]{2,1,0:T(8,128)S(1)}, u32[]{:S(2)}, u32[]{:S(2)}) collective-permute-start(f32[2,256,128]{2,1,0:T(8,128)S(1)} %get-tuple-element.32), channel_id=1, source_target_pairs={{1,2},{3,4},{5,6},{7,8},{9,10},{11,12},{13,14},{2,1},{4,3},{6,5},{... | collective-permute-start | bytes 786440 | tf_op jit(solution)/shard_map/ppermute | solution.py:305
  57.7 1.9 %collective-permute-start.6 = (f32[2,256,128]{2,1,0:T(8,128)S(1)}, f32[2,256,128]{2,1,0:T(8,128)S(1)}, u32[]{:S(2)}, u32[]{:S(2)}) collective-permute-start(f32[2,256,128]{2,1,0:T(8,128)S(1)} %get-tuple-element.33), channel_id=1, source_target_pairs={{0,1},{2,3},{4,5},{6,7},{8,9},{10,11},{12,13},{14,15},{1,0},{3,2},... | collective-permute-start | bytes 786440 | tf_op jit(solution)/shard_map/ppermute | solution.py:310
  59.6 4.1 %all-to-all-done = f32[64,16,128]{2,1,0:T(8,128)S(1)} async-done(((f32[64,16,128]{2,1,0:T(8,128)}), f32[64,16,128]{2,1,0:T(8,128)S(1)}, u32[]{:S(2)}, u32[]{:S(2)}) %all-to-all-start) | async-done | bytes 524320 | tf_op jit(solution)/shard_map/all_to_all | solution.py:366
  64.4 5.9 %all-to-all-start.1 = ((f32[8,16,128]{2,1,0:T(8,128)}), f32[8,16,128]{2,1,0:T(8,128)S(1)}, u32[]{:S(2)}, u32[]{:S(2)}) async-start(f32[8,16,128]{2,1,0:T(8,128)} %broadcast_in_dim.2), calls=%async_computation.1 | async-start | bytes 131072 | tf_op jit(solution)/shard_map/all_to_all | solution.py:369
  70.5 0.7 collective-permute-start.7
  71.2 5.8 %collective-permute-start.8 = (f32[4,64,128]{2,1,0:T(8,128)S(1)}, f32[4,64,128]{2,1,0:T(8,128)S(1)}, u32[]{:S(2)}, u32[]{:S(2)}) collective-permute-start(f32[4,64,128]{2,1,0:T(8,128)S(1)} %get-tuple-element.36), channel_id=1, source_target_pairs={{0,16},{32,48},{64,80},{96,112},{128,144},{160,176},{192,208},{224... | collective-permute-start | bytes 393224 | tf_op jit(solution)/shard_map/ppermute | solution.py:310
  77.0 6.3 %all-to-all-done.1.shares = f32[8,16,128]{2,1,0:T(8,128)S(1)} async-done(((f32[8,16,128]{2,1,0:T(8,128)}), f32[8,16,128]{2,1,0:T(8,128)S(1)}, u32[]{:S(2)}, u32[]{:S(2)}) %all-to-all-start.1) | async-done | bytes 65568 | tf_op jit(solution)/shard_map/all_to_all | solution.py:369
  83.2 0.8 shard_map.84
  84.1 6.2 %all-to-all-start.2 = ((f32[64,16,128]{2,1,0:T(8,128)}), f32[64,16,128]{2,1,0:T(8,128)S(1)}, u32[]{:S(2)}, u32[]{:S(2)}) async-start(f32[64,16,128]{2,1,0:T(8,128)} %shard_map.84), calls=%async_computation.2 | async-start | bytes 1048576 | tf_op jit(solution)/shard_map/all_to_all | solution.py:377
  90.3 0.7 shard_map.83
  91.1 11.1 %all-to-all-done.2 = f32[64,16,128]{2,1,0:T(8,128)S(1)} async-done(((f32[64,16,128]{2,1,0:T(8,128)}), f32[64,16,128]{2,1,0:T(8,128)S(1)}, u32[]{:S(2)}, u32[]{:S(2)}) %all-to-all-start.2) | async-done | bytes 524320 | tf_op jit(solution)/shard_map/all_to_all | solution.py:377
  102.2 0.8 shard_map.85
  (22 shorter events, 1.5 us)
Async XLA Ops:
  0.6 1.0 copy-start
  1.6 27.5 %copy-start.1 = (f32[2,4,128,128]{3,2,1,0:T(8,128)S(1)}, f32[2,4,128,128]{3,2,1,0:T(8,128)}, u32[]{:S(2)}) copy-start(f32[2,4,128,128]{3,2,1,0:T(8,128)} %param.7) | copy-start | bytes 1572868
  1.7 14.0 %collective-permute-start = (f32[4,64,128]{2,1,0:T(8,128)S(1)}, f32[4,64,128]{2,1,0:T(8,128)S(1)}, u32[]{:S(2)}, u32[]{:S(2)}) collective-permute-start(f32[4,64,128]{2,1,0:T(8,128)S(1)} %get-tuple-element.20), channel_id=1, source_target_pairs={{16,32},{48,64},{80,96},{112,128},{144,160},{176,192},{208,224},{2... | collective-permute-start | bytes 393224 | tf_op jit(solution)/shard_map/ppermute | solution.py:305
  2.5 13.2 %collective-permute-start.1 = (f32[4,64,128]{2,1,0:T(8,128)S(1)}, f32[4,64,128]{2,1,0:T(8,128)S(1)}, u32[]{:S(2)}, u32[]{:S(2)}) collective-permute-start(f32[4,64,128]{2,1,0:T(8,128)S(1)} %get-tuple-element.21), channel_id=1, source_target_pairs={{0,16},{32,48},{64,80},{96,112},{128,144},{160,176},{192,208},{224... | collective-permute-start | bytes 393224 | tf_op jit(solution)/shard_map/ppermute | solution.py:310
  9.8 19.3 %copy-start.2 = (f32[1,1,2,128,128]{4,3,2,1,0:T(8,128)S(1)}, f32[1,1,2,128,128]{4,3,2,1,0:T(8,128)}, u32[]{:S(2)}) copy-start(f32[1,1,2,128,128]{4,3,2,1,0:T(8,128)} %param.9) | copy-start | bytes 393220
  9.8 12.4 %collective-permute-start.2 = (f32[2,128,128]{2,1,0:T(8,128)S(1)}, f32[2,128,128]{2,1,0:T(8,128)S(1)}, u32[]{:S(2)}, u32[]{:S(2)}) collective-permute-start(f32[2,128,128]{2,1,0:T(8,128)S(1)} %get-tuple-element.22), channel_id=1, source_target_pairs={{1,2},{3,4},{5,6},{7,8},{9,10},{11,12},{13,14},{2,1},{4,3},{6,5},{... | collective-permute-start | bytes 393224 | tf_op jit(solution)/shard_map/ppermute | solution.py:305
  22.3 9.8 %collective-permute-start.4 = (f32[2,256,128]{2,1,0:T(8,128)S(1)}, f32[2,256,128]{2,1,0:T(8,128)S(1)}, u32[]{:S(2)}, u32[]{:S(2)}) collective-permute-start(f32[2,256,128]{2,1,0:T(8,128)S(1)} %get-tuple-element.26), channel_id=1, source_target_pairs={{0,1},{2,3},{4,5},{6,7},{8,9},{10,11},{12,13},{14,15},{1,0},{3,2},... | collective-permute-start | bytes 786440 | tf_op jit(solution)/shard_map/ppermute | solution.py:310
  24.3 4.8 %copy-start.4 = (s32[1,1,2,2]{3,2,1,0:T(2,128)S(1)}, s32[1,1,2,2]{3,2,1,0:T(2,128)}, u32[]{:S(2)}) copy-start(s32[1,1,2,2]{3,2,1,0:T(2,128)} %param.10) | copy-start | bytes 52
  24.3 7.9 %collective-permute-start.3 = (f32[2,128,128]{2,1,0:T(8,128)S(1)}, f32[2,128,128]{2,1,0:T(8,128)S(1)}, u32[]{:S(2)}, u32[]{:S(2)}) collective-permute-start(f32[2,128,128]{2,1,0:T(8,128)S(1)} %get-tuple-element.25), channel_id=1, source_target_pairs={{1,2},{3,4},{5,6},{7,8},{9,10},{11,12},{13,14},{2,1},{4,3},{6,5},{... | collective-permute-start | bytes 393224 | tf_op jit(solution)/shard_map/ppermute | solution.py:305
  29.1 0.7 copy-start.3
  37.8 25.9 %all-to-all-start = ((f32[64,16,128]{2,1,0:T(8,128)}), f32[64,16,128]{2,1,0:T(8,128)S(1)}, u32[]{:S(2)}, u32[]{:S(2)}) async-start(f32[64,16,128]{2,1,0:T(8,128)} %bitcast.4), calls=%async_computation | async-start | bytes 1048576 | tf_op jit(solution)/shard_map/all_to_all | solution.py:366
  52.7 17.7 %collective-permute-start.5 = (f32[2,256,128]{2,1,0:T(8,128)S(1)}, f32[2,256,128]{2,1,0:T(8,128)S(1)}, u32[]{:S(2)}, u32[]{:S(2)}) collective-permute-start(f32[2,256,128]{2,1,0:T(8,128)S(1)} %get-tuple-element.32), channel_id=1, source_target_pairs={{1,2},{3,4},{5,6},{7,8},{9,10},{11,12},{13,14},{2,1},{4,3},{6,5},{... | collective-permute-start | bytes 786440 | tf_op jit(solution)/shard_map/ppermute | solution.py:305
  57.7 12.6 %collective-permute-start.6 = (f32[2,256,128]{2,1,0:T(8,128)S(1)}, f32[2,256,128]{2,1,0:T(8,128)S(1)}, u32[]{:S(2)}, u32[]{:S(2)}) collective-permute-start(f32[2,256,128]{2,1,0:T(8,128)S(1)} %get-tuple-element.33), channel_id=1, source_target_pairs={{0,1},{2,3},{4,5},{6,7},{8,9},{10,11},{12,13},{14,15},{1,0},{3,2},... | collective-permute-start | bytes 786440 | tf_op jit(solution)/shard_map/ppermute | solution.py:310
  64.4 18.8 %all-to-all-start.1 = ((f32[8,16,128]{2,1,0:T(8,128)}), f32[8,16,128]{2,1,0:T(8,128)S(1)}, u32[]{:S(2)}, u32[]{:S(2)}) async-start(f32[8,16,128]{2,1,0:T(8,128)} %broadcast_in_dim.2), calls=%async_computation.1 | async-start | bytes 131072 | tf_op jit(solution)/shard_map/all_to_all | solution.py:369
  70.5 19.8 %collective-permute-start.7 = (f32[4,64,128]{2,1,0:T(8,128)S(1)}, f32[4,64,128]{2,1,0:T(8,128)S(1)}, u32[]{:S(2)}, u32[]{:S(2)}) collective-permute-start(f32[4,64,128]{2,1,0:T(8,128)S(1)} %get-tuple-element.35), channel_id=1, source_target_pairs={{16,32},{48,64},{80,96},{112,128},{144,160},{176,192},{208,224},{2... | collective-permute-start | bytes 393224 | tf_op jit(solution)/shard_map/ppermute | solution.py:305
  71.2 19.2 %collective-permute-start.8 = (f32[4,64,128]{2,1,0:T(8,128)S(1)}, f32[4,64,128]{2,1,0:T(8,128)S(1)}, u32[]{:S(2)}, u32[]{:S(2)}) collective-permute-start(f32[4,64,128]{2,1,0:T(8,128)S(1)} %get-tuple-element.36), channel_id=1, source_target_pairs={{0,16},{32,48},{64,80},{96,112},{128,144},{160,176},{192,208},{224... | collective-permute-start | bytes 393224 | tf_op jit(solution)/shard_map/ppermute | solution.py:310
  84.1 18.1 %all-to-all-start.2 = ((f32[64,16,128]{2,1,0:T(8,128)}), f32[64,16,128]{2,1,0:T(8,128)S(1)}, u32[]{:S(2)}, u32[]{:S(2)}) async-start(f32[64,16,128]{2,1,0:T(8,128)} %shard_map.84), calls=%async_computation.2 | async-start | bytes 1048576 | tf_op jit(solution)/shard_map/all_to_all | solution.py:377

commit v13 on v10

--- a/solution.py
+++ b/solution.py
@@ -50,8 +50,8 @@
     return lax.axis_index("core") == 0
 
 
-def even_row():
-    return lax.axis_index("zb") == 0
+def above_first():
+    return lax.axis_index("zb") == lax.axis_index("core")
 
 
 def by_parity(even, first, second):
@@ -71,9 +71,9 @@
 
 
 def columns_kernel(tile, from_cross, from_mate, tall, cross, mate):
-    even = even_row()
+    first = above_first()
     for p in range(4):
-        below, above = by_parity(even, from_mate[p], from_cross[p])
+        below, above = by_parity(first, from_mate[p], from_cross[p])
         tall[p, :HALF] = above
         tall[p, HALF:HALF + TILE] = tile[p]
         tall[p, HALF + TILE:] = below
@@ -252,19 +252,19 @@
 
 
 def fold_columns_kernel(grad_tall, from_cross, from_mate, part, cross, mate):
-    even, even_down = even_column(), even_row()
+    even, first = even_column(), above_first()
     for s in range(2):
         from_right, from_left = by_parity(even, from_mate[s], from_cross[s])
         for p, sides in zip((s, 2 + s), unpack_columns(from_right, from_left)):
             total = grad_tall[p] + sides
             part[p] = total[HALF:HALF + TILE]
-            mate[p], cross[p] = by_parity(even_down, total[HALF + TILE:], total[:HALF])
+            mate[p], cross[p] = by_parity(first, total[HALF + TILE:], total[:HALF])
 
 
 def fold_rows_kernel(part, from_cross, from_mate, result):
-    even = even_row()
+    first = above_first()
     for p in range(4):
-        below, above = by_parity(even, from_mate[p], from_cross[p])
+        below, above = by_parity(first, from_mate[p], from_cross[p])
         result[p, :HALF] = part[p, :HALF] + above
         result[p, HALF:] = part[p, HALF:] + below
 
@@ -279,13 +279,25 @@
         move.wait()
 
 
-def exchange(cross, mate, axes):
-    count = lax.axis_size(axes)
-    pairs = [(i, i + 1) for i in range(1, count - 1, 2)]
-    from_cross = lax.ppermute(cross, axes, pairs + [(b, a) for a, b in pairs])
-    pairs = [(i, i + 1) for i in range(0, count, 2)]
-    from_mate = lax.ppermute(mate, axes, pairs + [(b, a) for a, b in pairs])
-    return from_cross, from_mate
+def neighbours(count, start):
+    pairs = [(i, i + 1) for i in range(start, count - 1, 2)]
+    return pairs + [(b, a) for a, b in pairs]
+
+
+def exchange_columns(cross, mate):
+    count = lax.axis_size(COL_AXES)
+    from_cross = lax.ppermute(cross, COL_AXES, neighbours(count, 1))
+    return from_cross, lax.ppermute(mate, COL_AXES, neighbours(count, 0))
+
+
+def exchange_rows(first, second):
+    count = lax.axis_size(ROW_AXES)
+    axes = ROW_AXES + ("core",)
+    received = []
+    for value, starts in ((first, (1, 0)), (second, (0, 1))):
+        pairs = [(2 * a + c, 2 * b + c) for c in range(2) for a, b in neighbours(count, starts[c])]
+        received.append(lax.ppermute(value, axes, pairs))
+    return received
 
 
 def f32(*shape):
@@ -297,14 +309,14 @@
     planes, strip, half = f32(4, TILE, TILE), f32(2, TILE, TILE), f32(4, HALF, TILE)
     tall, tall_strip = f32(4, 2 * TILE, TILE), f32(2, 2 * TILE, TILE)
 
-    upper = jnp.where(even_row(), 0, HALF)
+    upper = jnp.where(above_first(), 0, HALF)
     cross = lax.dynamic_slice_in_dim(tile, upper, HALF, axis=1)
     mate = lax.dynamic_slice_in_dim(tile, HALF - upper, HALF, axis=1)
-    rims = exchange(cross, mate, ROW_AXES)
+    rims = exchange_rows(cross, mate)
     object_tall, cross, mate = call(
         columns_kernel, (tall, tall_strip, tall_strip), [VM] * 3, tile, *rims
     )
-    strips = exchange(cross, mate, COL_AXES)
+    strips = exchange_columns(cross, mate)
     ops, probe, targets = call(
         operator_kernel,
         (jax.ShapeDtypeStruct((4, 512, 256), BF16), f32(8, TILE, TILE), strip), [VM, VM, VM],
@@ -337,12 +349,12 @@
     rows = 8 * TILE // near
     shares = lax.all_to_all(probe_part.reshape(near, rows, TILE), NEAR_AXES, 0, 0, tiled=True)
     spread_share = jnp.broadcast_to(jnp.sum(shares, axis=0)[None], (far, rows, TILE))
-    strips = exchange(cross, mate, COL_AXES)
+    strips = exchange_columns(cross, mate)
     shares = lax.all_to_all(spread_share, FAR_AXES, 0, 0, tiled=True)
     part, cross, mate = call(
         fold_columns_kernel, (planes, half, half), [VM] * 3, grad_tall, *strips
     )
-    rims = exchange(cross, mate, ROW_AXES)
+    rims = exchange_rows(cross, mate)
     (spread_share,) = call(
         functools.partial(spread_sum, 1.0 / math.sqrt(near * far)), (f32(near, rows, TILE),), [VM], shares
     )

time: 99 us -> 98.5 us (level)
  starting transfers between devices: 57.9 us -> 52.3 us
  waiting for transfers between devices: 27 us -> 32 us
    ppermute x8, starting transfers between devices: 28.2 us -> 24.6 us  [the longest x4 11.8 us: exchange_rows(): received.append(lax.ppermute(value, axes, pairs))]
    all_to_all x1, waiting for transfers between devices: 6.26 us -> 8.95 us  [body(): shares = lax.all_to_all(spread_share, FAR_AXES, 0, 0, tiled=True)]
    ppermute x8, waiting for transfers between devices: 5.52 us -> 7.93 us  [the longest x2 5.52 us: exchange_columns(): from_cross = lax.ppermute(cross, COL_AXES, neighbours(count, 1))]
    all_to_all x1, starting transfers between devices: 7.73 us -> 6.56 us  [body(): shares = lax.all_to_all(spread_share, FAR_AXES, 0, 0, tiled=True)]
where the time goes in v13:
time: 98.5 us; the launch traced here: 97.9 us
  starting transfers between devices  52.3 us (53%)
  waiting for transfers between devices  32 us (32%)
  Pallas kernels  9.52 us (10%)
  local copies, waits for them, and re-layouts  2.48 us (3%)
  between operations  1.49 us (2%)
    all_to_all x1, starting transfers between devices, body(): lax.all_to_all(probe_part.reshape(near, rows, TILE), NEAR_AXES, 0, 0, til...  14.9 us
    ppermute x4, starting transfers between devices, exchange_rows(): received.append(lax.ppermute(value, axes, pairs))  11.8 us
    all_to_all x1, waiting for transfers between devices, body(): gathered = lax.all_to_all(spread_share, NEAR_AXES, 0, 0, tiled=True)  11.1 us
    pallas_call x8, Pallas kernels, call(): pl.pallas_call(kernel, out_shape=out_shape, in_specs=in_specs, out_specs=...  9.52 us
    all_to_all x1, waiting for transfers between devices, body(): shares = lax.all_to_all(spread_share, FAR_AXES, 0, 0, tiled=True)  8.95 us
    ppermute x2, starting transfers between devices, exchange_columns(): from_cross = lax.ppermute(cross, COL_AXES, neighbours(count, 1))  7.47 us
    all_to_all x1, starting transfers between devices, body(): shares = lax.all_to_all(spread_share, FAR_AXES, 0, 0, tiled=True)  6.56 us
    all_to_all x1, starting transfers between devices, body(): gathered = lax.all_to_all(spread_share, NEAR_AXES, 0, 0, tiled=True)  6.16 us
  transfers between devices with their start and end apart: 11, of which 5 were waited for; matrix products, arithmetic and copies ran while one was open for 1% of the time, Pallas kernels for 3%

profile of v13, /device:TPU:1, one launch (start us, length us, event | category | flops | bytes accessed | tf_op | source)
XLA Modules:
  0.0 97.9 jit_solution(10032476102975505474)
XLA Ops:
  0.7 1.1 %constant_dynamic-slice_fusion = (f32[4,64,128]{2,1,0:T(8,128)S(1)}, f32[4,64,128]{2,1,0:T(8,128)S(1)}) fusion(f32[4,128,128]{2,1,0:T(8,128)} %bitcast.8, s32[]{:T(128)S(6)} %select_n.9, s32[]{:T(128)S(6)} %select_n.8), kind=kLoop, calls=%fused_computation | loop fusion | bytes 524296 | tf_op jit(solution)/shard_map/dynamic_slice | solution.py:314
  1.7 0.7 collective-permute-start.1
  2.4 7.4 %collective-permute-start = (f32[4,64,128]{2,1,0:T(8,128)S(1)}, f32[4,64,128]{2,1,0:T(8,128)S(1)}, u32[]{:S(2)}, u32[]{:S(2)}) collective-permute-start(f32[4,64,128]{2,1,0:T(8,128)S(1)} %get-tuple-element.31), channel_id=1, source_target_pairs={{16,32},{48,64},{80,96},{112,128},{144,160},{176,192},{208,224},{2... | collective-permute-start | bytes 393224 | tf_op jit(solution)/shard_map/ppermute | solution.py:299
  9.8 2.4 %collective-permute-done.from_cross = f32[4,64,128]{2,1,0:T(8,128)S(1)} collective-permute-done((f32[4,64,128]{2,1,0:T(8,128)S(1)}, f32[4,64,128]{2,1,0:T(8,128)S(1)}, u32[]{:S(2)}, u32[]{:S(2)}) %collective-permute-start) | collective-permute-done | bytes 131104 | tf_op jit(solution)/shard_map/ppermute | solution.py:299
  12.4 2.4 %collective-permute-start.2 = (f32[2,256,128]{2,1,0:T(8,128)S(1)}, f32[2,256,128]{2,1,0:T(8,128)S(1)}, u32[]{:S(2)}, u32[]{:S(2)}) collective-permute-start(f32[2,256,128]{2,1,0:T(8,128)S(1)} %get-tuple-element.17), channel_id=1, source_target_pairs={{1,2},{3,4},{5,6},{7,8},{9,10},{11,12},{13,14},{2,1},{4,3},{6,5},{... | collective-permute-start | bytes 786440 | tf_op jit(solution)/shard_map/ppermute | solution.py:289
  14.8 3.4 %collective-permute-start.3 = (f32[2,256,128]{2,1,0:T(8,128)S(1)}, f32[2,256,128]{2,1,0:T(8,128)S(1)}, u32[]{:S(2)}, u32[]{:S(2)}) collective-permute-start(f32[2,256,128]{2,1,0:T(8,128)S(1)} %get-tuple-element.18), channel_id=1, source_target_pairs={{0,1},{2,3},{4,5},{6,7},{8,9},{10,11},{12,13},{14,15},{1,0},{3,2},... | collective-permute-start | bytes 786440 | tf_op jit(solution)/shard_map/ppermute | solution.py:290
  19.0 0.7 copy-done.3
  20.0 5.5 %collective-permute-done.2.from_cross = f32[2,256,128]{2,1,0:T(8,128)S(1)} collective-permute-done((f32[2,256,128]{2,1,0:T(8,128)S(1)}, f32[2,256,128]{2,1,0:T(8,128)S(1)}, u32[]{:S(2)}, u32[]{:S(2)}) %collective-permute-start.2) | collective-permute-done | bytes 262176 | tf_op jit(solution)/shard_map/ppermute | solution.py:289
  25.5 5.6 %shard_map.79 = (f32[8,128,128]{2,1,0:T(8,128)}, f32[2,4,128,128]{3,2,1,0:T(8,128)S(1)}) custom-call(s32[4]{0:T(128)S(1)} %reshape.30.offsets, s32[1,1]{1,0:T(1,128)S(6)} %copy.8.counts, f32[4,256,128]{2,1,0:T(8,128)S(1)} %get-tuple-element.16.tall, f32[2,256,128]{2,1,0:T(8,128)S(1)} %collective-permute-done.2.from_cross, ...), custom_call_target="tpu_custom_call" | custom-call | flops 3200000000 | bytes 4000000 | tf_op jit(solution)/shard_map/pallas_call | solution.py:29
  31.1 14.9 %all-to-all-start = ((f32[64,16,128]{2,1,0:T(8,128)}), f32[64,16,128]{2,1,0:T(8,128)S(1)}, u32[]{:S(2)}, u32[]{:S(2)}) async-start(f32[64,16,128]{2,1,0:T(8,128)} %bitcast.4), calls=%async_computation | async-start | bytes 1048576 | tf_op jit(solution)/shard_map/all_to_all | solution.py:350
  46.1 0.9 shard_map.80
  47.0 5.0 %collective-permute-start.4 = (f32[2,256,128]{2,1,0:T(8,128)S(1)}, f32[2,256,128]{2,1,0:T(8,128)S(1)}, u32[]{:S(2)}, u32[]{:S(2)}) collective-permute-start(f32[2,256,128]{2,1,0:T(8,128)S(1)} %get-tuple-element.24), channel_id=1, source_target_pairs={{1,2},{3,4},{5,6},{7,8},{9,10},{11,12},{13,14},{2,1},{4,3},{6,5},{... | collective-permute-start | bytes 786440 | tf_op jit(solution)/shard_map/ppermute | solution.py:289
  52.0 1.9 %collective-permute-start.5 = (f32[2,256,128]{2,1,0:T(8,128)S(1)}, f32[2,256,128]{2,1,0:T(8,128)S(1)}, u32[]{:S(2)}, u32[]{:S(2)}) collective-permute-start(f32[2,256,128]{2,1,0:T(8,128)S(1)} %get-tuple-element.25), channel_id=1, source_target_pairs={{0,1},{2,3},{4,5},{6,7},{8,9},{10,11},{12,13},{14,15},{1,0},{3,2},... | collective-permute-start | bytes 786440 | tf_op jit(solution)/shard_map/ppermute | solution.py:290
  54.0 4.1 %all-to-all-done = f32[64,16,128]{2,1,0:T(8,128)S(1)} async-done(((f32[64,16,128]{2,1,0:T(8,128)}), f32[64,16,128]{2,1,0:T(8,128)S(1)}, u32[]{:S(2)}, u32[]{:S(2)}) %all-to-all-start) | async-done | bytes 524320 | tf_op jit(solution)/shard_map/all_to_all | solution.py:350
  58.1 0.6 broadcast_in_dim.2
  58.8 6.6 %all-to-all-start.1 = ((f32[8,16,128]{2,1,0:T(8,128)}), f32[8,16,128]{2,1,0:T(8,128)S(1)}, u32[]{:S(2)}, u32[]{:S(2)}) async-start(f32[8,16,128]{2,1,0:T(8,128)} %broadcast_in_dim.2), calls=%async_computation.1 | async-start | bytes 131072 | tf_op jit(solution)/shard_map/all_to_all | solution.py:353
  65.5 3.1 %collective-permute-start.6 = (f32[4,64,128]{2,1,0:T(8,128)S(1)}, f32[4,64,128]{2,1,0:T(8,128)S(1)}, u32[]{:S(2)}, u32[]{:S(2)}) collective-permute-start(f32[4,64,128]{2,1,0:T(8,128)S(1)} %get-tuple-element.27), channel_id=1, source_target_pairs={{16,32},{48,64},{80,96},{112,128},{144,160},{176,192},{208,224},{2... | collective-permute-start | bytes 393224 | tf_op jit(solution)/shard_map/ppermute | solution.py:299
  68.6 0.7 collective-permute-start.7
  69.3 8.9 %all-to-all-done.1.shares = f32[8,16,128]{2,1,0:T(8,128)S(1)} async-done(((f32[8,16,128]{2,1,0:T(8,128)}), f32[8,16,128]{2,1,0:T(8,128)S(1)}, u32[]{:S(2)}, u32[]{:S(2)}) %all-to-all-start.1) | async-done | bytes 65568 | tf_op jit(solution)/shard_map/all_to_all | solution.py:353
  78.2 0.8 shard_map.83
  79.1 6.2 %all-to-all-start.2 = ((f32[64,16,128]{2,1,0:T(8,128)}), f32[64,16,128]{2,1,0:T(8,128)S(1)}, u32[]{:S(2)}, u32[]{:S(2)}) async-start(f32[64,16,128]{2,1,0:T(8,128)} %shard_map.83), calls=%async_computation.2 | async-start | bytes 1048576 | tf_op jit(solution)/shard_map/all_to_all | solution.py:361
  85.3 0.7 shard_map.82
  86.0 11.1 %all-to-all-done.2 = f32[64,16,128]{2,1,0:T(8,128)S(1)} async-done(((f32[64,16,128]{2,1,0:T(8,128)}), f32[64,16,128]{2,1,0:T(8,128)S(1)}, u32[]{:S(2)}, u32[]{:S(2)}) %all-to-all-start.2) | async-done | bytes 524320 | tf_op jit(solution)/shard_map/all_to_all | solution.py:361
  97.1 0.8 shard_map.84
  (20 shorter events, 0.8 us)
Async XLA Ops:
  0.6 11.6 %copy-start = (f32[2,2,128,128]{3,2,1,0:T(8,128)S(1)}, f32[2,2,128,128]{3,2,1,0:T(8,128)}, u32[]{:S(2)}) copy-start(f32[2,2,128,128]{3,2,1,0:T(8,128)} %param.6) | copy-start | bytes 786436
  0.6 18.3 %copy-start.1 = (f32[2,4,128,128]{3,2,1,0:T(8,128)S(1)}, f32[2,4,128,128]{3,2,1,0:T(8,128)}, u32[]{:S(2)}) copy-start(f32[2,4,128,128]{3,2,1,0:T(8,128)} %param.7) | copy-start | bytes 1572868
  1.7 8.1 %collective-permute-start.1 = (f32[4,64,128]{2,1,0:T(8,128)S(1)}, f32[4,64,128]{2,1,0:T(8,128)S(1)}, u32[]{:S(2)}, u32[]{:S(2)}) collective-permute-start(f32[4,64,128]{2,1,0:T(8,128)S(1)} %get-tuple-element.30), channel_id=1, source_target_pairs={{0,16},{32,48},{64,80},{96,112},{128,144},{160,176},{192,208},{224... | collective-permute-start | bytes 393224 | tf_op jit(solution)/shard_map/ppermute | solution.py:299
  2.4 16.6 %copy-start.2 = (f32[1,1,2,128,128]{4,3,2,1,0:T(8,128)S(1)}, f32[1,1,2,128,128]{4,3,2,1,0:T(8,128)}, u32[]{:S(2)}) copy-start(f32[1,1,2,128,128]{4,3,2,1,0:T(8,128)} %param.9) | copy-start | bytes 393220
  2.4 9.8 %collective-permute-start = (f32[4,64,128]{2,1,0:T(8,128)S(1)}, f32[4,64,128]{2,1,0:T(8,128)S(1)}, u32[]{:S(2)}, u32[]{:S(2)}) collective-permute-start(f32[4,64,128]{2,1,0:T(8,128)S(1)} %get-tuple-element.31), channel_id=1, source_target_pairs={{16,32},{48,64},{80,96},{112,128},{144,160},{176,192},{208,224},{2... | collective-permute-start | bytes 393224 | tf_op jit(solution)/shard_map/ppermute | solution.py:299
  12.4 13.2 %collective-permute-start.2 = (f32[2,256,128]{2,1,0:T(8,128)S(1)}, f32[2,256,128]{2,1,0:T(8,128)S(1)}, u32[]{:S(2)}, u32[]{:S(2)}) collective-permute-start(f32[2,256,128]{2,1,0:T(8,128)S(1)} %get-tuple-element.17), channel_id=1, source_target_pairs={{1,2},{3,4},{5,6},{7,8},{9,10},{11,12},{13,14},{2,1},{4,3},{6,5},{... | collective-permute-start | bytes 786440 | tf_op jit(solution)/shard_map/ppermute | solution.py:289
  14.8 4.1 %copy-start.4 = (s32[1,1,2,2]{3,2,1,0:T(2,128)S(1)}, s32[1,1,2,2]{3,2,1,0:T(2,128)}, u32[]{:S(2)}) copy-start(s32[1,1,2,2]{3,2,1,0:T(2,128)} %param.10) | copy-start | bytes 52
  14.8 10.7 %collective-permute-start.3 = (f32[2,256,128]{2,1,0:T(8,128)S(1)}, f32[2,256,128]{2,1,0:T(8,128)S(1)}, u32[]{:S(2)}, u32[]{:S(2)}) collective-permute-start(f32[2,256,128]{2,1,0:T(8,128)S(1)} %get-tuple-element.18), channel_id=1, source_target_pairs={{0,1},{2,3},{4,5},{6,7},{8,9},{10,11},{12,13},{14,15},{1,0},{3,2},... | collective-permute-start | bytes 786440 | tf_op jit(solution)/shard_map/ppermute | solution.py:290
  19.0 0.7 copy-start.3
  31.1 27.0 %all-to-all-start = ((f32[64,16,128]{2,1,0:T(8,128)}), f32[64,16,128]{2,1,0:T(8,128)S(1)}, u32[]{:S(2)}, u32[]{:S(2)}) async-start(f32[64,16,128]{2,1,0:T(8,128)} %bitcast.4), calls=%async_computation | async-start | bytes 1048576 | tf_op jit(solution)/shard_map/all_to_all | solution.py:350
  47.0 18.4 %collective-permute-start.4 = (f32[2,256,128]{2,1,0:T(8,128)S(1)}, f32[2,256,128]{2,1,0:T(8,128)S(1)}, u32[]{:S(2)}, u32[]{:S(2)}) collective-permute-start(f32[2,256,128]{2,1,0:T(8,128)S(1)} %get-tuple-element.24), channel_id=1, source_target_pairs={{1,2},{3,4},{5,6},{7,8},{9,10},{11,12},{13,14},{2,1},{4,3},{6,5},{... | collective-permute-start | bytes 786440 | tf_op jit(solution)/shard_map/ppermute | solution.py:289
  52.0 13.3 %collective-permute-start.5 = (f32[2,256,128]{2,1,0:T(8,128)S(1)}, f32[2,256,128]{2,1,0:T(8,128)S(1)}, u32[]{:S(2)}, u32[]{:S(2)}) collective-permute-start(f32[2,256,128]{2,1,0:T(8,128)S(1)} %get-tuple-element.25), channel_id=1, source_target_pairs={{0,1},{2,3},{4,5},{6,7},{8,9},{10,11},{12,13},{14,15},{1,0},{3,2},... | collective-permute-start | bytes 786440 | tf_op jit(solution)/shard_map/ppermute | solution.py:290
  58.8 19.4 %all-to-all-start.1 = ((f32[8,16,128]{2,1,0:T(8,128)}), f32[8,16,128]{2,1,0:T(8,128)S(1)}, u32[]{:S(2)}, u32[]{:S(2)}) async-start(f32[8,16,128]{2,1,0:T(8,128)} %broadcast_in_dim.2), calls=%async_computation.1 | async-start | bytes 131072 | tf_op jit(solution)/shard_map/all_to_all | solution.py:353
  65.5 19.7 %collective-permute-start.6 = (f32[4,64,128]{2,1,0:T(8,128)S(1)}, f32[4,64,128]{2,1,0:T(8,128)S(1)}, u32[]{:S(2)}, u32[]{:S(2)}) collective-permute-start(f32[4,64,128]{2,1,0:T(8,128)S(1)} %get-tuple-element.27), channel_id=1, source_target_pairs={{16,32},{48,64},{80,96},{112,128},{144,160},{176,192},{208,224},{2... | collective-permute-start | bytes 393224 | tf_op jit(solution)/shard_map/ppermute | solution.py:299
  68.6 16.6 %collective-permute-start.7 = (f32[4,64,128]{2,1,0:T(8,128)S(1)}, f32[4,64,128]{2,1,0:T(8,128)S(1)}, u32[]{:S(2)}, u32[]{:S(2)}) collective-permute-start(f32[4,64,128]{2,1,0:T(8,128)S(1)} %get-tuple-element.28), channel_id=1, source_target_pairs={{0,16},{32,48},{64,80},{96,112},{128,144},{160,176},{192,208},{224... | collective-permute-start | bytes 393224 | tf_op jit(solution)/shard_map/ppermute | solution.py:299
  79.1 18.0 %all-to-all-start.2 = ((f32[64,16,128]{2,1,0:T(8,128)}), f32[64,16,128]{2,1,0:T(8,128)S(1)}, u32[]{:S(2)}, u32[]{:S(2)}) async-start(f32[64,16,128]{2,1,0:T(8,128)} %shard_map.83), calls=%async_computation.2 | async-start | bytes 1048576 | tf_op jit(solution)/shard_map/all_to_all | solution.py:361

commit v14 on v13

--- a/solution.py
+++ b/solution.py
@@ -70,17 +70,27 @@
     return real, pltpu.roll(jnp.where(low, from_left, from_right), HALF, 1)
 
 
-def columns_kernel(tile, from_cross, from_mate, tall, cross, mate):
+def tall_kernel(tile, from_cross, from_mate, tall):
     first = above_first()
     for p in range(4):
         below, above = by_parity(first, from_mate[p], from_cross[p])
         tall[p, :HALF] = above
         tall[p, HALF:HALF + TILE] = tile[p]
         tall[p, HALF + TILE:] = below
-    even = even_column()
+
+
+def columns_kernel(tile, from_cross, from_mate, cross, mate):
+    first, even = above_first(), even_column()
     for s in range(2):
-        to_right, to_left = pack_columns(tall[s], tall[2 + s])
-        mate[s], cross[s] = by_parity(even, to_right, to_left)
+        below = [None, None]
+        above = [None, None]
+        for c, p in enumerate((s, 2 + s)):
+            below[c], above[c] = by_parity(first, from_mate[p], from_cross[p])
+        for start, end, planes in (
+            (0, HALF, above), (HALF, HALF + TILE, (tile[s], tile[2 + s])), (HALF + TILE, 2 * TILE, below)
+        ):
+            to_right, to_left = pack_columns(*planes)
+            mate[s, start:end], cross[s, start:end] = by_parity(even, to_right, to_left)
 
 
 def operator_kernel(taps, probe, measured, ops, probe_near, measured_near, padded):
@@ -122,8 +132,9 @@
 
 def main_kernel(
     offsets, counts, tall, from_cross, from_mate, probe, measured, ops,
-    probe_grad, object_grad,
-    beside, field_high, field_low, mid_high, mid_low, wave_one, wave_two,
+    probe_far, object_grad,
+    probe_grad, sems, beside, field_high, field_low, mid_high, mid_low, wave_one, wave_two,
+    slope_one, slope_zero,
 ):
     even = even_column()
     for s in range(2):
@@ -197,25 +208,18 @@
 
     propagate(0, after_second)
 
-    def add(slot, s, m, real, imag):
-        for p, value in zip((s, 2 + s), (real, imag)):
-            if m == 0:
-                object_grad[slot, p] = value
-            else:
-                object_grad[slot, p] += value
-
     def after_third(slot, m, hr, hi):
         o1r, o1i = views[slot][1], views[slot][3]
-        wr, wi = wave_one[slot, m, 0], wave_one[slot, m, 1]
-        add(slot, 1, m, wr * hr + wi * hi, wr * hi - wi * hr)
+        slope_one[slot, m, 0] = hr
+        slope_one[slot, m, 1] = hi
         put_field(slot, m, hr * o1r + hi * o1i, hi * o1r - hr * o1i)
 
     propagate(2, after_third)
 
     def after_fourth(slot, m, hr, hi):
         o0r, o0i = views[slot][0], views[slot][2]
-        pr, pi = probe[m], probe[4 + m]
-        add(slot, 0, m, pr * hr + pi * hi, pr * hi - pi * hr)
+        slope_zero[slot, m, 0] = hr
+        slope_zero[slot, m, 1] = hi
         dr = hr * o0r + hi * o0i
         di = hi * o0r - hr * o0i
         if slot == 0:
@@ -226,6 +230,26 @@
             probe_grad[4 + m] += di
 
     propagate(2, after_fourth)
+    moves = []
+    for i in range(4):
+        planes = pl.ds(2 * i, 2)
+        moves.append(pltpu.make_async_copy(probe_grad.at[planes], probe_far.at[planes], sems.at[i]))
+        moves[i].start()
+    for slot in range(2):
+        for s, slope in enumerate((slope_zero, slope_one)):
+            real = imag = None
+            for m in range(4):
+                hr, hi = slope[slot, m, 0], slope[slot, m, 1]
+                if s == 0:
+                    wr, wi = probe[m], probe[4 + m]
+                else:
+                    wr, wi = wave_one[slot, m, 0], wave_one[slot, m, 1]
+                terms = wr * hr + wi * hi, wr * hi - wi * hr
+                real, imag = terms if m == 0 else (real + terms[0], imag + terms[1])
+            object_grad[slot, s] = real
+            object_grad[slot, 2 + s] = imag
+    for move in moves:
+        move.wait()
 
 
 def object_kernel(offsets, object_grad, grad_tall, cross, mate, grad_beside):
@@ -313,9 +337,8 @@
     cross = lax.dynamic_slice_in_dim(tile, upper, HALF, axis=1)
     mate = lax.dynamic_slice_in_dim(tile, HALF - upper, HALF, axis=1)
     rims = exchange_rows(cross, mate)
-    object_tall, cross, mate = call(
-        columns_kernel, (tall, tall_strip, tall_strip), [VM] * 3, tile, *rims
-    )
+    cross, mate = call(columns_kernel, (tall_strip, tall_strip), [VM] * 3, tile, *rims)
+    (object_tall,) = call(tall_kernel, (tall,), [VM] * 3, tile, *rims)
     strips = exchange_columns(cross, mate)
     ops, probe, targets = call(
         operator_kernel,
@@ -327,14 +350,16 @@
         main_kernel,
         (f32(8, TILE, TILE), f32(2, 4, TILE, TILE)), [SM, SM] + [VM] * 6,
         offsets.reshape(-1), counts.reshape(1, 1), object_tall, *strips, probe, targets, ops,
+        out_specs=[FAR, VM],
         scratch=[
+            pltpu.VMEM((8, TILE, TILE), F32),
+            pltpu.SemaphoreType.DMA((4,)),
             pltpu.VMEM((4, 256, TILE), F32),
             pltpu.VMEM((2, 256, 512), BF16),
             pltpu.VMEM((2, 256, 512), BF16),
             pltpu.VMEM((2, 512, 256), BF16),
             pltpu.VMEM((2, 512, 256), BF16),
-            pltpu.VMEM((2, 4, 2, TILE, TILE), F32),
-            pltpu.VMEM((2, 4, 2, TILE, TILE), F32),
+            *[pltpu.VMEM((2, 4, 2, TILE, TILE), F32)] * 4,
         ],
         flops=3_200_000_000, moved=4_000_000,
     )

time: 98.5 us -> 98.7 us (level)
    pallas_call x8 -> x9, Pallas kernels: 9.52 us -> 9.67 us  [call(): pl.pallas_call(kernel, out_shape=out_shape, in_specs=in_specs, out_specs=...]
where the time goes in v14:
time: 98.7 us; the launch traced here: 98 us
  starting transfers between devices  52.3 us (53%)
  waiting for transfers between devices  32 us (32%)
  Pallas kernels  9.67 us (10%)
  local copies, waits for them, and re-layouts  2.48 us (3%)
  between operations  1.5 us (2%)
    all_to_all x1, starting transfers between devices, body(): lax.all_to_all(probe_part.reshape(near, rows, TILE), NEAR_AXES, 0, 0, til...  14.9 us
    ppermute x4, starting transfers between devices, exchange_rows(): received.append(lax.ppermute(value, axes, pairs))  11.8 us
    all_to_all x1, waiting for transfers between devices, body(): gathered = lax.all_to_all(spread_share, NEAR_AXES, 0, 0, tiled=True)  11.1 us
    pallas_call x9, Pallas kernels, call(): pl.pallas_call(kernel, out_shape=out_shape, in_specs=in_specs, out_specs=...  9.67 us
    all_to_all x1, waiting for transfers between devices, body(): shares = lax.all_to_all(spread_share, FAR_AXES, 0, 0, tiled=True)  8.95 us
    ppermute x2, starting transfers between devices, exchange_columns(): from_cross = lax.ppermute(cross, COL_AXES, neighbours(count, 1))  7.47 us
    all_to_all x1, starting transfers between devices, body(): shares = lax.all_to_all(spread_share, FAR_AXES, 0, 0, tiled=True)  6.58 us
    all_to_all x1, starting transfers between devices, body(): gathered = lax.all_to_all(spread_share, NEAR_AXES, 0, 0, tiled=True)  6.16 us
  transfers between devices with their start and end apart: 11, of which 5 were waited for; matrix products, arithmetic and copies ran while one was open for 1% of the time, Pallas kernels for 3%

profile of v14, /device:TPU:1, one launch (start us, length us, event | category | flops | bytes accessed | tf_op | source)
XLA Modules:
  0.0 98.0 jit_solution(13094379078597290227)
XLA Ops:
  0.7 1.1 %constant_dynamic-slice_fusion = (f32[4,64,128]{2,1,0:T(8,128)S(1)}, f32[4,64,128]{2,1,0:T(8,128)S(1)}) fusion(f32[4,128,128]{2,1,0:T(8,128)} %bitcast.7, s32[]{:T(128)S(6)} %select_n.9, s32[]{:T(128)S(6)} %select_n.8), kind=kLoop, calls=%fused_computation | loop fusion | bytes 524296 | tf_op jit(solution)/shard_map/dynamic_slice | solution.py:338
  1.7 0.7 collective-permute-start.1
  2.4 7.4 %collective-permute-start = (f32[4,64,128]{2,1,0:T(8,128)S(1)}, f32[4,64,128]{2,1,0:T(8,128)S(1)}, u32[]{:S(2)}, u32[]{:S(2)}) collective-permute-start(f32[4,64,128]{2,1,0:T(8,128)S(1)} %get-tuple-element.29), channel_id=1, source_target_pairs={{16,32},{48,64},{80,96},{112,128},{144,160},{176,192},{208,224},{2... | collective-permute-start | bytes 393224 | tf_op jit(solution)/shard_map/ppermute | solution.py:323
  9.8 2.4 %collective-permute-done.from_cross = f32[4,64,128]{2,1,0:T(8,128)S(1)} collective-permute-done((f32[4,64,128]{2,1,0:T(8,128)S(1)}, f32[4,64,128]{2,1,0:T(8,128)S(1)}, u32[]{:S(2)}, u32[]{:S(2)}) %collective-permute-start) | collective-permute-done | bytes 131104 | tf_op jit(solution)/shard_map/ppermute | solution.py:323
  12.4 2.4 %collective-permute-start.2 = (f32[2,256,128]{2,1,0:T(8,128)S(1)}, f32[2,256,128]{2,1,0:T(8,128)S(1)}, u32[]{:S(2)}, u32[]{:S(2)}) collective-permute-start(f32[2,256,128]{2,1,0:T(8,128)S(1)} %get-tuple-element.15), channel_id=1, source_target_pairs={{1,2},{3,4},{5,6},{7,8},{9,10},{11,12},{13,14},{2,1},{4,3},{6,5},{... | collective-permute-start | bytes 786440 | tf_op jit(solution)/shard_map/ppermute | solution.py:313
  14.8 3.4 %collective-permute-start.3 = (f32[2,256,128]{2,1,0:T(8,128)S(1)}, f32[2,256,128]{2,1,0:T(8,128)S(1)}, u32[]{:S(2)}, u32[]{:S(2)}) collective-permute-start(f32[2,256,128]{2,1,0:T(8,128)S(1)} %get-tuple-element.16), channel_id=1, source_target_pairs={{0,1},{2,3},{4,5},{6,7},{8,9},{10,11},{12,13},{14,15},{1,0},{3,2},... | collective-permute-start | bytes 786440 | tf_op jit(solution)/shard_map/ppermute | solution.py:314
  19.0 0.7 copy-done.3
  20.0 5.5 %collective-permute-done.2.from_cross = f32[2,256,128]{2,1,0:T(8,128)S(1)} collective-permute-done((f32[2,256,128]{2,1,0:T(8,128)S(1)}, f32[2,256,128]{2,1,0:T(8,128)S(1)}, u32[]{:S(2)}, u32[]{:S(2)}) %collective-permute-start.2) | collective-permute-done | bytes 262176 | tf_op jit(solution)/shard_map/ppermute | solution.py:313
  25.5 5.7 %shard_map.80 = (f32[8,128,128]{2,1,0:T(8,128)}, f32[2,4,128,128]{3,2,1,0:T(8,128)S(1)}) custom-call(s32[4]{0:T(128)S(1)} %reshape.30.offsets, s32[1,1]{1,0:T(1,128)S(6)} %copy.8.counts, f32[4,256,128]{2,1,0:T(8,128)S(1)} %shard_map.77.tall, f32[2,256,128]{2,1,0:T(8,128)S(1)} %collective-permute-done.2.from_cross, ...), custom_call_target="tpu_custom_call" | custom-call | flops 3200000000 | bytes 4000000 | tf_op jit(solution)/shard_map/pallas_call | solution.py:29
  31.2 14.9 %all-to-all-start = ((f32[64,16,128]{2,1,0:T(8,128)}), f32[64,16,128]{2,1,0:T(8,128)S(1)}, u32[]{:S(2)}, u32[]{:S(2)}) async-start(f32[64,16,128]{2,1,0:T(8,128)} %bitcast.4), calls=%async_computation | async-start | bytes 1048576 | tf_op jit(solution)/shard_map/all_to_all | solution.py:375
  46.2 0.9 shard_map.81
  47.1 5.0 %collective-permute-start.4 = (f32[2,256,128]{2,1,0:T(8,128)S(1)}, f32[2,256,128]{2,1,0:T(8,128)S(1)}, u32[]{:S(2)}, u32[]{:S(2)}) collective-permute-start(f32[2,256,128]{2,1,0:T(8,128)S(1)} %get-tuple-element.22), channel_id=1, source_target_pairs={{1,2},{3,4},{5,6},{7,8},{9,10},{11,12},{13,14},{2,1},{4,3},{6,5},{... | collective-permute-start | bytes 786440 | tf_op jit(solution)/shard_map/ppermute | solution.py:313
  52.2 1.9 %collective-permute-start.5 = (f32[2,256,128]{2,1,0:T(8,128)S(1)}, f32[2,256,128]{2,1,0:T(8,128)S(1)}, u32[]{:S(2)}, u32[]{:S(2)}) collective-permute-start(f32[2,256,128]{2,1,0:T(8,128)S(1)} %get-tuple-element.23), channel_id=1, source_target_pairs={{0,1},{2,3},{4,5},{6,7},{8,9},{10,11},{12,13},{14,15},{1,0},{3,2},... | collective-permute-start | bytes 786440 | tf_op jit(solution)/shard_map/ppermute | solution.py:314
  54.1 4.1 %all-to-all-done = f32[64,16,128]{2,1,0:T(8,128)S(1)} async-done(((f32[64,16,128]{2,1,0:T(8,128)}), f32[64,16,128]{2,1,0:T(8,128)S(1)}, u32[]{:S(2)}, u32[]{:S(2)}) %all-to-all-start) | async-done | bytes 524320 | tf_op jit(solution)/shard_map/all_to_all | solution.py:375
  58.3 0.6 broadcast_in_dim.2
  58.9 6.6 %all-to-all-start.1 = ((f32[8,16,128]{2,1,0:T(8,128)}), f32[8,16,128]{2,1,0:T(8,128)S(1)}, u32[]{:S(2)}, u32[]{:S(2)}) async-start(f32[8,16,128]{2,1,0:T(8,128)} %broadcast_in_dim.2), calls=%async_computation.1 | async-start | bytes 131072 | tf_op jit(solution)/shard_map/all_to_all | solution.py:378
  65.7 3.1 %collective-permute-start.6 = (f32[4,64,128]{2,1,0:T(8,128)S(1)}, f32[4,64,128]{2,1,0:T(8,128)S(1)}, u32[]{:S(2)}, u32[]{:S(2)}) collective-permute-start(f32[4,64,128]{2,1,0:T(8,128)S(1)} %get-tuple-element.25), channel_id=1, source_target_pairs={{16,32},{48,64},{80,96},{112,128},{144,160},{176,192},{208,224},{2... | collective-permute-start | bytes 393224 | tf_op jit(solution)/shard_map/ppermute | solution.py:323
  68.7 0.7 collective-permute-start.7
  69.4 8.9 %all-to-all-done.1.shares = f32[8,16,128]{2,1,0:T(8,128)S(1)} async-done(((f32[8,16,128]{2,1,0:T(8,128)}), f32[8,16,128]{2,1,0:T(8,128)S(1)}, u32[]{:S(2)}, u32[]{:S(2)}) %all-to-all-start.1) | async-done | bytes 65568 | tf_op jit(solution)/shard_map/all_to_all | solution.py:378
  78.4 0.8 shard_map.84
  79.2 6.2 %all-to-all-start.2 = ((f32[64,16,128]{2,1,0:T(8,128)}), f32[64,16,128]{2,1,0:T(8,128)S(1)}, u32[]{:S(2)}, u32[]{:S(2)}) async-start(f32[64,16,128]{2,1,0:T(8,128)} %shard_map.84), calls=%async_computation.2 | async-start | bytes 1048576 | tf_op jit(solution)/shard_map/all_to_all | solution.py:386
  85.4 0.7 shard_map.83
  86.1 11.1 %all-to-all-done.2 = f32[64,16,128]{2,1,0:T(8,128)S(1)} async-done(((f32[64,16,128]{2,1,0:T(8,128)}), f32[64,16,128]{2,1,0:T(8,128)S(1)}, u32[]{:S(2)}, u32[]{:S(2)}) %all-to-all-start.2) | async-done | bytes 524320 | tf_op jit(solution)/shard_map/all_to_all | solution.py:386
  97.2 0.8 shard_map.85
  (21 shorter events, 0.8 us)
Async XLA Ops:
  0.6 11.6 %copy-start = (f32[2,2,128,128]{3,2,1,0:T(8,128)S(1)}, f32[2,2,128,128]{3,2,1,0:T(8,128)}, u32[]{:S(2)}) copy-start(f32[2,2,128,128]{3,2,1,0:T(8,128)} %param.6) | copy-start | bytes 786436
  0.6 18.3 %copy-start.1 = (f32[2,4,128,128]{3,2,1,0:T(8,128)S(1)}, f32[2,4,128,128]{3,2,1,0:T(8,128)}, u32[]{:S(2)}) copy-start(f32[2,4,128,128]{3,2,1,0:T(8,128)} %param.7) | copy-start | bytes 1572868
  1.7 8.1 %collective-permute-start.1 = (f32[4,64,128]{2,1,0:T(8,128)S(1)}, f32[4,64,128]{2,1,0:T(8,128)S(1)}, u32[]{:S(2)}, u32[]{:S(2)}) collective-permute-start(f32[4,64,128]{2,1,0:T(8,128)S(1)} %get-tuple-element.28), channel_id=1, source_target_pairs={{0,16},{32,48},{64,80},{96,112},{128,144},{160,176},{192,208},{224... | collective-permute-start | bytes 393224 | tf_op jit(solution)/shard_map/ppermute | solution.py:323
  2.4 16.6 %copy-start.2 = (f32[1,1,2,128,128]{4,3,2,1,0:T(8,128)S(1)}, f32[1,1,2,128,128]{4,3,2,1,0:T(8,128)}, u32[]{:S(2)}) copy-start(f32[1,1,2,128,128]{4,3,2,1,0:T(8,128)} %param.9) | copy-start | bytes 393220
  2.4 9.8 %collective-permute-start = (f32[4,64,128]{2,1,0:T(8,128)S(1)}, f32[4,64,128]{2,1,0:T(8,128)S(1)}, u32[]{:S(2)}, u32[]{:S(2)}) collective-permute-start(f32[4,64,128]{2,1,0:T(8,128)S(1)} %get-tuple-element.29), channel_id=1, source_target_pairs={{16,32},{48,64},{80,96},{112,128},{144,160},{176,192},{208,224},{2... | collective-permute-start | bytes 393224 | tf_op jit(solution)/shard_map/ppermute | solution.py:323
  12.4 13.2 %collective-permute-start.2 = (f32[2,256,128]{2,1,0:T(8,128)S(1)}, f32[2,256,128]{2,1,0:T(8,128)S(1)}, u32[]{:S(2)}, u32[]{:S(2)}) collective-permute-start(f32[2,256,128]{2,1,0:T(8,128)S(1)} %get-tuple-element.15), channel_id=1, source_target_pairs={{1,2},{3,4},{5,6},{7,8},{9,10},{11,12},{13,14},{2,1},{4,3},{6,5},{... | collective-permute-start | bytes 786440 | tf_op jit(solution)/shard_map/ppermute | solution.py:313
  14.8 4.1 %copy-start.4 = (s32[1,1,2,2]{3,2,1,0:T(2,128)S(1)}, s32[1,1,2,2]{3,2,1,0:T(2,128)}, u32[]{:S(2)}) copy-start(s32[1,1,2,2]{3,2,1,0:T(2,128)} %param.10) | copy-start | bytes 52
  14.8 10.7 %collective-permute-start.3 = (f32[2,256,128]{2,1,0:T(8,128)S(1)}, f32[2,256,128]{2,1,0:T(8,128)S(1)}, u32[]{:S(2)}, u32[]{:S(2)}) collective-permute-start(f32[2,256,128]{2,1,0:T(8,128)S(1)} %get-tuple-element.16), channel_id=1, source_target_pairs={{0,1},{2,3},{4,5},{6,7},{8,9},{10,11},{12,13},{14,15},{1,0},{3,2},... | collective-permute-start | bytes 786440 | tf_op jit(solution)/shard_map/ppermute | solution.py:314
  19.0 0.7 copy-start.3
  31.2 27.0 %all-to-all-start = ((f32[64,16,128]{2,1,0:T(8,128)}), f32[64,16,128]{2,1,0:T(8,128)S(1)}, u32[]{:S(2)}, u32[]{:S(2)}) async-start(f32[64,16,128]{2,1,0:T(8,128)} %bitcast.4), calls=%async_computation | async-start | bytes 1048576 | tf_op jit(solution)/shard_map/all_to_all | solution.py:375
  47.1 18.4 %collective-permute-start.4 = (f32[2,256,128]{2,1,0:T(8,128)S(1)}, f32[2,256,128]{2,1,0:T(8,128)S(1)}, u32[]{:S(2)}, u32[]{:S(2)}) collective-permute-start(f32[2,256,128]{2,1,0:T(8,128)S(1)} %get-tuple-element.22), channel_id=1, source_target_pairs={{1,2},{3,4},{5,6},{7,8},{9,10},{11,12},{13,14},{2,1},{4,3},{6,5},{... | collective-permute-start | bytes 786440 | tf_op jit(solution)/shard_map/ppermute | solution.py:313
  52.2 13.3 %collective-permute-start.5 = (f32[2,256,128]{2,1,0:T(8,128)S(1)}, f32[2,256,128]{2,1,0:T(8,128)S(1)}, u32[]{:S(2)}, u32[]{:S(2)}) collective-permute-start(f32[2,256,128]{2,1,0:T(8,128)S(1)} %get-tuple-element.23), channel_id=1, source_target_pairs={{0,1},{2,3},{4,5},{6,7},{8,9},{10,11},{12,13},{14,15},{1,0},{3,2},... | collective-permute-start | bytes 786440 | tf_op jit(solution)/shard_map/ppermute | solution.py:314
  58.9 19.5 %all-to-all-start.1 = ((f32[8,16,128]{2,1,0:T(8,128)}), f32[8,16,128]{2,1,0:T(8,128)S(1)}, u32[]{:S(2)}, u32[]{:S(2)}) async-start(f32[8,16,128]{2,1,0:T(8,128)} %broadcast_in_dim.2), calls=%async_computation.1 | async-start | bytes 131072 | tf_op jit(solution)/shard_map/all_to_all | solution.py:378
  65.7 19.7 %collective-permute-start.6 = (f32[4,64,128]{2,1,0:T(8,128)S(1)}, f32[4,64,128]{2,1,0:T(8,128)S(1)}, u32[]{:S(2)}, u32[]{:S(2)}) collective-permute-start(f32[4,64,128]{2,1,0:T(8,128)S(1)} %get-tuple-element.25), channel_id=1, source_target_pairs={{16,32},{48,64},{80,96},{112,128},{144,160},{176,192},{208,224},{2... | collective-permute-start | bytes 393224 | tf_op jit(solution)/shard_map/ppermute | solution.py:323
  68.7 16.6 %collective-permute-start.7 = (f32[4,64,128]{2,1,0:T(8,128)S(1)}, f32[4,64,128]{2,1,0:T(8,128)S(1)}, u32[]{:S(2)}, u32[]{:S(2)}) collective-permute-start(f32[4,64,128]{2,1,0:T(8,128)S(1)} %get-tuple-element.26), channel_id=1, source_target_pairs={{0,16},{32,48},{64,80},{96,112},{128,144},{160,176},{192,208},{224... | collective-permute-start | bytes 393224 | tf_op jit(solution)/shard_map/ppermute | solution.py:323
  79.2 18.0 %all-to-all-start.2 = ((f32[64,16,128]{2,1,0:T(8,128)}), f32[64,16,128]{2,1,0:T(8,128)S(1)}, u32[]{:S(2)}, u32[]{:S(2)}) async-start(f32[64,16,128]{2,1,0:T(8,128)} %shard_map.84), calls=%async_computation.2 | async-start | bytes 1048576 | tf_op jit(solution)/shard_map/all_to_all | solution.py:386

commit v15 on v13

--- a/solution.py
+++ b/solution.py
@@ -13,8 +13,9 @@
 BF16 = jnp.bfloat16
 ROW_AXES = ("xl", "za", "zb")
 COL_AXES = ("y", "xh", "core")
-NEAR_AXES = ("xl", "zb", "y", "xh", "core")
-FAR_AXES = ("za",)
+PLANE_AXES = ("xl", "y", "xh", "core")
+NEAR_AXES = PLANE_AXES + ("zb",)
+FAR_AXES = ("za", "zb")
 VMEM_LIMIT = 12 * 1024 * 1024
 TILE = 128
 HALF = 64
@@ -246,9 +247,14 @@
 
 
 def spread_sum(scale, shares, spread_share):
-    share = jnp.sum(shares[...], axis=0) * scale
-    for i in range(spread_share.shape[0]):
-        spread_share[i] = share
+    count, rows = shares.shape[:2]
+    for member in range(2):
+        share = shares[member]
+        for i in range(member + 2, count, 2):
+            share += shares[i]
+        share *= scale
+        for i in range(spread_share.shape[0]):
+            spread_share[i, member * rows:(member + 1) * rows] = share
 
 
 def fold_columns_kernel(grad_tall, from_cross, from_mate, part, cross, mate):
@@ -345,20 +351,20 @@
     )
 
     near = lax.axis_size(NEAR_AXES)
-    far = lax.axis_size(FAR_AXES)
+    far, plane = lax.axis_size(FAR_AXES), lax.axis_size(PLANE_AXES)
     rows = 8 * TILE // near
     shares = lax.all_to_all(probe_part.reshape(near, rows, TILE), NEAR_AXES, 0, 0, tiled=True)
     spread_share = jnp.broadcast_to(jnp.sum(shares, axis=0)[None], (far, rows, TILE))
     strips = exchange_columns(cross, mate)
     shares = lax.all_to_all(spread_share, FAR_AXES, 0, 0, tiled=True)
     part, cross, mate = call(
-        fold_columns_kernel, (planes, half, half), [VM] * 3, grad_tall, *strips
+        fold_columns_kernel, (planes, half, half), [VM] * 3, grad_tall, *strips, flops=BESIDE, moved=1
     )
     rims = exchange_rows(cross, mate)
     (spread_share,) = call(
-        functools.partial(spread_sum, 1.0 / math.sqrt(near * far)), (f32(near, rows, TILE),), [VM], shares
-    )
-    gathered = lax.all_to_all(spread_share, NEAR_AXES, 0, 0, tiled=True)
+        functools.partial(spread_sum, 1.0 / math.sqrt(plane * far)), (f32(plane, 2 * rows, TILE),), [VM], shares
+    )
+    gathered = lax.all_to_all(spread_share, PLANE_AXES, 0, 0, tiled=True)
     (result,) = call(
         fold_rows_kernel, (planes,), [VM] * 3, part, *rims, flops=BESIDE, moved=1
     )

time: 98.5 us -> 99.1 us (level)
  starting transfers between devices: 52.3 us -> 53.8 us
  waiting for transfers between devices: 32 us -> 30.9 us
    all_to_all x1, starting transfers between devices: 6.16 us -> 7.37 us  [body(): gathered = lax.all_to_all(spread_share, PLANE_AXES, 0, 0, tiled=True)]
    all_to_all x1, waiting for transfers between devices: 8.95 us -> 7.86 us  [body(): shares = lax.all_to_all(spread_share, FAR_AXES, 0, 0, tiled=True)]
where the time goes in v15:
time: 99.1 us; the launch traced here: 98.4 us
  starting transfers between devices  53.8 us (54%)
  waiting for transfers between devices  30.9 us (31%)
  Pallas kernels  9.56 us (10%)
  local copies, waits for them, and re-layouts  2.51 us (3%)
  between operations  1.5 us (2%)
    all_to_all x1, starting transfers between devices, body(): lax.all_to_all(probe_part.reshape(near, rows, TILE), NEAR_AXES, 0, 0, til...  14.9 us
    ppermute x4, starting transfers between devices, exchange_rows(): received.append(lax.ppermute(value, axes, pairs))  12 us
    all_to_all x1, waiting for transfers between devices, body(): gathered = lax.all_to_all(spread_share, PLANE_AXES, 0, 0, tiled=True)  10.8 us
    pallas_call x8, Pallas kernels, call(): pl.pallas_call(kernel, out_shape=out_shape, in_specs=in_specs, out_specs=...  9.56 us
    all_to_all x1, waiting for transfers between devices, body(): shares = lax.all_to_all(spread_share, FAR_AXES, 0, 0, tiled=True)  7.86 us
    ppermute x2, starting transfers between devices, exchange_columns(): from_cross = lax.ppermute(cross, COL_AXES, neighbours(count, 1))  7.47 us
    all_to_all x1, starting transfers between devices, body(): gathered = lax.all_to_all(spread_share, PLANE_AXES, 0, 0, tiled=True)  7.37 us
    all_to_all x1, starting transfers between devices, body(): shares = lax.all_to_all(spread_share, FAR_AXES, 0, 0, tiled=True)  6.68 us
  transfers between devices with their start and end apart: 11, of which 5 were waited for; matrix products, arithmetic and copies ran while one was open for 1% of the time, Pallas kernels for 3%

profile of v15, /device:TPU:1, one launch (start us, length us, event | category | flops | bytes accessed | tf_op | source)
XLA Modules:
  0.0 98.4 jit_solution(15268307851347616780)
XLA Ops:
  0.7 1.1 %constant_dynamic-slice_fusion = (f32[4,64,128]{2,1,0:T(8,128)S(1)}, f32[4,64,128]{2,1,0:T(8,128)S(1)}) fusion(f32[4,128,128]{2,1,0:T(8,128)} %bitcast.8, s32[]{:T(128)S(6)} %select_n.9, s32[]{:T(128)S(6)} %select_n.8), kind=kLoop, calls=%fused_computation | loop fusion | bytes 524296 | tf_op jit(solution)/shard_map/dynamic_slice | solution.py:320
  1.7 0.7 collective-permute-start.1
  2.4 7.4 %collective-permute-start = (f32[4,64,128]{2,1,0:T(8,128)S(1)}, f32[4,64,128]{2,1,0:T(8,128)S(1)}, u32[]{:S(2)}, u32[]{:S(2)}) collective-permute-start(f32[4,64,128]{2,1,0:T(8,128)S(1)} %get-tuple-element.31), channel_id=1, source_target_pairs={{16,32},{48,64},{80,96},{112,128},{144,160},{176,192},{208,224},{2... | collective-permute-start | bytes 393224 | tf_op jit(solution)/shard_map/ppermute | solution.py:305
  9.8 2.4 %collective-permute-done.from_cross = f32[4,64,128]{2,1,0:T(8,128)S(1)} collective-permute-done((f32[4,64,128]{2,1,0:T(8,128)S(1)}, f32[4,64,128]{2,1,0:T(8,128)S(1)}, u32[]{:S(2)}, u32[]{:S(2)}) %collective-permute-start) | collective-permute-done | bytes 131104 | tf_op jit(solution)/shard_map/ppermute | solution.py:305
  12.4 2.4 %collective-permute-start.2 = (f32[2,256,128]{2,1,0:T(8,128)S(1)}, f32[2,256,128]{2,1,0:T(8,128)S(1)}, u32[]{:S(2)}, u32[]{:S(2)}) collective-permute-start(f32[2,256,128]{2,1,0:T(8,128)S(1)} %get-tuple-element.17), channel_id=1, source_target_pairs={{1,2},{3,4},{5,6},{7,8},{9,10},{11,12},{13,14},{2,1},{4,3},{6,5},{... | collective-permute-start | bytes 786440 | tf_op jit(solution)/shard_map/ppermute | solution.py:295
  14.8 3.4 %collective-permute-start.3 = (f32[2,256,128]{2,1,0:T(8,128)S(1)}, f32[2,256,128]{2,1,0:T(8,128)S(1)}, u32[]{:S(2)}, u32[]{:S(2)}) collective-permute-start(f32[2,256,128]{2,1,0:T(8,128)S(1)} %get-tuple-element.18), channel_id=1, source_target_pairs={{0,1},{2,3},{4,5},{6,7},{8,9},{10,11},{12,13},{14,15},{1,0},{3,2},... | collective-permute-start | bytes 786440 | tf_op jit(solution)/shard_map/ppermute | solution.py:296
  19.0 0.7 copy-done.3
  20.0 5.5 %collective-permute-done.2.from_cross = f32[2,256,128]{2,1,0:T(8,128)S(1)} collective-permute-done((f32[2,256,128]{2,1,0:T(8,128)S(1)}, f32[2,256,128]{2,1,0:T(8,128)S(1)}, u32[]{:S(2)}, u32[]{:S(2)}) %collective-permute-start.2) | collective-permute-done | bytes 262176 | tf_op jit(solution)/shard_map/ppermute | solution.py:295
  25.5 5.6 %shard_map.79 = (f32[8,128,128]{2,1,0:T(8,128)}, f32[2,4,128,128]{3,2,1,0:T(8,128)S(1)}) custom-call(s32[4]{0:T(128)S(1)} %reshape.30.offsets, s32[1,1]{1,0:T(1,128)S(6)} %copy.8.counts, f32[4,256,128]{2,1,0:T(8,128)S(1)} %get-tuple-element.16.tall, f32[2,256,128]{2,1,0:T(8,128)S(1)} %collective-permute-done.2.from_cross, ...), custom_call_target="tpu_custom_call" | custom-call | flops 3200000000 | bytes 4000000 | tf_op jit(solution)/shard_map/pallas_call | solution.py:30
  31.1 14.9 %all-to-all-start = ((f32[64,16,128]{2,1,0:T(8,128)}), f32[64,16,128]{2,1,0:T(8,128)S(1)}, u32[]{:S(2)}, u32[]{:S(2)}) async-start(f32[64,16,128]{2,1,0:T(8,128)} %bitcast.4), calls=%async_computation | async-start | bytes 1048576 | tf_op jit(solution)/shard_map/all_to_all | solution.py:356
  46.1 0.9 shard_map.80
  47.0 5.0 %collective-permute-start.4 = (f32[2,256,128]{2,1,0:T(8,128)S(1)}, f32[2,256,128]{2,1,0:T(8,128)S(1)}, u32[]{:S(2)}, u32[]{:S(2)}) collective-permute-start(f32[2,256,128]{2,1,0:T(8,128)S(1)} %get-tuple-element.24), channel_id=1, source_target_pairs={{1,2},{3,4},{5,6},{7,8},{9,10},{11,12},{13,14},{2,1},{4,3},{6,5},{... | collective-permute-start | bytes 786440 | tf_op jit(solution)/shard_map/ppermute | solution.py:295
  52.0 1.9 %collective-permute-start.5 = (f32[2,256,128]{2,1,0:T(8,128)S(1)}, f32[2,256,128]{2,1,0:T(8,128)S(1)}, u32[]{:S(2)}, u32[]{:S(2)}) collective-permute-start(f32[2,256,128]{2,1,0:T(8,128)S(1)} %get-tuple-element.25), channel_id=1, source_target_pairs={{0,1},{2,3},{4,5},{6,7},{8,9},{10,11},{12,13},{14,15},{1,0},{3,2},... | collective-permute-start | bytes 786440 | tf_op jit(solution)/shard_map/ppermute | solution.py:296
  54.0 4.3 %all-to-all-done = f32[64,16,128]{2,1,0:T(8,128)S(1)} async-done(((f32[64,16,128]{2,1,0:T(8,128)}), f32[64,16,128]{2,1,0:T(8,128)S(1)}, u32[]{:S(2)}, u32[]{:S(2)}) %all-to-all-start) | async-done | bytes 524320 | tf_op jit(solution)/shard_map/all_to_all | solution.py:356
  58.4 0.7 broadcast_in_dim.2
  59.1 6.7 %all-to-all-start.1 = ((f32[16,16,128]{2,1,0:T(8,128)}), f32[16,16,128]{2,1,0:T(8,128)S(1)}, u32[]{:S(2)}, u32[]{:S(2)}) async-start(f32[16,16,128]{2,1,0:T(8,128)} %broadcast_in_dim.2), calls=%async_computation.1 | async-start | bytes 262144 | tf_op jit(solution)/shard_map/all_to_all | solution.py:359
  65.9 3.3 %collective-permute-start.6 = (f32[4,64,128]{2,1,0:T(8,128)S(1)}, f32[4,64,128]{2,1,0:T(8,128)S(1)}, u32[]{:S(2)}, u32[]{:S(2)}) collective-permute-start(f32[4,64,128]{2,1,0:T(8,128)S(1)} %get-tuple-element.27), channel_id=1, source_target_pairs={{16,32},{48,64},{80,96},{112,128},{144,160},{176,192},{208,224},{2... | collective-permute-start | bytes 393224 | tf_op jit(solution)/shard_map/ppermute | solution.py:305
  69.2 0.7 collective-permute-start.7
  69.9 7.9 %all-to-all-done.1.shares = f32[16,16,128]{2,1,0:T(8,128)S(1)} async-done(((f32[16,16,128]{2,1,0:T(8,128)}), f32[16,16,128]{2,1,0:T(8,128)S(1)}, u32[]{:S(2)}, u32[]{:S(2)}) %all-to-all-start.1) | async-done | bytes 131104 | tf_op jit(solution)/shard_map/all_to_all | solution.py:359
  77.7 0.9 shard_map.83
  78.6 7.4 %all-to-all-start.2 = ((f32[32,32,128]{2,1,0:T(8,128)}), f32[32,32,128]{2,1,0:T(8,128)S(1)}, u32[]{:S(2)}, u32[]{:S(2)}) async-start(f32[32,32,128]{2,1,0:T(8,128)} %shard_map.83), calls=%async_computation.2 | async-start | bytes 1048576 | tf_op jit(solution)/shard_map/all_to_all | solution.py:367
  86.0 0.7 shard_map.82
  86.7 10.8 %all-to-all-done.2 = f32[32,32,128]{2,1,0:T(8,128)S(1)} async-done(((f32[32,32,128]{2,1,0:T(8,128)}), f32[32,32,128]{2,1,0:T(8,128)S(1)}, u32[]{:S(2)}, u32[]{:S(2)}) %all-to-all-start.2) | async-done | bytes 524320 | tf_op jit(solution)/shard_map/all_to_all | solution.py:367
  97.5 0.8 shard_map.84
  (20 shorter events, 0.8 us)
Async XLA Ops:
  0.6 11.6 %copy-start = (f32[2,2,128,128]{3,2,1,0:T(8,128)S(1)}, f32[2,2,128,128]{3,2,1,0:T(8,128)}, u32[]{:S(2)}) copy-start(f32[2,2,128,128]{3,2,1,0:T(8,128)} %param.6) | copy-start | bytes 786436
  0.6 18.3 %copy-start.1 = (f32[2,4,128,128]{3,2,1,0:T(8,128)S(1)}, f32[2,4,128,128]{3,2,1,0:T(8,128)}, u32[]{:S(2)}) copy-start(f32[2,4,128,128]{3,2,1,0:T(8,128)} %param.7) | copy-start | bytes 1572868
  1.7 8.1 %collective-permute-start.1 = (f32[4,64,128]{2,1,0:T(8,128)S(1)}, f32[4,64,128]{2,1,0:T(8,128)S(1)}, u32[]{:S(2)}, u32[]{:S(2)}) collective-permute-start(f32[4,64,128]{2,1,0:T(8,128)S(1)} %get-tuple-element.30), channel_id=1, source_target_pairs={{0,16},{32,48},{64,80},{96,112},{128,144},{160,176},{192,208},{224... | collective-permute-start | bytes 393224 | tf_op jit(solution)/shard_map/ppermute | solution.py:305
  2.4 16.6 %copy-start.2 = (f32[1,1,2,128,128]{4,3,2,1,0:T(8,128)S(1)}, f32[1,1,2,128,128]{4,3,2,1,0:T(8,128)}, u32[]{:S(2)}) copy-start(f32[1,1,2,128,128]{4,3,2,1,0:T(8,128)} %param.9) | copy-start | bytes 393220
  2.4 9.8 %collective-permute-start = (f32[4,64,128]{2,1,0:T(8,128)S(1)}, f32[4,64,128]{2,1,0:T(8,128)S(1)}, u32[]{:S(2)}, u32[]{:S(2)}) collective-permute-start(f32[4,64,128]{2,1,0:T(8,128)S(1)} %get-tuple-element.31), channel_id=1, source_target_pairs={{16,32},{48,64},{80,96},{112,128},{144,160},{176,192},{208,224},{2... | collective-permute-start | bytes 393224 | tf_op jit(solution)/shard_map/ppermute | solution.py:305
  12.4 13.2 %collective-permute-start.2 = (f32[2,256,128]{2,1,0:T(8,128)S(1)}, f32[2,256,128]{2,1,0:T(8,128)S(1)}, u32[]{:S(2)}, u32[]{:S(2)}) collective-permute-start(f32[2,256,128]{2,1,0:T(8,128)S(1)} %get-tuple-element.17), channel_id=1, source_target_pairs={{1,2},{3,4},{5,6},{7,8},{9,10},{11,12},{13,14},{2,1},{4,3},{6,5},{... | collective-permute-start | bytes 786440 | tf_op jit(solution)/shard_map/ppermute | solution.py:295
  14.8 4.1 %copy-start.4 = (s32[1,1,2,2]{3,2,1,0:T(2,128)S(1)}, s32[1,1,2,2]{3,2,1,0:T(2,128)}, u32[]{:S(2)}) copy-start(s32[1,1,2,2]{3,2,1,0:T(2,128)} %param.10) | copy-start | bytes 52
  14.8 10.7 %collective-permute-start.3 = (f32[2,256,128]{2,1,0:T(8,128)S(1)}, f32[2,256,128]{2,1,0:T(8,128)S(1)}, u32[]{:S(2)}, u32[]{:S(2)}) collective-permute-start(f32[2,256,128]{2,1,0:T(8,128)S(1)} %get-tuple-element.18), channel_id=1, source_target_pairs={{0,1},{2,3},{4,5},{6,7},{8,9},{10,11},{12,13},{14,15},{1,0},{3,2},... | collective-permute-start | bytes 786440 | tf_op jit(solution)/shard_map/ppermute | solution.py:296
  19.0 0.7 copy-start.3
  31.1 27.2 %all-to-all-start = ((f32[64,16,128]{2,1,0:T(8,128)}), f32[64,16,128]{2,1,0:T(8,128)S(1)}, u32[]{:S(2)}, u32[]{:S(2)}) async-start(f32[64,16,128]{2,1,0:T(8,128)} %bitcast.4), calls=%async_computation | async-start | bytes 1048576 | tf_op jit(solution)/shard_map/all_to_all | solution.py:356
  47.0 18.8 %collective-permute-start.4 = (f32[2,256,128]{2,1,0:T(8,128)S(1)}, f32[2,256,128]{2,1,0:T(8,128)S(1)}, u32[]{:S(2)}, u32[]{:S(2)}) collective-permute-start(f32[2,256,128]{2,1,0:T(8,128)S(1)} %get-tuple-element.24), channel_id=1, source_target_pairs={{1,2},{3,4},{5,6},{7,8},{9,10},{11,12},{13,14},{2,1},{4,3},{6,5},{... | collective-permute-start | bytes 786440 | tf_op jit(solution)/shard_map/ppermute | solution.py:295
  52.0 13.7 %collective-permute-start.5 = (f32[2,256,128]{2,1,0:T(8,128)S(1)}, f32[2,256,128]{2,1,0:T(8,128)S(1)}, u32[]{:S(2)}, u32[]{:S(2)}) collective-permute-start(f32[2,256,128]{2,1,0:T(8,128)S(1)} %get-tuple-element.25), channel_id=1, source_target_pairs={{0,1},{2,3},{4,5},{6,7},{8,9},{10,11},{12,13},{14,15},{1,0},{3,2},... | collective-permute-start | bytes 786440 | tf_op jit(solution)/shard_map/ppermute | solution.py:296
  59.1 18.7 %all-to-all-start.1 = ((f32[16,16,128]{2,1,0:T(8,128)}), f32[16,16,128]{2,1,0:T(8,128)S(1)}, u32[]{:S(2)}, u32[]{:S(2)}) async-start(f32[16,16,128]{2,1,0:T(8,128)} %broadcast_in_dim.2), calls=%async_computation.1 | async-start | bytes 262144 | tf_op jit(solution)/shard_map/all_to_all | solution.py:359
  65.9 20.1 %collective-permute-start.6 = (f32[4,64,128]{2,1,0:T(8,128)S(1)}, f32[4,64,128]{2,1,0:T(8,128)S(1)}, u32[]{:S(2)}, u32[]{:S(2)}) collective-permute-start(f32[4,64,128]{2,1,0:T(8,128)S(1)} %get-tuple-element.27), channel_id=1, source_target_pairs={{16,32},{48,64},{80,96},{112,128},{144,160},{176,192},{208,224},{2... | collective-permute-start | bytes 393224 | tf_op jit(solution)/shard_map/ppermute | solution.py:305
  69.2 16.8 %collective-permute-start.7 = (f32[4,64,128]{2,1,0:T(8,128)S(1)}, f32[4,64,128]{2,1,0:T(8,128)S(1)}, u32[]{:S(2)}, u32[]{:S(2)}) collective-permute-start(f32[4,64,128]{2,1,0:T(8,128)S(1)} %get-tuple-element.28), channel_id=1, source_target_pairs={{0,16},{32,48},{64,80},{96,112},{128,144},{160,176},{192,208},{224... | collective-permute-start | bytes 393224 | tf_op jit(solution)/shard_map/ppermute | solution.py:305
  78.6 18.9 %all-to-all-start.2 = ((f32[32,32,128]{2,1,0:T(8,128)}), f32[32,32,128]{2,1,0:T(8,128)S(1)}, u32[]{:S(2)}, u32[]{:S(2)}) async-start(f32[32,32,128]{2,1,0:T(8,128)} %shard_map.83), calls=%async_computation.2 | async-start | bytes 1048576 | tf_op jit(solution)/shard_map/all_to_all | solution.py:367

commit v16 on v10

--- a/solution.py
+++ b/solution.py
@@ -68,6 +68,12 @@
     low = low_lanes(from_left.shape)
     real = jnp.where(low, from_right, from_left)
     return real, pltpu.roll(jnp.where(low, from_left, from_right), HALF, 1)
+
+
+def rows_kernel(tile, cross, mate):
+    even = even_row()
+    for p in range(4):
+        mate[p], cross[p] = by_parity(even, tile[p, HALF:], tile[p, :HALF])
 
 
 def columns_kernel(tile, from_cross, from_mate, tall, cross, mate):
@@ -297,10 +303,7 @@
     planes, strip, half = f32(4, TILE, TILE), f32(2, TILE, TILE), f32(4, HALF, TILE)
     tall, tall_strip = f32(4, 2 * TILE, TILE), f32(2, 2 * TILE, TILE)
 
-    upper = jnp.where(even_row(), 0, HALF)
-    cross = lax.dynamic_slice_in_dim(tile, upper, HALF, axis=1)
-    mate = lax.dynamic_slice_in_dim(tile, HALF - upper, HALF, axis=1)
-    rims = exchange(cross, mate, ROW_AXES)
+    rims = exchange(*call(rows_kernel, (half, half), [VM], tile), ROW_AXES)
     object_tall, cross, mate = call(
         columns_kernel, (tall, tall_strip, tall_strip), [VM] * 3, tile, *rims
     )

time: 99 us -> 98.3 us (level)
  waiting for transfers between devices: 27 us -> 26 us
    ppermute x4, starting transfers between devices: 15 us -> 17 us  [exchange(): from_mate = lax.ppermute(mate, axes, pairs + [(b, a) for a, b in pairs])]
    ppermute x4, waiting for transfers between devices: 3.99 us -> 2.24 us  [exchange(): from_cross = lax.ppermute(cross, axes, pairs + [(b, a) for a, b in pairs])]
    all_to_all x1, starting transfers between devices: 7.73 us -> 6.51 us  [body(): shares = lax.all_to_all(spread_share, FAR_AXES, 0, 0, tiled=True)]
    dynamic_slice x1 -> x0, local copies, waits for them, and re-layouts: 1.06 us -> none  [body(): mate = lax.dynamic_slice_in_dim(tile, HALF - upper, HALF, axis=1)]
    pallas_call x8 -> x9, Pallas kernels: 9.53 us -> 9.55 us  [call(): pl.pallas_call(kernel, out_shape=out_shape, in_specs=in_specs, out_specs=...]
where the time goes in v16:
time: 98.3 us; the launch traced here: 97.7 us
  starting transfers between devices  58.2 us (59%)
  waiting for transfers between devices  26 us (26%)
  Pallas kernels  9.55 us (10%)
  local copies, waits for them, and re-layouts  2.35 us (2%)
  between operations  1.47 us (1%)
    ppermute x4, starting transfers between devices, exchange(): from_mate = lax.ppermute(mate, axes, pairs + [(b, a) for a, b in pairs])  17 us
    all_to_all x1, starting transfers between devices, body(): lax.all_to_all(probe_part.reshape(near, rows, TILE), NEAR_AXES, 0, 0, til...  15.3 us
    ppermute x4, starting transfers between devices, exchange(): from_cross = lax.ppermute(cross, axes, pairs + [(b, a) for a, b in pairs])  13.1 us
    all_to_all x1, waiting for transfers between devices, body(): gathered = lax.all_to_all(spread_share, NEAR_AXES, 0, 0, tiled=True)  11.1 us
    pallas_call x9, Pallas kernels, call(): pl.pallas_call(kernel, out_shape=out_shape, in_specs=in_specs, out_specs=...  9.55 us
    all_to_all x1, starting transfers between devices, body(): shares = lax.all_to_all(spread_share, FAR_AXES, 0, 0, tiled=True)  6.51 us
    all_to_all x1, waiting for transfers between devices, body(): shares = lax.all_to_all(spread_share, FAR_AXES, 0, 0, tiled=True)  6.26 us
    all_to_all x1, starting transfers between devices, body(): gathered = lax.all_to_all(spread_share, NEAR_AXES, 0, 0, tiled=True)  6.24 us
  transfers between devices with their start and end apart: 11, of which 5 were waited for; matrix products, arithmetic and copies ran while one was open for 1% of the time, Pallas kernels for 3%

profile of v16, /device:TPU:1, one launch (start us, length us, event | category | flops | bytes accessed | tf_op | source)
XLA Modules:
  0.0 97.7 jit_solution(15884441307332318610)
XLA Ops:
  0.6 0.9 copy-done
  1.6 0.8 collective-permute-start
  2.4 7.4 %collective-permute-start.1 = (f32[4,64,128]{2,1,0:T(8,128)S(1)}, f32[4,64,128]{2,1,0:T(8,128)S(1)}, u32[]{:S(2)}, u32[]{:S(2)}) collective-permute-start(f32[4,64,128]{2,1,0:T(8,128)S(1)} %get-tuple-element.19), channel_id=1, source_target_pairs={{0,16},{32,48},{64,80},{96,112},{128,144},{160,176},{192,208},{224... | collective-permute-start | bytes 393224 | tf_op jit(solution)/shard_map/ppermute | solution.py:293
  9.8 2.3 %collective-permute-done.1.from_mate = f32[4,64,128]{2,1,0:T(8,128)S(1)} collective-permute-done((f32[4,64,128]{2,1,0:T(8,128)S(1)}, f32[4,64,128]{2,1,0:T(8,128)S(1)}, u32[]{:S(2)}, u32[]{:S(2)}) %collective-permute-start.1) | collective-permute-done | bytes 131104 | tf_op jit(solution)/shard_map/ppermute | solution.py:293
  12.3 6.6 %collective-permute-start.2 = (f32[2,256,128]{2,1,0:T(8,128)S(1)}, f32[2,256,128]{2,1,0:T(8,128)S(1)}, u32[]{:S(2)}, u32[]{:S(2)}) collective-permute-start(f32[2,256,128]{2,1,0:T(8,128)S(1)} %get-tuple-element.21), channel_id=1, source_target_pairs={{1,2},{3,4},{5,6},{7,8},{9,10},{11,12},{13,14},{2,1},{4,3},{6,5},{... | collective-permute-start | bytes 786440 | tf_op jit(solution)/shard_map/ppermute | solution.py:291
  19.0 1.9 %collective-permute-start.3 = (f32[2,256,128]{2,1,0:T(8,128)S(1)}, f32[2,256,128]{2,1,0:T(8,128)S(1)}, u32[]{:S(2)}, u32[]{:S(2)}) collective-permute-start(f32[2,256,128]{2,1,0:T(8,128)S(1)} %get-tuple-element.22), channel_id=1, source_target_pairs={{0,1},{2,3},{4,5},{6,7},{8,9},{10,11},{12,13},{14,15},{1,0},{3,2},... | collective-permute-start | bytes 786440 | tf_op jit(solution)/shard_map/ppermute | solution.py:293
  21.6 0.7 copy-done.3
  22.6 2.2 %collective-permute-done.2.from_cross = f32[2,256,128]{2,1,0:T(8,128)S(1)} collective-permute-done((f32[2,256,128]{2,1,0:T(8,128)S(1)}, f32[2,256,128]{2,1,0:T(8,128)S(1)}, u32[]{:S(2)}, u32[]{:S(2)}) %collective-permute-start.2) | collective-permute-done | bytes 262176 | tf_op jit(solution)/shard_map/ppermute | solution.py:291
  24.9 5.6 %shard_map.80 = (f32[8,128,128]{2,1,0:T(8,128)}, f32[2,4,128,128]{3,2,1,0:T(8,128)S(1)}) custom-call(s32[4]{0:T(128)S(1)} %reshape.30.offsets, s32[1,1]{1,0:T(1,128)S(6)} %copy.8.counts, f32[4,256,128]{2,1,0:T(8,128)S(1)} %get-tuple-element.20.tall, f32[2,256,128]{2,1,0:T(8,128)S(1)} %collective-permute-done.2.from_cross, ...), custom_call_target="tpu_custom_call" | custom-call | flops 3200000000 | bytes 4000000 | tf_op jit(solution)/shard_map/pallas_call | solution.py:29
  30.5 15.3 %all-to-all-start = ((f32[64,16,128]{2,1,0:T(8,128)}), f32[64,16,128]{2,1,0:T(8,128)S(1)}, u32[]{:S(2)}, u32[]{:S(2)}) async-start(f32[64,16,128]{2,1,0:T(8,128)} %bitcast.4), calls=%async_computation | async-start | bytes 1048576 | tf_op jit(solution)/shard_map/all_to_all | solution.py:341
  45.8 0.9 shard_map.81
  46.7 5.0 %collective-permute-start.4 = (f32[2,256,128]{2,1,0:T(8,128)S(1)}, f32[2,256,128]{2,1,0:T(8,128)S(1)}, u32[]{:S(2)}, u32[]{:S(2)}) collective-permute-start(f32[2,256,128]{2,1,0:T(8,128)S(1)} %get-tuple-element.28), channel_id=1, source_target_pairs={{1,2},{3,4},{5,6},{7,8},{9,10},{11,12},{13,14},{2,1},{4,3},{6,5},{... | collective-permute-start | bytes 786440 | tf_op jit(solution)/shard_map/ppermute | solution.py:291
  51.7 1.9 %collective-permute-start.5 = (f32[2,256,128]{2,1,0:T(8,128)S(1)}, f32[2,256,128]{2,1,0:T(8,128)S(1)}, u32[]{:S(2)}, u32[]{:S(2)}) collective-permute-start(f32[2,256,128]{2,1,0:T(8,128)S(1)} %get-tuple-element.29), channel_id=1, source_target_pairs={{0,1},{2,3},{4,5},{6,7},{8,9},{10,11},{12,13},{14,15},{1,0},{3,2},... | collective-permute-start | bytes 786440 | tf_op jit(solution)/shard_map/ppermute | solution.py:293
  53.7 4.1 %all-to-all-done = f32[64,16,128]{2,1,0:T(8,128)S(1)} async-done(((f32[64,16,128]{2,1,0:T(8,128)}), f32[64,16,128]{2,1,0:T(8,128)S(1)}, u32[]{:S(2)}, u32[]{:S(2)}) %all-to-all-start) | async-done | bytes 524320 | tf_op jit(solution)/shard_map/all_to_all | solution.py:341
  57.8 0.6 broadcast_in_dim.2
  58.5 6.5 %all-to-all-start.1 = ((f32[8,16,128]{2,1,0:T(8,128)}), f32[8,16,128]{2,1,0:T(8,128)S(1)}, u32[]{:S(2)}, u32[]{:S(2)}) async-start(f32[8,16,128]{2,1,0:T(8,128)} %broadcast_in_dim.2), calls=%async_computation.1 | async-start | bytes 131072 | tf_op jit(solution)/shard_map/all_to_all | solution.py:344
  65.2 0.7 collective-permute-start.6
  65.8 5.8 %collective-permute-start.7 = (f32[4,64,128]{2,1,0:T(8,128)S(1)}, f32[4,64,128]{2,1,0:T(8,128)S(1)}, u32[]{:S(2)}, u32[]{:S(2)}) collective-permute-start(f32[4,64,128]{2,1,0:T(8,128)S(1)} %get-tuple-element.32), channel_id=1, source_target_pairs={{0,16},{32,48},{64,80},{96,112},{128,144},{160,176},{192,208},{224... | collective-permute-start | bytes 393224 | tf_op jit(solution)/shard_map/ppermute | solution.py:293
  71.6 6.3 %all-to-all-done.1.shares = f32[8,16,128]{2,1,0:T(8,128)S(1)} async-done(((f32[8,16,128]{2,1,0:T(8,128)}), f32[8,16,128]{2,1,0:T(8,128)S(1)}, u32[]{:S(2)}, u32[]{:S(2)}) %all-to-all-start.1) | async-done | bytes 65568 | tf_op jit(solution)/shard_map/all_to_all | solution.py:344
  77.9 0.8 shard_map.84
  78.7 6.2 %all-to-all-start.2 = ((f32[64,16,128]{2,1,0:T(8,128)}), f32[64,16,128]{2,1,0:T(8,128)S(1)}, u32[]{:S(2)}, u32[]{:S(2)}) async-start(f32[64,16,128]{2,1,0:T(8,128)} %shard_map.84), calls=%async_computation.2 | async-start | bytes 1048576 | tf_op jit(solution)/shard_map/all_to_all | solution.py:352
  85.0 0.7 shard_map.83
  85.7 11.1 %all-to-all-done.2 = f32[64,16,128]{2,1,0:T(8,128)S(1)} async-done(((f32[64,16,128]{2,1,0:T(8,128)}), f32[64,16,128]{2,1,0:T(8,128)S(1)}, u32[]{:S(2)}, u32[]{:S(2)}) %all-to-all-start.2) | async-done | bytes 524320 | tf_op jit(solution)/shard_map/all_to_all | solution.py:352
  96.8 0.8 shard_map.85
  (20 shorter events, 0.8 us)
Async XLA Ops:
  0.6 1.0 copy-start
  1.6 20.1 %copy-start.1 = (f32[2,4,128,128]{3,2,1,0:T(8,128)S(1)}, f32[2,4,128,128]{3,2,1,0:T(8,128)}, u32[]{:S(2)}) copy-start(f32[2,4,128,128]{3,2,1,0:T(8,128)} %param.7) | copy-start | bytes 1572868
  1.6 8.2 %collective-permute-start = (f32[4,64,128]{2,1,0:T(8,128)S(1)}, f32[4,64,128]{2,1,0:T(8,128)S(1)}, u32[]{:S(2)}, u32[]{:S(2)}) collective-permute-start(f32[4,64,128]{2,1,0:T(8,128)S(1)} %get-tuple-element.18), channel_id=1, source_target_pairs={{16,32},{48,64},{80,96},{112,128},{144,160},{176,192},{208,224},{2... | collective-permute-start | bytes 393224 | tf_op jit(solution)/shard_map/ppermute | solution.py:291
  2.4 19.2 %copy-start.2 = (f32[1,1,2,128,128]{4,3,2,1,0:T(8,128)S(1)}, f32[1,1,2,128,128]{4,3,2,1,0:T(8,128)}, u32[]{:S(2)}) copy-start(f32[1,1,2,128,128]{4,3,2,1,0:T(8,128)} %param.9) | copy-start | bytes 393220
  2.4 9.7 %collective-permute-start.1 = (f32[4,64,128]{2,1,0:T(8,128)S(1)}, f32[4,64,128]{2,1,0:T(8,128)S(1)}, u32[]{:S(2)}, u32[]{:S(2)}) collective-permute-start(f32[4,64,128]{2,1,0:T(8,128)S(1)} %get-tuple-element.19), channel_id=1, source_target_pairs={{0,16},{32,48},{64,80},{96,112},{128,144},{160,176},{192,208},{224... | collective-permute-start | bytes 393224 | tf_op jit(solution)/shard_map/ppermute | solution.py:293
  12.3 12.6 %collective-permute-start.2 = (f32[2,256,128]{2,1,0:T(8,128)S(1)}, f32[2,256,128]{2,1,0:T(8,128)S(1)}, u32[]{:S(2)}, u32[]{:S(2)}) collective-permute-start(f32[2,256,128]{2,1,0:T(8,128)S(1)} %get-tuple-element.21), channel_id=1, source_target_pairs={{1,2},{3,4},{5,6},{7,8},{9,10},{11,12},{13,14},{2,1},{4,3},{6,5},{... | collective-permute-start | bytes 786440 | tf_op jit(solution)/shard_map/ppermute | solution.py:291
  19.0 2.6 %copy-start.4 = (s32[1,1,2,2]{3,2,1,0:T(2,128)S(1)}, s32[1,1,2,2]{3,2,1,0:T(2,128)}, u32[]{:S(2)}) copy-start(s32[1,1,2,2]{3,2,1,0:T(2,128)} %param.10) | copy-start | bytes 52
  19.0 5.9 %collective-permute-start.3 = (f32[2,256,128]{2,1,0:T(8,128)S(1)}, f32[2,256,128]{2,1,0:T(8,128)S(1)}, u32[]{:S(2)}, u32[]{:S(2)}) collective-permute-start(f32[2,256,128]{2,1,0:T(8,128)S(1)} %get-tuple-element.22), channel_id=1, source_target_pairs={{0,1},{2,3},{4,5},{6,7},{8,9},{10,11},{12,13},{14,15},{1,0},{3,2},... | collective-permute-start | bytes 786440 | tf_op jit(solution)/shard_map/ppermute | solution.py:293
  21.6 0.7 copy-start.3
  30.5 27.3 %all-to-all-start = ((f32[64,16,128]{2,1,0:T(8,128)}), f32[64,16,128]{2,1,0:T(8,128)S(1)}, u32[]{:S(2)}, u32[]{:S(2)}) async-start(f32[64,16,128]{2,1,0:T(8,128)} %bitcast.4), calls=%async_computation | async-start | bytes 1048576 | tf_op jit(solution)/shard_map/all_to_all | solution.py:341
  46.7 18.3 %collective-permute-start.4 = (f32[2,256,128]{2,1,0:T(8,128)S(1)}, f32[2,256,128]{2,1,0:T(8,128)S(1)}, u32[]{:S(2)}, u32[]{:S(2)}) collective-permute-start(f32[2,256,128]{2,1,0:T(8,128)S(1)} %get-tuple-element.28), channel_id=1, source_target_pairs={{1,2},{3,4},{5,6},{7,8},{9,10},{11,12},{13,14},{2,1},{4,3},{6,5},{... | collective-permute-start | bytes 786440 | tf_op jit(solution)/shard_map/ppermute | solution.py:291
  51.7 13.3 %collective-permute-start.5 = (f32[2,256,128]{2,1,0:T(8,128)S(1)}, f32[2,256,128]{2,1,0:T(8,128)S(1)}, u32[]{:S(2)}, u32[]{:S(2)}) collective-permute-start(f32[2,256,128]{2,1,0:T(8,128)S(1)} %get-tuple-element.29), channel_id=1, source_target_pairs={{0,1},{2,3},{4,5},{6,7},{8,9},{10,11},{12,13},{14,15},{1,0},{3,2},... | collective-permute-start | bytes 786440 | tf_op jit(solution)/shard_map/ppermute | solution.py:293
  58.5 19.4 %all-to-all-start.1 = ((f32[8,16,128]{2,1,0:T(8,128)}), f32[8,16,128]{2,1,0:T(8,128)S(1)}, u32[]{:S(2)}, u32[]{:S(2)}) async-start(f32[8,16,128]{2,1,0:T(8,128)} %broadcast_in_dim.2), calls=%async_computation.1 | async-start | bytes 131072 | tf_op jit(solution)/shard_map/all_to_all | solution.py:344
  65.2 19.8 %collective-permute-start.6 = (f32[4,64,128]{2,1,0:T(8,128)S(1)}, f32[4,64,128]{2,1,0:T(8,128)S(1)}, u32[]{:S(2)}, u32[]{:S(2)}) collective-permute-start(f32[4,64,128]{2,1,0:T(8,128)S(1)} %get-tuple-element.31), channel_id=1, source_target_pairs={{16,32},{48,64},{80,96},{112,128},{144,160},{176,192},{208,224},{2... | collective-permute-start | bytes 393224 | tf_op jit(solution)/shard_map/ppermute | solution.py:291
  65.8 19.2 %collective-permute-start.7 = (f32[4,64,128]{2,1,0:T(8,128)S(1)}, f32[4,64,128]{2,1,0:T(8,128)S(1)}, u32[]{:S(2)}, u32[]{:S(2)}) collective-permute-start(f32[4,64,128]{2,1,0:T(8,128)S(1)} %get-tuple-element.32), channel_id=1, source_target_pairs={{0,16},{32,48},{64,80},{96,112},{128,144},{160,176},{192,208},{224... | collective-permute-start | bytes 393224 | tf_op jit(solution)/shard_map/ppermute | solution.py:293
  78.7 18.1 %all-to-all-start.2 = ((f32[64,16,128]{2,1,0:T(8,128)}), f32[64,16,128]{2,1,0:T(8,128)S(1)}, u32[]{:S(2)}, u32[]{:S(2)}) async-start(f32[64,16,128]{2,1,0:T(8,128)} %shard_map.84), calls=%async_computation.2 | async-start | bytes 1048576 | tf_op jit(solution)/shard_map/all_to_all | solution.py:352

commit v17 on v9

--- a/solution.py
+++ b/solution.py
@@ -76,17 +76,26 @@
         mate[p], cross[p] = by_parity(even, tile[p, HALF:], tile[p, :HALF])
 
 
-def columns_kernel(tile, from_cross, from_mate, tall, cross, mate):
+def tall_kernel(tile, from_cross, from_mate, tall):
     even = even_row()
     for p in range(4):
         below, above = by_parity(even, from_mate[p], from_cross[p])
         tall[p, :HALF] = above
         tall[p, HALF:HALF + TILE] = tile[p]
         tall[p, HALF + TILE:] = below
-    even = even_column()
+
+
+def columns_kernel(tile, from_cross, from_mate, cross, mate):
+    down, even = even_row(), even_column()
     for s in range(2):
-        to_right, to_left = pack_columns(tall[s], tall[2 + s])
-        mate[s], cross[s] = by_parity(even, to_right, to_left)
+        ends = [by_parity(down, from_mate[p], from_cross[p]) for p in (s, 2 + s)]
+        for start, end, planes in (
+            (0, HALF, (ends[0][1], ends[1][1])),
+            (HALF, HALF + TILE, (tile[s], tile[2 + s])),
+            (HALF + TILE, 2 * TILE, (ends[0][0], ends[1][0])),
+        ):
+            to_right, to_left = pack_columns(*planes)
+            mate[s, start:end], cross[s, start:end] = by_parity(even, to_right, to_left)
 
 
 def operator_kernel(taps, probe, measured, ops, probe_near, measured_near, padded):
@@ -305,9 +314,8 @@
     tall, tall_strip = f32(4, 2 * TILE, TILE), f32(2, 2 * TILE, TILE)
 
     rims = exchange(*call(rows_kernel, (half, half), [VM], tile), ROW_AXES)
-    object_tall, cross, mate = call(
-        columns_kernel, (tall, tall_strip, tall_strip), [VM] * 3, tile, *rims
-    )
+    cross, mate = call(columns_kernel, (tall_strip, tall_strip), [VM] * 3, tile, *rims)
+    (object_tall,) = call(tall_kernel, (tall,), [VM] * 3, tile, *rims)
     strips = exchange(cross, mate, COL_AXES)
     ops, probe, targets = call(
         operator_kernel,

time: 98.4 us -> 98.5 us (level)
    unnamed x10 -> x12, local copies, waits for them, and re-layouts: 1.64 us -> 2.25 us
    pallas_call x10 -> x11, Pallas kernels: 9.66 us -> 9.77 us  [call(): pl.pallas_call(kernel, out_shape=out_shape, in_specs=in_specs, out_specs=...]
where the time goes in v17:
time: 98.5 us; the launch traced here: 97.8 us
  starting transfers between devices  58.2 us (59%)
  waiting for transfers between devices  26.1 us (26%)
  Pallas kernels  9.77 us (10%)
  local copies, waits for them, and re-layouts  2.34 us (2%)
  between operations  1.48 us (2%)
    ppermute x4, starting transfers between devices, exchange(): from_mate = lax.ppermute(mate, axes, pairs + [(b, a) for a, b in pairs])  17 us
    all_to_all x1, starting transfers between devices, body(): lax.all_to_all(probe_part.reshape(near, rows, TILE), NEAR_AXES, 0, 0, til...  15.3 us
    ppermute x4, starting transfers between devices, exchange(): from_cross = lax.ppermute(cross, axes, pairs + [(b, a) for a, b in pairs])  13.1 us
    all_to_all x1, waiting for transfers between devices, body(): gathered = lax.all_to_all(spread_share, NEAR_AXES, 0, 0, tiled=True)  11.8 us
    pallas_call x11, Pallas kernels, call(): pl.pallas_call(kernel, out_shape=out_shape, in_specs=in_specs, out_specs=...  9.77 us
    all_to_all x1, starting transfers between devices, body(): shares = lax.all_to_all(spread_share, FAR_AXES, 0, 0, tiled=True)  6.51 us
    all_to_all x1, waiting for transfers between devices, body(): shares = lax.all_to_all(spread_share, FAR_AXES, 0, 0, tiled=True)  6.26 us
    all_to_all x1, starting transfers between devices, body(): gathered = lax.all_to_all(spread_share, NEAR_AXES, 0, 0, tiled=True)  6.24 us
  transfers between devices with their start and end apart: 11, of which 5 were waited for; matrix products, arithmetic and copies ran while one was open for 0% of the time, Pallas kernels for 3%

profile of v17, /device:TPU:1, one launch (start us, length us, event | category | flops | bytes accessed | tf_op | source)
XLA Modules:
  0.0 97.8 jit_solution(12138187867331124483)
XLA Ops:
  0.6 0.9 copy-done
  1.6 0.8 collective-permute-start
  2.4 7.4 %collective-permute-start.1 = (f32[4,64,128]{2,1,0:T(8,128)S(1)}, f32[4,64,128]{2,1,0:T(8,128)S(1)}, u32[]{:S(2)}, u32[]{:S(2)}) collective-permute-start(f32[4,64,128]{2,1,0:T(8,128)S(1)} %get-tuple-element.20), channel_id=1, source_target_pairs={{0,16},{32,48},{64,80},{96,112},{128,144},{160,176},{192,208},{224... | collective-permute-start | bytes 393224 | tf_op jit(solution)/shard_map/ppermute | solution.py:303
  9.8 2.3 %collective-permute-done.1.from_mate = f32[4,64,128]{2,1,0:T(8,128)S(1)} collective-permute-done((f32[4,64,128]{2,1,0:T(8,128)S(1)}, f32[4,64,128]{2,1,0:T(8,128)S(1)}, u32[]{:S(2)}, u32[]{:S(2)}) %collective-permute-start.1) | collective-permute-done | bytes 131104 | tf_op jit(solution)/shard_map/ppermute | solution.py:303
  12.3 6.6 %collective-permute-start.2 = (f32[2,256,128]{2,1,0:T(8,128)S(1)}, f32[2,256,128]{2,1,0:T(8,128)S(1)}, u32[]{:S(2)}, u32[]{:S(2)}) collective-permute-start(f32[2,256,128]{2,1,0:T(8,128)S(1)} %get-tuple-element.21), channel_id=1, source_target_pairs={{1,2},{3,4},{5,6},{7,8},{9,10},{11,12},{13,14},{2,1},{4,3},{6,5},{... | collective-permute-start | bytes 786440 | tf_op jit(solution)/shard_map/ppermute | solution.py:301
  19.0 1.9 %collective-permute-start.3 = (f32[2,256,128]{2,1,0:T(8,128)S(1)}, f32[2,256,128]{2,1,0:T(8,128)S(1)}, u32[]{:S(2)}, u32[]{:S(2)}) collective-permute-start(f32[2,256,128]{2,1,0:T(8,128)S(1)} %get-tuple-element.22), channel_id=1, source_target_pairs={{0,1},{2,3},{4,5},{6,7},{8,9},{10,11},{12,13},{14,15},{1,0},{3,2},... | collective-permute-start | bytes 786440 | tf_op jit(solution)/shard_map/ppermute | solution.py:303
  21.6 0.7 copy-done.4
  22.7 0.6 copy-done.1
  23.3 1.6 %collective-permute-done.2.from_cross = f32[2,256,128]{2,1,0:T(8,128)S(1)} collective-permute-done((f32[2,256,128]{2,1,0:T(8,128)S(1)}, f32[2,256,128]{2,1,0:T(8,128)S(1)}, u32[]{:S(2)}, u32[]{:S(2)}) %collective-permute-start.2) | collective-permute-done | bytes 262176 | tf_op jit(solution)/shard_map/ppermute | solution.py:301
  24.9 5.7 %shard_map.81 = (f32[8,128,128]{2,1,0:T(8,128)}, f32[2,4,128,128]{3,2,1,0:T(8,128)S(1)}) custom-call(s32[4]{0:T(128)S(1)} %reshape.29.offsets, s32[1,1]{1,0:T(1,128)S(6)} %copy.8.counts, f32[4,256,128]{2,1,0:T(8,128)S(1)} %shard_map.78.tall, f32[2,256,128]{2,1,0:T(8,128)S(1)} %collective-permute-done.2.from_cross, ...), custom_call_target="tpu_custom_call" | custom-call | flops 3200000000 | bytes 4000000 | tf_op jit(solution)/shard_map/pallas_call | solution.py:29
  30.5 15.3 %all-to-all-start = ((f32[64,16,128]{2,1,0:T(8,128)}), f32[64,16,128]{2,1,0:T(8,128)S(1)}, u32[]{:S(2)}, u32[]{:S(2)}) async-start(f32[64,16,128]{2,1,0:T(8,128)} %bitcast.3), calls=%async_computation | async-start | bytes 1048576 | tf_op jit(solution)/shard_map/all_to_all | solution.py:350
  45.8 0.9 shard_map.82
  46.8 5.0 %collective-permute-start.4 = (f32[2,256,128]{2,1,0:T(8,128)S(1)}, f32[2,256,128]{2,1,0:T(8,128)S(1)}, u32[]{:S(2)}, u32[]{:S(2)}) collective-permute-start(f32[2,256,128]{2,1,0:T(8,128)S(1)} %get-tuple-element.28), channel_id=1, source_target_pairs={{1,2},{3,4},{5,6},{7,8},{9,10},{11,12},{13,14},{2,1},{4,3},{6,5},{... | collective-permute-start | bytes 786440 | tf_op jit(solution)/shard_map/ppermute | solution.py:301
  51.8 1.9 %collective-permute-start.5 = (f32[2,256,128]{2,1,0:T(8,128)S(1)}, f32[2,256,128]{2,1,0:T(8,128)S(1)}, u32[]{:S(2)}, u32[]{:S(2)}) collective-permute-start(f32[2,256,128]{2,1,0:T(8,128)S(1)} %get-tuple-element.29), channel_id=1, source_target_pairs={{0,1},{2,3},{4,5},{6,7},{8,9},{10,11},{12,13},{14,15},{1,0},{3,2},... | collective-permute-start | bytes 786440 | tf_op jit(solution)/shard_map/ppermute | solution.py:303
  53.7 4.1 %all-to-all-done.shares = f32[64,16,128]{2,1,0:T(8,128)S(1)} async-done(((f32[64,16,128]{2,1,0:T(8,128)}), f32[64,16,128]{2,1,0:T(8,128)S(1)}, u32[]{:S(2)}, u32[]{:S(2)}) %all-to-all-start) | async-done | bytes 524320 | tf_op jit(solution)/shard_map/all_to_all | solution.py:350
  57.8 0.7 shard_map.85
  58.5 6.5 %all-to-all-start.1 = ((f32[8,16,128]{2,1,0:T(8,128)}), f32[8,16,128]{2,1,0:T(8,128)S(1)}, u32[]{:S(2)}, u32[]{:S(2)}) async-start(f32[8,16,128]{2,1,0:T(8,128)} %shard_map.85), calls=%async_computation.1 | async-start | bytes 131072 | tf_op jit(solution)/shard_map/all_to_all | solution.py:355
  65.2 0.7 collective-permute-start.6
  65.9 5.8 %collective-permute-start.7 = (f32[4,64,128]{2,1,0:T(8,128)S(1)}, f32[4,64,128]{2,1,0:T(8,128)S(1)}, u32[]{:S(2)}, u32[]{:S(2)}) collective-permute-start(f32[4,64,128]{2,1,0:T(8,128)S(1)} %get-tuple-element.32), channel_id=1, source_target_pairs={{0,16},{32,48},{64,80},{96,112},{128,144},{160,176},{192,208},{224... | collective-permute-start | bytes 393224 | tf_op jit(solution)/shard_map/ppermute | solution.py:303
  71.7 6.3 %all-to-all-done.1.shares = f32[8,16,128]{2,1,0:T(8,128)S(1)} async-done(((f32[8,16,128]{2,1,0:T(8,128)}), f32[8,16,128]{2,1,0:T(8,128)S(1)}, u32[]{:S(2)}, u32[]{:S(2)}) %all-to-all-start.1) | async-done | bytes 65568 | tf_op jit(solution)/shard_map/all_to_all | solution.py:355
  77.9 0.8 shard_map.86
  78.8 6.2 %all-to-all-start.2 = ((f32[64,16,128]{2,1,0:T(8,128)}), f32[64,16,128]{2,1,0:T(8,128)S(1)}, u32[]{:S(2)}, u32[]{:S(2)}) async-start(f32[64,16,128]{2,1,0:T(8,128)} %shard_map.86), calls=%async_computation.2 | async-start | bytes 1048576 | tf_op jit(solution)/shard_map/all_to_all | solution.py:363
  85.1 11.8 %all-to-all-done.2 = f32[64,16,128]{2,1,0:T(8,128)S(1)} async-done(((f32[64,16,128]{2,1,0:T(8,128)}), f32[64,16,128]{2,1,0:T(8,128)S(1)}, u32[]{:S(2)}, u32[]{:S(2)}) %all-to-all-start.2) | async-done | bytes 524320 | tf_op jit(solution)/shard_map/all_to_all | solution.py:363
  96.9 0.9 shard_map.87
  (22 shorter events, 0.8 us)
Async XLA Ops:
  0.6 1.0 copy-start
  1.6 20.1 %copy-start.2 = (f32[2,4,128,128]{3,2,1,0:T(8,128)S(1)}, f32[2,4,128,128]{3,2,1,0:T(8,128)}, u32[]{:S(2)}) copy-start(f32[2,4,128,128]{3,2,1,0:T(8,128)} %param.7) | copy-start | bytes 1572868
  1.6 8.2 %collective-permute-start = (f32[4,64,128]{2,1,0:T(8,128)S(1)}, f32[4,64,128]{2,1,0:T(8,128)S(1)}, u32[]{:S(2)}, u32[]{:S(2)}) collective-permute-start(f32[4,64,128]{2,1,0:T(8,128)S(1)} %get-tuple-element.19), channel_id=1, source_target_pairs={{16,32},{48,64},{80,96},{112,128},{144,160},{176,192},{208,224},{2... | collective-permute-start | bytes 393224 | tf_op jit(solution)/shard_map/ppermute | solution.py:301
  2.4 19.2 %copy-start.3 = (f32[1,1,2,128,128]{4,3,2,1,0:T(8,128)S(1)}, f32[1,1,2,128,128]{4,3,2,1,0:T(8,128)}, u32[]{:S(2)}) copy-start(f32[1,1,2,128,128]{4,3,2,1,0:T(8,128)} %param.9) | copy-start | bytes 393220
  2.4 9.7 %collective-permute-start.1 = (f32[4,64,128]{2,1,0:T(8,128)S(1)}, f32[4,64,128]{2,1,0:T(8,128)S(1)}, u32[]{:S(2)}, u32[]{:S(2)}) collective-permute-start(f32[4,64,128]{2,1,0:T(8,128)S(1)} %get-tuple-element.20), channel_id=1, source_target_pairs={{0,16},{32,48},{64,80},{96,112},{128,144},{160,176},{192,208},{224... | collective-permute-start | bytes 393224 | tf_op jit(solution)/shard_map/ppermute | solution.py:303
  12.3 12.6 %collective-permute-start.2 = (f32[2,256,128]{2,1,0:T(8,128)S(1)}, f32[2,256,128]{2,1,0:T(8,128)S(1)}, u32[]{:S(2)}, u32[]{:S(2)}) collective-permute-start(f32[2,256,128]{2,1,0:T(8,128)S(1)} %get-tuple-element.21), channel_id=1, source_target_pairs={{1,2},{3,4},{5,6},{7,8},{9,10},{11,12},{13,14},{2,1},{4,3},{6,5},{... | collective-permute-start | bytes 786440 | tf_op jit(solution)/shard_map/ppermute | solution.py:301
  19.0 2.6 %copy-start.5 = (s32[1,1,2,2]{3,2,1,0:T(2,128)S(1)}, s32[1,1,2,2]{3,2,1,0:T(2,128)}, u32[]{:S(2)}) copy-start(s32[1,1,2,2]{3,2,1,0:T(2,128)} %param.10) | copy-start | bytes 52
  19.0 5.9 %collective-permute-start.3 = (f32[2,256,128]{2,1,0:T(8,128)S(1)}, f32[2,256,128]{2,1,0:T(8,128)S(1)}, u32[]{:S(2)}, u32[]{:S(2)}) collective-permute-start(f32[2,256,128]{2,1,0:T(8,128)S(1)} %get-tuple-element.22), channel_id=1, source_target_pairs={{0,1},{2,3},{4,5},{6,7},{8,9},{10,11},{12,13},{14,15},{1,0},{3,2},... | collective-permute-start | bytes 786440 | tf_op jit(solution)/shard_map/ppermute | solution.py:303
  21.6 0.7 copy-start.4
  22.3 0.9 copy-start.1
  30.5 27.3 %all-to-all-start = ((f32[64,16,128]{2,1,0:T(8,128)}), f32[64,16,128]{2,1,0:T(8,128)S(1)}, u32[]{:S(2)}, u32[]{:S(2)}) async-start(f32[64,16,128]{2,1,0:T(8,128)} %bitcast.3), calls=%async_computation | async-start | bytes 1048576 | tf_op jit(solution)/shard_map/all_to_all | solution.py:350
  46.8 18.3 %collective-permute-start.4 = (f32[2,256,128]{2,1,0:T(8,128)S(1)}, f32[2,256,128]{2,1,0:T(8,128)S(1)}, u32[]{:S(2)}, u32[]{:S(2)}) collective-permute-start(f32[2,256,128]{2,1,0:T(8,128)S(1)} %get-tuple-element.28), channel_id=1, source_target_pairs={{1,2},{3,4},{5,6},{7,8},{9,10},{11,12},{13,14},{2,1},{4,3},{6,5},{... | collective-permute-start | bytes 786440 | tf_op jit(solution)/shard_map/ppermute | solution.py:301
  51.8 13.2 %collective-permute-start.5 = (f32[2,256,128]{2,1,0:T(8,128)S(1)}, f32[2,256,128]{2,1,0:T(8,128)S(1)}, u32[]{:S(2)}, u32[]{:S(2)}) collective-permute-start(f32[2,256,128]{2,1,0:T(8,128)S(1)} %get-tuple-element.29), channel_id=1, source_target_pairs={{0,1},{2,3},{4,5},{6,7},{8,9},{10,11},{12,13},{14,15},{1,0},{3,2},... | collective-permute-start | bytes 786440 | tf_op jit(solution)/shard_map/ppermute | solution.py:303
  58.5 19.4 %all-to-all-start.1 = ((f32[8,16,128]{2,1,0:T(8,128)}), f32[8,16,128]{2,1,0:T(8,128)S(1)}, u32[]{:S(2)}, u32[]{:S(2)}) async-start(f32[8,16,128]{2,1,0:T(8,128)} %shard_map.85), calls=%async_computation.1 | async-start | bytes 131072 | tf_op jit(solution)/shard_map/all_to_all | solution.py:355
  65.2 19.8 %collective-permute-start.6 = (f32[4,64,128]{2,1,0:T(8,128)S(1)}, f32[4,64,128]{2,1,0:T(8,128)S(1)}, u32[]{:S(2)}, u32[]{:S(2)}) collective-permute-start(f32[4,64,128]{2,1,0:T(8,128)S(1)} %get-tuple-element.31), channel_id=1, source_target_pairs={{16,32},{48,64},{80,96},{112,128},{144,160},{176,192},{208,224},{2... | collective-permute-start | bytes 393224 | tf_op jit(solution)/shard_map/ppermute | solution.py:301
  65.9 19.2 %collective-permute-start.7 = (f32[4,64,128]{2,1,0:T(8,128)S(1)}, f32[4,64,128]{2,1,0:T(8,128)S(1)}, u32[]{:S(2)}, u32[]{:S(2)}) collective-permute-start(f32[4,64,128]{2,1,0:T(8,128)S(1)} %get-tuple-element.32), channel_id=1, source_target_pairs={{0,16},{32,48},{64,80},{96,112},{128,144},{160,176},{192,208},{224... | collective-permute-start | bytes 393224 | tf_op jit(solution)/shard_map/ppermute | solution.py:303
  78.8 18.1 %all-to-all-start.2 = ((f32[64,16,128]{2,1,0:T(8,128)}), f32[64,16,128]{2,1,0:T(8,128)S(1)}, u32[]{:S(2)}, u32[]{:S(2)}) async-start(f32[64,16,128]{2,1,0:T(8,128)} %shard_map.86), calls=%async_computation.2 | async-start | bytes 1048576 | tf_op jit(solution)/shard_map/all_to_all | solution.py:363
